TPU v7x, 32 devices: a whole 2x2x4 slice. The times are simulated.
32 devices in a mesh: dp: 8 (over z, y), tensor: 4 (over x, core).
Axes of the slice: x: 2, y: 2, z: 4, core: 2. Of those that a mesh axis runs over, the one named last changes fastest.
Arguments:
- x_in: bfloat16 [2048, 5120], P('dp', 'tensor'), parts along dimension 0, may hold values from -6 to 6
- out_grad: bfloat16 [2048, 5120], P('dp', 'tensor'), parts along dimension 0, may hold values from -6 to 6
- gate_pre: bfloat16 [2048, 18432], P('dp', 'tensor'), parts along dimension 0, may hold values from -6 to 6
- up_pre: bfloat16 [2048, 18432], P('dp', 'tensor'), parts along dimension 0, may hold values from -6 to 6
- down_weight: bfloat16 [18432, 5120], P('tensor'), may hold values from -0.046875 to 0.046875
- x_factor: bfloat16 [5120, 64], P('tensor'), may hold values from -0.078125 to 0.078125
- gate_factor: bfloat16 [18432, 64], P('tensor'), may hold values from -0.046875 to 0.046875
- up_factor: bfloat16 [18432, 64], P('tensor'), may hold values from -0.046875 to 0.046875
- h_factor: bfloat16 [18432, 64], P('tensor'), may hold values from -0.046875 to 0.046875
- dy_factor: bfloat16 [5120, 64], P('tensor'), may hold values from -0.078125 to 0.078125
Outputs:
- gate_grad: float32 [16, 64, 64], P('dp'), parts along dimension 0
- up_grad: float32 [16, 64, 64], P('dp'), parts along dimension 0
- down_grad: float32 [16, 64, 64], P('dp'), parts along dimension 0
There are 8 independent parts, one for each index of `dp`. A program takes and returns all parts, laid end to end along the dimension named above; an argument that names none is the same for every part. Nothing has to cross between parts.
All inputs are finite; a program needn't handle non-finite values.
Results may differ from a plain program's by a relative error of at most 0.0031.
Values may be sent and summed in bfloat16 or wider, within the bound.
No kernel may reach another device: no remote copies, remote signals or barrier semaphores. Data moves between devices by JAX's collectives and lax.ppermute only.
A program may use at most 128 MiB of HBM per device.

v0:
```python
import jax
import jax.numpy as jnp
from jax import lax
from jax.sharding import PartitionSpec as P

SEQS = 2
LEN = 128


def product(left, right):
    return jnp.dot(left, right, preferred_element_type=jnp.float32)


def per_sequence(projected):
    row_count = projected.shape[0]
    rank_dim = projected.shape[1] // 5
    seq_index = lax.iota(jnp.int32, row_count) // LEN
    onehot = (seq_index[:, None] == lax.iota(jnp.int32, SEQS)[None, :]).astype(jnp.float32)
    inputs = projected[:, :rank_dim]
    gate_up = projected[:, rank_dim : 3 * rank_dim]
    hiddens = projected[:, 3 * rank_dim : 4 * rank_dim]
    outputs = projected[:, 4 * rank_dim :]
    spread_in = (onehot[:, :, None] * inputs[:, None, :]).reshape(row_count, SEQS * rank_dim)
    spread_hidden = (onehot[:, :, None] * hiddens[:, None, :]).reshape(row_count, SEQS * rank_dim)
    contract = (((0,), (0,)), ((), ()))
    highest = lax.Precision.HIGHEST
    gate_sums = lax.dot_general(
        spread_in, gate_up, contract, precision=highest, preferred_element_type=jnp.float32
    )
    down_sums = lax.dot_general(
        spread_hidden, outputs, contract, precision=highest, preferred_element_type=jnp.float32
    )
    gate_part = gate_sums[:, :rank_dim].reshape(SEQS, rank_dim, rank_dim)
    up_part = gate_sums[:, rank_dim:].reshape(SEQS, rank_dim, rank_dim)
    down_part = down_sums.reshape(SEQS, rank_dim, rank_dim)
    return (gate_part, up_part, down_part)


def per_device(
    x_in,
    out_grad,
    gate_pre,
    up_pre,
    down_weight,
    x_factor,
    gate_factor,
    up_factor,
    h_factor,
    dy_factor,
):
    hidden_grad = lax.dot_general(
        lax.all_gather(out_grad, "tensor", axis=1, tiled=True),
        down_weight,
        (((1,), (1,)), ((), ())),
        preferred_element_type=jnp.float32,
    )
    gate_val = gate_pre.astype(jnp.float32)
    up_val = up_pre.astype(jnp.float32)
    sigmoid_gate = jax.nn.sigmoid(gate_val)
    silu_gate = gate_val * sigmoid_gate
    hidden = (silu_gate * up_val).astype(jnp.bfloat16)
    d_gate = (hidden_grad * up_val * sigmoid_gate * (1.0 + gate_val * (1.0 - sigmoid_gate))).astype(
        jnp.bfloat16
    )
    d_up = (hidden_grad * silu_gate).astype(jnp.bfloat16)
    partial_rows = jnp.concatenate(
        [
            product(x_in, x_factor),
            product(d_gate, gate_factor),
            product(d_up, up_factor),
            product(hidden, h_factor),
            product(out_grad, dy_factor),
        ],
        axis=1,
    )
    totals = lax.psum(partial_rows, "tensor")
    gate_grad, up_grad, down_grad = per_sequence(totals)
    return (gate_grad, up_grad, down_grad)


def solution(mesh):
    return jax.shard_map(
        per_device,
        mesh=mesh,
        in_specs=(
            P("dp", "tensor"),
            P("dp", "tensor"),
            P("dp", "tensor"),
            P("dp", "tensor"),
            P("tensor", None),
            P("tensor", None),
            P("tensor", None),
            P("tensor", None),
            P("tensor", None),
            P("tensor", None),
        ),
        out_specs=(P("dp", None, None), P("dp", None, None), P("dp", None, None)),
        check_vma=False,
    )
```

profile of v0, /device:TPU:0, one launch (start us, length us, event | category | flops | bytes accessed | tf_op | source)
XLA Modules:
  0.0 114.2 jit_solution(1858316593705136239)
XLA Ops:
  7.2 0.0 copy-start
  7.2 0.0 all-gather.2.cloned.1.call-start
  7.2 0.7 all-gather.2.cloned.1.call-update
  7.9 0.0 all-reduce.2.cloned.1.call-start
  8.0 0.3 copy-done
  8.3 1.2 %convolution_dynamic-update-slice_fusion.1 = f32[256,320]{0,1:T(8,128)S(1)} fusion(bf16[256,1280]{1,0:T(8,128)(2,1)S(1)} %copy-done, bf16[1280,64]{0,1:T(8,128)(2,1)} %param.15), kind=kOutput, calls=%fused_computation.18 | convolution fusion | flops 41943040 | bytes 884736 | tf_op jit(solution)/shard_map/dot_general | solution.py:11
  9.5 0.0 copy-start.4
  9.5 28.3 %all-gather.2.cloned.1.call-done = bf16[256,5120]{1,0:T(8,128)(2,1)} async-done(((bf16[256,1280]{1,0:T(8,128)(2,1)}), bf16[256,5120]{1,0:T(8,128)(2,1)}) %all-gather.2.cloned.1.call-update) | async-done | bytes 2621456 | tf_op jit(solution)/shard_map/all_gather | solution.py:52
  37.9 22.1 %fusion.32 = f32[256,4608]{1,0:T(8,128)} fusion(bf16[256,5120]{1,0:T(8,128)(2,1)} %all-gather.2.cloned.1.call-done, bf16[4608,5120]{1,0:T(8,128)(2,1)} %param.14), kind=kOutput, calls=%fused_computation.41 | convolution fusion | flops 12079595520 | bytes 54525952 | tf_op jit(solution)/shard_map/dot_general | solution.py:51
  60.0 0.0 copy-done.4
  60.0 0.0 copy-start.5
  60.0 0.0 copy-start.6
  60.0 0.0 copy-start.8
  60.0 5.4 %fusion.13 = f32[256,320]{0,1:T(8,128)S(1)} fusion(f32[256,320]{0,1:T(8,128)S(1)} %convolution_dynamic-update-slice_fusion.1, bf16[4608,64]{0,1:T(8,128)(2,1)} %param.16, f32[256,4608]{1,0:T(8,128)} %fusion.32, bf16[256,4608]{1,0:T(8,128)(2,1)S(1)} %copy-done.4, bf16[256,4608]{1,0:T(8,128)(2,1)} %param.12), kind=kOutput, calls=%fused_computation.19 | convolution fusion | flops 165150720 | bytes 10092544 | tf_op jit(solution)/shard_map/dot_general | solution.py:11
  65.4 0.0 copy-done.5
  65.4 0.0 copy-done.6
  65.4 0.1 copy-done.8
  65.4 0.0 copy-start.7
  65.5 1.4 %fusion.19 = f32[256,320]{0,1:T(8,128)S(1)} fusion(f32[256,320]{0,1:T(8,128)S(1)} %fusion.13, bf16[4608,64]{0,1:T(8,128)(2,1)S(1)} %copy-done.6, f32[256,4608]{1,0:T(8,128)S(1)} %copy-done.8, bf16[256,4608]{1,0:T(8,128)(2,1)S(1)} %copy-done.5), kind=kOutput, calls=%fused_computation.21 | convolution fusion | flops 159252480 | bytes 7733248 | tf_op jit(solution)/shard_map/dot_general | solution.py:11
  66.9 0.0 copy-done.7
  66.9 0.0 copy-start.1
  66.9 0.0 copy-start.3
  66.9 1.6 %fusion.16 = f32[256,320]{0,1:T(8,128)S(1)} fusion(f32[256,320]{0,1:T(8,128)S(1)} %fusion.19, bf16[4608,64]{0,1:T(8,128)(2,1)S(1)} %copy-done.7, bf16[256,4608]{1,0:T(8,128)(2,1)S(1)} %copy-done.4, bf16[256,4608]{1,0:T(8,128)(2,1)S(1)} %copy-done.5), kind=kOutput, calls=%fused_computation.20 | convolution fusion | flops 160432128 | bytes 5373952 | tf_op jit(solution)/shard_map/dot_general | solution.py:11
  68.4 0.0 copy-done.1
  68.5 0.0 copy-done.3
  68.5 0.3 convolution_dynamic-update-slice_fusion
  68.8 0.0 copy-start.2
  68.8 0.7 copy-done.2
  69.5 0.0 all-reduce.2.cloned.1.call-update
  69.6 32.4 %all-reduce.2.cloned.1.call-done = f32[256,320]{0,1:T(8,128)} async-done(((f32[256,320]{0,1:T(8,128)}), f32[256,320]{0,1:T(8,128)}) %all-reduce.2.cloned.1.call-update) | async-done | bytes 327696 | tf_op jit(solution)/shard_map/psum | solution.py:76
  102.0 0.9 fusion.30
  102.9 1.2 %fusion.20 = f32[128,128]{0,1:T(8,128)S(1)} fusion(f32[256,128]{0,1:T(8,128)S(1)} %bitcast.23, f32[256,320]{0,1:T(8,128)} %all-reduce.2.cloned.1.call-done), kind=kOutput, calls=%fused_computation.22 | convolution fusion | flops 50331648 | bytes 327680 | tf_op jit(solution)/shard_map/dot_general | solution.py:27
  104.1 0.7 copy.15
  104.9 0.7 copy.16
  105.6 1.7 %fusion.22 = f32[2,64,64]{2,1,0:T(8,128)} fusion(f32[256,320]{0,1:T(8,128)} %all-reduce.2.cloned.1.call-done, f32[256,64]{0,1:T(8,128)S(1)} %get-tuple-element.6, f32[256,2]{0,1:T(2,128)S(1)} %compare_convert_fusion), kind=kOutput, calls=%fused_computation.24 | convolution fusion | flops 25198592 | bytes 165888 | tf_op jit(solution)/shard_map/dot_general | solution.py:30
  (4 shorter events, 0.0 us)
Async XLA Ops:
  7.2 1.1 copy-start
  7.2 30.7 %all-gather.2.cloned.1.call-start = ((), (), s32[]{:S(2)}) async-start(), calls=%async_computation | async-start | bytes 3276800 | tf_op jit(solution)/shard_map/all_gather | solution.py:52
  7.9 94.1 %all-reduce.2.cloned.1.call-start = ((), (), s32[]{:S(2)}) async-start(), calls=%async_computation.1 | async-start | bytes 655360 | tf_op jit(solution)/shard_map/psum | solution.py:76
  9.5 50.5 %copy-start.4 = (bf16[256,4608]{1,0:T(8,128)(2,1)S(1)}, bf16[256,4608]{1,0:T(8,128)(2,1)}, u32[]{:S(2)}) copy-start(bf16[256,4608]{1,0:T(8,128)(2,1)} %param.13) | copy-start | bytes 7077892
  60.0 5.4 %copy-start.5 = (bf16[256,4608]{1,0:T(8,128)(2,1)S(1)}, bf16[256,4608]{1,0:T(8,128)(2,1)}, u32[]{:S(2)}) copy-start(bf16[256,4608]{1,0:T(8,128)(2,1)} %param.12) | copy-start | bytes 7077892
  60.0 5.4 %copy-start.6 = (bf16[4608,64]{0,1:T(8,128)(2,1)S(1)}, bf16[4608,64]{0,1:T(8,128)(2,1)}, u32[]{:S(2)}) copy-start(bf16[4608,64]{0,1:T(8,128)(2,1)} %param.17) | copy-start | bytes 1769476
  60.0 5.4 %copy-start.8 = (f32[256,4608]{1,0:T(8,128)S(1)}, f32[256,4608]{1,0:T(8,128)}, u32[]{:S(2)}) copy-start(f32[256,4608]{1,0:T(8,128)} %fusion.32) | copy-start | bytes 14155780
  65.4 1.4 %copy-start.7 = (bf16[4608,64]{0,1:T(8,128)(2,1)S(1)}, bf16[4608,64]{0,1:T(8,128)(2,1)}, u32[]{:S(2)}) copy-start(bf16[4608,64]{0,1:T(8,128)(2,1)} %param.18) | copy-start | bytes 1769476
  66.9 1.6 %copy-start.1 = (bf16[256,1280]{1,0:T(8,128)(2,1)S(1)}, bf16[256,1280]{1,0:T(8,128)(2,1)}, u32[]{:S(2)}) copy-start(bf16[256,1280]{1,0:T(8,128)(2,1)} %param.11) | copy-start | bytes 1966084
  66.9 1.6 %copy-start.3 = (bf16[1280,64]{0,1:T(8,128)(2,1)S(1)}, bf16[1280,64]{0,1:T(8,128)(2,1)}, u32[]{:S(2)}) copy-start(bf16[1280,64]{0,1:T(8,128)(2,1)} %param.19) | copy-start | bytes 491524
  68.8 0.8 copy-start.2
Sparse Core Ops, SparseCore 0:
  9.6 28.2 all-gather.1
  69.7 32.2 all-reduce.1
where the time goes:
time: 115 us; the launch traced here: 114 us
  waiting for transfers between devices  61.5 us (53%)
  matrix products  34.9 us (30%)
  between operations  14.2 us (12%)
  local copies, waits for them, and re-layouts  3.51 us (3%)
    psum x1, waiting for transfers between devices, per_device(): totals = lax.psum(partial_rows, 'tensor')  32.4 us
    all_gather x1, waiting for transfers between devices, per_device(): lax.all_gather(out_grad, 'tensor', axis=1, tiled=True)  28.3 us
    dot_general x1, matrix products, per_device(): lax.dot_general(lax.all_gather(out_grad, 'tensor', axis=1, tiled=True), d...  22.1 us
    dot_general x5, matrix products, product(): return jnp.dot(left, right, preferred_element_type=jnp.float32)  9.84 us
    unnamed x20, local copies, waits for them, and re-layouts  2.62 us
  transfers between devices with their start and end apart: 2, of which 2 were waited for; matrix products, arithmetic and copies ran while one was open for 1% of the time, Pallas kernels for 0%

commit v1 on v0

v1 whole, which is shorter than its diff:
```python
import jax
import jax.numpy as jnp
from jax import lax
from jax.experimental import pallas as pl
from jax.experimental.pallas import tpu as pltpu
from jax.sharding import PartitionSpec as P

SEQS = 2
LEN = 128
BLOCK = 512
MIB = 1 << 20
HBM = pl.BlockSpec(memory_space=pl.ANY)
VMEM = pl.BlockSpec(memory_space=pltpu.VMEM)


def product(left, right):
    return jnp.dot(left, right, preferred_element_type=jnp.float32)


def rows_by_rows(left, right, precision=None):
    return lax.dot_general(
        left, right, (((1,), (1,)), ((), ())), precision=precision, preferred_element_type=jnp.float32
    )


def per_sequence(matrix):
    return matrix.reshape(SEQS, matrix.shape[0] // SEQS, matrix.shape[1])


def plain(x_in, out_grad, gate_pre, up_pre, down_weight, x_factor, gate_factor, up_factor, h_factor, dy_factor):
    hidden_grad = rows_by_rows(lax.all_gather(out_grad, "tensor", axis=1, tiled=True), down_weight)
    gate_val = gate_pre.astype(jnp.float32)
    up_val = up_pre.astype(jnp.float32)
    sigmoid_gate = jax.nn.sigmoid(gate_val)
    silu_gate = gate_val * sigmoid_gate
    hidden = (silu_gate * up_val).astype(jnp.bfloat16)
    d_gate = (hidden_grad * up_val * sigmoid_gate * (1.0 + gate_val * (1.0 - sigmoid_gate))).astype(jnp.bfloat16)
    d_up = (hidden_grad * silu_gate).astype(jnp.bfloat16)
    rows = [
        product(x_in, x_factor),
        product(d_gate, gate_factor),
        product(d_up, up_factor),
        product(hidden, h_factor),
        product(out_grad, dy_factor),
    ]
    totals = lax.psum(jnp.stack(rows), "tensor")
    p_x, q_gate, q_up, p_h, q_y = [per_sequence(totals[i]) for i in range(5)]
    highest = lax.Precision.HIGHEST
    return (
        jnp.einsum("sli,slj->sij", p_x, q_gate, precision=highest),
        jnp.einsum("sli,slj->sij", p_x, q_up, precision=highest),
        jnp.einsum("sli,slj->sij", p_h, q_y, precision=highest),
    )


def own_kernel(
    x_hbm, og_hbm, gate_hbm, up_hbm, w_hbm, xf_hbm, yf_hbm, hf_hbm,
    acc_ref, a_ref, b_ref, pq_ref, ph_ref,
    x_v, og_v, gate_v, up_v, w_v, xf_v, yf_v, hf_v, sems, block_sems,
):
    me = lax.axis_index("tensor")
    blocks, _, width = w_v.shape
    columns = pl.ds(pl.multiple_of(me * width, 128), width)

    def plain_copies():
        pairs = ((og_hbm, og_v), (hf_hbm, hf_v), (x_hbm, x_v), (xf_hbm, xf_v), (yf_hbm, yf_v))
        return [pltpu.make_async_copy(src, dst, sems.at[i]) for i, (src, dst) in enumerate(pairs)]

    def block_copies(i):
        units = pl.ds(i * BLOCK, BLOCK)
        return (
            pltpu.make_async_copy(w_hbm.at[units, columns], w_v.at[i], block_sems.at[i, 0]),
            pltpu.make_async_copy(gate_hbm.at[:, units], gate_v.at[i], block_sems.at[i, 1]),
            pltpu.make_async_copy(up_hbm.at[:, units], up_v.at[i], block_sems.at[i, 2]),
        )

    early = plain_copies()
    for copy in early[:2]:
        copy.start()
    for i in range(blocks):
        for copy in block_copies(i):
            copy.start()
    for copy in early[2:]:
        copy.start()
    for copy in early[:2]:
        copy.wait()
    ph_ref[...] = jnp.zeros_like(ph_ref)

    @pl.loop(0, blocks)
    def _(i):
        units = pl.ds(pl.multiple_of(i * BLOCK, BLOCK), BLOCK)
        for ref, dst, k in ((w_hbm, w_v, 0), (gate_hbm, gate_v, 1), (up_hbm, up_v, 2)):
            src = ref.at[units, columns] if k == 0 else ref.at[:, units]
            pltpu.make_async_copy(src, dst.at[i], block_sems.at[i, k]).wait()
        acc_ref[i] = rows_by_rows(og_v[...], w_v[i])
        g = gate_v[i].astype(jnp.float32)
        u = up_v[i].astype(jnp.float32)
        s = 0.5 * jnp.tanh(0.5 * g) + 0.5
        silu = g * s
        a_ref[i] = u * s * (1.0 + g * (1.0 - s))
        b_ref[i] = silu
        ph_ref[...] += rows_by_rows(hf_v[:, units], (silu * u).astype(jnp.bfloat16))

    for copy in early[2:]:
        copy.wait()
    rank = ph_ref.shape[0]
    pq_ref[:rank] = rows_by_rows(xf_v[...], x_v[...])
    pq_ref[rank:] = rows_by_rows(yf_v[...], og_v[...])


def mate_kernel(acc_in, og_ref, w_hbm, acc_ref, w_v, sems):
    mate = lax.axis_index("tensor") ^ 1
    blocks, _, width = w_v.shape
    columns = pl.ds(pl.multiple_of(mate * width, 128), width)

    def copy(i):
        units = pl.ds(i * BLOCK, BLOCK)
        return pltpu.make_async_copy(w_hbm.at[units, columns], w_v.at[i], sems.at[i])

    for i in range(blocks):
        copy(i).start()

    @pl.loop(0, blocks)
    def _(i):
        copy(i).wait()
        acc_ref[i] = acc_in[i] + rows_by_rows(og_ref[...], w_v[i])


def fetch_kernel(w_hbm, token_ref, near_ref, far_ref, sems):
    me = lax.axis_index("tensor")
    width = near_ref.shape[2]
    copies = []
    for k, (owner, ref) in enumerate(((me ^ 2, near_ref), (me ^ 3, far_ref))):
        columns = pl.ds(pl.multiple_of(owner * width, 128), width)
        for i in range(ref.shape[0]):
            copies.append(
                pltpu.make_async_copy(w_hbm.at[pl.ds(i * BLOCK, BLOCK), columns], ref.at[i], sems.at[k, i])
            )
    for copy in copies:
        copy.start()
    for copy in copies:
        copy.wait()


def near_kernel(acc_in, og_ref, w_ref, acc_ref):
    @pl.loop(0, acc_in.shape[0])
    def _(i):
        acc_ref[i] = acc_in[i] + rows_by_rows(og_ref[...], w_ref[i])


def far_kernel(
    acc_ref, og_ref, w_ref, a_ref, b_ref, gf_ref, uf_ref, mine_ref, theirs_ref, ph_ref, gu_ref, dn_ref, q_ref
):
    q_ref[...] = jnp.zeros_like(q_ref)
    rank = ph_ref.shape[0]

    @pl.loop(0, acc_ref.shape[0])
    def _(i):
        units = pl.ds(pl.multiple_of(i * BLOCK, BLOCK), BLOCK)
        hidden_grad = acc_ref[i] + rows_by_rows(og_ref[...], w_ref[i])
        d_gate = (hidden_grad * a_ref[i]).astype(jnp.bfloat16)
        d_up = (hidden_grad * b_ref[i]).astype(jnp.bfloat16)
        q_ref[:rank] += rows_by_rows(gf_ref[:, units], d_gate)
        q_ref[rank:] += rows_by_rows(uf_ref[:, units], d_up)

    first = lax.rem(lax.axis_index("tensor"), 2) == 0
    mine, theirs = mine_ref[...], theirs_ref[...]
    p_x = jnp.where(first, mine, theirs)
    q_y = jnp.where(first, theirs, mine)
    highest = lax.Precision.HIGHEST
    for s in range(SEQS):
        tokens = slice(s * LEN, (s + 1) * LEN)
        gu_ref[s] = rows_by_rows(p_x[:, tokens], q_ref[:, tokens], highest)
        dn_ref[s] = rows_by_rows(ph_ref[:, tokens], q_y[:, tokens], highest)


def sum_kernel(*refs):
    gu, dn, (gate_ref, up_ref, down_ref) = refs[:4], refs[4:8], refs[8:]
    rank = gate_ref.shape[1]
    total = (gu[0][...] + gu[1][...]) + (gu[2][...] + gu[3][...])
    gate_ref[...] = total[:, :, :rank]
    up_ref[...] = total[:, :, rank:]
    down_ref[...] = (dn[0][...] + dn[1][...]) + (dn[2][...] + dn[3][...])


def f32(*shape):
    return jax.ShapeDtypeStruct(shape, jnp.float32)


def fast(x_in, out_grad, gate_pre, up_pre, down_weight, x_factor, gate_factor, up_factor, h_factor, dy_factor):
    tokens, width = out_grad.shape
    units, rank = h_factor.shape
    blocks = units // BLOCK
    bf16 = jnp.bfloat16
    dma = pltpu.SemaphoreType.DMA

    def swap(array, bits):
        return lax.ppermute(array, "tensor", [(i, i ^ bits) for i in range(4)])

    def call(kernel, out_shape, in_specs, out_specs, mib, flops=0, moved=0, scratch=(), **kwargs):
        return pl.pallas_call(
            kernel,
            out_shape=out_shape,
            in_specs=in_specs,
            out_specs=out_specs,
            scratch_shapes=list(scratch),
            compiler_params=pltpu.CompilerParams(vmem_limit_bytes=mib * MIB),
            cost_estimate=pl.CostEstimate(flops=flops, bytes_accessed=moved, transcendentals=0),
            **kwargs,
        )

    per_product = 2 * tokens * width * units
    near = swap(out_grad, 2)
    mate = swap(out_grad, 1)
    held = pltpu.VMEM((blocks, tokens, BLOCK), jnp.float32)
    columns = pltpu.VMEM((blocks, BLOCK, width), bf16)

    acc, a, b, pq, ph = call(
        own_kernel,
        (held, held, held, f32(2 * rank, tokens), f32(rank, tokens)),
        [HBM] * 8,
        (VMEM,) * 5,
        26,
        per_product,
        2 * units * (width + 2 * tokens),
        [
            pltpu.VMEM((tokens, width), bf16),
            pltpu.VMEM((tokens, width), bf16),
            pltpu.VMEM((blocks, tokens, BLOCK), bf16),
            pltpu.VMEM((blocks, tokens, BLOCK), bf16),
            pltpu.VMEM((blocks, BLOCK, width), bf16),
            pltpu.VMEM((rank, width), bf16),
            pltpu.VMEM((rank, width), bf16),
            pltpu.VMEM((rank, units), bf16),
            dma((5,)),
            dma((blocks, 3)),
        ],
    )(x_in, out_grad, gate_pre, up_pre, down_weight, x_factor.T, dy_factor.T, h_factor.T)

    pq_mate = swap(pq, 1)
    acc = call(
        mate_kernel, held, [VMEM, VMEM, HBM], VMEM, 16, per_product, 2 * units * width,
        [pltpu.VMEM((blocks, BLOCK, width), bf16), dma((blocks,))],
        input_output_aliases={0: 0},
    )(acc, mate, down_weight)

    core = lax.rem(lax.axis_index("tensor"), 2)
    half = lax.dynamic_slice_in_dim(pq + pq_mate, core * rank, rank, 0)
    half_across = swap(half, 2)
    w_near, w_far = call(
        fetch_kernel, (columns, columns), [HBM, HBM], (VMEM, VMEM), 4, 0, 4 * units * width, [dma((2, blocks))]
    )(down_weight, half)
    half = half + half_across
    half_mate = swap(half, 1)
    far = swap(near, 1)
    acc = call(
        near_kernel, held, [VMEM] * 3, VMEM, 16, per_product, input_output_aliases={0: 0}
    )(acc, near, w_near)
    gu, dn = call(
        far_kernel,
        (f32(SEQS, rank, 2 * rank), f32(SEQS, rank, rank)),
        [VMEM] * 10,
        (VMEM, VMEM),
        16,
        per_product,
        0,
        [pltpu.VMEM((2 * rank, tokens), jnp.float32)],
    )(acc, far, w_far, a, b, gate_factor.T, up_factor.T, half, half_mate, ph)

    shares = [gu] + [swap(gu, k) for k in (1, 2, 3)] + [dn] + [swap(dn, k) for k in (1, 2, 3)]
    out = f32(SEQS, rank, rank)
    return tuple(call(sum_kernel, (out, out, out), [VMEM] * 8, (VMEM,) * 3, 4)(*shares))


def solution(mesh):
    def per_device(*arrays):
        out_grad, h_factor = arrays[1], arrays[8]
        fits = mesh.shape["tensor"] == 4 and out_grad.shape[1] % 128 == 0 and h_factor.shape[0] % BLOCK == 0
        return (fast if fits else plain)(*arrays)

    return jax.shard_map(
        per_device,
        mesh=mesh,
        in_specs=(P("dp", "tensor"),) * 4 + (P("tensor", None),) * 6,
        out_specs=(P("dp", None, None),) * 3,
        check_vma=False,
    )
```

time: 115 us -> 76.9 us (0.67)
  waiting for transfers between devices: 61.5 us -> 5.38 us
  Pallas kernels: 0 us -> 37.1 us
  matrix products: 34.9 us -> 0 us
  local copies, waits for them, and re-layouts: 3.51 us -> 25.1 us
  between operations: 14.2 us -> 0.87 us
  starting transfers between devices: 0.08 us -> 7.96 us
    pallas_call x0 -> x6, Pallas kernels: none -> 37.1 us  [the longest x1 8.43 us: fast(): call(own_kernel, (held, held, held, f32(2 * rank, tokens), f32(rank, toke...]
    dot_general x8 -> x0, matrix products: 34.9 us -> none  [the longest x1 22.1 us: per_device(): lax.dot_general(lax.all_gather(out_grad, 'tensor', axis=1, tiled=True), d...]
    psum x1 -> x0, waiting for transfers between devices: 32.4 us -> none  [per_device(): totals = lax.psum(partial_rows, 'tensor')]
    all_gather x1 -> x0, waiting for transfers between devices: 28.3 us -> none  [per_device(): lax.all_gather(out_grad, 'tensor', axis=1, tiled=True)]
    unnamed x20 -> x40, local copies, waits for them, and re-layouts: 2.62 us -> 25.1 us
    ppermute x0 -> x12, starting transfers between devices: none -> 7.96 us  [swap(): return lax.ppermute(array, 'tensor', [(i, i ^ bits) for i in range(4)])]
    ppermute x0 -> x12, waiting for transfers between devices: none -> 5.38 us  [swap(): return lax.ppermute(array, 'tensor', [(i, i ^ bits) for i in range(4)])]
  transfers between devices with their start and end apart: 2 -> 12, of which waited for: 2 -> 3; matrix products, arithmetic and copies ran while one was open for 1% -> 0% of each run, Pallas kernels for 0% -> 38%
where the time goes in v1:
time: 76.9 us; the launch traced here: 76.4 us
  Pallas kernels  37.1 us (48%)
  local copies, waits for them, and re-layouts  25.1 us (33%)
  starting transfers between devices  7.96 us (10%)
  waiting for transfers between devices  5.38 us (7%)
  between operations  0.87 us (1%)
    unnamed x40, local copies, waits for them, and re-layouts  25.1 us
    pallas_call x1, Pallas kernels, fast(): call(own_kernel, (held, held, held, f32(2 * rank, tokens), f32(rank, toke...  8.43 us
    pallas_call x1, Pallas kernels, fast(): call(fetch_kernel, (columns, columns), [HBM, HBM], (VMEM, VMEM), 4, 0, 4...  8.13 us
    ppermute x12, starting transfers between devices, swap(): return lax.ppermute(array, 'tensor', [(i, i ^ bits) for i in range(4)])  7.96 us
    pallas_call x1, Pallas kernels, fast(): call(far_kernel, (f32(SEQS, rank, 2 * rank), f32(SEQS, rank, rank)), [VME...  7.27 us
    pallas_call x1, Pallas kernels, fast(): call(mate_kernel, held, [VMEM, VMEM, HBM], VMEM, 16, per_product, 2 * uni...  6.47 us
    pallas_call x1, Pallas kernels, fast(): call(near_kernel, held, [VMEM] * 3, VMEM, 16, per_product, input_output_a...  6.02 us
    ppermute x12, waiting for transfers between devices, swap(): return lax.ppermute(array, 'tensor', [(i, i ^ bits) for i in range(4)])  5.38 us
  transfers between devices with their start and end apart: 12, of which 3 were waited for; matrix products, arithmetic and copies ran while one was open for 0% of the time, Pallas kernels for 38%

profile of v1, /device:TPU:0, one launch (start us, length us, event | category | flops | bytes accessed | tf_op | source)
XLA Modules:
  0.0 76.4 jit_solution(16037670443038599278)
XLA Ops:
  0.6 3.0 %collective-permute-start.1 = (bf16[256,1280]{1,0:T(8,128)(2,1)}, bf16[256,1280]{1,0:T(8,128)(2,1)}, u32[]{:S(2)}, u32[]{:S(2)}) collective-permute-start(bf16[256,1280]{1,0:T(8,128)(2,1)} %og_hbm.1), channel_id=1, source_target_pairs={{0,2},{1,3},{2,0},{3,1},{4,6},{5,7},{6,4},{7,5},{8,10},{9,11},{10,... | collective-permute-start | bytes 1966088 | tf_op jit(solution)/shard_map/ppermute | solution.py:198
  3.6 0.0 collective-permute-start
  3.6 0.0 copy-start.5
  3.6 1.7 %copy-done.5 = bf16[256,4608]{1,0:T(8,128)(2,1)S(1)} copy-done((bf16[256,4608]{1,0:T(8,128)(2,1)S(1)}, bf16[256,4608]{1,0:T(8,128)(2,1)}, u32[]{:S(2)}) %copy-start.5) | copy-done | bytes 2359320
  5.3 1.7 %copy-done.6 = bf16[256,4608]{1,0:T(8,128)(2,1)S(1)} copy-done((bf16[256,4608]{1,0:T(8,128)(2,1)S(1)}, bf16[256,4608]{1,0:T(8,128)(2,1)}, u32[]{:S(2)}) %copy-start.6) | copy-done | bytes 2359320
  7.0 0.0 copy-start.7
  7.0 1.1 %copy-done.7 = bf16[256,1280]{1,0:T(8,128)(2,1)S(1)} copy-done((bf16[256,1280]{1,0:T(8,128)(2,1)S(1)}, bf16[256,1280]{1,0:T(8,128)(2,1)}, u32[]{:S(2)}) %copy-start.7) | copy-done | bytes 655384
  8.1 0.0 copy-start.8
  8.1 1.1 %copy-done.8 = bf16[256,1280]{1,0:T(8,128)(2,1)S(1)} copy-done((bf16[256,1280]{1,0:T(8,128)(2,1)S(1)}, bf16[256,1280]{1,0:T(8,128)(2,1)}, u32[]{:S(2)}) %copy-start.8) | copy-done | bytes 655384
  9.1 0.0 copy-start.11
  9.1 1.1 %copy-done.11 = bf16[4608,64]{0,1:T(8,128)(2,1)S(1)} copy-done((bf16[4608,64]{0,1:T(8,128)(2,1)S(1)}, bf16[4608,64]{0,1:T(8,128)(2,1)}, u32[]{:S(2)}) %copy-start.11) | copy-done | bytes 589848
  10.2 0.0 copy-start.12
  10.2 0.9 %copy-done.12 = bf16[1280,64]{0,1:T(8,128)(2,1)S(1)} copy-done((bf16[1280,64]{0,1:T(8,128)(2,1)S(1)}, bf16[1280,64]{0,1:T(8,128)(2,1)}, u32[]{:S(2)}) %copy-start.12) | copy-done | bytes 163864
  11.1 0.0 copy-start.13
  11.1 0.9 %copy-done.13 = bf16[1280,64]{0,1:T(8,128)(2,1)S(1)} copy-done((bf16[1280,64]{0,1:T(8,128)(2,1)S(1)}, bf16[1280,64]{0,1:T(8,128)(2,1)}, u32[]{:S(2)}) %copy-start.13) | copy-done | bytes 163864
  12.0 8.4 %shard_map.121 = (f32[9,256,512]{2,1,0:T(8,128)S(1)}, f32[9,256,512]{2,1,0:T(8,128)S(1)}, f32[9,256,512]{2,1,0:T(8,128)S(1)}, f32[128,256]{1,0:T(8,128)S(1)}, f32[64,256]{1,0:T(8,128)S(1)}) custom-call(bf16[256,1280]{1,0:T(8,128)(2,1)S(1)} %copy-done.7, bf16[256,1280]{1,0:T(8,128)(2,1)S(1)} %copy-done.8, bf16[256,4608]{1,0:T(8,128)(2,1)S(1)} %copy-done.5, ...), custom_call_target="tpu_custom_call" | custom-call | flops 3019898880 | bytes 16515072 | tf_op jit(solution)/shard_map/pallas_call | solution.py:218
  20.5 0.0 copy-start
  20.5 2.2 %copy-done = f32[9,256,512]{2,1,0:T(8,128)} copy-done((f32[9,256,512]{2,1,0:T(8,128)}, f32[9,256,512]{2,1,0:T(8,128)S(1)}, u32[]{:S(2)}) %copy-start) | copy-done | bytes 4718616
  22.7 2.1 %copy-done.3 = f32[9,256,512]{2,1,0:T(8,128)} copy-done((f32[9,256,512]{2,1,0:T(8,128)}, f32[9,256,512]{2,1,0:T(8,128)S(1)}, u32[]{:S(2)}) %copy-start.3) | copy-done | bytes 4718616
  24.8 2.1 %copy-done.4 = f32[9,256,512]{2,1,0:T(8,128)} copy-done((f32[9,256,512]{2,1,0:T(8,128)}, f32[9,256,512]{2,1,0:T(8,128)S(1)}, u32[]{:S(2)}) %copy-start.4) | copy-done | bytes 4718616
  26.9 0.5 collective-permute-start.2
  27.4 0.0 collective-permute-done.1.og_ref
  27.4 0.0 collective-permute-start.3
  27.4 1.1 %collective-permute-done.2 = f32[128,256]{1,0:T(8,128)S(1)} collective-permute-done((f32[128,256]{1,0:T(8,128)S(1)}, f32[128,256]{1,0:T(8,128)S(1)}, u32[]{:S(2)}, u32[]{:S(2)}) %collective-permute-start.2) | collective-permute-done | bytes 131104 | tf_op jit(solution)/shard_map/ppermute | solution.py:198
  28.5 0.0 slice-start.1
  28.5 0.1 collective-permute-start.4
  28.6 0.0 slice-start.2
  28.6 0.0 slice-start.4
  28.6 8.1 %shard_map.123 = (bf16[9,512,1280]{2,1,0:T(8,128)(2,1)S(1)}, bf16[9,512,1280]{2,1,0:T(8,128)(2,1)S(1)}) custom-call(bf16[4608,5120]{1,0:T(8,128)(2,1)} %w_hbm.5, f32[64,256]{1,0:T(8,128)S(1)} %dynamic-slice_add_fusion.token_ref), custom_call_target="tpu_custom_call" | custom-call | bytes 23592960 | tf_op jit(solution)/shard_map/pallas_call | solution.py:250
  36.7 0.0 copy-start.1
  36.8 6.0 %copy-done.1 = bf16[9,512,1280]{2,1,0:T(8,128)(2,1)} copy-done((bf16[9,512,1280]{2,1,0:T(8,128)(2,1)}, bf16[9,512,1280]{2,1,0:T(8,128)(2,1)S(1)}, u32[]{:S(2)}) %copy-start.1) | copy-done | bytes 11796504
  42.7 0.0 collective-permute-done.4
  42.7 0.4 collective-permute-start.5
  43.2 0.0 collective-permute-done.og_ref
  43.2 0.0 slice-done
  43.2 0.0 slice-done.1
  43.2 0.0 slice-start.3
  43.2 0.0 slice-start.5
  43.2 6.5 %shard_map.122.acc_in = f32[9,256,512]{2,1,0:T(8,128)S(1)} custom-call(f32[9,256,512]{2,1,0:T(8,128)S(1)} %bitcast.6, bf16[256,1280]{1,0:T(8,128)(2,1)S(1)} %collective-permute-done.og_ref, bf16[4608,5120]{1,0:T(8,128)(2,1)} %w_hbm.5), custom_call_target="tpu_custom_call", output_to_operand_aliasing={{}: (0, {})} | custom-call | flops 3019898880 | bytes 11796480 | tf_op jit(solution)/shard_map/pallas_call | solution.py:241
  49.7 0.0 copy-start.2
  49.7 4.3 %copy-done.2 = bf16[9,512,1280]{2,1,0:T(8,128)(2,1)S(1)} copy-done((bf16[9,512,1280]{2,1,0:T(8,128)(2,1)S(1)}, bf16[9,512,1280]{2,1,0:T(8,128)(2,1)}, u32[]{:S(2)}) %copy-start.2) | copy-done | bytes 11796504
  54.1 6.0 %shard_map.124.acc_ref = f32[9,256,512]{2,1,0:T(8,128)S(1)} custom-call(f32[9,256,512]{2,1,0:T(8,128)S(1)} %shard_map.122.acc_in, bf16[256,1280]{1,0:T(8,128)(2,1)} %collective-permute-done.1.og_ref, bf16[9,512,1280]{2,1,0:T(8,128)(2,1)S(1)} %copy-done.2), custom_call_target="tpu_custom_call", output_to_operand_aliasing={{}: (0, {})} | custom-call | flops 3019898880 | tf_op jit(solution)/shard_map/pallas_call | solution.py:256
  60.1 0.0 collective-permute-done.5.theirs_ref
  60.1 0.0 collective-permute-done.3.og_ref
  60.1 0.0 slice-done.2
  60.1 0.0 slice-done.4
  60.1 0.0 slice-done.3
  60.1 0.0 slice-done.5
  60.1 0.0 copy-done.9
  60.2 0.0 copy-done.10
  60.2 7.3 %shard_map.125 = (f32[2,64,128]{2,1,0:T(8,128)S(1)}, f32[2,64,64]{2,1,0:T(8,128)S(1)}) custom-call(f32[9,256,512]{2,1,0:T(8,128)S(1)} %shard_map.124.acc_ref, bf16[256,1280]{1,0:T(8,128)(2,1)S(1)} %collective-permute-done.3.og_ref, bf16[9,512,1280]{2,1,0:T(8,128)(2,1)S(1)} %get-tuple-element.15.w_ref, f32[9,256,512]{2,1,0:T(8,128)S(1)} %bitcast.8, ...), custom_call_target="tpu_custom_call" | custom-call | flops 3019898880 | tf_op jit(solution)/shard_map/pallas_call | solution.py:259
  67.5 0.9 %collective-permute-start.10 = (f32[2,64,64]{2,1,0:T(8,128)S(1)}, f32[2,64,64]{2,1,0:T(8,128)S(1)}, u32[]{:S(2)}, u32[]{:S(2)}) collective-permute-start(f32[2,64,64]{2,1,0:T(8,128)S(1)} %get-tuple-element.20.refs_4_), channel_id=1, source_target_pairs={{0,2},{1,3},{2,0},{3,1},{4,6},{5,7},{6,4},{7,5},{8,10},{9,11},{10,... | collective-permute-start | bytes 98312 | tf_op jit(solution)/shard_map/ppermute | solution.py:198
  68.4 0.2 collective-permute-start.6
  68.5 1.1 %collective-permute-start.7 = (f32[2,64,128]{2,1,0:T(8,128)S(1)}, f32[2,64,128]{2,1,0:T(8,128)S(1)}, u32[]{:S(2)}, u32[]{:S(2)}) collective-permute-start(f32[2,64,128]{2,1,0:T(8,128)S(1)} %get-tuple-element.19.refs_0_), channel_id=1, source_target_pairs={{0,2},{1,3},{2,0},{3,1},{4,6},{5,7},{6,4},{7,5},{8,10},{9,11},{10,... | collective-permute-start | bytes 196616 | tf_op jit(solution)/shard_map/ppermute | solution.py:198
  69.6 0.6 collective-permute-start.8
  70.2 1.2 %collective-permute-start.11 = (f32[2,64,64]{2,1,0:T(8,128)S(1)}, f32[2,64,64]{2,1,0:T(8,128)S(1)}, u32[]{:S(2)}, u32[]{:S(2)}) collective-permute-start(f32[2,64,64]{2,1,0:T(8,128)S(1)} %get-tuple-element.20.refs_4_), channel_id=1, source_target_pairs={{0,3},{1,2},{2,1},{3,0},{4,7},{5,6},{6,5},{7,4},{8,11},{9,10},{10,... | collective-permute-start | bytes 98312 | tf_op jit(solution)/shard_map/ppermute | solution.py:198
  71.4 0.9 %collective-permute-done.10.refs_6_ = f32[2,64,64]{2,1,0:T(8,128)S(1)} collective-permute-done((f32[2,64,64]{2,1,0:T(8,128)S(1)}, f32[2,64,64]{2,1,0:T(8,128)S(1)}, u32[]{:S(2)}, u32[]{:S(2)}) %collective-permute-start.10) | collective-permute-done | bytes 32800 | tf_op jit(solution)/shard_map/ppermute | solution.py:198
  72.3 0.0 collective-permute-start.9
  72.3 3.3 %collective-permute-done.11.refs_7_ = f32[2,64,64]{2,1,0:T(8,128)S(1)} collective-permute-done((f32[2,64,64]{2,1,0:T(8,128)S(1)}, f32[2,64,64]{2,1,0:T(8,128)S(1)}, u32[]{:S(2)}, u32[]{:S(2)}) %collective-permute-start.11) | collective-permute-done | bytes 32800 | tf_op jit(solution)/shard_map/ppermute | solution.py:198
  75.7 0.0 collective-permute-done.9.refs_5_
  75.7 0.0 collective-permute-done.6.refs_1_
  75.7 0.0 collective-permute-done.7.refs_2_
  75.7 0.0 collective-permute-done.8.refs_3_
  75.7 0.7 shard_map.126
  (11 shorter events, 0.0 us)
Async XLA Ops:
  0.6 26.8 %collective-permute-start.1 = (bf16[256,1280]{1,0:T(8,128)(2,1)}, bf16[256,1280]{1,0:T(8,128)(2,1)}, u32[]{:S(2)}, u32[]{:S(2)}) collective-permute-start(bf16[256,1280]{1,0:T(8,128)(2,1)} %og_hbm.1), channel_id=1, source_target_pairs={{0,2},{1,3},{2,0},{3,1},{4,6},{5,7},{6,4},{7,5},{8,10},{9,11},{10,... | collective-permute-start | bytes 1966088 | tf_op jit(solution)/shard_map/ppermute | solution.py:198
  3.6 39.5 %collective-permute-start = (bf16[256,1280]{1,0:T(8,128)(2,1)}, bf16[256,1280]{1,0:T(8,128)(2,1)S(1)}, u32[]{:S(2)}, u32[]{:S(2)}) collective-permute-start(bf16[256,1280]{1,0:T(8,128)(2,1)} %og_hbm.1), channel_id=1, source_target_pairs={{0,1},{1,0},{2,3},{3,2},{4,5},{5,4},{6,7},{7,6},{8,9},{9,8},{10,11... | collective-permute-start | bytes 1966088 | tf_op jit(solution)/shard_map/ppermute | solution.py:198
  3.6 1.7 %copy-start.5 = (bf16[256,4608]{1,0:T(8,128)(2,1)S(1)}, bf16[256,4608]{1,0:T(8,128)(2,1)}, u32[]{:S(2)}) copy-start(bf16[256,4608]{1,0:T(8,128)(2,1)} %gate_hbm.1) | copy-start | bytes 7077892
  5.3 1.7 %copy-start.6 = (bf16[256,4608]{1,0:T(8,128)(2,1)S(1)}, bf16[256,4608]{1,0:T(8,128)(2,1)}, u32[]{:S(2)}) copy-start(bf16[256,4608]{1,0:T(8,128)(2,1)} %up_hbm.1) | copy-start | bytes 7077892
  7.0 1.1 %copy-start.7 = (bf16[256,1280]{1,0:T(8,128)(2,1)S(1)}, bf16[256,1280]{1,0:T(8,128)(2,1)}, u32[]{:S(2)}) copy-start(bf16[256,1280]{1,0:T(8,128)(2,1)} %x_hbm.1) | copy-start | bytes 1966084
  8.1 1.1 %copy-start.8 = (bf16[256,1280]{1,0:T(8,128)(2,1)S(1)}, bf16[256,1280]{1,0:T(8,128)(2,1)}, u32[]{:S(2)}) copy-start(bf16[256,1280]{1,0:T(8,128)(2,1)} %og_hbm.1) | copy-start | bytes 1966084
  9.1 1.1 %copy-start.11 = (bf16[4608,64]{0,1:T(8,128)(2,1)S(1)}, bf16[4608,64]{0,1:T(8,128)(2,1)}, u32[]{:S(2)}) copy-start(bf16[4608,64]{0,1:T(8,128)(2,1)} %param.18) | copy-start | bytes 1769476
  10.2 0.9 %copy-start.12 = (bf16[1280,64]{0,1:T(8,128)(2,1)S(1)}, bf16[1280,64]{0,1:T(8,128)(2,1)}, u32[]{:S(2)}) copy-start(bf16[1280,64]{0,1:T(8,128)(2,1)} %param.15) | copy-start | bytes 491524
  11.1 0.9 %copy-start.13 = (bf16[1280,64]{0,1:T(8,128)(2,1)S(1)}, bf16[1280,64]{0,1:T(8,128)(2,1)}, u32[]{:S(2)}) copy-start(bf16[1280,64]{0,1:T(8,128)(2,1)} %param.19) | copy-start | bytes 491524
  20.5 2.2 %copy-start = (f32[9,256,512]{2,1,0:T(8,128)}, f32[9,256,512]{2,1,0:T(8,128)S(1)}, u32[]{:S(2)}) copy-start(f32[9,256,512]{2,1,0:T(8,128)S(1)} %get-tuple-element.12.acc_in) | copy-start | bytes 14155780
  22.7 2.1 %copy-start.3 = (f32[9,256,512]{2,1,0:T(8,128)}, f32[9,256,512]{2,1,0:T(8,128)S(1)}, u32[]{:S(2)}) copy-start(f32[9,256,512]{2,1,0:T(8,128)S(1)} %get-tuple-element.16.a_ref) | copy-start | bytes 14155780
  24.8 2.1 %copy-start.4 = (f32[9,256,512]{2,1,0:T(8,128)}, f32[9,256,512]{2,1,0:T(8,128)S(1)}, u32[]{:S(2)}) copy-start(f32[9,256,512]{2,1,0:T(8,128)S(1)} %get-tuple-element.17.b_ref) | copy-start | bytes 14155780
  26.9 1.6 %collective-permute-start.2 = (f32[128,256]{1,0:T(8,128)S(1)}, f32[128,256]{1,0:T(8,128)S(1)}, u32[]{:S(2)}, u32[]{:S(2)}) collective-permute-start(f32[128,256]{1,0:T(8,128)S(1)} %get-tuple-element.13), channel_id=1, source_target_pairs={{0,1},{1,0},{2,3},{3,2},{4,5},{5,4},{6,7},{7,6},{8,9},{9,8},{10,11... | collective-permute-start | bytes 393224 | tf_op jit(solution)/shard_map/ppermute | solution.py:198
  27.4 32.7 %collective-permute-start.3 = (bf16[256,1280]{1,0:T(8,128)(2,1)}, bf16[256,1280]{1,0:T(8,128)(2,1)S(1)}, u32[]{:S(2)}, u32[]{:S(2)}) collective-permute-start(bf16[256,1280]{1,0:T(8,128)(2,1)} %collective-permute-done.1.og_ref), channel_id=1, source_target_pairs={{0,1},{1,0},{2,3},{3,2},{4,5},{5,4},{6,7},{7,6},{8,9},{9,8},{10,11... | collective-permute-start | bytes 1966088 | tf_op jit(solution)/shard_map/ppermute | solution.py:198
  28.5 14.7 %slice-start = ((s8[4718592]{0:T(1024)(128)(4,1)}), s8[4194304]{0:T(1024)(128)(4,1)S(1)}, s32[]{:S(2)}) async-start(s8[4718592]{0:T(1024)(128)(4,1)} %bitcast.5), calls=%async_computation | async-start | bytes 8388608
  28.5 14.7 %slice-start.1 = ((s8[4718592]{0:T(1024)(128)(4,1)}), s8[524288]{0:T(1024)(128)(4,1)S(1)}, s32[]{:S(2)}) async-start(s8[4718592]{0:T(1024)(128)(4,1)} %bitcast.5), calls=%async_computation.1 | async-start | bytes 1048576
  28.5 14.2 %collective-permute-start.4 = (f32[64,256]{1,0:T(8,128)S(1)}, f32[64,256]{1,0:T(8,128)S(1)}, u32[]{:S(2)}, u32[]{:S(2)}) collective-permute-start(f32[64,256]{1,0:T(8,128)S(1)} %dynamic-slice_add_fusion.token_ref), channel_id=1, source_target_pairs={{0,2},{1,3},{2,0},{3,1},{4,6},{5,7},{6,4},{7,5},{8,10},{9,11},{10,... | collective-permute-start | bytes 196616 | tf_op jit(solution)/shard_map/ppermute | solution.py:198
  28.6 31.5 %slice-start.2 = ((s8[4718592]{0:T(1024)(128)(4,1)}), s8[4194304]{0:T(1024)(128)(4,1)S(1)}, s32[]{:S(2)}) async-start(s8[4718592]{0:T(1024)(128)(4,1)} %bitcast.7), calls=%async_computation.2 | async-start | bytes 8388608
  28.6 31.5 %slice-start.4 = ((s8[4718592]{0:T(1024)(128)(4,1)}), s8[4194304]{0:T(1024)(128)(4,1)S(1)}, s32[]{:S(2)}) async-start(s8[4718592]{0:T(1024)(128)(4,1)} %bitcast.9), calls=%async_computation.4 | async-start | bytes 8388608
  36.7 6.0 %copy-start.1 = (bf16[9,512,1280]{2,1,0:T(8,128)(2,1)}, bf16[9,512,1280]{2,1,0:T(8,128)(2,1)S(1)}, u32[]{:S(2)}) copy-start(bf16[9,512,1280]{2,1,0:T(8,128)(2,1)S(1)} %get-tuple-element.14.w_ref) | copy-start | bytes 35389444
  42.7 17.3 %collective-permute-start.5 = (f32[64,256]{1,0:T(8,128)S(1)}, f32[64,256]{1,0:T(8,128)S(1)}, u32[]{:S(2)}, u32[]{:S(2)}) collective-permute-start(f32[64,256]{1,0:T(8,128)S(1)} %add.11.mine_ref), channel_id=1, source_target_pairs={{0,1},{1,0},{2,3},{3,2},{4,5},{5,4},{6,7},{7,6},{8,9},{9,8},{10,11... | collective-permute-start | bytes 196616 | tf_op jit(solution)/shard_map/ppermute | solution.py:198
  43.2 16.9 %slice-start.3 = ((s8[4718592]{0:T(1024)(128)(4,1)}), s8[524288]{0:T(1024)(128)(4,1)S(1)}, s32[]{:S(2)}) async-start(s8[4718592]{0:T(1024)(128)(4,1)} %bitcast.7), calls=%async_computation.3 | async-start | bytes 1048576
  43.2 16.9 %slice-start.5 = ((s8[4718592]{0:T(1024)(128)(4,1)}), s8[524288]{0:T(1024)(128)(4,1)S(1)}, s32[]{:S(2)}) async-start(s8[4718592]{0:T(1024)(128)(4,1)} %bitcast.9), calls=%async_computation.5 | async-start | bytes 1048576
  49.7 4.4 %copy-start.2 = (bf16[9,512,1280]{2,1,0:T(8,128)(2,1)S(1)}, bf16[9,512,1280]{2,1,0:T(8,128)(2,1)}, u32[]{:S(2)}) copy-start(bf16[9,512,1280]{2,1,0:T(8,128)(2,1)} %copy-done.1) | copy-start | bytes 35389444
  54.1 6.1 %copy-start.9 = (bf16[4608,64]{0,1:T(8,128)(2,1)S(1)}, bf16[4608,64]{0,1:T(8,128)(2,1)}, u32[]{:S(2)}) copy-start(bf16[4608,64]{0,1:T(8,128)(2,1)} %param.16) | copy-start | bytes 1769476
  54.1 6.1 %copy-start.10 = (bf16[4608,64]{0,1:T(8,128)(2,1)S(1)}, bf16[4608,64]{0,1:T(8,128)(2,1)}, u32[]{:S(2)}) copy-start(bf16[4608,64]{0,1:T(8,128)(2,1)} %param.17) | copy-start | bytes 1769476
  67.5 4.9 %collective-permute-start.10 = (f32[2,64,64]{2,1,0:T(8,128)S(1)}, f32[2,64,64]{2,1,0:T(8,128)S(1)}, u32[]{:S(2)}, u32[]{:S(2)}) collective-permute-start(f32[2,64,64]{2,1,0:T(8,128)S(1)} %get-tuple-element.20.refs_4_), channel_id=1, source_target_pairs={{0,2},{1,3},{2,0},{3,1},{4,6},{5,7},{6,4},{7,5},{8,10},{9,11},{10,... | collective-permute-start | bytes 98312 | tf_op jit(solution)/shard_map/ppermute | solution.py:198
  68.4 7.3 %collective-permute-start.6 = (f32[2,64,128]{2,1,0:T(8,128)S(1)}, f32[2,64,128]{2,1,0:T(8,128)S(1)}, u32[]{:S(2)}, u32[]{:S(2)}) collective-permute-start(f32[2,64,128]{2,1,0:T(8,128)S(1)} %get-tuple-element.19.refs_0_), channel_id=1, source_target_pairs={{0,1},{1,0},{2,3},{3,2},{4,5},{5,4},{6,7},{7,6},{8,9},{9,8},{10,11... | collective-permute-start | bytes 196616 | tf_op jit(solution)/shard_map/ppermute | solution.py:198
  68.5 7.2 %collective-permute-start.7 = (f32[2,64,128]{2,1,0:T(8,128)S(1)}, f32[2,64,128]{2,1,0:T(8,128)S(1)}, u32[]{:S(2)}, u32[]{:S(2)}) collective-permute-start(f32[2,64,128]{2,1,0:T(8,128)S(1)} %get-tuple-element.19.refs_0_), channel_id=1, source_target_pairs={{0,2},{1,3},{2,0},{3,1},{4,6},{5,7},{6,4},{7,5},{8,10},{9,11},{10,... | collective-permute-start | bytes 196616 | tf_op jit(solution)/shard_map/ppermute | solution.py:198
  69.6 6.0 %collective-permute-start.8 = (f32[2,64,128]{2,1,0:T(8,128)S(1)}, f32[2,64,128]{2,1,0:T(8,128)S(1)}, u32[]{:S(2)}, u32[]{:S(2)}) collective-permute-start(f32[2,64,128]{2,1,0:T(8,128)S(1)} %get-tuple-element.19.refs_0_), channel_id=1, source_target_pairs={{0,3},{1,2},{2,1},{3,0},{4,7},{5,6},{6,5},{7,4},{8,11},{9,10},{10,... | collective-permute-start | bytes 196616 | tf_op jit(solution)/shard_map/ppermute | solution.py:198
  70.2 5.5 %collective-permute-start.11 = (f32[2,64,64]{2,1,0:T(8,128)S(1)}, f32[2,64,64]{2,1,0:T(8,128)S(1)}, u32[]{:S(2)}, u32[]{:S(2)}) collective-permute-start(f32[2,64,64]{2,1,0:T(8,128)S(1)} %get-tuple-element.20.refs_4_), channel_id=1, source_target_pairs={{0,3},{1,2},{2,1},{3,0},{4,7},{5,6},{6,5},{7,4},{8,11},{9,10},{10,... | collective-permute-start | bytes 98312 | tf_op jit(solution)/shard_map/ppermute | solution.py:198
  72.3 3.4 %collective-permute-start.9 = (f32[2,64,64]{2,1,0:T(8,128)S(1)}, f32[2,64,64]{2,1,0:T(8,128)S(1)}, u32[]{:S(2)}, u32[]{:S(2)}) collective-permute-start(f32[2,64,64]{2,1,0:T(8,128)S(1)} %get-tuple-element.20.refs_4_), channel_id=1, source_target_pairs={{0,1},{1,0},{2,3},{3,2},{4,5},{5,4},{6,7},{7,6},{8,9},{9,8},{10,11... | collective-permute-start | bytes 98312 | tf_op jit(solution)/shard_map/ppermute | solution.py:198

commit v2 on v0

v2 whole, which is shorter than its diff:
```python
import functools

import jax
import jax.numpy as jnp
from jax import lax
from jax.experimental import pallas as pl
from jax.experimental.pallas import tpu as pltpu
from jax.sharding import PartitionSpec as P

SEQS = 2
LEN = 128
BLOCK = 512
HEAD = 2
AHEAD = 4
FIRST = 768
MIB = 1 << 20
ANY = pl.BlockSpec(memory_space=pl.ANY)
VMEM = pl.BlockSpec(memory_space=pltpu.VMEM)
BF16 = jnp.bfloat16
F32 = jnp.float32


def product(left, right):
    return jnp.dot(left, right, preferred_element_type=F32)


def rows_by_rows(left, right, precision=None):
    return lax.dot_general(
        left, right, (((1,), (1,)), ((), ())), precision=precision, preferred_element_type=F32
    )


def per_sequence(matrix):
    return matrix.reshape(SEQS, matrix.shape[0] // SEQS, matrix.shape[1])


def plain(x_in, out_grad, gate_pre, up_pre, down_weight, x_factor, gate_factor, up_factor, h_factor, dy_factor):
    hidden_grad = rows_by_rows(lax.all_gather(out_grad, "tensor", axis=1, tiled=True), down_weight)
    gate_val = gate_pre.astype(F32)
    up_val = up_pre.astype(F32)
    sigmoid_gate = jax.nn.sigmoid(gate_val)
    silu_gate = gate_val * sigmoid_gate
    hidden = (silu_gate * up_val).astype(BF16)
    d_gate = (hidden_grad * up_val * sigmoid_gate * (1.0 + gate_val * (1.0 - sigmoid_gate))).astype(BF16)
    d_up = (hidden_grad * silu_gate).astype(BF16)
    rows = [
        product(x_in, x_factor),
        product(d_gate, gate_factor),
        product(d_up, up_factor),
        product(hidden, h_factor),
        product(out_grad, dy_factor),
    ]
    totals = lax.psum(jnp.stack(rows), "tensor")
    p_x, q_gate, q_up, p_h, q_y = [per_sequence(totals[i]) for i in range(5)]
    highest = lax.Precision.HIGHEST
    return (
        jnp.einsum("sli,slj->sij", p_x, q_gate, precision=highest),
        jnp.einsum("sli,slj->sij", p_x, q_up, precision=highest),
        jnp.einsum("sli,slj->sij", p_h, q_y, precision=highest),
    )


class Columns:
    def __init__(self, bits, start, width):
        self.bits, self.start, self.width = bits, start, width

    def copy(self, w_hbm, i, dst, sem, per_device):
        owner = lax.axis_index("tensor") ^ self.bits
        columns = pl.ds(pl.multiple_of(owner * per_device + self.start, 128), self.width)
        units = pl.ds(pl.multiple_of(i * BLOCK, BLOCK), BLOCK)
        return pltpu.make_async_copy(w_hbm.at[units, columns], dst, sem)


def stream(step, following, blocks, per_device, w_hbm, head, w_v, next_head, sems, body):
    def start(j):
        @pl.when(j < blocks)
        def _():
            step.copy(w_hbm, j, w_v.at[j - HEAD], sems.at[j], per_device).start()

        if following is not None:

            @pl.when((j >= blocks) & (j < blocks + HEAD))
            def _():
                following.copy(w_hbm, j - blocks, next_head.at[j - blocks], sems.at[j], per_device).start()

    for j in range(HEAD, HEAD + AHEAD):
        step.copy(w_hbm, j, w_v.at[j - HEAD], sems.at[j], per_device).start()
    for i in range(HEAD):
        body(i, head[i])

    @pl.loop(HEAD, blocks)
    def _(i):
        start(i + AHEAD)
        step.copy(w_hbm, i, w_v.at[i - HEAD], sems.at[i], per_device).wait()
        body(i, w_v[i - HEAD])

    if following is not None:
        for j in range(HEAD):
            following.copy(w_hbm, j, next_head.at[j], sems.at[blocks + j], per_device).wait()


def two_terms(value):
    high = value.astype(BF16)
    return high, (value - high.astype(F32)).astype(BF16)


def entry_kernel(first_step, x_hbm, og_hbm, xf_hbm, yf_hbm, w_hbm, mate_ref, piece_ref, pq_ref, head_ref,
                 x_v, og_v, xf_v, yf_v, sems):
    width = og_hbm.shape[1]
    rank = xf_hbm.shape[0]
    pairs = ((og_hbm, og_v), (x_hbm, x_v), (xf_hbm, xf_v), (yf_hbm, yf_v))
    copies = [pltpu.make_async_copy(src, dst, sems.at[i]) for i, (src, dst) in enumerate(pairs)]
    copies += [first_step.copy(w_hbm, i, head_ref.at[i], sems.at[4 + i], width) for i in range(HEAD)]
    for copy in copies:
        copy.start()
    copies[0].wait()
    features = og_v[...].T
    mate_ref[:width] = features
    piece_ref[...] = features[:FIRST]
    for copy in copies[1:4]:
        copy.wait()
    pq_ref[:rank] = rows_by_rows(xf_v[...], x_v[...])
    pq_ref[rank:] = product(yf_v[...], mate_ref[:width])
    high, rest = two_terms(pq_ref[...])
    mate_ref[width : width + 2 * rank] = high
    mate_ref[width + 2 * rank :] = rest
    for copy in copies[4:]:
        copy.wait()


def own_kernel(step, following, og_ref, head_ref, gate_hbm, up_hbm, w_hbm, hf_hbm,
               acc_ref, a_ref, b_ref, ph_ref, next_ref, gate_v, up_v, w_v, hf_v, sems, gate_sems, up_sems, hf_sem):
    blocks = acc_ref.shape[0]
    width = step.width

    def units(i):
        return pl.ds(pl.multiple_of(i * BLOCK, BLOCK), BLOCK)

    def gate_up(i):
        return (
            pltpu.make_async_copy(gate_hbm.at[:, units(i)], gate_v.at[i], gate_sems.at[i]),
            pltpu.make_async_copy(up_hbm.at[:, units(i)], up_v.at[i], up_sems.at[i]),
        )

    whole = pltpu.make_async_copy(hf_hbm, hf_v, hf_sem)
    for copy in gate_up(0):
        copy.start()
    whole.start()
    for i in range(1, AHEAD):
        for copy in gate_up(i):
            copy.start()
    ph_ref[...] = jnp.zeros_like(ph_ref)

    def body(i, weights):
        @pl.when(i + AHEAD < blocks)
        def _():
            for copy in gate_up(i + AHEAD):
                copy.start()

        acc_ref[i] = product(weights, og_ref[:width])
        for copy in gate_up(i):
            copy.wait()
        if isinstance(i, int) and i == 0:
            whole.wait()
        g = gate_v[i].T.astype(F32)
        u = up_v[i].T.astype(F32)
        s = 0.5 * jnp.tanh(0.5 * g) + 0.5
        silu = g * s
        a_ref[i] = u * s * (1.0 + g * (1.0 - s))
        b_ref[i] = silu
        ph_ref[...] += product(hf_v[:, units(i)], (silu * u).astype(BF16))

    stream(step, following, blocks, width, w_hbm, head_ref, w_v, next_ref, sems, body)


def pack_kernel(mine_ref, theirs_ref, pq_ref, token_ref, chip_ref, across_ref):
    width = mine_ref.shape[0] - 2 * pq_ref.shape[0]
    rank = pq_ref.shape[0] // 2
    high = theirs_ref[width : width + 2 * rank].astype(F32)
    rest = theirs_ref[width + 2 * rank :].astype(F32)
    chip = pq_ref[...] + (high + rest)
    chip_ref[...] = chip
    even = lax.rem(lax.axis_index("tensor"), 2) == 0
    high, rest = two_terms(jnp.where(even, chip[:rank], chip[rank:]))
    across_ref[: width - FIRST] = mine_ref[FIRST:width]
    across_ref[width - FIRST : width - FIRST + rank] = high
    across_ref[width - FIRST + rank :] = rest


def step_kernel(step, following, per_device, acc_in, og_ref, head_ref, w_hbm, token_ref, acc_ref, next_ref, w_v, sems):
    def body(i, weights):
        acc_ref[i] = acc_in[i] + product(weights, og_ref[: step.width])

    stream(step, following, acc_in.shape[0], per_device, w_hbm, head_ref, w_v, next_ref, sems, body)


def after_kernel(array_ref, token_ref, same_ref):
    pass


def last_kernel(step, per_device, acc_ref, og_ref, head_ref, w_hbm, a_ref, b_ref, gf_ref, uf_ref, chip_ref, near_ref, ph_ref,
                share_ref, w_v, q_ref, sems):
    q_ref[...] = jnp.zeros_like(q_ref)
    rank = ph_ref.shape[0]

    def body(i, weights):
        hidden_grad = acc_ref[i] + product(weights, og_ref[: step.width])
        units = pl.ds(pl.multiple_of(i * BLOCK, BLOCK), BLOCK)
        q_ref[:rank] += product(gf_ref[:, units], (hidden_grad * a_ref[i]).astype(BF16))
        q_ref[rank:] += product(uf_ref[:, units], (hidden_grad * b_ref[i]).astype(BF16))

    stream(step, None, acc_ref.shape[0], per_device, w_hbm, head_ref, w_v, None, sems, body)

    def sums(ref):
        return ref[step.width : step.width + rank].astype(F32) + ref[step.width + rank :].astype(F32)

    even = lax.rem(lax.axis_index("tensor"), 2) == 0
    near, far = sums(near_ref), sums(og_ref)
    p_x = chip_ref[:rank] + jnp.where(even, near, far)
    q_y = chip_ref[rank:] + jnp.where(even, far, near)
    highest = lax.Precision.HIGHEST
    for s in range(SEQS):
        tokens = slice(s * LEN, (s + 1) * LEN)
        share_ref[s * rank : (s + 1) * rank] = rows_by_rows(p_x[:, tokens], q_ref[:, tokens], highest)
        share_ref[SEQS * rank :, s * rank : (s + 1) * rank] = rows_by_rows(ph_ref[:, tokens], q_y[:, tokens], highest)


def sum_kernel(mine_ref, theirs_ref, gate_ref, up_ref, down_ref):
    rank = gate_ref.shape[1]
    total = mine_ref[...] + theirs_ref[...]
    for s in range(SEQS):
        gate_ref[s] = total[s * rank : (s + 1) * rank, :rank]
        up_ref[s] = total[s * rank : (s + 1) * rank, rank:]
        down_ref[s] = total[SEQS * rank :, s * rank : (s + 1) * rank]


def fast(x_in, out_grad, gate_pre, up_pre, down_weight, x_factor, gate_factor, up_factor, h_factor, dy_factor):
    tokens, width = out_grad.shape
    units, rank = h_factor.shape
    blocks = units // BLOCK
    dma = pltpu.SemaphoreType.DMA

    def in_hbm(array):
        return pltpu.with_memory_space_constraint(array, pltpu.HBM)

    def swap(array, bits):
        return lax.ppermute(array, "tensor", [(i, i ^ bits) for i in range(4)])

    def call(kernel, out_shape, in_specs, scratch, mib, flops=0, moved=0, **kwargs):
        several = isinstance(out_shape, tuple)
        return pl.pallas_call(
            kernel,
            out_shape=out_shape,
            in_specs=in_specs,
            out_specs=(VMEM,) * len(out_shape) if several else VMEM,
            scratch_shapes=list(scratch),
            compiler_params=pltpu.CompilerParams(vmem_limit_bytes=mib * MIB),
            cost_estimate=pl.CostEstimate(flops=flops, bytes_accessed=moved, transcendentals=0),
            **kwargs,
        )

    def head(step):
        return pltpu.VMEM((HEAD, BLOCK, step.width), BF16)

    def body(step):
        return pltpu.VMEM((blocks - HEAD, BLOCK, step.width), BF16)

    own, mate = Columns(0, 0, width), Columns(1, 0, width)
    near_a, far_a = Columns(2, 0, FIRST), Columns(3, 0, FIRST)
    near_b, far_b = Columns(2, FIRST, width - FIRST), Columns(3, FIRST, width - FIRST)
    held = pltpu.VMEM((blocks, BLOCK, tokens), F32)
    weight, x_hbm, og_hbm = in_hbm(down_weight), in_hbm(x_in), in_hbm(out_grad)
    xf_hbm, yf_hbm, hf_hbm = in_hbm(x_factor.T), in_hbm(dy_factor.T), in_hbm(h_factor.T)

    to_mate, piece, pq, heads = call(
        functools.partial(entry_kernel, own),
        (
            pltpu.VMEM((width + 4 * rank, tokens), BF16),
            pltpu.VMEM((FIRST, tokens), BF16),
            pltpu.VMEM((2 * rank, tokens), F32),
            head(own),
        ),
        [ANY] * 5,
        [
            pltpu.VMEM((tokens, width), BF16),
            pltpu.VMEM((tokens, width), BF16),
            pltpu.VMEM((rank, width), BF16),
            pltpu.VMEM((rank, width), BF16),
            dma((4 + HEAD,)),
        ],
        8,
    )(x_hbm, og_hbm, xf_hbm, yf_hbm, weight)
    near_first = swap(piece, 2)
    from_mate = swap(to_mate, 1)

    acc, a, b, ph, heads = call(
        functools.partial(own_kernel, own, mate),
        (held, held, held, pltpu.VMEM((rank, tokens), F32), head(mate)),
        [VMEM, VMEM] + [ANY] * 4,
        [
            pltpu.VMEM((blocks, tokens, BLOCK), BF16),
            pltpu.VMEM((blocks, tokens, BLOCK), BF16),
            body(own),
            pltpu.VMEM((rank, units), BF16),
            dma((blocks + HEAD,)),
            dma((blocks,)),
            dma((blocks,)),
            dma,
        ],
        22,
        2 * tokens * width * units,
        2 * units * (width + 2 * tokens),
    )(to_mate, heads, in_hbm(gate_pre), in_hbm(up_pre), weight, hf_hbm)

    chip, across = call(
        pack_kernel,
        (pltpu.VMEM((2 * rank, tokens), F32), pltpu.VMEM((width - FIRST + 2 * rank, tokens), BF16)),
        [VMEM] * 3 + [ANY],
        [],
        4,
    )(to_mate, from_mate, pq, ph)
    near_second = swap(across, 2)

    def add(step, following, acc, features, heads, token):
        return call(
            functools.partial(step_kernel, step, following, width),
            (held, head(following)),
            [VMEM] * 3 + [ANY] * 2,
            [body(step), dma((blocks + HEAD,))],
            16,
            2 * tokens * step.width * units,
            2 * units * step.width,
            input_output_aliases={0: 0},
        )(acc, features, heads, weight, token)

    def after(array, token):
        return pl.pallas_call(
            after_kernel,
            out_shape=pltpu.VMEM(array.shape, array.dtype),
            in_specs=[ANY, ANY],
            out_specs=ANY,
            input_output_aliases={0: 0},
        )(array, token)

    acc, heads = add(mate, near_a, acc, from_mate, heads, chip)
    near_first = after(near_first, heads)
    far_first = swap(near_first, 1)
    acc, heads = add(near_a, far_a, acc, near_first, heads, chip)
    acc, heads = add(far_a, near_b, acc, far_first, heads, chip)
    near_second = after(near_second, heads)
    far_second = swap(near_second, 1)
    acc, heads = add(near_b, far_b, acc, near_second, heads, chip)
    share = call(
        functools.partial(last_kernel, far_b, width),
        pltpu.VMEM(((SEQS + 1) * rank, 2 * rank), F32),
        [VMEM] * 3 + [ANY] + [VMEM] * 7,
        [body(far_b), pltpu.VMEM((2 * rank, tokens), F32), dma((blocks,))],
        16,
        2 * tokens * far_b.width * units,
        2 * units * far_b.width,
    )(acc, far_second, heads, weight, a, b, gate_factor.T, up_factor.T, chip, near_second, ph)

    chip_share = share + swap(share, 1)
    out = jax.ShapeDtypeStruct((SEQS, rank, rank), F32)
    return call(sum_kernel, (out, out, out), [VMEM] * 2, [], 4)(chip_share, swap(chip_share, 2))


def solution(mesh):
    def per_device(*arrays):
        (tokens, width), (units, rank) = arrays[1].shape, arrays[8].shape
        fits = (
            mesh.shape["tensor"] == 4
            and (tokens, rank) == (SEQS * LEN, LEN // 2)
            and width % 128 == 0
            and width > FIRST
            and units % BLOCK == 0
            and units // BLOCK > HEAD + AHEAD
        )
        return tuple((fast if fits else plain)(*arrays))

    return jax.shard_map(
        per_device,
        mesh=mesh,
        in_specs=(P("dp", "tensor"),) * 4 + (P("tensor", None),) * 6,
        out_specs=(P("dp", None, None),) * 3,
        check_vma=False,
    )
```

time: 115 us -> 67.6 us (0.59)
  waiting for transfers between devices: 61.5 us -> 4.26 us
  Pallas kernels: 0 us -> 39.9 us
  matrix products: 34.9 us -> 0 us
  between operations: 14.2 us -> 0.82 us
  local copies, waits for them, and re-layouts: 3.51 us -> 16.3 us
  starting transfers between devices: 0.08 us -> 5.88 us
    pallas_call x0 -> x11, Pallas kernels: none -> 39.9 us  [the longest x4 20.1 us: add(): call(functools.partial(step_kernel, step, following, width), (held, head(...]
    dot_general x8 -> x0, matrix products: 34.9 us -> none  [the longest x1 22.1 us: per_device(): lax.dot_general(lax.all_gather(out_grad, 'tensor', axis=1, tiled=True), d...]
    psum x1 -> x0, waiting for transfers between devices: 32.4 us -> none  [per_device(): totals = lax.psum(partial_rows, 'tensor')]
    all_gather x1 -> x0, waiting for transfers between devices: 28.3 us -> none  [per_device(): lax.all_gather(out_grad, 'tensor', axis=1, tiled=True)]
    unnamed x20 -> x30, local copies, waits for them, and re-layouts: 2.62 us -> 16.3 us
    ppermute x0 -> x7, starting transfers between devices: none -> 5.88 us  [swap(): return lax.ppermute(array, 'tensor', [(i, i ^ bits) for i in range(4)])]
    ppermute x0 -> x7, waiting for transfers between devices: none -> 4.26 us  [swap(): return lax.ppermute(array, 'tensor', [(i, i ^ bits) for i in range(4)])]
  transfers between devices with their start and end apart: 2 -> 7, of which waited for: 2 -> 2; matrix products, arithmetic and copies ran while one was open for 1% -> 0% of each run, Pallas kernels for 0% -> 47%
where the time goes in v2:
time: 67.6 us; the launch traced here: 67.2 us
  Pallas kernels  39.9 us (59%)
  local copies, waits for them, and re-layouts  16.3 us (24%)
  starting transfers between devices  5.88 us (9%)
  waiting for transfers between devices  4.26 us (6%)
  between operations  0.82 us (1%)
    pallas_call x4, Pallas kernels, add(): call(functools.partial(step_kernel, step, following, width), (held, head(...  20.1 us
    unnamed x30, local copies, waits for them, and re-layouts  16.3 us
    pallas_call x1, Pallas kernels, fast(): call(functools.partial(own_kernel, own, mate), (held, held, held, pltpu.V...  11.1 us
    ppermute x7, starting transfers between devices, swap(): return lax.ppermute(array, 'tensor', [(i, i ^ bits) for i in range(4)])  5.88 us
    pallas_call x1, Pallas kernels, fast(): call(functools.partial(last_kernel, far_b, width), pltpu.VMEM(((SEQS + 1)...  5.64 us
    ppermute x7, waiting for transfers between devices, swap(): return lax.ppermute(array, 'tensor', [(i, i ^ bits) for i in range(4)])  4.26 us
    pallas_call x1, Pallas kernels, fast(): call(functools.partial(entry_kernel, own), (pltpu.VMEM((width + 4 * rank,...  2.27 us
  transfers between devices with their start and end apart: 7, of which 2 were waited for; matrix products, arithmetic and copies ran while one was open for 0% of the time, Pallas kernels for 47%

profile of v2, /device:TPU:0, one launch (start us, length us, event | category | flops | bytes accessed | tf_op | source)
XLA Modules:
  0.0 67.2 jit_solution(790418444632105880)
XLA Ops:
  0.6 2.3 %shard_map.121 = (bf16[1536,256]{1,0:T(8,128)(2,1)S(1)}, bf16[768,256]{1,0:T(8,128)(2,1)S(1)}, f32[128,256]{1,0:T(8,128)S(1)}, bf16[2,512,1280]{2,1,0:T(8,128)(2,1)S(1)}) custom-call(bf16[256,1280]{1,0:T(8,128)(2,1)} %x_hbm.1, bf16[256,1280]{1,0:T(8,128)(2,1)} %og_hbm.1, bf16[64,1280]{1,0:T(8,128)(2,1)} %bitcast.10, bf16[64,1280]{1,0:T(8,128)(2,1)} %bitcast.11, ...), custom_call_target="tpu_custom_call" | custom-call | tf_op jit(solution)/shard_map/pallas_call | solution.py:275
  2.9 0.5 collective-permute-start
  3.4 2.6 %collective-permute-start.1 = (bf16[768,256]{1,0:T(8,128)(2,1)S(1)}, bf16[768,256]{1,0:T(8,128)(2,1)S(1)}, u32[]{:S(2)}, u32[]{:S(2)}) collective-permute-start(bf16[768,256]{1,0:T(8,128)(2,1)S(1)} %get-tuple-element.30), channel_id=1, source_target_pairs={{0,2},{1,3},{2,0},{3,1},{4,6},{5,7},{6,4},{7,5},{8,10},{9,11},{10,... | collective-permute-start | bytes 1179656 | tf_op jit(solution)/shard_map/ppermute | solution.py:247
  6.0 11.1 %shard_map.122 = (f32[9,512,256]{2,1,0:T(8,128)S(1)}, f32[9,512,256]{2,1,0:T(8,128)S(1)}, f32[9,512,256]{2,1,0:T(8,128)S(1)}, f32[64,256]{1,0:T(8,128)S(1)}, bf16[2,512,1280]{2,1,0:T(8,128)(2,1)S(1)}) custom-call(bf16[1536,256]{1,0:T(8,128)(2,1)S(1)} %get-tuple-element.22.og_ref.mine_ref, bf16[2,512,1280]{2,1,0:T(8,128)(2,1)S(1)} %get-tuple-element.23.head_ref, ...), custom_call_target="tpu_custom_call" | custom-call | flops 3019898880 | bytes 16515072 | tf_op jit(solution)/shard_map/pallas_call | solution.py:296
  17.1 0.0 copy-start.6
  17.1 0.0 copy-start.7
  17.1 0.0 collective-permute-done.theirs_ref.og_ref
  17.2 7.9 %shard_map.124 = (f32[9,512,256]{2,1,0:T(8,128)S(1)}, bf16[2,512,768]{2,1,0:T(8,128)(2,1)S(1)}) custom-call(f32[9,512,256]{2,1,0:T(8,128)S(1)} %get-tuple-element.24.acc_in, bf16[1536,256]{1,0:T(8,128)(2,1)S(1)} %collective-permute-done.theirs_ref.og_ref, bf16[2,512,1280]{2,1,0:T(8,128)(2,1)S(1)} %get-tuple-element.25.head_ref, ...), custom_call_target="tpu_custom_call", output_to_operand_aliasing={{0}: (0, {})} | custom-call | flops 3019898880 | bytes 11796480 | tf_op jit(solution)/shard_map/pallas_call | solution.py:325
  25.0 0.0 copy-done.6
  25.1 0.0 copy-done.7
  25.1 0.0 copy-start
  25.1 2.2 %copy-done = f32[9,512,256]{2,1,0:T(8,128)} copy-done((f32[9,512,256]{2,1,0:T(8,128)}, f32[9,512,256]{2,1,0:T(8,128)S(1)}, u32[]{:S(2)}) %copy-start) | copy-done | bytes 4718616
  27.3 0.0 copy-start.4
  27.3 1.2 %copy-done.4 = bf16[2,512,768]{2,1,0:T(8,128)(2,1)} copy-done((bf16[2,512,768]{2,1,0:T(8,128)(2,1)}, bf16[2,512,768]{2,1,0:T(8,128)(2,1)S(1)}, u32[]{:S(2)}) %copy-start.4) | copy-done | bytes 1572888
  28.5 0.0 collective-permute-done.1.array_ref
  28.5 0.2 collective-permute-start.2
  28.7 0.3 collective-permute-start.3
  28.9 0.0 copy-start.1
  28.9 2.3 %copy-done.1 = f32[9,512,256]{2,1,0:T(8,128)S(1)} copy-done((f32[9,512,256]{2,1,0:T(8,128)S(1)}, f32[9,512,256]{2,1,0:T(8,128)}, u32[]{:S(2)}) %copy-start.1) | copy-done | bytes 4718616
  31.3 0.0 copy-start.5
  31.3 1.4 %copy-done.5 = bf16[2,512,768]{2,1,0:T(8,128)(2,1)S(1)} copy-done((bf16[2,512,768]{2,1,0:T(8,128)(2,1)S(1)}, bf16[2,512,768]{2,1,0:T(8,128)(2,1)}, u32[]{:S(2)}) %copy-start.5) | copy-done | bytes 1572888
  32.7 4.1 %shard_map.126 = (f32[9,512,256]{2,1,0:T(8,128)S(1)}, bf16[2,512,768]{2,1,0:T(8,128)(2,1)S(1)}) custom-call(f32[9,512,256]{2,1,0:T(8,128)S(1)} %copy-done.1, bf16[768,256]{1,0:T(8,128)(2,1)S(1)} %shard_map.125.og_ref, bf16[2,512,768]{2,1,0:T(8,128)(2,1)S(1)} %copy-done.5, bf16[4608,5120]{1,0:T(8,128)(2,1)} %w_hbm.13, ...), custom_call_target="tpu_custom_call", output_to_operand_aliasing={{0}: (0, {})} | custom-call | flops 1811939328 | bytes 7077888 | tf_op jit(solution)/shard_map/pallas_call | solution.py:325
  36.8 0.0 collective-permute-done.2.og_ref
  36.8 4.0 %shard_map.127 = (f32[9,512,256]{2,1,0:T(8,128)S(1)}, bf16[2,512,512]{2,1,0:T(8,128)(2,1)S(1)}) custom-call(f32[9,512,256]{2,1,0:T(8,128)S(1)} %get-tuple-element.32.acc_in, bf16[768,256]{1,0:T(8,128)(2,1)S(1)} %collective-permute-done.2.og_ref, bf16[2,512,768]{2,1,0:T(8,128)(2,1)S(1)} %get-tuple-element.33.head_ref, ...), custom_call_target="tpu_custom_call", output_to_operand_aliasing={{0}: (0, {})} | custom-call | flops 1811939328 | bytes 7077888 | tf_op jit(solution)/shard_map/pallas_call | solution.py:325
  40.7 0.0 copy-start.2
  40.7 2.2 %copy-done.2 = f32[9,512,256]{2,1,0:T(8,128)} copy-done((f32[9,512,256]{2,1,0:T(8,128)}, f32[9,512,256]{2,1,0:T(8,128)S(1)}, u32[]{:S(2)}) %copy-start.2) | copy-done | bytes 4718616
  43.0 0.0 copy-start.9
  43.0 1.0 %copy-done.9 = bf16[2,512,512]{2,1,0:T(8,128)(2,1)} copy-done((bf16[2,512,512]{2,1,0:T(8,128)(2,1)}, bf16[2,512,512]{2,1,0:T(8,128)(2,1)S(1)}, u32[]{:S(2)}) %copy-start.9) | copy-done | bytes 1048600
  44.0 0.0 collective-permute-done.3.array_ref
  44.0 0.0 slice-start
  44.0 0.1 collective-permute-start.4
  44.0 0.0 copy-start.3
  44.0 2.4 %copy-done.3 = f32[9,512,256]{2,1,0:T(8,128)S(1)} copy-done((f32[9,512,256]{2,1,0:T(8,128)S(1)}, f32[9,512,256]{2,1,0:T(8,128)}, u32[]{:S(2)}) %copy-start.3) | copy-done | bytes 4718616
  46.4 0.0 copy-start.10
  46.4 1.2 %copy-done.10 = bf16[2,512,512]{2,1,0:T(8,128)(2,1)S(1)} copy-done((bf16[2,512,512]{2,1,0:T(8,128)(2,1)S(1)}, bf16[2,512,512]{2,1,0:T(8,128)(2,1)}, u32[]{:S(2)}) %copy-start.10) | copy-done | bytes 1048600
  47.6 0.0 slice-start.1
  47.6 0.0 copy-start.11
  47.7 0.0 copy-start.12
  47.7 4.3 %shard_map.129 = (f32[9,512,256]{2,1,0:T(8,128)S(1)}, bf16[2,512,512]{2,1,0:T(8,128)(2,1)S(1)}) custom-call(f32[9,512,256]{2,1,0:T(8,128)S(1)} %copy-done.3, bf16[640,256]{1,0:T(8,128)(2,1)S(1)} %shard_map.128.og_ref.near_ref, bf16[2,512,512]{2,1,0:T(8,128)(2,1)S(1)} %copy-done.10, bf16[4608,5120]{1,0:T(8,128)(2,1)} %w_hbm.13, ...), custom_call_target="tpu_custom_call", output_to_operand_aliasing={{0}: (0, {})} | custom-call | flops 1207959552 | bytes 4718592 | tf_op jit(solution)/shard_map/pallas_call | solution.py:325
  51.9 0.0 collective-permute-done.4.og_ref
  51.9 0.0 slice-done
  51.9 0.0 slice-done.1
  51.9 0.0 copy-done.11
  52.0 0.0 copy-done.12
  52.0 0.0 copy-start.8
  52.0 2.3 %copy-done.8 = f32[9,512,256]{2,1,0:T(8,128)S(1)} copy-done((f32[9,512,256]{2,1,0:T(8,128)S(1)}, f32[9,512,256]{2,1,0:T(8,128)}, u32[]{:S(2)}) %copy-start.8) | copy-done | bytes 4718616
  54.3 5.6 %shard_map.130 = f32[192,128]{1,0:T(8,128)S(1)} custom-call(f32[9,512,256]{2,1,0:T(8,128)S(1)} %get-tuple-element.37.acc_ref, bf16[640,256]{1,0:T(8,128)(2,1)S(1)} %collective-permute-done.4.og_ref, bf16[2,512,512]{2,1,0:T(8,128)(2,1)S(1)} %get-tuple-element.38.head_ref, bf16[4608,5120]{1,0:T(8,128)(2,1)} %w_hbm.13, f32[9,512,256]{2,1,0:T(8,128)S(1)} %bitcast.6, ...), custom_call_target="tpu_custom_call" | custom-call | flops 1207959552 | bytes 4718592 | tf_op jit(solution)/shard_map/pallas_call | solution.py:353
  60.0 0.4 collective-permute-start.5
  60.4 0.9 %collective-permute-done.5 = f32[192,128]{1,0:T(8,128)S(1)} collective-permute-done((f32[192,128]{1,0:T(8,128)S(1)}, f32[192,128]{1,0:T(8,128)S(1)}, u32[]{:S(2)}, u32[]{:S(2)}) %collective-permute-start.5) | collective-permute-done | bytes 98336 | tf_op jit(solution)/shard_map/ppermute | solution.py:247
  61.4 1.8 %collective-permute-start.6 = (f32[192,128]{1,0:T(8,128)S(1)}, f32[192,128]{1,0:T(8,128)S(1)}, u32[]{:S(2)}, u32[]{:S(2)}) collective-permute-start(f32[192,128]{1,0:T(8,128)S(1)} %add.3.mine_ref), channel_id=1, source_target_pairs={{0,2},{1,3},{2,0},{3,1},{4,6},{5,7},{6,4},{7,5},{8,10},{9,11},{10,... | collective-permute-start | bytes 294920 | tf_op jit(solution)/shard_map/ppermute | solution.py:247
  63.2 3.3 %collective-permute-done.6.theirs_ref = f32[192,128]{1,0:T(8,128)S(1)} collective-permute-done((f32[192,128]{1,0:T(8,128)S(1)}, f32[192,128]{1,0:T(8,128)S(1)}, u32[]{:S(2)}, u32[]{:S(2)}) %collective-permute-start.6) | collective-permute-done | bytes 98336 | tf_op jit(solution)/shard_map/ppermute | solution.py:247
  66.5 0.7 %shard_map.131 = (f32[2,64,64]{2,1,0:T(8,128)}, f32[2,64,64]{2,1,0:T(8,128)}, f32[2,64,64]{2,1,0:T(8,128)}) custom-call(f32[192,128]{1,0:T(8,128)S(1)} %add.3.mine_ref, f32[192,128]{1,0:T(8,128)S(1)} %collective-permute-done.6.theirs_ref), custom_call_target="tpu_custom_call" | custom-call | tf_op jit(solution)/shard_map/pallas_call | solution.py:365
  (5 shorter events, 0.1 us)
Async XLA Ops:
  2.9 14.2 %collective-permute-start = (bf16[1536,256]{1,0:T(8,128)(2,1)S(1)}, bf16[1536,256]{1,0:T(8,128)(2,1)S(1)}, u32[]{:S(2)}, u32[]{:S(2)}) collective-permute-start(bf16[1536,256]{1,0:T(8,128)(2,1)S(1)} %get-tuple-element.22.og_ref.mine_ref), channel_id=1, source_target_pairs={{0,1},{1,0},{2,3},{3,2},{4,5},{5,4},{6,7},{7,6},{8,9},{9,8},{10,11... | collective-permute-start | bytes 2359304 | tf_op jit(solution)/shard_map/ppermute | solution.py:247
  3.4 25.1 %collective-permute-start.1 = (bf16[768,256]{1,0:T(8,128)(2,1)S(1)}, bf16[768,256]{1,0:T(8,128)(2,1)S(1)}, u32[]{:S(2)}, u32[]{:S(2)}) collective-permute-start(bf16[768,256]{1,0:T(8,128)(2,1)S(1)} %get-tuple-element.30), channel_id=1, source_target_pairs={{0,2},{1,3},{2,0},{3,1},{4,6},{5,7},{6,4},{7,5},{8,10},{9,11},{10,... | collective-permute-start | bytes 1179656 | tf_op jit(solution)/shard_map/ppermute | solution.py:247
  17.1 8.0 %copy-start.6 = (f32[9,512,256]{2,1,0:T(8,128)}, f32[9,512,256]{2,1,0:T(8,128)S(1)}, u32[]{:S(2)}) copy-start(f32[9,512,256]{2,1,0:T(8,128)S(1)} %get-tuple-element.39.a_ref) | copy-start | bytes 14155780
  17.1 8.0 %copy-start.7 = (f32[9,512,256]{2,1,0:T(8,128)}, f32[9,512,256]{2,1,0:T(8,128)S(1)}, u32[]{:S(2)}) copy-start(f32[9,512,256]{2,1,0:T(8,128)S(1)} %get-tuple-element.40.b_ref) | copy-start | bytes 14155780
  25.1 2.2 %copy-start = (f32[9,512,256]{2,1,0:T(8,128)}, f32[9,512,256]{2,1,0:T(8,128)S(1)}, u32[]{:S(2)}) copy-start(f32[9,512,256]{2,1,0:T(8,128)S(1)} %get-tuple-element.29.acc_in) | copy-start | bytes 14155780
  27.3 1.2 %copy-start.4 = (bf16[2,512,768]{2,1,0:T(8,128)(2,1)}, bf16[2,512,768]{2,1,0:T(8,128)(2,1)S(1)}, u32[]{:S(2)}) copy-start(bf16[2,512,768]{2,1,0:T(8,128)(2,1)S(1)} %get-tuple-element.31.token_ref.head_ref) | copy-start | bytes 4718596
  28.5 8.3 %collective-permute-start.2 = (bf16[768,256]{1,0:T(8,128)(2,1)S(1)}, bf16[768,256]{1,0:T(8,128)(2,1)S(1)}, u32[]{:S(2)}, u32[]{:S(2)}) collective-permute-start(bf16[768,256]{1,0:T(8,128)(2,1)S(1)} %shard_map.125.og_ref), channel_id=1, source_target_pairs={{0,1},{1,0},{2,3},{3,2},{4,5},{5,4},{6,7},{7,6},{8,9},{9,8},{10,11... | collective-permute-start | bytes 1179656 | tf_op jit(solution)/shard_map/ppermute | solution.py:247
  28.7 15.3 %collective-permute-start.3 = (bf16[640,256]{1,0:T(8,128)(2,1)S(1)}, bf16[640,256]{1,0:T(8,128)(2,1)S(1)}, u32[]{:S(2)}, u32[]{:S(2)}) collective-permute-start(bf16[640,256]{1,0:T(8,128)(2,1)S(1)} %get-tuple-element.35), channel_id=1, source_target_pairs={{0,2},{1,3},{2,0},{3,1},{4,6},{5,7},{6,4},{7,5},{8,10},{9,11},{10,... | collective-permute-start | bytes 983048 | tf_op jit(solution)/shard_map/ppermute | solution.py:247
  28.9 2.3 %copy-start.1 = (f32[9,512,256]{2,1,0:T(8,128)S(1)}, f32[9,512,256]{2,1,0:T(8,128)}, u32[]{:S(2)}) copy-start(f32[9,512,256]{2,1,0:T(8,128)} %copy-done) | copy-start | bytes 14155780
  31.3 1.4 %copy-start.5 = (bf16[2,512,768]{2,1,0:T(8,128)(2,1)S(1)}, bf16[2,512,768]{2,1,0:T(8,128)(2,1)}, u32[]{:S(2)}) copy-start(bf16[2,512,768]{2,1,0:T(8,128)(2,1)} %copy-done.4) | copy-start | bytes 4718596
  40.7 2.2 %copy-start.2 = (f32[9,512,256]{2,1,0:T(8,128)}, f32[9,512,256]{2,1,0:T(8,128)S(1)}, u32[]{:S(2)}) copy-start(f32[9,512,256]{2,1,0:T(8,128)S(1)} %get-tuple-element.34.acc_in) | copy-start | bytes 14155780
  43.0 1.0 %copy-start.9 = (bf16[2,512,512]{2,1,0:T(8,128)(2,1)}, bf16[2,512,512]{2,1,0:T(8,128)(2,1)S(1)}, u32[]{:S(2)}) copy-start(bf16[2,512,512]{2,1,0:T(8,128)(2,1)S(1)} %get-tuple-element.36.token_ref.head_ref) | copy-start | bytes 3145732
  44.0 8.0 %slice-start = ((s8[4718592]{0:T(1024)(128)(4,1)}), s8[524288]{0:T(1024)(128)(4,1)S(1)}, s32[]{:S(2)}) async-start(s8[4718592]{0:T(1024)(128)(4,1)} %bitcast.5), calls=%async_computation | async-start | bytes 1048576
  44.0 8.0 %collective-permute-start.4 = (bf16[640,256]{1,0:T(8,128)(2,1)S(1)}, bf16[640,256]{1,0:T(8,128)(2,1)S(1)}, u32[]{:S(2)}, u32[]{:S(2)}) collective-permute-start(bf16[640,256]{1,0:T(8,128)(2,1)S(1)} %shard_map.128.og_ref.near_ref), channel_id=1, source_target_pairs={{0,1},{1,0},{2,3},{3,2},{4,5},{5,4},{6,7},{7,6},{8,9},{9,8},{10,11... | collective-permute-start | bytes 983048 | tf_op jit(solution)/shard_map/ppermute | solution.py:247
  44.0 2.4 %copy-start.3 = (f32[9,512,256]{2,1,0:T(8,128)S(1)}, f32[9,512,256]{2,1,0:T(8,128)}, u32[]{:S(2)}) copy-start(f32[9,512,256]{2,1,0:T(8,128)} %copy-done.2) | copy-start | bytes 14155780
  46.4 1.2 %copy-start.10 = (bf16[2,512,512]{2,1,0:T(8,128)(2,1)S(1)}, bf16[2,512,512]{2,1,0:T(8,128)(2,1)}, u32[]{:S(2)}) copy-start(bf16[2,512,512]{2,1,0:T(8,128)(2,1)} %copy-done.9) | copy-start | bytes 3145732
  47.6 4.3 %slice-start.1 = ((s8[4718592]{0:T(1024)(128)(4,1)}), s8[4194304]{0:T(1024)(128)(4,1)S(1)}, s32[]{:S(2)}) async-start(s8[4718592]{0:T(1024)(128)(4,1)} %bitcast.5), calls=%async_computation.1 | async-start | bytes 8388608
  47.6 4.3 %copy-start.11 = (bf16[4608,64]{0,1:T(8,128)(2,1)S(1)}, bf16[4608,64]{0,1:T(8,128)(2,1)}, u32[]{:S(2)}) copy-start(bf16[4608,64]{0,1:T(8,128)(2,1)} %param.16) | copy-start | bytes 1769476
  47.7 4.3 %copy-start.12 = (bf16[4608,64]{0,1:T(8,128)(2,1)S(1)}, bf16[4608,64]{0,1:T(8,128)(2,1)}, u32[]{:S(2)}) copy-start(bf16[4608,64]{0,1:T(8,128)(2,1)} %param.17) | copy-start | bytes 1769476
  52.0 2.3 %copy-start.8 = (f32[9,512,256]{2,1,0:T(8,128)S(1)}, f32[9,512,256]{2,1,0:T(8,128)}, u32[]{:S(2)}) copy-start(f32[9,512,256]{2,1,0:T(8,128)} %copy-done.7) | copy-start | bytes 14155780
  60.0 1.4 %collective-permute-start.5 = (f32[192,128]{1,0:T(8,128)S(1)}, f32[192,128]{1,0:T(8,128)S(1)}, u32[]{:S(2)}, u32[]{:S(2)}) collective-permute-start(f32[192,128]{1,0:T(8,128)S(1)} %shard_map.130), channel_id=1, source_target_pairs={{0,1},{1,0},{2,3},{3,2},{4,5},{5,4},{6,7},{7,6},{8,9},{9,8},{10,11... | collective-permute-start | bytes 294920 | tf_op jit(solution)/shard_map/ppermute | solution.py:247
  61.4 5.1 %collective-permute-start.6 = (f32[192,128]{1,0:T(8,128)S(1)}, f32[192,128]{1,0:T(8,128)S(1)}, u32[]{:S(2)}, u32[]{:S(2)}) collective-permute-start(f32[192,128]{1,0:T(8,128)S(1)} %add.3.mine_ref), channel_id=1, source_target_pairs={{0,2},{1,3},{2,0},{3,1},{4,6},{5,7},{6,4},{7,5},{8,10},{9,11},{10,... | collective-permute-start | bytes 294920 | tf_op jit(solution)/shard_map/ppermute | solution.py:247

commit v3 on v2

v3 whole, which is shorter than its diff:
```python
import functools

import jax
import jax.numpy as jnp
from jax import lax
from jax.experimental import pallas as pl
from jax.experimental.pallas import tpu as pltpu
from jax.sharding import PartitionSpec as P

SEQS = 2
LEN = 128
FIRST = 768
MIB = 1 << 20
ANY = pl.BlockSpec(memory_space=pl.ANY)
VMEM = pl.BlockSpec(memory_space=pltpu.VMEM)
BF16 = jnp.bfloat16
F32 = jnp.float32


def product(left, right):
    return jnp.dot(left, right, preferred_element_type=F32)


def rows_by_rows(left, right, precision=None):
    return lax.dot_general(
        left, right, (((1,), (1,)), ((), ())), precision=precision, preferred_element_type=F32
    )


def per_sequence(matrix):
    return matrix.reshape(SEQS, matrix.shape[0] // SEQS, matrix.shape[1])


def plain(x_in, out_grad, gate_pre, up_pre, down_weight, x_factor, gate_factor, up_factor, h_factor, dy_factor):
    hidden_grad = rows_by_rows(lax.all_gather(out_grad, "tensor", axis=1, tiled=True), down_weight)
    gate_val = gate_pre.astype(F32)
    up_val = up_pre.astype(F32)
    sigmoid_gate = jax.nn.sigmoid(gate_val)
    silu_gate = gate_val * sigmoid_gate
    hidden = (silu_gate * up_val).astype(BF16)
    d_gate = (hidden_grad * up_val * sigmoid_gate * (1.0 + gate_val * (1.0 - sigmoid_gate))).astype(BF16)
    d_up = (hidden_grad * silu_gate).astype(BF16)
    rows = [
        product(x_in, x_factor),
        product(d_gate, gate_factor),
        product(d_up, up_factor),
        product(hidden, h_factor),
        product(out_grad, dy_factor),
    ]
    totals = lax.psum(jnp.stack(rows), "tensor")
    p_x, q_gate, q_up, p_h, q_y = [per_sequence(totals[i]) for i in range(5)]
    highest = lax.Precision.HIGHEST
    return (
        jnp.einsum("sli,slj->sij", p_x, q_gate, precision=highest),
        jnp.einsum("sli,slj->sij", p_x, q_up, precision=highest),
        jnp.einsum("sli,slj->sij", p_h, q_y, precision=highest),
    )


class Step:
    def __init__(self, bits, start, width, block, heads, ahead):
        self.bits, self.start, self.width = bits, start, width
        self.block, self.heads, self.ahead = block, heads, ahead

    def copy(self, w_hbm, i, dst, sem, per_device):
        owner = lax.axis_index("tensor") ^ self.bits
        columns = pl.ds(pl.multiple_of(owner * per_device + self.start, 128), self.width)
        return pltpu.make_async_copy(w_hbm.at[self.units(i), columns], dst, sem)

    def units(self, i):
        return pl.ds(pl.multiple_of(i * self.block, self.block), self.block)

    def head(self):
        return pltpu.VMEM((self.heads, self.block, self.width), BF16)

    def body(self, units):
        return pltpu.VMEM((units // self.block - self.heads, self.block, self.width), BF16)


def stream(step, following, units, per_device, w_hbm, head, w_v, next_head, sems, body):
    blocks = units // step.block

    def following_copy(j):
        return following.copy(w_hbm, j, next_head.at[j], sems.at[blocks + j], per_device)

    def start(j):
        @pl.when(j < blocks)
        def _():
            step.copy(w_hbm, j, w_v.at[j - step.heads], sems.at[j], per_device).start()

        if following is not None:

            @pl.when(j == blocks)
            def _():
                for k in range(following.heads):
                    following_copy(k).start()

    for j in range(step.heads, step.heads + step.ahead):
        step.copy(w_hbm, j, w_v.at[j - step.heads], sems.at[j], per_device).start()
    for i in range(step.heads):
        body(i, head.at[i])

    @pl.loop(step.heads, blocks)
    def _(i):
        start(i + step.ahead)
        step.copy(w_hbm, i, w_v.at[i - step.heads], sems.at[i], per_device).wait()
        body(i, w_v.at[i - step.heads])

    if following is not None:
        for j in range(following.heads):
            following_copy(j).wait()


def two_terms(value):
    high = value.astype(BF16)
    return high, (value - high.astype(F32)).astype(BF16)


def entry_kernel(first_step, x_hbm, og_hbm, xf_hbm, yf_hbm, w_hbm, mate_ref, piece_ref, pq_ref, head_ref,
                 x_v, og_v, xf_v, yf_v, sems):
    tokens, width = og_hbm.shape
    rank = xf_hbm.shape[0]
    pairs = ((og_hbm, og_v), (x_hbm, x_v), (xf_hbm, xf_v), (yf_hbm, yf_v))
    copies = [pltpu.make_async_copy(src, dst, sems.at[i]) for i, (src, dst) in enumerate(pairs)]
    copies += [first_step.copy(w_hbm, i, head_ref.at[i], sems.at[4 + i], width) for i in range(first_step.heads)]
    for copy in copies:
        copy.start()
    copies[0].wait()
    mate_ref[:tokens] = og_v[...]
    piece_ref[...] = og_v[:, :FIRST]
    for copy in copies[1:4]:
        copy.wait()
    pq_ref[:rank] = rows_by_rows(xf_v[...], x_v[...])
    pq_ref[rank:] = rows_by_rows(yf_v[...], og_v[...])
    high, rest = two_terms(pq_ref[...])
    for k, part in enumerate((high[:rank], high[rank:], rest[:rank], rest[rank:])):
        mate_ref[tokens:, k * tokens : (k + 1) * tokens] = part
    mate_ref[tokens:, 4 * tokens :] = jnp.zeros_like(mate_ref[tokens:, 4 * tokens :])
    for copy in copies[4:]:
        copy.wait()


def own_kernel(step, following, og_ref, head_ref, gate_hbm, up_hbm, w_hbm, hf_hbm,
               acc_ref, a_ref, b_ref, ph_ref, next_ref, gate_v, up_v, w_v, hf_v, sems, gate_sems, up_sems, hf_sem):
    tokens, units = acc_ref.shape
    blocks = units // step.block

    def gate_up(i):
        return (
            pltpu.make_async_copy(gate_hbm.at[:, step.units(i)], gate_v.at[i], gate_sems.at[i]),
            pltpu.make_async_copy(up_hbm.at[:, step.units(i)], up_v.at[i], up_sems.at[i]),
        )

    whole = pltpu.make_async_copy(hf_hbm, hf_v, hf_sem)
    for copy in gate_up(0):
        copy.start()
    whole.start()
    for i in range(1, step.ahead):
        for copy in gate_up(i):
            copy.start()
    ph_ref[...] = jnp.zeros_like(ph_ref)

    def body(i, weights):
        @pl.when(i + step.ahead < blocks)
        def _():
            for copy in gate_up(i + step.ahead):
                copy.start()

        for copy in gate_up(i):
            copy.wait()
        if isinstance(i, int) and i == 0:
            whole.wait()
        at = step.units(i)
        acc_ref[:, at] = rows_by_rows(og_ref[:tokens], weights[...])
        g = gate_v[i].astype(F32)
        u = up_v[i].astype(F32)
        s = 0.5 * jnp.tanh(0.5 * g) + 0.5
        silu = g * s
        a_ref[:, at] = u * s * (1.0 + g * (1.0 - s))
        b_ref[:, at] = silu
        ph_ref[...] += rows_by_rows(hf_v[:, at], (silu * u).astype(BF16))

    stream(step, following, units, step.width, w_hbm, head_ref, w_v, next_ref, sems, body)


def pack_kernel(mine_ref, theirs_ref, pq_ref, token_ref, chip_ref, across_ref):
    rank, tokens = pq_ref.shape[0] // 2, pq_ref.shape[1]

    def theirs(k):
        part = theirs_ref[tokens:, k * tokens : (k + 1) * tokens]
        return part.astype(F32)

    p_x = pq_ref[:rank] + (theirs(0) + theirs(2))
    q_y = pq_ref[rank:] + (theirs(1) + theirs(3))
    chip_ref[:rank] = p_x
    chip_ref[rank:] = q_y
    even = lax.rem(lax.axis_index("tensor"), 2) == 0
    high, rest = two_terms(jnp.where(even, p_x, q_y))
    across_ref[:tokens] = mine_ref[:tokens, FIRST:]
    across_ref[tokens:, :tokens] = high
    across_ref[tokens:, tokens:] = rest


def step_kernel(step, following, per_device, acc_in, og_ref, head_ref, w_hbm, token_ref, acc_ref, next_ref, w_v, sems):
    tokens, units = acc_in.shape

    def body(i, weights):
        at = step.units(i)
        acc_ref[:, at] = acc_in[:, at] + rows_by_rows(og_ref[:tokens], weights[...])

    stream(step, following, units, per_device, w_hbm, head_ref, w_v, next_ref, sems, body)


def after_kernel(array_ref, token_ref, same_ref):
    pass


def last_kernel(step, per_device, acc_ref, og_ref, head_ref, w_hbm, a_ref, b_ref, gf_ref, uf_ref, chip_ref, near_ref, ph_ref,
                share_ref, w_v, q_ref, sems):
    q_ref[...] = jnp.zeros_like(q_ref)
    rank = ph_ref.shape[0]
    tokens, units = acc_ref.shape

    def body(i, weights):
        at = step.units(i)
        hidden_grad = acc_ref[:, at] + rows_by_rows(og_ref[:tokens], weights[...])
        q_ref[:rank] += rows_by_rows(gf_ref[:, at], (hidden_grad * a_ref[:, at]).astype(BF16))
        q_ref[rank:] += rows_by_rows(uf_ref[:, at], (hidden_grad * b_ref[:, at]).astype(BF16))

    stream(step, None, units, per_device, w_hbm, head_ref, w_v, None, sems, body)

    def sums(ref):
        high, rest = ref[tokens:, :tokens], ref[tokens:, tokens:]
        return high.astype(F32) + rest.astype(F32)

    even = lax.rem(lax.axis_index("tensor"), 2) == 0
    near, far = sums(near_ref), sums(og_ref)
    p_x = chip_ref[:rank] + jnp.where(even, near, far)
    q_y = chip_ref[rank:] + jnp.where(even, far, near)
    highest = lax.Precision.HIGHEST
    for s in range(SEQS):
        at = slice(s * LEN, (s + 1) * LEN)
        share_ref[s * rank : (s + 1) * rank] = rows_by_rows(p_x[:, at], q_ref[:, at], highest)
        share_ref[SEQS * rank :, s * rank : (s + 1) * rank] = rows_by_rows(ph_ref[:, at], q_y[:, at], highest)


def sum_kernel(mine_ref, theirs_ref, gate_ref, up_ref, down_ref):
    rank = gate_ref.shape[1]
    total = mine_ref[...] + theirs_ref[...]
    for s in range(SEQS):
        gate_ref[s] = total[s * rank : (s + 1) * rank, :rank]
        up_ref[s] = total[s * rank : (s + 1) * rank, rank:]
        down_ref[s] = total[SEQS * rank :, s * rank : (s + 1) * rank]


def fast(x_in, out_grad, gate_pre, up_pre, down_weight, x_factor, gate_factor, up_factor, h_factor, dy_factor):
    tokens, width = out_grad.shape
    units, rank = h_factor.shape
    dma = pltpu.SemaphoreType.DMA

    def in_hbm(array):
        return pltpu.with_memory_space_constraint(array, pltpu.HBM)

    def swap(array, bits):
        return lax.ppermute(array, "tensor", [(i, i ^ bits) for i in range(4)])

    def call(kernel, out_shape, in_specs, scratch, mib, flops=0, moved=0, **kwargs):
        several = isinstance(out_shape, tuple)
        return pl.pallas_call(
            kernel,
            out_shape=out_shape,
            in_specs=in_specs,
            out_specs=(VMEM,) * len(out_shape) if several else VMEM,
            scratch_shapes=list(scratch),
            compiler_params=pltpu.CompilerParams(vmem_limit_bytes=mib * MIB),
            cost_estimate=pl.CostEstimate(flops=flops, bytes_accessed=moved, transcendentals=0),
            **kwargs,
        )

    own, mate = Step(0, 0, width, 512, 2, 4), Step(1, 0, width, 1536, 1, 2)
    near_a, far_a = Step(2, 0, FIRST, 768, 2, 3), Step(3, 0, FIRST, 1152, 1, 2)
    near_b, far_b = Step(2, FIRST, width - FIRST, 1536, 1, 2), Step(3, FIRST, width - FIRST, 768, 2, 3)
    held = pltpu.VMEM((tokens, units), F32)
    rows = tokens + rank
    weight, x_hbm, og_hbm = in_hbm(down_weight), in_hbm(x_in), in_hbm(out_grad)
    xf_hbm, yf_hbm, hf_hbm = in_hbm(x_factor.T), in_hbm(dy_factor.T), in_hbm(h_factor.T)

    to_mate, piece, pq, heads = call(
        functools.partial(entry_kernel, own),
        (
            pltpu.VMEM((rows, width), BF16),
            pltpu.VMEM((tokens, FIRST), BF16),
            pltpu.VMEM((2 * rank, tokens), F32),
            own.head(),
        ),
        [ANY] * 5,
        [
            pltpu.VMEM((tokens, width), BF16),
            pltpu.VMEM((tokens, width), BF16),
            pltpu.VMEM((rank, width), BF16),
            pltpu.VMEM((rank, width), BF16),
            dma((4 + own.heads,)),
        ],
        8,
    )(x_hbm, og_hbm, xf_hbm, yf_hbm, weight)
    near_first = swap(piece, 2)
    from_mate = swap(to_mate, 1)

    acc, a, b, ph, heads = call(
        functools.partial(own_kernel, own, mate),
        (held, held, held, pltpu.VMEM((rank, tokens), F32), mate.head()),
        [VMEM, VMEM] + [ANY] * 4,
        [
            pltpu.VMEM((units // own.block, tokens, own.block), BF16),
            pltpu.VMEM((units // own.block, tokens, own.block), BF16),
            own.body(units),
            pltpu.VMEM((rank, units), BF16),
            dma((units // own.block + mate.heads,)),
            dma((units // own.block,)),
            dma((units // own.block,)),
            dma,
        ],
        22,
        2 * tokens * width * units,
        2 * units * (width + 2 * tokens),
    )(to_mate, heads, in_hbm(gate_pre), in_hbm(up_pre), weight, hf_hbm)

    chip, across = call(
        pack_kernel,
        (pltpu.VMEM((2 * rank, tokens), F32), pltpu.VMEM((rows, width - FIRST), BF16)),
        [VMEM] * 3 + [ANY],
        [],
        4,
    )(to_mate, from_mate, pq, ph)
    near_second = swap(across, 2)

    def add(step, following, acc, features, heads, token):
        return call(
            functools.partial(step_kernel, step, following, width),
            (held, following.head()),
            [VMEM] * 3 + [ANY] * 2,
            [step.body(units), dma((units // step.block + following.heads,))],
            16,
            2 * tokens * step.width * units,
            2 * units * step.width,
            input_output_aliases={0: 0},
        )(acc, features, heads, weight, token)

    def after(array, token):
        return pl.pallas_call(
            after_kernel,
            out_shape=pltpu.VMEM(array.shape, array.dtype),
            in_specs=[ANY, ANY],
            out_specs=ANY,
            input_output_aliases={0: 0},
            compiler_params=pltpu.CompilerParams(vmem_limit_bytes=MIB),
        )(array, token)

    acc, heads = add(mate, near_a, acc, from_mate, heads, chip)
    near_first = after(near_first, heads)
    far_first = swap(near_first, 1)
    acc, heads = add(near_a, far_a, acc, near_first, heads, chip)
    acc, heads = add(far_a, near_b, acc, far_first, heads, chip)
    near_second = after(near_second, heads)
    far_second = swap(near_second, 1)
    acc, heads = add(near_b, far_b, acc, near_second, heads, chip)
    share = call(
        functools.partial(last_kernel, far_b, width),
        pltpu.VMEM(((SEQS + 1) * rank, 2 * rank), F32),
        [VMEM] * 3 + [ANY] + [VMEM] * 7,
        [far_b.body(units), pltpu.VMEM((2 * rank, tokens), F32), dma((units // far_b.block,))],
        16,
        2 * tokens * far_b.width * units,
        2 * units * far_b.width,
    )(acc, far_second, heads, weight, a, b, gate_factor.T, up_factor.T, chip, near_second, ph)

    chip_share = share + swap(share, 1)
    out = jax.ShapeDtypeStruct((SEQS, rank, rank), F32)
    return call(sum_kernel, (out, out, out), [VMEM] * 2, [], 4)(chip_share, swap(chip_share, 2))


def solution(mesh):
    def per_device(*arrays):
        (tokens, width), (units, rank) = arrays[1].shape, arrays[8].shape
        fits = (
            mesh.shape["tensor"] == 4
            and (tokens, rank) == (SEQS * LEN, LEN // 2)
            and width == FIRST + 2 * tokens
            and units % 4608 == 0
        )
        return tuple((fast if fits else plain)(*arrays))

    return jax.shard_map(
        per_device,
        mesh=mesh,
        in_specs=(P("dp", "tensor"),) * 4 + (P("tensor", None),) * 6,
        out_specs=(P("dp", None, None),) * 3,
        check_vma=False,
    )
```

time: 67.6 us -> 45.9 us (0.68)
  local copies, waits for them, and re-layouts: 16.3 us -> 0.01 us
  Pallas kernels: 39.9 us -> 32.7 us
  waiting for transfers between devices: 4.26 us -> 7.83 us
  starting transfers between devices: 5.88 us -> 4.48 us
    unnamed x30 -> x4, local copies, waits for them, and re-layouts: 16.3 us -> 0.01 us
    pallas_call x6, Pallas kernels: 22.5 us -> 17.6 us  [the longest x4 15.3 us: add(): call(functools.partial(step_kernel, step, following, width), (held, follo...]
    ppermute x7, waiting for transfers between devices: 4.26 us -> 7.83 us  [swap(): return lax.ppermute(array, 'tensor', [(i, i ^ bits) for i in range(4)])]
    pallas_call x1, Pallas kernels: 11.1 us -> 9.12 us  [fast(): call(functools.partial(own_kernel, own, mate), (held, held, held, pltpu.V...]
    ppermute x7, starting transfers between devices: 5.88 us -> 4.48 us  [swap(): return lax.ppermute(array, 'tensor', [(i, i ^ bits) for i in range(4)])]
  transfers between devices with their start and end apart: 7 -> 7, of which waited for: 2 -> 3; matrix products, arithmetic and copies ran while one was open for 0% -> 0% of each run, Pallas kernels for 47% -> 53%
where the time goes in v3:
time: 45.9 us; the launch traced here: 45.8 us
  Pallas kernels  32.7 us (71%)
  waiting for transfers between devices  7.83 us (17%)
  starting transfers between devices  4.48 us (10%)
  between operations  0.76 us (2%)
    pallas_call x4, Pallas kernels, add(): call(functools.partial(step_kernel, step, following, width), (held, follo...  15.3 us
    pallas_call x1, Pallas kernels, fast(): call(functools.partial(own_kernel, own, mate), (held, held, held, pltpu.V...  9.12 us
    ppermute x7, waiting for transfers between devices, swap(): return lax.ppermute(array, 'tensor', [(i, i ^ bits) for i in range(4)])  7.83 us
    pallas_call x1, Pallas kernels, fast(): call(functools.partial(last_kernel, far_b, width), pltpu.VMEM(((SEQS + 1)...  5.17 us
    ppermute x7, starting transfers between devices, swap(): return lax.ppermute(array, 'tensor', [(i, i ^ bits) for i in range(4)])  4.48 us
    pallas_call x1, Pallas kernels, fast(): call(functools.partial(entry_kernel, own), (pltpu.VMEM((rows, width), BF1...  2.27 us
  transfers between devices with their start and end apart: 7, of which 3 were waited for; matrix products, arithmetic and copies ran while one was open for 0% of the time, Pallas kernels for 53%

profile of v3, /device:TPU:0, one launch (start us, length us, event | category | flops | bytes accessed | tf_op | source)
XLA Modules:
  0.0 45.8 jit_solution(5173688998953163242)
XLA Ops:
  0.6 2.3 %shard_map.121 = (bf16[320,1280]{1,0:T(8,128)(2,1)S(1)}, bf16[256,768]{1,0:T(8,128)(2,1)S(1)}, f32[128,256]{1,0:T(8,128)S(1)}, bf16[2,512,1280]{2,1,0:T(8,128)(2,1)S(1)}) custom-call(bf16[256,1280]{1,0:T(8,128)(2,1)} %x_hbm.1, bf16[256,1280]{1,0:T(8,128)(2,1)} %og_hbm.1, bf16[64,1280]{1,0:T(8,128)(2,1)} %bitcast.8, bf16[64,1280]{1,0:T(8,128)(2,1)} %bitcast.9, ...), custom_call_target="tpu_custom_call" | custom-call | tf_op jit(solution)/shard_map/pallas_call | solution.py:288
  2.9 0.5 %collective-permute-start = (bf16[320,1280]{1,0:T(8,128)(2,1)S(1)}, bf16[320,1280]{1,0:T(8,128)(2,1)S(1)}, u32[]{:S(2)}, u32[]{:S(2)}) collective-permute-start(bf16[320,1280]{1,0:T(8,128)(2,1)S(1)} %get-tuple-element.22.og_ref.mine_ref), channel_id=1, source_target_pairs={{0,1},{1,0},{2,3},{3,2},{4,5},{5,4},{6,7},{7,6},{8,9},{9,8},{10,11... | collective-permute-start | bytes 2457608 | tf_op jit(solution)/shard_map/ppermute | solution.py:265
  3.4 2.6 %collective-permute-start.1 = (bf16[256,768]{1,0:T(8,128)(2,1)S(1)}, bf16[256,768]{1,0:T(8,128)(2,1)S(1)}, u32[]{:S(2)}, u32[]{:S(2)}) collective-permute-start(bf16[256,768]{1,0:T(8,128)(2,1)S(1)} %get-tuple-element.30), channel_id=1, source_target_pairs={{0,2},{1,3},{2,0},{3,1},{4,6},{5,7},{6,4},{7,5},{8,10},{9,11},{10,... | collective-permute-start | bytes 1179656 | tf_op jit(solution)/shard_map/ppermute | solution.py:265
  6.0 9.1 %shard_map.122 = (f32[256,4608]{1,0:T(8,128)S(1)}, f32[256,4608]{1,0:T(8,128)S(1)}, f32[256,4608]{1,0:T(8,128)S(1)}, f32[64,256]{1,0:T(8,128)S(1)}, bf16[1,1536,1280]{2,1,0:T(8,128)(2,1)S(1)}) custom-call(bf16[320,1280]{1,0:T(8,128)(2,1)S(1)} %get-tuple-element.22.og_ref.mine_ref, bf16[2,512,1280]{2,1,0:T(8,128)(2,1)S(1)} %get-tuple-element.23.head_ref, ...), custom_call_target="tpu_custom_call" | custom-call | flops 3019898880 | bytes 16515072 | tf_op jit(solution)/shard_map/pallas_call | solution.py:309
  15.1 0.0 collective-permute-done.theirs_ref.og_ref
  15.2 4.8 %shard_map.124 = (f32[256,4608]{1,0:T(8,128)S(1)}, bf16[2,768,768]{2,1,0:T(8,128)(2,1)S(1)}) custom-call(f32[256,4608]{1,0:T(8,128)S(1)} %get-tuple-element.24.acc_in, bf16[320,1280]{1,0:T(8,128)(2,1)S(1)} %collective-permute-done.theirs_ref.og_ref, bf16[1,1536,1280]{2,1,0:T(8,128)(2,1)S(1)} %get-tuple-element.25.head_ref, ...), custom_call_target="tpu_custom_call", output_to_operand_aliasing={{0}: (0, {})} | custom-call | flops 3019898880 | bytes 11796480 | tf_op jit(solution)/shard_map/pallas_call | solution.py:338
  20.0 0.0 collective-permute-done.1.array_ref
  20.0 0.2 collective-permute-start.2
  20.3 0.3 collective-permute-start.3
  20.5 3.6 %shard_map.126 = (f32[256,4608]{1,0:T(8,128)S(1)}, bf16[1,1152,768]{2,1,0:T(8,128)(2,1)S(1)}) custom-call(f32[256,4608]{1,0:T(8,128)S(1)} %get-tuple-element.29.acc_in, bf16[256,768]{1,0:T(8,128)(2,1)S(1)} %shard_map.125.og_ref, bf16[2,768,768]{2,1,0:T(8,128)(2,1)S(1)} %get-tuple-element.31.token_ref.head_ref, ...), custom_call_target="tpu_custom_call", output_to_operand_aliasing={{0}: (0, {})} | custom-call | flops 1811939328 | bytes 7077888 | tf_op jit(solution)/shard_map/pallas_call | solution.py:338
  24.2 0.0 collective-permute-done.2.og_ref
  24.2 3.9 %shard_map.127 = (f32[256,4608]{1,0:T(8,128)S(1)}, bf16[1,1536,512]{2,1,0:T(8,128)(2,1)S(1)}) custom-call(f32[256,4608]{1,0:T(8,128)S(1)} %get-tuple-element.32.acc_in, bf16[256,768]{1,0:T(8,128)(2,1)S(1)} %collective-permute-done.2.og_ref, bf16[1,1152,768]{2,1,0:T(8,128)(2,1)S(1)} %get-tuple-element.33.head_ref, ...), custom_call_target="tpu_custom_call", output_to_operand_aliasing={{0}: (0, {})} | custom-call | flops 1811939328 | bytes 7077888 | tf_op jit(solution)/shard_map/pallas_call | solution.py:338
  28.1 2.2 %collective-permute-done.3.array_ref = bf16[320,512]{1,0:T(8,128)(2,1)S(1)} collective-permute-done((bf16[320,512]{1,0:T(8,128)(2,1)S(1)}, bf16[320,512]{1,0:T(8,128)(2,1)S(1)}, u32[]{:S(2)}, u32[]{:S(2)}) %collective-permute-start.3) | collective-permute-done | bytes 327712 | tf_op jit(solution)/shard_map/ppermute | solution.py:265
  30.2 0.0 collective-permute-start.4
  30.2 0.0 copy-start
  30.2 0.0 copy-start.1
  30.2 3.0 %shard_map.129 = (f32[256,4608]{1,0:T(8,128)S(1)}, bf16[2,768,512]{2,1,0:T(8,128)(2,1)S(1)}) custom-call(f32[256,4608]{1,0:T(8,128)S(1)} %get-tuple-element.34.acc_in, bf16[320,512]{1,0:T(8,128)(2,1)S(1)} %shard_map.128.og_ref.near_ref, bf16[1,1536,512]{2,1,0:T(8,128)(2,1)S(1)} %get-tuple-element.36.token_ref.head_ref, ...), custom_call_target="tpu_custom_call", output_to_operand_aliasing={{0}: (0, {})} | custom-call | flops 1207959552 | bytes 4718592 | tf_op jit(solution)/shard_map/pallas_call | solution.py:338
  33.2 0.0 collective-permute-done.4.og_ref
  33.3 0.0 copy-done
  33.3 0.0 copy-done.1
  33.3 5.2 %shard_map.130 = f32[192,128]{1,0:T(8,128)S(1)} custom-call(f32[256,4608]{1,0:T(8,128)S(1)} %get-tuple-element.37.acc_ref, bf16[320,512]{1,0:T(8,128)(2,1)S(1)} %collective-permute-done.4.og_ref, bf16[2,768,512]{2,1,0:T(8,128)(2,1)S(1)} %get-tuple-element.38.head_ref, bf16[4608,5120]{1,0:T(8,128)(2,1)} %w_hbm.13, f32[256,4608]{1,0:T(8,128)S(1)} %get-tuple-element.39.a_ref, ...), custom_call_target="tpu_custom_call" | custom-call | flops 1207959552 | bytes 4718592 | tf_op jit(solution)/shard_map/pallas_call | solution.py:367
  38.5 0.5 %collective-permute-start.5 = (f32[192,128]{1,0:T(8,128)S(1)}, f32[192,128]{1,0:T(8,128)S(1)}, u32[]{:S(2)}, u32[]{:S(2)}) collective-permute-start(f32[192,128]{1,0:T(8,128)S(1)} %shard_map.130), channel_id=1, source_target_pairs={{0,1},{1,0},{2,3},{3,2},{4,5},{5,4},{6,7},{7,6},{8,9},{9,8},{10,11... | collective-permute-start | bytes 294920 | tf_op jit(solution)/shard_map/ppermute | solution.py:265
  39.0 0.9 %collective-permute-done.5 = f32[192,128]{1,0:T(8,128)S(1)} collective-permute-done((f32[192,128]{1,0:T(8,128)S(1)}, f32[192,128]{1,0:T(8,128)S(1)}, u32[]{:S(2)}, u32[]{:S(2)}) %collective-permute-start.5) | collective-permute-done | bytes 98336 | tf_op jit(solution)/shard_map/ppermute | solution.py:265
  39.9 0.4 collective-permute-start.6
  40.3 4.7 %collective-permute-done.6.theirs_ref = f32[192,128]{1,0:T(8,128)S(1)} collective-permute-done((f32[192,128]{1,0:T(8,128)S(1)}, f32[192,128]{1,0:T(8,128)S(1)}, u32[]{:S(2)}, u32[]{:S(2)}) %collective-permute-start.6) | collective-permute-done | bytes 98336 | tf_op jit(solution)/shard_map/ppermute | solution.py:265
  45.0 0.7 %shard_map.131 = (f32[2,64,64]{2,1,0:T(8,128)}, f32[2,64,64]{2,1,0:T(8,128)}, f32[2,64,64]{2,1,0:T(8,128)}) custom-call(f32[192,128]{1,0:T(8,128)S(1)} %add.3.mine_ref, f32[192,128]{1,0:T(8,128)S(1)} %collective-permute-done.6.theirs_ref), custom_call_target="tpu_custom_call" | custom-call | tf_op jit(solution)/shard_map/pallas_call | solution.py:379
  (4 shorter events, 0.1 us)
Async XLA Ops:
  2.9 12.2 %collective-permute-start = (bf16[320,1280]{1,0:T(8,128)(2,1)S(1)}, bf16[320,1280]{1,0:T(8,128)(2,1)S(1)}, u32[]{:S(2)}, u32[]{:S(2)}) collective-permute-start(bf16[320,1280]{1,0:T(8,128)(2,1)S(1)} %get-tuple-element.22.og_ref.mine_ref), channel_id=1, source_target_pairs={{0,1},{1,0},{2,3},{3,2},{4,5},{5,4},{6,7},{7,6},{8,9},{9,8},{10,11... | collective-permute-start | bytes 2457608 | tf_op jit(solution)/shard_map/ppermute | solution.py:265
  3.4 16.6 %collective-permute-start.1 = (bf16[256,768]{1,0:T(8,128)(2,1)S(1)}, bf16[256,768]{1,0:T(8,128)(2,1)S(1)}, u32[]{:S(2)}, u32[]{:S(2)}) collective-permute-start(bf16[256,768]{1,0:T(8,128)(2,1)S(1)} %get-tuple-element.30), channel_id=1, source_target_pairs={{0,2},{1,3},{2,0},{3,1},{4,6},{5,7},{6,4},{7,5},{8,10},{9,11},{10,... | collective-permute-start | bytes 1179656 | tf_op jit(solution)/shard_map/ppermute | solution.py:265
  20.0 4.1 %collective-permute-start.2 = (bf16[256,768]{1,0:T(8,128)(2,1)S(1)}, bf16[256,768]{1,0:T(8,128)(2,1)S(1)}, u32[]{:S(2)}, u32[]{:S(2)}) collective-permute-start(bf16[256,768]{1,0:T(8,128)(2,1)S(1)} %shard_map.125.og_ref), channel_id=1, source_target_pairs={{0,1},{1,0},{2,3},{3,2},{4,5},{5,4},{6,7},{7,6},{8,9},{9,8},{10,11... | collective-permute-start | bytes 1179656 | tf_op jit(solution)/shard_map/ppermute | solution.py:265
  20.3 10.0 %collective-permute-start.3 = (bf16[320,512]{1,0:T(8,128)(2,1)S(1)}, bf16[320,512]{1,0:T(8,128)(2,1)S(1)}, u32[]{:S(2)}, u32[]{:S(2)}) collective-permute-start(bf16[320,512]{1,0:T(8,128)(2,1)S(1)} %get-tuple-element.35), channel_id=1, source_target_pairs={{0,2},{1,3},{2,0},{3,1},{4,6},{5,7},{6,4},{7,5},{8,10},{9,11},{10,... | collective-permute-start | bytes 983048 | tf_op jit(solution)/shard_map/ppermute | solution.py:265
  30.2 3.0 %collective-permute-start.4 = (bf16[320,512]{1,0:T(8,128)(2,1)S(1)}, bf16[320,512]{1,0:T(8,128)(2,1)S(1)}, u32[]{:S(2)}, u32[]{:S(2)}) collective-permute-start(bf16[320,512]{1,0:T(8,128)(2,1)S(1)} %shard_map.128.og_ref.near_ref), channel_id=1, source_target_pairs={{0,1},{1,0},{2,3},{3,2},{4,5},{5,4},{6,7},{7,6},{8,9},{9,8},{10,11... | collective-permute-start | bytes 983048 | tf_op jit(solution)/shard_map/ppermute | solution.py:265
  30.2 3.0 %copy-start = (bf16[4608,64]{0,1:T(8,128)(2,1)S(1)}, bf16[4608,64]{0,1:T(8,128)(2,1)}, u32[]{:S(2)}) copy-start(bf16[4608,64]{0,1:T(8,128)(2,1)} %param.16) | copy-start | bytes 1769476
  30.2 3.0 %copy-start.1 = (bf16[4608,64]{0,1:T(8,128)(2,1)S(1)}, bf16[4608,64]{0,1:T(8,128)(2,1)}, u32[]{:S(2)}) copy-start(bf16[4608,64]{0,1:T(8,128)(2,1)} %param.17) | copy-start | bytes 1769476
  38.5 1.4 %collective-permute-start.5 = (f32[192,128]{1,0:T(8,128)S(1)}, f32[192,128]{1,0:T(8,128)S(1)}, u32[]{:S(2)}, u32[]{:S(2)}) collective-permute-start(f32[192,128]{1,0:T(8,128)S(1)} %shard_map.130), channel_id=1, source_target_pairs={{0,1},{1,0},{2,3},{3,2},{4,5},{5,4},{6,7},{7,6},{8,9},{9,8},{10,11... | collective-permute-start | bytes 294920 | tf_op jit(solution)/shard_map/ppermute | solution.py:265
  39.9 5.1 %collective-permute-start.6 = (f32[192,128]{1,0:T(8,128)S(1)}, f32[192,128]{1,0:T(8,128)S(1)}, u32[]{:S(2)}, u32[]{:S(2)}) collective-permute-start(f32[192,128]{1,0:T(8,128)S(1)} %add.3.mine_ref), channel_id=1, source_target_pairs={{0,2},{1,3},{2,0},{3,1},{4,6},{5,7},{6,4},{7,5},{8,10},{9,11},{10,... | collective-permute-start | bytes 294920 | tf_op jit(solution)/shard_map/ppermute | solution.py:265

commit v4 on v0

v4 whole, which is shorter than its diff:
```python
import functools

import jax
import jax.numpy as jnp
from jax import lax
from jax.experimental import pallas as pl
from jax.experimental.pallas import tpu as pltpu
from jax.sharding import PartitionSpec as P

SEQS = 2
LEN = 128
PIECE = 512
BLOCK = 1536
LAST = 768
MIB = 1 << 20
ANY = pl.BlockSpec(memory_space=pl.ANY)
VMEM = pl.BlockSpec(memory_space=pltpu.VMEM)
BF16 = jnp.bfloat16
F32 = jnp.float32


def product(left, right):
    return jnp.dot(left, right, preferred_element_type=F32)


def rows_by_rows(left, right, precision=None):
    return lax.dot_general(
        left, right, (((1,), (1,)), ((), ())), precision=precision, preferred_element_type=F32
    )


def per_sequence(matrix):
    return matrix.reshape(SEQS, matrix.shape[0] // SEQS, matrix.shape[1])


def plain(x_in, out_grad, gate_pre, up_pre, down_weight, x_factor, gate_factor, up_factor, h_factor, dy_factor):
    hidden_grad = rows_by_rows(lax.all_gather(out_grad, "tensor", axis=1, tiled=True), down_weight)
    gate_val = gate_pre.astype(F32)
    up_val = up_pre.astype(F32)
    sigmoid_gate = jax.nn.sigmoid(gate_val)
    silu_gate = gate_val * sigmoid_gate
    hidden = (silu_gate * up_val).astype(BF16)
    d_gate = (hidden_grad * up_val * sigmoid_gate * (1.0 + gate_val * (1.0 - sigmoid_gate))).astype(BF16)
    d_up = (hidden_grad * silu_gate).astype(BF16)
    rows = [
        product(x_in, x_factor),
        product(d_gate, gate_factor),
        product(d_up, up_factor),
        product(hidden, h_factor),
        product(out_grad, dy_factor),
    ]
    totals = lax.psum(jnp.stack(rows), "tensor")
    p_x, q_gate, q_up, p_h, q_y = [per_sequence(totals[i]) for i in range(5)]
    highest = lax.Precision.HIGHEST
    return (
        jnp.einsum("sli,slj->sij", p_x, q_gate, precision=highest),
        jnp.einsum("sli,slj->sij", p_x, q_up, precision=highest),
        jnp.einsum("sli,slj->sij", p_h, q_y, precision=highest),
    )


def weight_copies(w_hbm, bits, dst, sems, first_row=0):
    width = dst.shape[1]
    columns = pl.ds(pl.multiple_of((lax.axis_index("tensor") ^ bits) * width, 128), width)
    return [
        pltpu.make_async_copy(
            w_hbm.at[pl.ds(first_row + k * PIECE, PIECE), columns], dst.at[pl.ds(k * PIECE, PIECE)], sems.at[k]
        )
        for k in range(dst.shape[0] // PIECE)
    ]


def start(copies):
    for copy in copies:
        copy.start()


def wait(copies):
    for copy in copies:
        copy.wait()


def own_kernel(x_hbm, og_hbm, gate_hbm, up_hbm, w_hbm, xf_hbm, yf_hbm, hf_hbm,
               acc_ref, a_ref, b_ref, ph_ref, pq_ref, next_ref,
               x_v, og_v, gate_v, up_v, w_v, xf_v, yf_v, hf_v, hidden_v, sems, gate_sems, up_sems, w_sems, next_sems):
    units = acc_ref.shape[1]
    rank = ph_ref.shape[0]
    per_turn = BLOCK // PIECE
    turns = units // BLOCK

    def gate_up(k):
        at, slot, to = pl.ds(k * PIECE, PIECE), k // per_turn % 2, pl.ds(k % per_turn * PIECE, PIECE)
        return [
            pltpu.make_async_copy(gate_hbm.at[:, at], gate_v.at[slot, :, to], gate_sems.at[k]),
            pltpu.make_async_copy(up_hbm.at[:, at], up_v.at[slot, :, to], up_sems.at[k]),
        ]

    def weights(i):
        return weight_copies(w_hbm, 0, w_v.at[i % 2], w_sems.at[i], i * BLOCK)

    pairs = ((og_hbm, og_v), (hf_hbm, hf_v), (x_hbm, x_v), (xf_hbm, xf_v), (yf_hbm, yf_v))
    small = [pltpu.make_async_copy(src, dst, sems.at[i]) for i, (src, dst) in enumerate(pairs)]
    following = weight_copies(w_hbm, 1, next_ref, next_sems)

    def start_turn(i):
        for k in range(i * per_turn, (i + 1) * per_turn):
            start(gate_up(k))
            if k == 0:
                start(small[:2])
        start(weights(i))

    start_turn(0)
    start_turn(1)
    start(small[2:])
    ph_ref[...] = jnp.zeros_like(ph_ref)
    for i in range(turns):
        slot = i % 2
        for k in range(per_turn):
            at = slice(i * BLOCK + k * PIECE, i * BLOCK + (k + 1) * PIECE)
            part = slice(k * PIECE, (k + 1) * PIECE)
            wait(gate_up(i * per_turn + k))
            g = gate_v[slot, :, part].astype(F32)
            u = up_v[slot, :, part].astype(F32)
            s = 0.5 * jnp.tanh(0.5 * g) + 0.5
            silu = g * s
            a_ref[:, at] = u * s * (1.0 + g * (1.0 - s))
            b_ref[:, at] = silu
            hidden_v[:, part] = (silu * u).astype(BF16)
        at = slice(i * BLOCK, (i + 1) * BLOCK)
        if i == 0:
            wait(small[:2])
        wait(weights(i))
        acc_ref[:, at] = rows_by_rows(og_v[...], w_v[slot])
        ph_ref[...] += rows_by_rows(hf_v[:, at], hidden_v[...])
        if i + 2 < turns:
            start_turn(i + 2)
        if i + 2 == turns:
            start(following)
    wait(small[2:])
    pq_ref[:rank] = rows_by_rows(xf_v[...], x_v[...])
    pq_ref[rank:] = rows_by_rows(yf_v[...], og_v[...])
    wait(following)


def add_kernel(bits, following_bits, acc_in, og_ref, head_ref, w_hbm, acc_ref, next_ref, w_v, sems, next_sems):
    first = head_ref.shape[0]
    weights = weight_copies(w_hbm, bits, w_v, sems, first)
    following = weight_copies(w_hbm, following_bits, next_ref, next_sems)
    start(weights)
    start(following)
    for i in range(acc_in.shape[1] // BLOCK):
        row = i * BLOCK
        at = slice(row, row + BLOCK)
        if row < first:
            block = head_ref[at]
        else:
            wait(weights[(row - first) // PIECE : (row + BLOCK - first) // PIECE])
            block = w_v[row - first : row + BLOCK - first]
        acc_ref[:, at] = acc_in[:, at] + rows_by_rows(og_ref[...], block)
    wait(following)


def far_kernel(bits, acc_ref, og_ref, head_ref, w_hbm, a_ref, b_ref, gf_ref, uf_ref, q_ref, w_v, sems):
    rank = gf_ref.shape[0]
    first = head_ref.shape[0]
    weights = weight_copies(w_hbm, bits, w_v, sems, first)
    start(weights)
    q_ref[...] = jnp.zeros_like(q_ref)

    def turn(at, block):
        hidden_grad = acc_ref[:, at] + rows_by_rows(og_ref[...], block)
        q_ref[:rank] += rows_by_rows(gf_ref[:, at], (hidden_grad * a_ref[:, at]).astype(BF16))
        q_ref[rank:] += rows_by_rows(uf_ref[:, at], (hidden_grad * b_ref[:, at]).astype(BF16))

    @pl.loop(0, first // LAST)
    def _(i):
        at = pl.ds(pl.multiple_of(i * LAST, LAST), LAST)
        turn(at, head_ref[at])

    wait(weights)

    @pl.loop(0, w_v.shape[0] // LAST)
    def _(i):
        row = pl.multiple_of(i * LAST, LAST)
        turn(pl.ds(pl.multiple_of(first + row, LAST), LAST), w_v[pl.ds(row, LAST)])


def after_kernel(array_ref, token_ref, same_ref):
    pass


def chip_kernel(mine_ref, theirs_ref, token_ref, chip_ref):
    chip_ref[...] = mine_ref[...] + theirs_ref[...]


def gradients_kernel(chip_ref, other_ref, q_ref, ph_ref, share_ref):
    rank = ph_ref.shape[0]
    highest = lax.Precision.HIGHEST
    total = chip_ref[...] + other_ref[...]
    for s in range(SEQS):
        at = slice(s * LEN, (s + 1) * LEN)
        share_ref[s * rank : (s + 1) * rank] = rows_by_rows(total[:rank, at], q_ref[:, at], highest)
        share_ref[SEQS * rank :, s * rank : (s + 1) * rank] = rows_by_rows(ph_ref[:, at], total[rank:, at], highest)


def sum_kernel(mine_ref, theirs_ref, gate_ref, up_ref, down_ref):
    rank = gate_ref.shape[1]
    total = mine_ref[...] + theirs_ref[...]
    for s in range(SEQS):
        gate_ref[s] = total[s * rank : (s + 1) * rank, :rank]
        up_ref[s] = total[s * rank : (s + 1) * rank, rank:]
        down_ref[s] = total[SEQS * rank :, s * rank : (s + 1) * rank]


def fast(x_in, out_grad, gate_pre, up_pre, down_weight, x_factor, gate_factor, up_factor, h_factor, dy_factor):
    tokens, width = out_grad.shape
    units, rank = h_factor.shape
    dma = pltpu.SemaphoreType.DMA

    def in_hbm(array):
        return pltpu.with_memory_space_constraint(array, pltpu.HBM)

    def swap(array, bits):
        return lax.ppermute(array, "tensor", [(i, i ^ bits) for i in range(4)])

    def call(kernel, out_shape, in_specs, scratch, mib, flops=0, moved=0, **kwargs):
        several = isinstance(out_shape, tuple)
        return pl.pallas_call(
            kernel,
            out_shape=out_shape,
            in_specs=in_specs,
            out_specs=(VMEM,) * len(out_shape) if several else VMEM,
            scratch_shapes=list(scratch),
            compiler_params=pltpu.CompilerParams(vmem_limit_bytes=mib * MIB),
            cost_estimate=pl.CostEstimate(flops=flops, bytes_accessed=moved, transcendentals=0),
            **kwargs,
        )

    held = pltpu.VMEM((tokens, units), F32)
    per_product = 2 * tokens * width * units
    pieces = units // PIECE
    per_turn = BLOCK // PIECE
    weight, og_hbm = in_hbm(down_weight), in_hbm(out_grad)

    near = swap(out_grad, 2)
    mate = swap(out_grad, 1)
    acc, a, b, ph, pq, head = call(
        own_kernel,
        (held, held, held, pltpu.VMEM((rank, tokens), F32), pltpu.VMEM((2 * rank, tokens), F32), pltpu.VMEM((BLOCK, width), BF16)),
        [ANY] * 8,
        [
            pltpu.VMEM((tokens, width), BF16),
            pltpu.VMEM((tokens, width), BF16),
            pltpu.VMEM((2, tokens, BLOCK), BF16),
            pltpu.VMEM((2, tokens, BLOCK), BF16),
            pltpu.VMEM((2, BLOCK, width), BF16),
            pltpu.VMEM((rank, width), BF16),
            pltpu.VMEM((rank, width), BF16),
            pltpu.VMEM((rank, units), BF16),
            pltpu.VMEM((tokens, BLOCK), BF16),
            dma((5,)),
            dma((pieces,)),
            dma((pieces,)),
            dma((units // BLOCK, per_turn)),
            dma((per_turn,)),
        ],
        20,
        per_product,
        2 * units * (width + 2 * tokens),
    )(in_hbm(x_in), og_hbm, in_hbm(gate_pre), in_hbm(up_pre), weight, in_hbm(x_factor.T), in_hbm(dy_factor.T), in_hbm(h_factor.T))
    pq_mate = swap(pq, 1)

    def add(bits, following_bits, acc, features, head):
        rest = units - head.shape[0]
        return call(
            functools.partial(add_kernel, bits, following_bits),
            (held, pltpu.VMEM((2 * BLOCK, width), BF16)),
            [VMEM] * 3 + [ANY],
            [pltpu.VMEM((rest, width), BF16), dma((rest // PIECE,)), dma((2 * per_turn,))],
            12,
            per_product,
            4 * units * width,
            input_output_aliases={0: 0},
        )(acc, features, head, weight)

    acc, head = add(1, 2, acc, mate, head)
    near = pl.pallas_call(
        after_kernel,
        out_shape=pltpu.VMEM(near.shape, near.dtype),
        in_specs=[ANY, ANY],
        out_specs=ANY,
        input_output_aliases={0: 0},
        compiler_params=pltpu.CompilerParams(vmem_limit_bytes=MIB),
    )(near, head)
    far = swap(near, 1)
    acc, head = add(2, 3, acc, near, head)
    chip = call(chip_kernel, pltpu.VMEM(pq.shape, F32), [VMEM, VMEM, ANY], [], 1)(pq, pq_mate, head)
    chip_across = swap(chip, 2)
    rest = units - 2 * BLOCK
    q = call(
        functools.partial(far_kernel, 3),
        pltpu.VMEM((2 * rank, tokens), F32),
        [VMEM] * 3 + [ANY] + [VMEM] * 4,
        [pltpu.VMEM((rest, width), BF16), dma((rest // PIECE,))],
        10,
        per_product,
        2 * units * width,
    )(acc, far, head, weight, a, b, gate_factor.T, up_factor.T)
    share = call(gradients_kernel, pltpu.VMEM(((SEQS + 1) * rank, 2 * rank), F32), [VMEM] * 4, [], 4)(chip, chip_across, q, ph)
    chip_share = share + swap(share, 1)
    out = jax.ShapeDtypeStruct((SEQS, rank, rank), F32)
    return call(sum_kernel, (out, out, out), [VMEM] * 2, [], 4)(chip_share, swap(chip_share, 2))


def solution(mesh):
    def per_device(*arrays):
        (tokens, width), (units, rank) = arrays[1].shape, arrays[8].shape
        fits = (
            mesh.shape["tensor"] == 4
            and (tokens, rank) == (SEQS * LEN, LEN // 2)
            and width % 128 == 0
            and units % BLOCK == 0
            and units // BLOCK > 2
        )
        return tuple((fast if fits else plain)(*arrays))

    return jax.shard_map(
        per_device,
        mesh=mesh,
        in_specs=(P("dp", "tensor"),) * 4 + (P("tensor", None),) * 6,
        out_specs=(P("dp", None, None),) * 3,
        check_vma=False,
    )
```

time: 115 us -> 44.8 us (0.39)
  waiting for transfers between devices: 61.5 us -> 5.15 us
  matrix products: 34.9 us -> 0 us
  Pallas kernels: 0 us -> 32.8 us
  between operations: 14.2 us -> 0.73 us
  starting transfers between devices: 0.08 us -> 5.02 us
  local copies, waits for them, and re-layouts: 3.51 us -> 0.92 us
    dot_general x8 -> x0, matrix products: 34.9 us -> none  [the longest x1 22.1 us: per_device(): lax.dot_general(lax.all_gather(out_grad, 'tensor', axis=1, tiled=True), d...]
    pallas_call x0 -> x8, Pallas kernels: none -> 32.8 us  [the longest x2 13.6 us: add(): call(functools.partial(add_kernel, bits, following_bits), (held, pltpu.VM...]
    psum x1 -> x0, waiting for transfers between devices: 32.4 us -> none  [per_device(): totals = lax.psum(partial_rows, 'tensor')]
    all_gather x1 -> x0, waiting for transfers between devices: 28.3 us -> none  [per_device(): lax.all_gather(out_grad, 'tensor', axis=1, tiled=True)]
    ppermute x0 -> x7, waiting for transfers between devices: none -> 5.15 us  [swap(): return lax.ppermute(array, 'tensor', [(i, i ^ bits) for i in range(4)])]
    ppermute x0 -> x7, starting transfers between devices: none -> 5.02 us  [swap(): return lax.ppermute(array, 'tensor', [(i, i ^ bits) for i in range(4)])]
    unnamed x20 -> x4, local copies, waits for them, and re-layouts: 2.62 us -> 0.92 us
  transfers between devices with their start and end apart: 2 -> 7, of which waited for: 2 -> 2; matrix products, arithmetic and copies ran while one was open for 1% -> 0% of each run, Pallas kernels for 0% -> 71%
where the time goes in v4:
time: 44.8 us; the launch traced here: 44.6 us
  Pallas kernels  32.8 us (73%)
  waiting for transfers between devices  5.15 us (11%)
  starting transfers between devices  5.02 us (11%)
  local copies, waits for them, and re-layouts  0.92 us (2%)
  between operations  0.73 us (2%)
    pallas_call x2, Pallas kernels, add(): call(functools.partial(add_kernel, bits, following_bits), (held, pltpu.VM...  13.6 us
    pallas_call x1, Pallas kernels, fast(): call(own_kernel, (held, held, held, pltpu.VMEM((rank, tokens), F32), pltp...  10.4 us
    pallas_call x1, Pallas kernels, fast(): call(functools.partial(far_kernel, 3), pltpu.VMEM((2 * rank, tokens), F32...  7.49 us
    ppermute x7, waiting for transfers between devices, swap(): return lax.ppermute(array, 'tensor', [(i, i ^ bits) for i in range(4)])  5.15 us
    ppermute x7, starting transfers between devices, swap(): return lax.ppermute(array, 'tensor', [(i, i ^ bits) for i in range(4)])  5.02 us
    unnamed x4, local copies, waits for them, and re-layouts  0.92 us
  transfers between devices with their start and end apart: 7, of which 2 were waited for; matrix products, arithmetic and copies ran while one was open for 0% of the time, Pallas kernels for 71%

profile of v4, /device:TPU:0, one launch (start us, length us, event | category | flops | bytes accessed | tf_op | source)
XLA Modules:
  0.0 44.6 jit_solution(13552538531026398330)
XLA Ops:
  0.6 0.5 %collective-permute-start.1 = (bf16[256,1280]{1,0:T(8,128)(2,1)}, bf16[256,1280]{1,0:T(8,128)(2,1)S(1)}, u32[]{:S(2)}, u32[]{:S(2)}) collective-permute-start(bf16[256,1280]{1,0:T(8,128)(2,1)} %og_hbm.1), channel_id=1, source_target_pairs={{0,1},{1,0},{2,3},{3,2},{4,5},{5,4},{6,7},{7,6},{8,9},{9,8},{10,11... | collective-permute-start | bytes 1966088 | tf_op jit(solution)/shard_map/ppermute | solution.py:224
  1.2 2.6 %collective-permute-start.2 = (bf16[256,1280]{1,0:T(8,128)(2,1)}, bf16[256,1280]{1,0:T(8,128)(2,1)S(1)}, u32[]{:S(2)}, u32[]{:S(2)}) collective-permute-start(bf16[256,1280]{1,0:T(8,128)(2,1)} %og_hbm.1), channel_id=1, source_target_pairs={{0,2},{1,3},{2,0},{3,1},{4,6},{5,7},{6,4},{7,5},{8,10},{9,11},{10,... | collective-permute-start | bytes 1966088 | tf_op jit(solution)/shard_map/ppermute | solution.py:224
  3.7 10.4 %shard_map.121 = (f32[256,4608]{1,0:T(8,128)S(1)}, f32[256,4608]{1,0:T(8,128)S(1)}, f32[256,4608]{1,0:T(8,128)S(1)}, f32[64,256]{1,0:T(8,128)S(1)}, f32[128,256]...) custom-call(bf16[256,1280]{1,0:T(8,128)(2,1)} %x_hbm.1, bf16[256,1280]{1,0:T(8,128)(2,1)} %og_hbm.1, ...), custom_call_target="tpu_custom_call" | custom-call | flops 3019898880 | bytes 16515072 | tf_op jit(solution)/shard_map/pallas_call | solution.py:247
  14.1 0.0 collective-permute-done.1.og_ref
  14.1 7.6 %shard_map.122 = (f32[256,4608]{1,0:T(8,128)S(1)}, bf16[3072,1280]{1,0:T(8,128)(2,1)S(1)}) custom-call(f32[256,4608]{1,0:T(8,128)S(1)} %get-tuple-element.14.acc_in, bf16[256,1280]{1,0:T(8,128)(2,1)S(1)} %collective-permute-done.1.og_ref, bf16[1536,1280]{1,0:T(8,128)(2,1)S(1)} %get-tuple-element.15.head_ref, ...), custom_call_target="tpu_custom_call", output_to_operand_aliasing={{0}: (0, {})} | custom-call | flops 3019898880 | bytes 23592960 | tf_op jit(solution)/shard_map/pallas_call | solution.py:275
  21.7 0.0 collective-permute-done.2.array_ref
  21.8 0.2 collective-permute-start.4
  21.9 0.4 collective-permute-start
  22.3 6.0 %shard_map.124 = (f32[256,4608]{1,0:T(8,128)S(1)}, bf16[3072,1280]{1,0:T(8,128)(2,1)S(1)}) custom-call(f32[256,4608]{1,0:T(8,128)S(1)} %get-tuple-element.16.acc_in, bf16[256,1280]{1,0:T(8,128)(2,1)S(1)} %shard_map.123.og_ref, bf16[3072,1280]{1,0:T(8,128)(2,1)S(1)} %get-tuple-element.17.token_ref.head_ref, ...), custom_call_target="tpu_custom_call", output_to_operand_aliasing={{0}: (0, {})} | custom-call | flops 3019898880 | bytes 23592960 | tf_op jit(solution)/shard_map/pallas_call | solution.py:275
  28.3 0.0 copy-start
  28.4 0.0 copy-start.1
  28.4 0.0 collective-permute-done.theirs_ref
  28.4 0.3 collective-permute-start.3
  28.7 0.0 collective-permute-done.4.og_ref
  28.7 0.7 %copy-done = bf16[4608,64]{0,1:T(8,128)(2,1)S(1)} copy-done((bf16[4608,64]{0,1:T(8,128)(2,1)S(1)}, bf16[4608,64]{0,1:T(8,128)(2,1)}, u32[]{:S(2)}) %copy-start) | copy-done | bytes 589848
  29.4 0.2 copy-done.1
  29.6 7.5 %shard_map.126.q_ref = f32[128,256]{1,0:T(8,128)S(1)} custom-call(f32[256,4608]{1,0:T(8,128)S(1)} %get-tuple-element.19.acc_ref, bf16[256,1280]{1,0:T(8,128)(2,1)S(1)} %collective-permute-done.4.og_ref, bf16[3072,1280]{1,0:T(8,128)(2,1)S(1)} %get-tuple-element.18.token_ref.head_ref, bf16[4608,5120]{1,0:T(8,128)(2,1)} %w_hbm.7, ...), custom_call_target="tpu_custom_call" | custom-call | flops 3019898880 | bytes 11796480 | tf_op jit(solution)/shard_map/pallas_call | solution.py:300
  37.1 0.0 collective-permute-done.3.other_ref
  37.1 0.5 %shard_map.127 = f32[192,128]{1,0:T(8,128)S(1)} custom-call(f32[128,256]{1,0:T(8,128)S(1)} %shard_map.125.chip_ref, f32[128,256]{1,0:T(8,128)S(1)} %collective-permute-done.3.other_ref, f32[128,256]{1,0:T(8,128)S(1)} %shard_map.126.q_ref, f32[64,256]{1,0:T(8,128)S(1)} %get-tuple-element.22.ph_ref), custom_call_target="tpu_custom_call" | custom-call | tf_op jit(solution)/shard_map/pallas_call | solution.py:309
  37.6 0.1 collective-permute-start.5
  37.7 1.2 %collective-permute-done.5 = f32[192,128]{1,0:T(8,128)S(1)} collective-permute-done((f32[192,128]{1,0:T(8,128)S(1)}, f32[192,128]{1,0:T(8,128)S(1)}, u32[]{:S(2)}, u32[]{:S(2)}) %collective-permute-start.5) | collective-permute-done | bytes 98336 | tf_op jit(solution)/shard_map/ppermute | solution.py:224
  38.9 1.0 %collective-permute-start.6 = (f32[192,128]{1,0:T(8,128)S(1)}, f32[192,128]{1,0:T(8,128)S(1)}, u32[]{:S(2)}, u32[]{:S(2)}) collective-permute-start(f32[192,128]{1,0:T(8,128)S(1)} %add.3.mine_ref), channel_id=1, source_target_pairs={{0,2},{1,3},{2,0},{3,1},{4,6},{5,7},{6,4},{7,5},{8,10},{9,11},{10,... | collective-permute-start | bytes 294920 | tf_op jit(solution)/shard_map/ppermute | solution.py:224
  39.9 3.9 %collective-permute-done.6.theirs_ref = f32[192,128]{1,0:T(8,128)S(1)} collective-permute-done((f32[192,128]{1,0:T(8,128)S(1)}, f32[192,128]{1,0:T(8,128)S(1)}, u32[]{:S(2)}, u32[]{:S(2)}) %collective-permute-start.6) | collective-permute-done | bytes 98336 | tf_op jit(solution)/shard_map/ppermute | solution.py:224
  43.9 0.7 %shard_map.128 = (f32[2,64,64]{2,1,0:T(8,128)}, f32[2,64,64]{2,1,0:T(8,128)}, f32[2,64,64]{2,1,0:T(8,128)}) custom-call(f32[192,128]{1,0:T(8,128)S(1)} %add.3.mine_ref, f32[192,128]{1,0:T(8,128)S(1)} %collective-permute-done.6.theirs_ref), custom_call_target="tpu_custom_call" | custom-call | tf_op jit(solution)/shard_map/pallas_call | solution.py:312
  (3 shorter events, 0.0 us)
Async XLA Ops:
  0.6 13.5 %collective-permute-start.1 = (bf16[256,1280]{1,0:T(8,128)(2,1)}, bf16[256,1280]{1,0:T(8,128)(2,1)S(1)}, u32[]{:S(2)}, u32[]{:S(2)}) collective-permute-start(bf16[256,1280]{1,0:T(8,128)(2,1)} %og_hbm.1), channel_id=1, source_target_pairs={{0,1},{1,0},{2,3},{3,2},{4,5},{5,4},{6,7},{7,6},{8,9},{9,8},{10,11... | collective-permute-start | bytes 1966088 | tf_op jit(solution)/shard_map/ppermute | solution.py:224
  1.2 20.6 %collective-permute-start.2 = (bf16[256,1280]{1,0:T(8,128)(2,1)}, bf16[256,1280]{1,0:T(8,128)(2,1)S(1)}, u32[]{:S(2)}, u32[]{:S(2)}) collective-permute-start(bf16[256,1280]{1,0:T(8,128)(2,1)} %og_hbm.1), channel_id=1, source_target_pairs={{0,2},{1,3},{2,0},{3,1},{4,6},{5,7},{6,4},{7,5},{8,10},{9,11},{10,... | collective-permute-start | bytes 1966088 | tf_op jit(solution)/shard_map/ppermute | solution.py:224
  21.8 6.9 %collective-permute-start.4 = (bf16[256,1280]{1,0:T(8,128)(2,1)S(1)}, bf16[256,1280]{1,0:T(8,128)(2,1)S(1)}, u32[]{:S(2)}, u32[]{:S(2)}) collective-permute-start(bf16[256,1280]{1,0:T(8,128)(2,1)S(1)} %shard_map.123.og_ref), channel_id=1, source_target_pairs={{0,1},{1,0},{2,3},{3,2},{4,5},{5,4},{6,7},{7,6},{8,9},{9,8},{10,11... | collective-permute-start | bytes 1966088 | tf_op jit(solution)/shard_map/ppermute | solution.py:224
  21.9 6.4 %collective-permute-start = (f32[128,256]{1,0:T(8,128)S(1)}, f32[128,256]{1,0:T(8,128)S(1)}, u32[]{:S(2)}, u32[]{:S(2)}) collective-permute-start(f32[128,256]{1,0:T(8,128)S(1)} %get-tuple-element.13.mine_ref), channel_id=1, source_target_pairs={{0,1},{1,0},{2,3},{3,2},{4,5},{5,4},{6,7},{7,6},{8,9},{9,8},{10,11... | collective-permute-start | bytes 393224 | tf_op jit(solution)/shard_map/ppermute | solution.py:224
  28.3 1.1 %copy-start = (bf16[4608,64]{0,1:T(8,128)(2,1)S(1)}, bf16[4608,64]{0,1:T(8,128)(2,1)}, u32[]{:S(2)}) copy-start(bf16[4608,64]{0,1:T(8,128)(2,1)} %param.16) | copy-start | bytes 1769476
  28.4 1.2 %copy-start.1 = (bf16[4608,64]{0,1:T(8,128)(2,1)S(1)}, bf16[4608,64]{0,1:T(8,128)(2,1)}, u32[]{:S(2)}) copy-start(bf16[4608,64]{0,1:T(8,128)(2,1)} %param.17) | copy-start | bytes 1769476
  28.4 8.7 %collective-permute-start.3 = (f32[128,256]{1,0:T(8,128)S(1)}, f32[128,256]{1,0:T(8,128)S(1)}, u32[]{:S(2)}, u32[]{:S(2)}) collective-permute-start(f32[128,256]{1,0:T(8,128)S(1)} %shard_map.125.chip_ref), channel_id=1, source_target_pairs={{0,2},{1,3},{2,0},{3,1},{4,6},{5,7},{6,4},{7,5},{8,10},{9,11},{10,... | collective-permute-start | bytes 393224 | tf_op jit(solution)/shard_map/ppermute | solution.py:224
  37.6 1.3 %collective-permute-start.5 = (f32[192,128]{1,0:T(8,128)S(1)}, f32[192,128]{1,0:T(8,128)S(1)}, u32[]{:S(2)}, u32[]{:S(2)}) collective-permute-start(f32[192,128]{1,0:T(8,128)S(1)} %shard_map.127), channel_id=1, source_target_pairs={{0,1},{1,0},{2,3},{3,2},{4,5},{5,4},{6,7},{7,6},{8,9},{9,8},{10,11... | collective-permute-start | bytes 294920 | tf_op jit(solution)/shard_map/ppermute | solution.py:224
  38.9 4.9 %collective-permute-start.6 = (f32[192,128]{1,0:T(8,128)S(1)}, f32[192,128]{1,0:T(8,128)S(1)}, u32[]{:S(2)}, u32[]{:S(2)}) collective-permute-start(f32[192,128]{1,0:T(8,128)S(1)} %add.3.mine_ref), channel_id=1, source_target_pairs={{0,2},{1,3},{2,0},{3,1},{4,6},{5,7},{6,4},{7,5},{8,10},{9,11},{10,... | collective-permute-start | bytes 294920 | tf_op jit(solution)/shard_map/ppermute | solution.py:224

commit v5 on v4

v5 whole, which is shorter than its diff:
```python
import functools

import jax
import jax.numpy as jnp
from jax import lax
from jax.experimental import pallas as pl
from jax.experimental.pallas import tpu as pltpu
from jax.sharding import PartitionSpec as P

SEQS = 2
LEN = 128
PIECE = 384
BLOCK = 1152
MIB = 1 << 20
ANY = pl.BlockSpec(memory_space=pl.ANY)
VMEM = pl.BlockSpec(memory_space=pltpu.VMEM)
BF16 = jnp.bfloat16
F32 = jnp.float32


def product(left, right):
    return jnp.dot(left, right, preferred_element_type=F32)


def rows_by_rows(left, right, precision=None):
    return lax.dot_general(
        left, right, (((1,), (1,)), ((), ())), precision=precision, preferred_element_type=F32
    )


def per_sequence(matrix):
    return matrix.reshape(SEQS, matrix.shape[0] // SEQS, matrix.shape[1])


def plain(x_in, out_grad, gate_pre, up_pre, down_weight, x_factor, gate_factor, up_factor, h_factor, dy_factor):
    hidden_grad = rows_by_rows(lax.all_gather(out_grad, "tensor", axis=1, tiled=True), down_weight)
    gate_val = gate_pre.astype(F32)
    up_val = up_pre.astype(F32)
    sigmoid_gate = jax.nn.sigmoid(gate_val)
    silu_gate = gate_val * sigmoid_gate
    hidden = (silu_gate * up_val).astype(BF16)
    d_gate = (hidden_grad * up_val * sigmoid_gate * (1.0 + gate_val * (1.0 - sigmoid_gate))).astype(BF16)
    d_up = (hidden_grad * silu_gate).astype(BF16)
    rows = [
        product(x_in, x_factor),
        product(d_gate, gate_factor),
        product(d_up, up_factor),
        product(hidden, h_factor),
        product(out_grad, dy_factor),
    ]
    totals = lax.psum(jnp.stack(rows), "tensor")
    p_x, q_gate, q_up, p_h, q_y = [per_sequence(totals[i]) for i in range(5)]
    highest = lax.Precision.HIGHEST
    return (
        jnp.einsum("sli,slj->sij", p_x, q_gate, precision=highest),
        jnp.einsum("sli,slj->sij", p_x, q_up, precision=highest),
        jnp.einsum("sli,slj->sij", p_h, q_y, precision=highest),
    )


def weight_copies(w_hbm, owner, first_row, dst, sems):
    width = dst.shape[1]
    columns = pl.ds(pl.multiple_of(owner * width, 128), width)
    return [
        pltpu.make_async_copy(
            w_hbm.at[pl.ds(pl.multiple_of(first_row + k * PIECE, PIECE), PIECE), columns],
            dst.at[pl.ds(k * PIECE, PIECE)],
            sems.at[k],
        )
        for k in range(dst.shape[0] // PIECE)
    ]


def start(copies):
    for copy in copies:
        copy.start()


def wait(copies):
    for copy in copies:
        copy.wait()


def rows(i):
    return pl.ds(pl.multiple_of(i * BLOCK, BLOCK), BLOCK)


def chip_features_kernel(x_hbm, og_hbm, mate_ref, gate_hbm, up_hbm, w_hbm, xf_hbm, yf_hbm, hf_hbm,
                         acc_ref, a_ref, b_ref, ph_ref, pq_ref, next_ref,
                         x_v, og_v, gate_v, up_v, w_v, xf_v, yf_v, hf_v, sems, gate_sems, up_sems, w_sems, next_sems):
    me = lax.axis_index("tensor")
    width = og_hbm.shape[1]
    units = acc_ref.shape[1]
    rank = ph_ref.shape[1]
    turns = units // BLOCK
    mine = pl.ds(pl.multiple_of(me % 2 * width, 128), width)
    theirs = pl.ds(pl.multiple_of((me + 1) % 2 * width, 128), width)

    def gate_up(i):
        slot = i % 2
        return [
            pltpu.make_async_copy(gate_hbm.at[:, rows(i)], gate_v.at[slot], gate_sems.at[i]),
            pltpu.make_async_copy(up_hbm.at[:, rows(i)], up_v.at[slot], up_sems.at[i]),
        ]

    def weights(i):
        return weight_copies(w_hbm, me // 2, i * BLOCK, w_v.at[i % 2], w_sems.at[i])

    def elementwise(i):
        wait(gate_up(i))
        at = rows(i)
        slot = i % 2
        g = gate_v[slot].astype(F32)
        u = up_v[slot].astype(F32)
        s = 0.5 * jnp.tanh(0.5 * g) + 0.5
        silu = g * s
        a_ref[:, at] = u * s * ((1.0 + g) - silu)
        b_ref[:, at] = silu
        ph_ref[...] += rows_by_rows((silu * u).astype(BF16), hf_v[:, at])

    def multiply(i):
        acc_ref[:, rows(i)] = rows_by_rows(og_v[...], w_v[i % 2])

    pairs = ((og_hbm, og_v.at[:, mine]), (hf_hbm, hf_v), (x_hbm, x_v), (xf_hbm, xf_v), (yf_hbm, yf_v))
    small = [pltpu.make_async_copy(src, dst, sems.at[i]) for i, (src, dst) in enumerate(pairs)]
    following = weight_copies(w_hbm, me ^ 2, 0, next_ref, next_sems)

    start(gate_up(0))
    start(small[:2])
    start(weights(0))
    start(gate_up(1))
    start(weights(1))
    start(small[2:])
    ph_ref[...] = jnp.zeros_like(ph_ref)
    og_v[:, theirs] = mate_ref[...]
    wait(small[:2])
    elementwise(0)

    @pl.loop(0, turns - 1)
    def _(i):
        @pl.when(i + 2 < turns)
        def _():
            start(gate_up(i + 2))

        wait(weights(i))
        multiply(i)

        @pl.when(i + 2 < turns)
        def _():
            start(weights(i + 2))

        @pl.when(i + 2 == turns)
        def _():
            start(following)

        elementwise(i + 1)

    wait(small[2:])
    pq_ref[:rank] = rows_by_rows(xf_v[...], x_v[...])
    pq_ref[rank:] = rows_by_rows(yf_v[...], og_v[:, mine])
    wait(weights(turns - 1))
    multiply(turns - 1)
    wait(following)


def add_kernel(bits, following_bits, acc_in, og_ref, head_ref, w_hbm, acc_ref, next_ref, w_v, sems, next_sems):
    me = lax.axis_index("tensor")
    first = head_ref.shape[0]
    turns = w_v.shape[0] // BLOCK

    def weights(i):
        return weight_copies(w_hbm, me ^ bits, first + i * BLOCK, w_v.at[rows(i)], sems.at[i])

    following = weight_copies(w_hbm, me ^ following_bits, 0, next_ref, next_sems)
    for i in range(turns):
        start(weights(i))
    start(following)

    def add(at, block):
        acc_ref[:, at] = acc_in[:, at] + rows_by_rows(og_ref[...], block)

    @pl.loop(0, first // BLOCK)
    def _(i):
        add(rows(i), head_ref[rows(i)])

    @pl.loop(0, turns)
    def _(i):
        wait(weights(i))
        add(rows(first // BLOCK + i), w_v[rows(i)])

    wait(following)


def far_kernel(bits, acc_ref, og_ref, head_ref, w_hbm, a_ref, b_ref, gf_hbm, uf_hbm, gate_ref, up_ref, w_v, gf_ref, uf_ref,
               sems, factor_sems):
    me = lax.axis_index("tensor")
    first = head_ref.shape[0]
    turns = w_v.shape[0] // BLOCK

    def weights(i):
        return weight_copies(w_hbm, me ^ bits, first + i * BLOCK, w_v.at[rows(i)], sems.at[i])

    factors = [
        pltpu.make_async_copy(src, dst, factor_sems.at[k]) for k, (src, dst) in enumerate(((gf_hbm, gf_ref), (uf_hbm, uf_ref)))
    ]
    start(factors)
    for i in range(turns):
        start(weights(i))
    gate_ref[...] = jnp.zeros_like(gate_ref)
    up_ref[...] = jnp.zeros_like(up_ref)

    def add(at, block):
        hidden_grad = acc_ref[:, at] + rows_by_rows(og_ref[...], block)
        gate_ref[...] += rows_by_rows((hidden_grad * a_ref[:, at]).astype(BF16), gf_ref[:, at])
        up_ref[...] += rows_by_rows((hidden_grad * b_ref[:, at]).astype(BF16), uf_ref[:, at])

    @pl.loop(0, first // BLOCK)
    def _(i):
        @pl.when(i == 0)
        def _():
            wait(factors)

        add(rows(i), head_ref[rows(i)])

    @pl.loop(0, turns)
    def _(i):
        wait(weights(i))
        add(rows(first // BLOCK + i), w_v[rows(i)])


def after_kernel(array_ref, token_ref, same_ref):
    pass


def chip_kernel(mine_ref, theirs_ref, token_ref, chip_ref):
    chip_ref[...] = mine_ref[...] + theirs_ref[...]


def gradients_kernel(chip_ref, other_ref, gate_ref, up_ref, ph_ref, share_ref):
    rank = ph_ref.shape[1]
    total = chip_ref[...] + other_ref[...]

    def columns(left, right):
        return jnp.dot(left, right, precision=lax.Precision.HIGHEST, preferred_element_type=F32)

    for s in range(SEQS):
        at = slice(s * LEN, (s + 1) * LEN)
        out = slice(s * rank, (s + 1) * rank)
        share_ref[out, :rank] = columns(total[:rank, at], gate_ref[at])
        share_ref[out, rank:] = columns(total[:rank, at], up_ref[at])
        share_ref[SEQS * rank :, out] = columns(total[rank:, at], ph_ref[at]).T


def sum_kernel(mine_ref, theirs_ref, gate_ref, up_ref, down_ref):
    rank = gate_ref.shape[1]
    total = mine_ref[...] + theirs_ref[...]
    for s in range(SEQS):
        gate_ref[s] = total[s * rank : (s + 1) * rank, :rank]
        up_ref[s] = total[s * rank : (s + 1) * rank, rank:]
        down_ref[s] = total[SEQS * rank :, s * rank : (s + 1) * rank]


def fast(x_in, out_grad, gate_pre, up_pre, down_weight, x_factor, gate_factor, up_factor, h_factor, dy_factor):
    tokens, width = out_grad.shape
    units, rank = h_factor.shape
    dma = pltpu.SemaphoreType.DMA

    def in_hbm(array):
        return pltpu.with_memory_space_constraint(array, pltpu.HBM)

    def swap(array, bits):
        return lax.ppermute(array, "tensor", [(i, i ^ bits) for i in range(4)])

    def call(kernel, out_shape, in_specs, scratch, mib, flops=0, moved=0, **kwargs):
        several = isinstance(out_shape, tuple)
        return pl.pallas_call(
            kernel,
            out_shape=out_shape,
            in_specs=in_specs,
            out_specs=(VMEM,) * len(out_shape) if several else VMEM,
            scratch_shapes=list(scratch),
            compiler_params=pltpu.CompilerParams(vmem_limit_bytes=mib * MIB),
            cost_estimate=pl.CostEstimate(flops=flops, bytes_accessed=moved, transcendentals=0),
            **kwargs,
        )

    held = pltpu.VMEM((tokens, units), F32)
    per_product = 2 * tokens * width * units
    turns, per_turn = units // BLOCK, BLOCK // PIECE
    first = turns // 2 * BLOCK
    rest = units - first
    narrow = pltpu.VMEM((tokens, rank), F32)
    head = pltpu.VMEM((first, width), BF16)
    weight = in_hbm(down_weight)

    near = swap(out_grad, 2)
    mate = swap(out_grad, 1)
    acc, a, b, ph, pq, w_head = call(
        chip_features_kernel,
        (held, held, held, narrow, pltpu.VMEM((2 * rank, tokens), F32), head),
        [ANY] * 2 + [VMEM] + [ANY] * 6,
        [
            pltpu.VMEM((tokens, width), BF16),
            pltpu.VMEM((tokens, 2 * width), BF16),
            pltpu.VMEM((2, tokens, BLOCK), BF16),
            pltpu.VMEM((2, tokens, BLOCK), BF16),
            pltpu.VMEM((2, BLOCK, 2 * width), BF16),
            pltpu.VMEM((rank, width), BF16),
            pltpu.VMEM((rank, width), BF16),
            pltpu.VMEM((rank, units), BF16),
            dma((5,)),
            dma((turns,)),
            dma((turns,)),
            dma((turns, per_turn)),
            dma((first // PIECE,)),
        ],
        24,
        2 * per_product,
        2 * units * (2 * width + 2 * tokens),
    )(
        in_hbm(x_in),
        in_hbm(out_grad),
        mate,
        in_hbm(gate_pre),
        in_hbm(up_pre),
        weight,
        in_hbm(x_factor.T),
        in_hbm(dy_factor.T),
        in_hbm(h_factor.T),
    )
    pq_mate = swap(pq, 1)

    near = pl.pallas_call(
        after_kernel,
        out_shape=pltpu.VMEM(near.shape, near.dtype),
        in_specs=[ANY, ANY],
        out_specs=ANY,
        input_output_aliases={0: 0},
        compiler_params=pltpu.CompilerParams(vmem_limit_bytes=MIB),
    )(near, w_head)
    far = swap(near, 1)
    acc, w_head = call(
        functools.partial(add_kernel, 2, 3),
        (held, head),
        [VMEM] * 3 + [ANY],
        [pltpu.VMEM((rest, width), BF16), dma((rest // BLOCK, per_turn)), dma((first // PIECE,))],
        10,
        per_product,
        2 * units * width,
        input_output_aliases={0: 0},
    )(acc, near, w_head, weight)
    chip = call(chip_kernel, pltpu.VMEM(pq.shape, F32), [VMEM, VMEM, ANY], [], 1)(pq, pq_mate, w_head)
    chip_across = swap(chip, 2)
    q_gate, q_up = call(
        functools.partial(far_kernel, 3),
        (narrow, narrow),
        [VMEM] * 3 + [ANY] + [VMEM] * 2 + [ANY] * 2,
        [
            pltpu.VMEM((rest, width), BF16),
            pltpu.VMEM((rank, units), BF16),
            pltpu.VMEM((rank, units), BF16),
            dma((rest // BLOCK, per_turn)),
            dma((2,)),
        ],
        10,
        per_product,
        2 * units * width,
    )(acc, far, w_head, weight, a, b, in_hbm(gate_factor.T), in_hbm(up_factor.T))
    share = call(gradients_kernel, pltpu.VMEM(((SEQS + 1) * rank, 2 * rank), F32), [VMEM] * 5, [], 4)(
        chip, chip_across, q_gate, q_up, ph
    )
    chip_share = share + swap(share, 1)
    out = jax.ShapeDtypeStruct((SEQS, rank, rank), F32)
    return call(sum_kernel, (out, out, out), [VMEM] * 2, [], 4)(chip_share, swap(chip_share, 2))


def solution(mesh):
    def per_device(*arrays):
        (tokens, width), (units, rank) = arrays[1].shape, arrays[8].shape
        fits = (
            mesh.shape["tensor"] == 4
            and (tokens, rank) == (SEQS * LEN, LEN // 2)
            and width % 128 == 0
            and units % BLOCK == 0
            and units // BLOCK > 3
        )
        return tuple((fast if fits else plain)(*arrays))

    return jax.shard_map(
        per_device,
        mesh=mesh,
        in_specs=(P("dp", "tensor"),) * 4 + (P("tensor", None),) * 6,
        out_specs=(P("dp", None, None),) * 3,
        check_vma=False,
    )
```

time: 44.8 us -> 43.5 us (0.971)
  Pallas kernels: 32.8 us -> 30.4 us
  starting transfers between devices: 5.02 us -> 6.04 us
  waiting for transfers between devices: 5.15 us -> 6.13 us
  local copies, waits for them, and re-layouts: 0.92 us -> 0 us
    pallas_call x4 -> x3, Pallas kernels: 31.5 us -> 29.1 us  [the longest x1 16.2 us: fast(): call(chip_features_kernel, (held, held, held, narrow, pltpu.VMEM((2 * ran...]
    ppermute x7, starting transfers between devices: 5.02 us -> 6.04 us  [swap(): return lax.ppermute(array, 'tensor', [(i, i ^ bits) for i in range(4)])]
    ppermute x7, waiting for transfers between devices: 5.15 us -> 6.13 us  [swap(): return lax.ppermute(array, 'tensor', [(i, i ^ bits) for i in range(4)])]
    unnamed x4 -> x0, local copies, waits for them, and re-layouts: 0.92 us -> none
  transfers between devices with their start and end apart: 7 -> 7, of which waited for: 2 -> 2; matrix products, arithmetic and copies ran while one was open for 0% -> 0% of each run, Pallas kernels for 71% -> 67%
where the time goes in v5:
time: 43.5 us; the launch traced here: 43.3 us
  Pallas kernels  30.4 us (70%)
  waiting for transfers between devices  6.13 us (14%)
  starting transfers between devices  6.04 us (14%)
  between operations  0.71 us (2%)
    pallas_call x1, Pallas kernels, fast(): call(chip_features_kernel, (held, held, held, narrow, pltpu.VMEM((2 * ran...  16.2 us
    pallas_call x1, Pallas kernels, fast(): call(functools.partial(far_kernel, 3), (narrow, narrow), [VMEM] * 3 + [AN...  7.55 us
    ppermute x7, waiting for transfers between devices, swap(): return lax.ppermute(array, 'tensor', [(i, i ^ bits) for i in range(4)])  6.13 us
    ppermute x7, starting transfers between devices, swap(): return lax.ppermute(array, 'tensor', [(i, i ^ bits) for i in range(4)])  6.04 us
    pallas_call x1, Pallas kernels, fast(): call(functools.partial(add_kernel, 2, 3), (held, head), [VMEM] * 3 + [ANY...  5.37 us
  transfers between devices with their start and end apart: 7, of which 2 were waited for; matrix products, arithmetic and copies ran while one was open for 0% of the time, Pallas kernels for 67%

profile of v5, /device:TPU:0, one launch (start us, length us, event | category | flops | bytes accessed | tf_op | source)
XLA Modules:
  0.0 43.3 jit_solution(9126622621729991035)
XLA Ops:
  0.6 0.5 %collective-permute-start = (bf16[256,1280]{1,0:T(8,128)(2,1)}, bf16[256,1280]{1,0:T(8,128)(2,1)S(1)}, u32[]{:S(2)}, u32[]{:S(2)}) collective-permute-start(bf16[256,1280]{1,0:T(8,128)(2,1)} %og_hbm.1), channel_id=1, source_target_pairs={{0,1},{1,0},{2,3},{3,2},{4,5},{5,4},{6,7},{7,6},{8,9},{9,8},{10,11... | collective-permute-start | bytes 1966088 | tf_op jit(solution)/shard_map/ppermute | solution.py:272
  1.2 2.6 %collective-permute-start.2 = (bf16[256,1280]{1,0:T(8,128)(2,1)}, bf16[256,1280]{1,0:T(8,128)(2,1)S(1)}, u32[]{:S(2)}, u32[]{:S(2)}) collective-permute-start(bf16[256,1280]{1,0:T(8,128)(2,1)} %og_hbm.1), channel_id=1, source_target_pairs={{0,2},{1,3},{2,0},{3,1},{4,6},{5,7},{6,4},{7,5},{8,10},{9,11},{10,... | collective-permute-start | bytes 1966088 | tf_op jit(solution)/shard_map/ppermute | solution.py:272
  3.7 0.0 collective-permute-done.mate_ref
  3.7 16.2 %shard_map.121 = (f32[256,4608]{1,0:T(8,128)S(1)}, f32[256,4608]{1,0:T(8,128)S(1)}, f32[256,4608]{1,0:T(8,128)S(1)}, f32[256,64]{1,0:T(8,128)S(1)}, f32[128,256]...) custom-call(bf16[256,1280]{1,0:T(8,128)(2,1)} %x_hbm.1, bf16[256,1280]{1,0:T(8,128)(2,1)} %og_hbm.1, ...), custom_call_target="tpu_custom_call" | custom-call | flops 6039797760 | bytes 28311552 | tf_op jit(solution)/shard_map/pallas_call | solution.py:298
  19.9 0.0 collective-permute-done.2.array_ref
  19.9 0.2 collective-permute-start.4
  20.2 0.3 collective-permute-start.1
  20.5 5.4 %shard_map.123 = (f32[256,4608]{1,0:T(8,128)S(1)}, bf16[2304,1280]{1,0:T(8,128)(2,1)S(1)}) custom-call(f32[256,4608]{1,0:T(8,128)S(1)} %get-tuple-element.14.acc_in, bf16[256,1280]{1,0:T(8,128)(2,1)S(1)} %shard_map.122.og_ref, bf16[2304,1280]{1,0:T(8,128)(2,1)S(1)} %get-tuple-element.15.token_ref.head_ref, ...), custom_call_target="tpu_custom_call", output_to_operand_aliasing={{0}: (0, {})} | custom-call | flops 3019898880 | bytes 11796480 | tf_op jit(solution)/shard_map/pallas_call | solution.py:342
  25.9 0.0 collective-permute-done.1.theirs_ref
  25.9 2.2 %collective-permute-start.3 = (f32[128,256]{1,0:T(8,128)S(1)}, f32[128,256]{1,0:T(8,128)S(1)}, u32[]{:S(2)}, u32[]{:S(2)}) collective-permute-start(f32[128,256]{1,0:T(8,128)S(1)} %shard_map.124.chip_ref), channel_id=1, source_target_pairs={{0,2},{1,3},{2,0},{3,1},{4,6},{5,7},{6,4},{7,5},{8,10},{9,11},{10,... | collective-permute-start | bytes 393224 | tf_op jit(solution)/shard_map/ppermute | solution.py:272
  28.1 0.0 collective-permute-done.4.og_ref
  28.1 7.5 %shard_map.125 = (f32[256,64]{1,0:T(8,128)S(1)}, f32[256,64]{1,0:T(8,128)S(1)}) custom-call(f32[256,4608]{1,0:T(8,128)S(1)} %get-tuple-element.17.acc_ref, bf16[256,1280]{1,0:T(8,128)(2,1)S(1)} %collective-permute-done.4.og_ref, bf16[2304,1280]{1,0:T(8,128)(2,1)S(1)} %get-tuple-element.16.token_ref.head_ref, bf16[4608,5120]{1,0:T(8,128)(2,1)} %w_hbm.5, ...), custom_call_target="tpu_custom_call" | custom-call | flops 3019898880 | bytes 11796480 | tf_op jit(solution)/shard_map/pallas_call | solution.py:354
  35.7 0.0 collective-permute-done.3.other_ref
  35.7 0.6 %shard_map.126 = f32[192,128]{1,0:T(8,128)S(1)} custom-call(f32[128,256]{1,0:T(8,128)S(1)} %shard_map.124.chip_ref, f32[128,256]{1,0:T(8,128)S(1)} %collective-permute-done.3.other_ref, f32[256,64]{1,0:T(8,128)S(1)} %get-tuple-element.20.gate_ref, f32[256,64]{1,0:T(8,128)S(1)} %get-tuple-element.21.up_ref, f32[256,64]{1,0:T(8,128)S(1)} %get-tuple-element.22.ph_ref), custom_call_target="tpu_custom_call" | custom-call | tf_op jit(solution)/shard_map/pallas_call | solution.py:369
  36.3 0.1 collective-permute-start.5
  36.4 1.3 %collective-permute-done.5 = f32[192,128]{1,0:T(8,128)S(1)} collective-permute-done((f32[192,128]{1,0:T(8,128)S(1)}, f32[192,128]{1,0:T(8,128)S(1)}, u32[]{:S(2)}, u32[]{:S(2)}) %collective-permute-start.5) | collective-permute-done | bytes 98336 | tf_op jit(solution)/shard_map/ppermute | solution.py:272
  37.7 0.1 collective-permute-start.6
  37.8 4.8 %collective-permute-done.6.theirs_ref = f32[192,128]{1,0:T(8,128)S(1)} collective-permute-done((f32[192,128]{1,0:T(8,128)S(1)}, f32[192,128]{1,0:T(8,128)S(1)}, u32[]{:S(2)}, u32[]{:S(2)}) %collective-permute-start.6) | collective-permute-done | bytes 98336 | tf_op jit(solution)/shard_map/ppermute | solution.py:272
  42.6 0.7 %shard_map.127 = (f32[2,64,64]{2,1,0:T(8,128)}, f32[2,64,64]{2,1,0:T(8,128)}, f32[2,64,64]{2,1,0:T(8,128)}) custom-call(f32[192,128]{1,0:T(8,128)S(1)} %add.3.mine_ref, f32[192,128]{1,0:T(8,128)S(1)} %collective-permute-done.6.theirs_ref), custom_call_target="tpu_custom_call" | custom-call | tf_op jit(solution)/shard_map/pallas_call | solution.py:374
  (3 shorter events, 0.0 us)
Async XLA Ops:
  0.6 3.1 %collective-permute-start = (bf16[256,1280]{1,0:T(8,128)(2,1)}, bf16[256,1280]{1,0:T(8,128)(2,1)S(1)}, u32[]{:S(2)}, u32[]{:S(2)}) collective-permute-start(bf16[256,1280]{1,0:T(8,128)(2,1)} %og_hbm.1), channel_id=1, source_target_pairs={{0,1},{1,0},{2,3},{3,2},{4,5},{5,4},{6,7},{7,6},{8,9},{9,8},{10,11... | collective-permute-start | bytes 1966088 | tf_op jit(solution)/shard_map/ppermute | solution.py:272
  1.2 18.8 %collective-permute-start.2 = (bf16[256,1280]{1,0:T(8,128)(2,1)}, bf16[256,1280]{1,0:T(8,128)(2,1)S(1)}, u32[]{:S(2)}, u32[]{:S(2)}) collective-permute-start(bf16[256,1280]{1,0:T(8,128)(2,1)} %og_hbm.1), channel_id=1, source_target_pairs={{0,2},{1,3},{2,0},{3,1},{4,6},{5,7},{6,4},{7,5},{8,10},{9,11},{10,... | collective-permute-start | bytes 1966088 | tf_op jit(solution)/shard_map/ppermute | solution.py:272
  19.9 8.2 %collective-permute-start.4 = (bf16[256,1280]{1,0:T(8,128)(2,1)S(1)}, bf16[256,1280]{1,0:T(8,128)(2,1)S(1)}, u32[]{:S(2)}, u32[]{:S(2)}) collective-permute-start(bf16[256,1280]{1,0:T(8,128)(2,1)S(1)} %shard_map.122.og_ref), channel_id=1, source_target_pairs={{0,1},{1,0},{2,3},{3,2},{4,5},{5,4},{6,7},{7,6},{8,9},{9,8},{10,11... | collective-permute-start | bytes 1966088 | tf_op jit(solution)/shard_map/ppermute | solution.py:272
  20.2 5.7 %collective-permute-start.1 = (f32[128,256]{1,0:T(8,128)S(1)}, f32[128,256]{1,0:T(8,128)S(1)}, u32[]{:S(2)}, u32[]{:S(2)}) collective-permute-start(f32[128,256]{1,0:T(8,128)S(1)} %get-tuple-element.13.mine_ref), channel_id=1, source_target_pairs={{0,1},{1,0},{2,3},{3,2},{4,5},{5,4},{6,7},{7,6},{8,9},{9,8},{10,11... | collective-permute-start | bytes 393224 | tf_op jit(solution)/shard_map/ppermute | solution.py:272
  25.9 9.8 %collective-permute-start.3 = (f32[128,256]{1,0:T(8,128)S(1)}, f32[128,256]{1,0:T(8,128)S(1)}, u32[]{:S(2)}, u32[]{:S(2)}) collective-permute-start(f32[128,256]{1,0:T(8,128)S(1)} %shard_map.124.chip_ref), channel_id=1, source_target_pairs={{0,2},{1,3},{2,0},{3,1},{4,6},{5,7},{6,4},{7,5},{8,10},{9,11},{10,... | collective-permute-start | bytes 393224 | tf_op jit(solution)/shard_map/ppermute | solution.py:272
  36.3 1.4 %collective-permute-start.5 = (f32[192,128]{1,0:T(8,128)S(1)}, f32[192,128]{1,0:T(8,128)S(1)}, u32[]{:S(2)}, u32[]{:S(2)}) collective-permute-start(f32[192,128]{1,0:T(8,128)S(1)} %shard_map.126), channel_id=1, source_target_pairs={{0,1},{1,0},{2,3},{3,2},{4,5},{5,4},{6,7},{7,6},{8,9},{9,8},{10,11... | collective-permute-start | bytes 294920 | tf_op jit(solution)/shard_map/ppermute | solution.py:272
  37.7 4.9 %collective-permute-start.6 = (f32[192,128]{1,0:T(8,128)S(1)}, f32[192,128]{1,0:T(8,128)S(1)}, u32[]{:S(2)}, u32[]{:S(2)}) collective-permute-start(f32[192,128]{1,0:T(8,128)S(1)} %add.3.mine_ref), channel_id=1, source_target_pairs={{0,2},{1,3},{2,0},{3,1},{4,6},{5,7},{6,4},{7,5},{8,10},{9,11},{10,... | collective-permute-start | bytes 294920 | tf_op jit(solution)/shard_map/ppermute | solution.py:272

commit v6 on v5

v6 whole, which is shorter than its diff:
```python
import functools

import jax
import jax.numpy as jnp
from jax import lax
from jax.experimental import pallas as pl
from jax.experimental.pallas import tpu as pltpu
from jax.sharding import PartitionSpec as P

SEQS = 2
LEN = 128
BLOCK = 1152
CHIP_BLOCK = 768
AHEAD = 2
PARTS = 2
SUMS = 3
MIB = 1 << 20
ANY = pl.BlockSpec(memory_space=pl.ANY)
VMEM = pl.BlockSpec(memory_space=pltpu.VMEM)
BF16 = jnp.bfloat16
F32 = jnp.float32


def product(left, right):
    return jnp.dot(left, right, preferred_element_type=F32)


def rows_by_rows(left, right, precision=None):
    return lax.dot_general(
        left, right, (((1,), (1,)), ((), ())), precision=precision, preferred_element_type=F32
    )


def per_sequence(matrix):
    return matrix.reshape(SEQS, matrix.shape[0] // SEQS, matrix.shape[1])


def plain(x_in, out_grad, gate_pre, up_pre, down_weight, x_factor, gate_factor, up_factor, h_factor, dy_factor):
    hidden_grad = rows_by_rows(lax.all_gather(out_grad, "tensor", axis=1, tiled=True), down_weight)
    gate_val = gate_pre.astype(F32)
    up_val = up_pre.astype(F32)
    sigmoid_gate = jax.nn.sigmoid(gate_val)
    silu_gate = gate_val * sigmoid_gate
    hidden = (silu_gate * up_val).astype(BF16)
    d_gate = (hidden_grad * up_val * sigmoid_gate * (1.0 + gate_val * (1.0 - sigmoid_gate))).astype(BF16)
    d_up = (hidden_grad * silu_gate).astype(BF16)
    rows = [
        product(x_in, x_factor),
        product(d_gate, gate_factor),
        product(d_up, up_factor),
        product(hidden, h_factor),
        product(out_grad, dy_factor),
    ]
    totals = lax.psum(jnp.stack(rows), "tensor")
    p_x, q_gate, q_up, p_h, q_y = [per_sequence(totals[i]) for i in range(5)]
    highest = lax.Precision.HIGHEST
    return (
        jnp.einsum("sli,slj->sij", p_x, q_gate, precision=highest),
        jnp.einsum("sli,slj->sij", p_x, q_up, precision=highest),
        jnp.einsum("sli,slj->sij", p_h, q_y, precision=highest),
    )


class Step:
    def __init__(self, owner, width, block, w_hbm):
        self.owner, self.width, self.block, self.w_hbm = owner, width, block, w_hbm

    def units(self, i):
        return pl.ds(pl.multiple_of(i * self.block, self.block), self.block)

    def copies(self, i, dst, sems):
        columns = pl.ds(pl.multiple_of(self.owner * self.width, 128), self.width)
        part = self.block // PARTS
        return [
            pltpu.make_async_copy(
                self.w_hbm.at[pl.ds(pl.multiple_of(i * self.block + k * part, part), part), columns],
                dst.at[pl.ds(k * part, part)],
                sems.at[k],
            )
            for k in range(PARTS)
        ]


def start(copies):
    for copy in copies:
        copy.start()


def wait(copies):
    for copy in copies:
        copy.wait()


def stream(step, following, blocks, head, w_v, next_head, sems, body):
    heads = head.shape[0]
    slots = w_v.shape[0]

    def copies(j):
        return step.copies(j, w_v.at[(j - heads) % slots], sems.at[j])

    def next_copies(j):
        return following.copies(j, next_head.at[j], sems.at[blocks + j])

    last = blocks + (0 if following is None else next_head.shape[0])

    def begin(j):
        @pl.when(j < blocks)
        def _():
            start(copies(j))

        if following is not None:

            @pl.when((j >= blocks) & (j < last))
            def _():
                start(next_copies(j - blocks))

    for j in range(heads, AHEAD):
        start(copies(j))

    @pl.loop(0, heads)
    def _(i):
        begin(i + AHEAD)
        body(i, head.at[i])

    @pl.loop(heads, blocks)
    def _(i):
        begin(i + AHEAD)
        wait(copies(i))
        body(i, w_v.at[(i - heads) % slots])

    for j in range(blocks + AHEAD, last):
        start(next_copies(j - blocks))
    for j in range(last - blocks):
        wait(next_copies(j))


def project(sums_ref, rows, factor):
    parts = sums_ref.shape[0]
    part = factor.shape[1] // parts
    for k in range(parts):
        at = slice(k * part, (k + 1) * part)
        sums_ref[k] += rows_by_rows(rows[:, at], factor[:, at])


def elementwise_kernel(x_hbm, og_hbm, gate_hbm, up_hbm, w_hbm, xf_hbm, yf_hbm, hf_hbm,
                       a_ref, b_ref, ph_ref, pq_ref, head_ref, og_v,
                       x_v, gate_v, up_v, xf_v, yf_v, hf_v, sums_v, sems, gate_sems, up_sems, w_sems):
    tokens, units = a_ref.shape
    rank = ph_ref.shape[1]
    turns = units // BLOCK

    def at(i):
        return pl.ds(pl.multiple_of(i * BLOCK, BLOCK), BLOCK)

    def gate_up(i):
        return [
            pltpu.make_async_copy(gate_hbm.at[:, at(i)], gate_v.at[i], gate_sems.at[i]),
            pltpu.make_async_copy(up_hbm.at[:, at(i)], up_v.at[i], up_sems.at[i]),
        ]

    pairs = ((hf_hbm, hf_v), (og_hbm, og_v), (x_hbm, x_v), (xf_hbm, xf_v), (yf_hbm, yf_v))
    small = [pltpu.make_async_copy(src, dst, sems.at[i]) for i, (src, dst) in enumerate(pairs)]
    following = Step(lax.axis_index("tensor") // 2, head_ref.shape[2], head_ref.shape[1], w_hbm)
    heads = head_ref.shape[0]

    start(gate_up(0))
    start(small[:1])
    start(gate_up(1))
    start(small[1:])
    sums_v[...] = jnp.zeros_like(sums_v)
    wait(gate_up(0))
    wait(small[:1])

    @pl.loop(0, turns)
    def _(i):
        @pl.when(i + 2 < turns)
        def _():
            start(gate_up(i + 2))

        @pl.when(i < heads)
        def _():
            start(following.copies(i, head_ref.at[i], w_sems.at[i]))

        @pl.when(i > 0)
        def _():
            wait(gate_up(i))

        g = gate_v[i].astype(F32)
        u = up_v[i].astype(F32)
        s = 0.5 * jnp.tanh(0.5 * g) + 0.5
        silu = g * s
        a_ref[:, at(i)] = u * s * ((1.0 + g) - silu)
        b_ref[:, at(i)] = silu
        project(sums_v, (silu * u).astype(BF16), hf_v.at[:, at(i)])

    wait(small[1:])
    pq_ref[:rank] = rows_by_rows(xf_v[...], x_v[...])
    pq_ref[rank:] = rows_by_rows(yf_v[...], og_v[...])
    ph_ref[...] = jnp.sum(sums_v[...], axis=0)
    for i in range(heads):
        wait(following.copies(i, head_ref.at[i], w_sems.at[i]))


def chip_features_kernel(own_ref, mate_ref, head_ref, w_hbm, acc_ref, next_ref, og_v, w_v, sems):
    me = lax.axis_index("tensor")
    width = own_ref.shape[1]
    step = Step(me // 2, 2 * width, w_v.shape[1], w_hbm)
    following = Step(me ^ 2, width, next_ref.shape[1], w_hbm)
    mine = pl.ds(pl.multiple_of(me % 2 * width, 128), width)
    theirs = pl.ds(pl.multiple_of((me + 1) % 2 * width, 128), width)
    og_v[:, mine] = own_ref[...]
    og_v[:, theirs] = mate_ref[...]

    def body(i, weights):
        acc_ref[:, step.units(i)] = rows_by_rows(og_v[...], weights[...])

    stream(step, following, acc_ref.shape[1] // step.block, head_ref, w_v, next_ref, sems, body)


def add_kernel(bits, following_bits, acc_in, og_ref, head_ref, w_hbm, acc_ref, next_ref, w_v, sems):
    me = lax.axis_index("tensor")
    _, block, width = w_v.shape
    step = Step(me ^ bits, width, block, w_hbm)
    following = Step(me ^ following_bits, width, block, w_hbm)

    def body(i, weights):
        at = step.units(i)
        acc_ref[:, at] = acc_in[:, at] + rows_by_rows(og_ref[...], weights[...])

    stream(step, following, acc_in.shape[1] // block, head_ref, w_v, next_ref, sems, body)


def far_kernel(bits, acc_ref, og_ref, head_ref, w_hbm, a_ref, b_ref, gf_hbm, uf_hbm, gate_ref, up_ref,
               w_v, gf_ref, uf_ref, gate_v, up_v, sems, factor_sems):
    _, block, width = w_v.shape
    step = Step(lax.axis_index("tensor") ^ bits, width, block, w_hbm)
    factors = [
        pltpu.make_async_copy(src, dst, factor_sems.at[k]) for k, (src, dst) in enumerate(((gf_hbm, gf_ref), (uf_hbm, uf_ref)))
    ]
    start(factors)
    gate_v[...] = jnp.zeros_like(gate_v)
    up_v[...] = jnp.zeros_like(up_v)

    def body(i, weights):
        at = step.units(i)
        hidden_grad = acc_ref[:, at] + rows_by_rows(og_ref[...], weights[...])

        @pl.when(i == 0)
        def _():
            wait(factors)

        project(gate_v, (hidden_grad * a_ref[:, at]).astype(BF16), gf_ref.at[:, at])
        project(up_v, (hidden_grad * b_ref[:, at]).astype(BF16), uf_ref.at[:, at])

    stream(step, None, acc_ref.shape[1] // block, head_ref, w_v, None, sems, body)
    gate_ref[...] = jnp.sum(gate_v[...], axis=0)
    up_ref[...] = jnp.sum(up_v[...], axis=0)


def after_kernel(array_ref, token_ref, same_ref):
    pass


def chip_kernel(mine_ref, theirs_ref, token_ref, chip_ref):
    chip_ref[...] = mine_ref[...] + theirs_ref[...]


def gradients_kernel(chip_ref, other_ref, gate_ref, up_ref, ph_ref, share_ref):
    rank = ph_ref.shape[1]
    total = chip_ref[...] + other_ref[...]

    def columns(left, right):
        return jnp.dot(left, right, precision=lax.Precision.HIGHEST, preferred_element_type=F32)

    for s in range(SEQS):
        at = slice(s * LEN, (s + 1) * LEN)
        out = slice(s * rank, (s + 1) * rank)
        share_ref[out, :rank] = columns(total[:rank, at], gate_ref[at])
        share_ref[out, rank:] = columns(total[:rank, at], up_ref[at])
        share_ref[SEQS * rank :, out] = columns(total[rank:, at], ph_ref[at]).T


def sum_kernel(mine_ref, theirs_ref, gate_ref, up_ref, down_ref):
    rank = gate_ref.shape[1]
    total = mine_ref[...] + theirs_ref[...]
    for s in range(SEQS):
        gate_ref[s] = total[s * rank : (s + 1) * rank, :rank]
        up_ref[s] = total[s * rank : (s + 1) * rank, rank:]
        down_ref[s] = total[SEQS * rank :, s * rank : (s + 1) * rank]


def fast(x_in, out_grad, gate_pre, up_pre, down_weight, x_factor, gate_factor, up_factor, h_factor, dy_factor):
    tokens, width = out_grad.shape
    units, rank = h_factor.shape
    dma = pltpu.SemaphoreType.DMA

    def in_hbm(array):
        return pltpu.with_memory_space_constraint(array, pltpu.HBM)

    def swap(array, bits):
        return lax.ppermute(array, "tensor", [(i, i ^ bits) for i in range(4)])

    def call(kernel, out_shape, in_specs, scratch, mib, flops=0, moved=0, **kwargs):
        several = isinstance(out_shape, tuple)
        return pl.pallas_call(
            kernel,
            out_shape=out_shape,
            in_specs=in_specs,
            out_specs=(VMEM,) * len(out_shape) if several else VMEM,
            scratch_shapes=list(scratch),
            compiler_params=pltpu.CompilerParams(vmem_limit_bytes=mib * MIB),
            cost_estimate=pl.CostEstimate(flops=flops, bytes_accessed=moved, transcendentals=0),
            **kwargs,
        )

    held = pltpu.VMEM((tokens, units), F32)
    per_product = 2 * tokens * width * units
    turns = units // BLOCK
    narrow = pltpu.VMEM((tokens, rank), F32)
    sums = pltpu.VMEM((SUMS, tokens, rank), F32)
    weight = in_hbm(down_weight)

    def blocks(count):
        return pltpu.VMEM((count, BLOCK, width), BF16)

    def chip_blocks(count):
        return pltpu.VMEM((count, CHIP_BLOCK, 2 * width), BF16)

    near = swap(out_grad, 2)
    mate = swap(out_grad, 1)
    a, b, ph, pq, head, own = call(
        elementwise_kernel,
        (held, held, narrow, pltpu.VMEM((2 * rank, tokens), F32), chip_blocks(2), pltpu.VMEM((tokens, width), BF16)),
        [ANY] * 8,
        [
            pltpu.VMEM((tokens, width), BF16),
            pltpu.VMEM((turns, tokens, BLOCK), BF16),
            pltpu.VMEM((turns, tokens, BLOCK), BF16),
            pltpu.VMEM((rank, width), BF16),
            pltpu.VMEM((rank, width), BF16),
            pltpu.VMEM((rank, units), BF16),
            sums,
            dma((5,)),
            dma((turns,)),
            dma((turns,)),
            dma((2, PARTS)),
        ],
        14,
        per_product // 4,
        4 * units * tokens,
    )(
        in_hbm(x_in),
        in_hbm(out_grad),
        in_hbm(gate_pre),
        in_hbm(up_pre),
        weight,
        in_hbm(x_factor.T),
        in_hbm(dy_factor.T),
        in_hbm(h_factor.T),
    )
    pq_mate = swap(pq, 1)
    acc, head = call(
        chip_features_kernel,
        (held, blocks(2)),
        [VMEM] * 3 + [ANY],
        [pltpu.VMEM((tokens, 2 * width), BF16), chip_blocks(AHEAD + 1), dma((units // CHIP_BLOCK + 2, PARTS))],
        16,
        2 * per_product,
        4 * units * width,
    )(own, mate, head, weight)

    near = pl.pallas_call(
        after_kernel,
        out_shape=pltpu.VMEM(near.shape, near.dtype),
        in_specs=[ANY, ANY],
        out_specs=ANY,
        input_output_aliases={0: 0},
        compiler_params=pltpu.CompilerParams(vmem_limit_bytes=MIB),
    )(near, head)
    far = swap(near, 1)
    acc, head = call(
        functools.partial(add_kernel, 2, 3),
        (held, blocks(1)),
        [VMEM] * 3 + [ANY],
        [blocks(AHEAD), dma((turns + 1, PARTS))],
        10,
        per_product,
        2 * units * width,
        input_output_aliases={0: 0},
    )(acc, near, head, weight)
    chip = call(chip_kernel, pltpu.VMEM(pq.shape, F32), [VMEM, VMEM, ANY], [], 1)(pq, pq_mate, head)
    chip_across = swap(chip, 2)
    factor = pltpu.VMEM((rank, units), BF16)
    q_gate, q_up = call(
        functools.partial(far_kernel, 3),
        (narrow, narrow),
        [VMEM] * 3 + [ANY] + [VMEM] * 2 + [ANY] * 2,
        [blocks(AHEAD + 1), factor, factor, sums, sums, dma((turns, PARTS)), dma((2,))],
        16,
        per_product,
        2 * units * width,
    )(acc, far, head, weight, a, b, in_hbm(gate_factor.T), in_hbm(up_factor.T))
    share = call(gradients_kernel, pltpu.VMEM(((SEQS + 1) * rank, 2 * rank), F32), [VMEM] * 5, [], 4)(
        chip, chip_across, q_gate, q_up, ph
    )
    chip_share = share + swap(share, 1)
    out = jax.ShapeDtypeStruct((SEQS, rank, rank), F32)
    return call(sum_kernel, (out, out, out), [VMEM] * 2, [], 4)(chip_share, swap(chip_share, 2))


def solution(mesh):
    def per_device(*arrays):
        (tokens, width), (units, rank) = arrays[1].shape, arrays[8].shape
        fits = (
            mesh.shape["tensor"] == 4
            and (tokens, rank) == (SEQS * LEN, LEN // 2)
            and width % 128 == 0
            and units % BLOCK == 0
            and units % CHIP_BLOCK == 0
            and units // BLOCK > 3
        )
        return tuple((fast if fits else plain)(*arrays))

    return jax.shard_map(
        per_device,
        mesh=mesh,
        in_specs=(P("dp", "tensor"),) * 4 + (P("tensor", None),) * 6,
        out_specs=(P("dp", None, None),) * 3,
        check_vma=False,
    )
```

time: 43.5 us -> 43.5 us (level)
  Pallas kernels: 30.4 us -> 31.2 us
  waiting for transfers between devices: 6.13 us -> 5.46 us
    pallas_call x1, Pallas kernels: 7.55 us -> 8.77 us  [fast(): call(functools.partial(far_kernel, 3), (narrow, narrow), [VMEM] * 3 + [AN...]
    ppermute x7, waiting for transfers between devices: 6.13 us -> 5.46 us  [swap(): return lax.ppermute(array, 'tensor', [(i, i ^ bits) for i in range(4)])]
    pallas_call x2 -> x3, Pallas kernels: 21.5 us -> 21.1 us  [the longest x1 9.27 us: fast(): call(chip_features_kernel, (held, blocks(2)), [VMEM] * 3 + [ANY], [pltpu....]
  transfers between devices with their start and end apart: 7 -> 7, of which waited for: 2 -> 2; matrix products, arithmetic and copies ran while one was open for 0% -> 0% of each run, Pallas kernels for 67% -> 69%
where the time goes in v6:
time: 43.5 us; the launch traced here: 43.3 us
  Pallas kernels  31.2 us (72%)
  starting transfers between devices  5.9 us (14%)
  waiting for transfers between devices  5.46 us (13%)
  between operations  0.73 us (2%)
    pallas_call x1, Pallas kernels, fast(): call(chip_features_kernel, (held, blocks(2)), [VMEM] * 3 + [ANY], [pltpu....  9.27 us
    pallas_call x1, Pallas kernels, fast(): call(functools.partial(far_kernel, 3), (narrow, narrow), [VMEM] * 3 + [AN...  8.77 us
    pallas_call x1, Pallas kernels, fast(): call(elementwise_kernel, (held, held, narrow, pltpu.VMEM((2 * rank, token...  6.57 us
    ppermute x7, starting transfers between devices, swap(): return lax.ppermute(array, 'tensor', [(i, i ^ bits) for i in range(4)])  5.9 us
    ppermute x7, waiting for transfers between devices, swap(): return lax.ppermute(array, 'tensor', [(i, i ^ bits) for i in range(4)])  5.46 us
    pallas_call x1, Pallas kernels, fast(): call(functools.partial(add_kernel, 2, 3), (held, blocks(1)), [VMEM] * 3 +...  5.25 us
  transfers between devices with their start and end apart: 7, of which 2 were waited for; matrix products, arithmetic and copies ran while one was open for 0% of the time, Pallas kernels for 69%

profile of v6, /device:TPU:0, one launch (start us, length us, event | category | flops | bytes accessed | tf_op | source)
XLA Modules:
  0.0 43.3 jit_solution(3272683623804046455)
XLA Ops:
  0.6 0.5 %collective-permute-start.1 = (bf16[256,1280]{1,0:T(8,128)(2,1)}, bf16[256,1280]{1,0:T(8,128)(2,1)S(1)}, u32[]{:S(2)}, u32[]{:S(2)}) collective-permute-start(bf16[256,1280]{1,0:T(8,128)(2,1)} %og_hbm.1), channel_id=1, source_target_pairs={{0,1},{1,0},{2,3},{3,2},{4,5},{5,4},{6,7},{7,6},{8,9},{9,8},{10,11... | collective-permute-start | bytes 1966088 | tf_op jit(solution)/shard_map/ppermute | solution.py:301
  1.2 2.6 %collective-permute-start.2 = (bf16[256,1280]{1,0:T(8,128)(2,1)}, bf16[256,1280]{1,0:T(8,128)(2,1)S(1)}, u32[]{:S(2)}, u32[]{:S(2)}) collective-permute-start(bf16[256,1280]{1,0:T(8,128)(2,1)} %og_hbm.1), channel_id=1, source_target_pairs={{0,2},{1,3},{2,0},{3,1},{4,6},{5,7},{6,4},{7,5},{8,10},{9,11},{10,... | collective-permute-start | bytes 1966088 | tf_op jit(solution)/shard_map/ppermute | solution.py:301
  3.7 6.6 %shard_map.121 = (f32[256,4608]{1,0:T(8,128)S(1)}, f32[256,4608]{1,0:T(8,128)S(1)}, f32[256,64]{1,0:T(8,128)S(1)}, f32[128,256]{1,0:T(8,128)S(1)}, bf16[2,768,25...) custom-call(bf16[256,1280]{1,0:T(8,128)(2,1)} %x_hbm.1, bf16[256,1280]{1,0:T(8,128)(2,1)} %og_hbm.1, ...), custom_call_target="tpu_custom_call" | custom-call | flops 754974720 | bytes 4718592 | tf_op jit(solution)/shard_map/pallas_call | solution.py:331
  10.3 0.0 collective-permute-done.1.mate_ref
  10.3 9.3 %shard_map.122 = (f32[256,4608]{1,0:T(8,128)S(1)}, bf16[2,1152,1280]{2,1,0:T(8,128)(2,1)S(1)}) custom-call(bf16[256,1280]{1,0:T(8,128)(2,1)S(1)} %get-tuple-element.16.own_ref, bf16[256,1280]{1,0:T(8,128)(2,1)S(1)} %collective-permute-done.1.mate_ref, bf16[2,768,2560]{2,1,0:T(8,128)(2,1)S(1)} %get-tuple-element.17.head_ref, bf16[4608,5120]{1,0:T(8,128)(2,1)} %w_hbm.7), custom_call_target="tpu_custom_call" | custom-call | flops 6039797760 | bytes 23592960 | tf_op jit(solution)/shard_map/pallas_call | solution.py:362
  19.6 0.0 collective-permute-done.2.array_ref
  19.6 0.2 collective-permute-start.4
  19.8 0.3 collective-permute-start
  20.2 5.3 %shard_map.124 = (f32[256,4608]{1,0:T(8,128)S(1)}, bf16[1,1152,1280]{2,1,0:T(8,128)(2,1)S(1)}) custom-call(f32[256,4608]{1,0:T(8,128)S(1)} %get-tuple-element.18.acc_in, bf16[256,1280]{1,0:T(8,128)(2,1)S(1)} %shard_map.123.og_ref, bf16[2,1152,1280]{2,1,0:T(8,128)(2,1)S(1)} %get-tuple-element.19.token_ref.head_ref, ...), custom_call_target="tpu_custom_call", output_to_operand_aliasing={{0}: (0, {})} | custom-call | flops 3019898880 | bytes 11796480 | tf_op jit(solution)/shard_map/pallas_call | solution.py:381
  25.4 0.0 collective-permute-done.theirs_ref
  25.5 1.4 %collective-permute-start.3 = (f32[128,256]{1,0:T(8,128)S(1)}, f32[128,256]{1,0:T(8,128)S(1)}, u32[]{:S(2)}, u32[]{:S(2)}) collective-permute-start(f32[128,256]{1,0:T(8,128)S(1)} %shard_map.125.chip_ref), channel_id=1, source_target_pairs={{0,2},{1,3},{2,0},{3,1},{4,6},{5,7},{6,4},{7,5},{8,10},{9,11},{10,... | collective-permute-start | bytes 393224 | tf_op jit(solution)/shard_map/ppermute | solution.py:301
  26.9 0.0 collective-permute-done.4.og_ref
  26.9 8.8 %shard_map.126 = (f32[256,64]{1,0:T(8,128)S(1)}, f32[256,64]{1,0:T(8,128)S(1)}) custom-call(f32[256,4608]{1,0:T(8,128)S(1)} %get-tuple-element.21.acc_ref, bf16[256,1280]{1,0:T(8,128)(2,1)S(1)} %collective-permute-done.4.og_ref, bf16[1,1152,1280]{2,1,0:T(8,128)(2,1)S(1)} %get-tuple-element.20.token_ref.head_ref, bf16[4608,5120]{1,0:T(8,128)(2,1)} %w_hbm.7, ...), custom_call_target="tpu_custom_call" | custom-call | flops 3019898880 | bytes 11796480 | tf_op jit(solution)/shard_map/pallas_call | solution.py:394
  35.7 0.0 collective-permute-done.3.other_ref
  35.7 0.6 %shard_map.127 = f32[192,128]{1,0:T(8,128)S(1)} custom-call(f32[128,256]{1,0:T(8,128)S(1)} %shard_map.125.chip_ref, f32[128,256]{1,0:T(8,128)S(1)} %collective-permute-done.3.other_ref, f32[256,64]{1,0:T(8,128)S(1)} %get-tuple-element.24.gate_ref, f32[256,64]{1,0:T(8,128)S(1)} %get-tuple-element.25.up_ref, f32[256,64]{1,0:T(8,128)S(1)} %get-tuple-element.26.ph_ref), custom_call_target="tpu_custom_call" | custom-call | tf_op jit(solution)/shard_map/pallas_call | solution.py:403
  36.3 0.1 collective-permute-start.5
  36.3 1.3 %collective-permute-done.5 = f32[192,128]{1,0:T(8,128)S(1)} collective-permute-done((f32[192,128]{1,0:T(8,128)S(1)}, f32[192,128]{1,0:T(8,128)S(1)}, u32[]{:S(2)}, u32[]{:S(2)}) %collective-permute-start.5) | collective-permute-done | bytes 98336 | tf_op jit(solution)/shard_map/ppermute | solution.py:301
  37.6 0.8 %collective-permute-start.6 = (f32[192,128]{1,0:T(8,128)S(1)}, f32[192,128]{1,0:T(8,128)S(1)}, u32[]{:S(2)}, u32[]{:S(2)}) collective-permute-start(f32[192,128]{1,0:T(8,128)S(1)} %add.3.mine_ref), channel_id=1, source_target_pairs={{0,2},{1,3},{2,0},{3,1},{4,6},{5,7},{6,4},{7,5},{8,10},{9,11},{10,... | collective-permute-start | bytes 294920 | tf_op jit(solution)/shard_map/ppermute | solution.py:301
  38.4 4.2 %collective-permute-done.6.theirs_ref = f32[192,128]{1,0:T(8,128)S(1)} collective-permute-done((f32[192,128]{1,0:T(8,128)S(1)}, f32[192,128]{1,0:T(8,128)S(1)}, u32[]{:S(2)}, u32[]{:S(2)}) %collective-permute-start.6) | collective-permute-done | bytes 98336 | tf_op jit(solution)/shard_map/ppermute | solution.py:301
  42.6 0.7 %shard_map.128 = (f32[2,64,64]{2,1,0:T(8,128)}, f32[2,64,64]{2,1,0:T(8,128)}, f32[2,64,64]{2,1,0:T(8,128)}) custom-call(f32[192,128]{1,0:T(8,128)S(1)} %add.3.mine_ref, f32[192,128]{1,0:T(8,128)S(1)} %collective-permute-done.6.theirs_ref), custom_call_target="tpu_custom_call" | custom-call | tf_op jit(solution)/shard_map/pallas_call | solution.py:408
  (3 shorter events, 0.0 us)
Async XLA Ops:
  0.6 9.7 %collective-permute-start.1 = (bf16[256,1280]{1,0:T(8,128)(2,1)}, bf16[256,1280]{1,0:T(8,128)(2,1)S(1)}, u32[]{:S(2)}, u32[]{:S(2)}) collective-permute-start(bf16[256,1280]{1,0:T(8,128)(2,1)} %og_hbm.1), channel_id=1, source_target_pairs={{0,1},{1,0},{2,3},{3,2},{4,5},{5,4},{6,7},{7,6},{8,9},{9,8},{10,11... | collective-permute-start | bytes 1966088 | tf_op jit(solution)/shard_map/ppermute | solution.py:301
  1.2 18.4 %collective-permute-start.2 = (bf16[256,1280]{1,0:T(8,128)(2,1)}, bf16[256,1280]{1,0:T(8,128)(2,1)S(1)}, u32[]{:S(2)}, u32[]{:S(2)}) collective-permute-start(bf16[256,1280]{1,0:T(8,128)(2,1)} %og_hbm.1), channel_id=1, source_target_pairs={{0,2},{1,3},{2,0},{3,1},{4,6},{5,7},{6,4},{7,5},{8,10},{9,11},{10,... | collective-permute-start | bytes 1966088 | tf_op jit(solution)/shard_map/ppermute | solution.py:301
  19.6 7.3 %collective-permute-start.4 = (bf16[256,1280]{1,0:T(8,128)(2,1)S(1)}, bf16[256,1280]{1,0:T(8,128)(2,1)S(1)}, u32[]{:S(2)}, u32[]{:S(2)}) collective-permute-start(bf16[256,1280]{1,0:T(8,128)(2,1)S(1)} %shard_map.123.og_ref), channel_id=1, source_target_pairs={{0,1},{1,0},{2,3},{3,2},{4,5},{5,4},{6,7},{7,6},{8,9},{9,8},{10,11... | collective-permute-start | bytes 1966088 | tf_op jit(solution)/shard_map/ppermute | solution.py:301
  19.8 5.6 %collective-permute-start = (f32[128,256]{1,0:T(8,128)S(1)}, f32[128,256]{1,0:T(8,128)S(1)}, u32[]{:S(2)}, u32[]{:S(2)}) collective-permute-start(f32[128,256]{1,0:T(8,128)S(1)} %get-tuple-element.15.mine_ref), channel_id=1, source_target_pairs={{0,1},{1,0},{2,3},{3,2},{4,5},{5,4},{6,7},{7,6},{8,9},{9,8},{10,11... | collective-permute-start | bytes 393224 | tf_op jit(solution)/shard_map/ppermute | solution.py:301
  25.5 10.2 %collective-permute-start.3 = (f32[128,256]{1,0:T(8,128)S(1)}, f32[128,256]{1,0:T(8,128)S(1)}, u32[]{:S(2)}, u32[]{:S(2)}) collective-permute-start(f32[128,256]{1,0:T(8,128)S(1)} %shard_map.125.chip_ref), channel_id=1, source_target_pairs={{0,2},{1,3},{2,0},{3,1},{4,6},{5,7},{6,4},{7,5},{8,10},{9,11},{10,... | collective-permute-start | bytes 393224 | tf_op jit(solution)/shard_map/ppermute | solution.py:301
  36.3 1.4 %collective-permute-start.5 = (f32[192,128]{1,0:T(8,128)S(1)}, f32[192,128]{1,0:T(8,128)S(1)}, u32[]{:S(2)}, u32[]{:S(2)}) collective-permute-start(f32[192,128]{1,0:T(8,128)S(1)} %shard_map.127), channel_id=1, source_target_pairs={{0,1},{1,0},{2,3},{3,2},{4,5},{5,4},{6,7},{7,6},{8,9},{9,8},{10,11... | collective-permute-start | bytes 294920 | tf_op jit(solution)/shard_map/ppermute | solution.py:301
  37.6 4.9 %collective-permute-start.6 = (f32[192,128]{1,0:T(8,128)S(1)}, f32[192,128]{1,0:T(8,128)S(1)}, u32[]{:S(2)}, u32[]{:S(2)}) collective-permute-start(f32[192,128]{1,0:T(8,128)S(1)} %add.3.mine_ref), channel_id=1, source_target_pairs={{0,2},{1,3},{2,0},{3,1},{4,6},{5,7},{6,4},{7,5},{8,10},{9,11},{10,... | collective-permute-start | bytes 294920 | tf_op jit(solution)/shard_map/ppermute | solution.py:301

commit v7 on v6

--- a/solution.py
+++ b/solution.py
@@ -13,7 +13,6 @@
 CHIP_BLOCK = 768
 AHEAD = 2
 PARTS = 2
-SUMS = 3
 MIB = 1 << 20
 ANY = pl.BlockSpec(memory_space=pl.ANY)
 VMEM = pl.BlockSpec(memory_space=pltpu.VMEM)
@@ -134,19 +133,11 @@
         wait(next_copies(j))
 
 
-def project(sums_ref, rows, factor):
-    parts = sums_ref.shape[0]
-    part = factor.shape[1] // parts
-    for k in range(parts):
-        at = slice(k * part, (k + 1) * part)
-        sums_ref[k] += rows_by_rows(rows[:, at], factor[:, at])
-
-
 def elementwise_kernel(x_hbm, og_hbm, gate_hbm, up_hbm, w_hbm, xf_hbm, yf_hbm, hf_hbm,
-                       a_ref, b_ref, ph_ref, pq_ref, head_ref, og_v,
-                       x_v, gate_v, up_v, xf_v, yf_v, hf_v, sums_v, sems, gate_sems, up_sems, w_sems):
-    tokens, units = a_ref.shape
-    rank = ph_ref.shape[1]
+                       a_ref, b_ref, ph_ref, pq_ref, head_ref, own_ref,
+                       x_v, og_v, gate_v, up_v, xf_v, yf_v, hf_v, sems, gate_sems, up_sems, w_sems):
+    units = a_ref.shape[0]
+    rank = ph_ref.shape[0]
     turns = units // BLOCK
 
     def at(i):
@@ -167,7 +158,7 @@
     start(small[:1])
     start(gate_up(1))
     start(small[1:])
-    sums_v[...] = jnp.zeros_like(sums_v)
+    ph_ref[...] = jnp.zeros_like(ph_ref)
     wait(gate_up(0))
     wait(small[:1])
 
@@ -185,76 +176,77 @@
         def _():
             wait(gate_up(i))
 
-        g = gate_v[i].astype(F32)
-        u = up_v[i].astype(F32)
+        g = gate_v[i].T.astype(F32)
+        u = up_v[i].T.astype(F32)
         s = 0.5 * jnp.tanh(0.5 * g) + 0.5
         silu = g * s
-        a_ref[:, at(i)] = u * s * ((1.0 + g) - silu)
-        b_ref[:, at(i)] = silu
-        project(sums_v, (silu * u).astype(BF16), hf_v.at[:, at(i)])
+        a_ref[at(i)] = u * s * ((1.0 + g) - silu)
+        b_ref[at(i)] = silu
+        ph_ref[...] += product(hf_v[:, at(i)], (silu * u).astype(BF16))
 
     wait(small[1:])
     pq_ref[:rank] = rows_by_rows(xf_v[...], x_v[...])
-    pq_ref[rank:] = rows_by_rows(yf_v[...], og_v[...])
-    ph_ref[...] = jnp.sum(sums_v[...], axis=0)
+    own_ref[...] = og_v[...].T
+    pq_ref[rank:] = product(yf_v[...], own_ref[...])
     for i in range(heads):
         wait(following.copies(i, head_ref.at[i], w_sems.at[i]))
 
 
 def chip_features_kernel(own_ref, mate_ref, head_ref, w_hbm, acc_ref, next_ref, og_v, w_v, sems):
     me = lax.axis_index("tensor")
-    width = own_ref.shape[1]
+    width = own_ref.shape[0]
     step = Step(me // 2, 2 * width, w_v.shape[1], w_hbm)
     following = Step(me ^ 2, width, next_ref.shape[1], w_hbm)
     mine = pl.ds(pl.multiple_of(me % 2 * width, 128), width)
     theirs = pl.ds(pl.multiple_of((me + 1) % 2 * width, 128), width)
-    og_v[:, mine] = own_ref[...]
-    og_v[:, theirs] = mate_ref[...]
+    og_v[mine] = own_ref[...]
+    og_v[theirs] = mate_ref[...].T
 
     def body(i, weights):
-        acc_ref[:, step.units(i)] = rows_by_rows(og_v[...], weights[...])
-
-    stream(step, following, acc_ref.shape[1] // step.block, head_ref, w_v, next_ref, sems, body)
-
-
-def add_kernel(bits, following_bits, acc_in, og_ref, head_ref, w_hbm, acc_ref, next_ref, w_v, sems):
+        acc_ref[step.units(i)] = product(weights[...], og_v[...])
+
+    stream(step, following, acc_ref.shape[0] // step.block, head_ref, w_v, next_ref, sems, body)
+
+
+def add_kernel(bits, following_bits, acc_in, og_ref, head_ref, w_hbm, acc_ref, next_ref, og_v, w_v, sems):
     me = lax.axis_index("tensor")
     _, block, width = w_v.shape
     step = Step(me ^ bits, width, block, w_hbm)
     following = Step(me ^ following_bits, width, block, w_hbm)
 
+    og_v[...] = og_ref[...].T
+
     def body(i, weights):
         at = step.units(i)
-        acc_ref[:, at] = acc_in[:, at] + rows_by_rows(og_ref[...], weights[...])
-
-    stream(step, following, acc_in.shape[1] // block, head_ref, w_v, next_ref, sems, body)
+        acc_ref[at] = acc_in[at] + product(weights[...], og_v[...])
+
+    stream(step, following, acc_in.shape[0] // block, head_ref, w_v, next_ref, sems, body)
 
 
 def far_kernel(bits, acc_ref, og_ref, head_ref, w_hbm, a_ref, b_ref, gf_hbm, uf_hbm, gate_ref, up_ref,
-               w_v, gf_ref, uf_ref, gate_v, up_v, sems, factor_sems):
+               og_v, w_v, gf_ref, uf_ref, sems, factor_sems):
     _, block, width = w_v.shape
     step = Step(lax.axis_index("tensor") ^ bits, width, block, w_hbm)
     factors = [
         pltpu.make_async_copy(src, dst, factor_sems.at[k]) for k, (src, dst) in enumerate(((gf_hbm, gf_ref), (uf_hbm, uf_ref)))
     ]
     start(factors)
-    gate_v[...] = jnp.zeros_like(gate_v)
-    up_v[...] = jnp.zeros_like(up_v)
+    gate_ref[...] = jnp.zeros_like(gate_ref)
+    up_ref[...] = jnp.zeros_like(up_ref)
+    og_v[...] = og_ref[...].T
 
     def body(i, weights):
         at = step.units(i)
-        hidden_grad = acc_ref[:, at] + rows_by_rows(og_ref[...], weights[...])
+        hidden_grad = acc_ref[at] + product(weights[...], og_v[...])
 
         @pl.when(i == 0)
         def _():
             wait(factors)
 
-        project(gate_v, (hidden_grad * a_ref[:, at]).astype(BF16), gf_ref.at[:, at])
-        project(up_v, (hidden_grad * b_ref[:, at]).astype(BF16), uf_ref.at[:, at])
-
-    stream(step, None, acc_ref.shape[1] // block, head_ref, w_v, None, sems, body)
-    gate_ref[...] = jnp.sum(gate_v[...], axis=0)
-    up_ref[...] = jnp.sum(up_v[...], axis=0)
+        gate_ref[...] += product(gf_ref[:, at], (hidden_grad * a_ref[at]).astype(BF16))
+        up_ref[...] += product(uf_ref[:, at], (hidden_grad * b_ref[at]).astype(BF16))
+
+    stream(step, None, acc_ref.shape[0] // block, head_ref, w_v, None, sems, body)
 
 
 def after_kernel(array_ref, token_ref, same_ref):
@@ -266,18 +258,15 @@
 
 
 def gradients_kernel(chip_ref, other_ref, gate_ref, up_ref, ph_ref, share_ref):
-    rank = ph_ref.shape[1]
+    rank = ph_ref.shape[0]
     total = chip_ref[...] + other_ref[...]
-
-    def columns(left, right):
-        return jnp.dot(left, right, precision=lax.Precision.HIGHEST, preferred_element_type=F32)
-
+    highest = lax.Precision.HIGHEST
     for s in range(SEQS):
         at = slice(s * LEN, (s + 1) * LEN)
         out = slice(s * rank, (s + 1) * rank)
-        share_ref[out, :rank] = columns(total[:rank, at], gate_ref[at])
-        share_ref[out, rank:] = columns(total[:rank, at], up_ref[at])
-        share_ref[SEQS * rank :, out] = columns(total[rank:, at], ph_ref[at]).T
+        share_ref[out, :rank] = rows_by_rows(total[:rank, at], gate_ref[:, at], highest)
+        share_ref[out, rank:] = rows_by_rows(total[:rank, at], up_ref[:, at], highest)
+        share_ref[SEQS * rank :, out] = rows_by_rows(ph_ref[:, at], total[rank:, at], highest)
 
 
 def sum_kernel(mine_ref, theirs_ref, gate_ref, up_ref, down_ref):
@@ -313,11 +302,11 @@
             **kwargs,
         )
 
-    held = pltpu.VMEM((tokens, units), F32)
+    held = pltpu.VMEM((units, tokens), F32)
     per_product = 2 * tokens * width * units
     turns = units // BLOCK
-    narrow = pltpu.VMEM((tokens, rank), F32)
-    sums = pltpu.VMEM((SUMS, tokens, rank), F32)
+    narrow = pltpu.VMEM((rank, tokens), F32)
+    turned = pltpu.VMEM((width, tokens), BF16)
     weight = in_hbm(down_weight)
 
     def blocks(count):
@@ -330,16 +319,16 @@
     mate = swap(out_grad, 1)
     a, b, ph, pq, head, own = call(
         elementwise_kernel,
-        (held, held, narrow, pltpu.VMEM((2 * rank, tokens), F32), chip_blocks(2), pltpu.VMEM((tokens, width), BF16)),
+        (held, held, narrow, pltpu.VMEM((2 * rank, tokens), F32), chip_blocks(2), turned),
         [ANY] * 8,
         [
+            pltpu.VMEM((tokens, width), BF16),
             pltpu.VMEM((tokens, width), BF16),
             pltpu.VMEM((turns, tokens, BLOCK), BF16),
             pltpu.VMEM((turns, tokens, BLOCK), BF16),
             pltpu.VMEM((rank, width), BF16),
             pltpu.VMEM((rank, width), BF16),
             pltpu.VMEM((rank, units), BF16),
-            sums,
             dma((5,)),
             dma((turns,)),
             dma((turns,)),
@@ -363,7 +352,7 @@
         chip_features_kernel,
         (held, blocks(2)),
         [VMEM] * 3 + [ANY],
-        [pltpu.VMEM((tokens, 2 * width), BF16), chip_blocks(AHEAD + 1), dma((units // CHIP_BLOCK + 2, PARTS))],
+        [pltpu.VMEM((2 * width, tokens), BF16), chip_blocks(AHEAD + 1), dma((units // CHIP_BLOCK + 2, PARTS))],
         16,
         2 * per_product,
         4 * units * width,
@@ -382,7 +371,7 @@
         functools.partial(add_kernel, 2, 3),
         (held, blocks(1)),
         [VMEM] * 3 + [ANY],
-        [blocks(AHEAD), dma((turns + 1, PARTS))],
+        [turned, blocks(AHEAD), dma((turns + 1, PARTS))],
         10,
         per_product,
         2 * units * width,
@@ -395,7 +384,7 @@
         functools.partial(far_kernel, 3),
         (narrow, narrow),
         [VMEM] * 3 + [ANY] + [VMEM] * 2 + [ANY] * 2,
-        [blocks(AHEAD + 1), factor, factor, sums, sums, dma((turns, PARTS)), dma((2,))],
+        [turned, blocks(AHEAD + 1), factor, factor, dma((turns, PARTS)), dma((2,))],
         16,
         per_product,
         2 * units * width,

time: 43.5 us -> 42.1 us (0.968)
  Pallas kernels: 31.2 us -> 29.9 us
    pallas_call x1, Pallas kernels: 8.77 us -> 7.69 us  [fast(): call(functools.partial(far_kernel, 3), (narrow, narrow), [VMEM] * 3 + [AN...]
  transfers between devices with their start and end apart: 7 -> 7, of which waited for: 2 -> 2; matrix products, arithmetic and copies ran while one was open for 0% -> 0% of each run, Pallas kernels for 69% -> 68%
where the time goes in v7:
time: 42.1 us; the launch traced here: 41.9 us
  Pallas kernels  29.9 us (71%)
  starting transfers between devices  5.89 us (14%)
  waiting for transfers between devices  5.36 us (13%)
  between operations  0.73 us (2%)
    pallas_call x1, Pallas kernels, fast(): call(chip_features_kernel, (held, blocks(2)), [VMEM] * 3 + [ANY], [pltpu....  9.38 us
    pallas_call x1, Pallas kernels, fast(): call(functools.partial(far_kernel, 3), (narrow, narrow), [VMEM] * 3 + [AN...  7.69 us
    pallas_call x1, Pallas kernels, fast(): call(elementwise_kernel, (held, held, narrow, pltpu.VMEM((2 * rank, token...  6.56 us
    ppermute x7, starting transfers between devices, swap(): return lax.ppermute(array, 'tensor', [(i, i ^ bits) for i in range(4)])  5.89 us
    ppermute x7, waiting for transfers between devices, swap(): return lax.ppermute(array, 'tensor', [(i, i ^ bits) for i in range(4)])  5.36 us
    pallas_call x1, Pallas kernels, fast(): call(functools.partial(add_kernel, 2, 3), (held, blocks(1)), [VMEM] * 3 +...  5.04 us
  transfers between devices with their start and end apart: 7, of which 2 were waited for; matrix products, arithmetic and copies ran while one was open for 0% of the time, Pallas kernels for 68%

profile of v7, /device:TPU:0, one launch (start us, length us, event | category | flops | bytes accessed | tf_op | source)
XLA Modules:
  0.0 41.9 jit_solution(662600915746788865)
XLA Ops:
  0.6 0.5 %collective-permute-start.1 = (bf16[256,1280]{1,0:T(8,128)(2,1)}, bf16[256,1280]{1,0:T(8,128)(2,1)S(1)}, u32[]{:S(2)}, u32[]{:S(2)}) collective-permute-start(bf16[256,1280]{1,0:T(8,128)(2,1)} %og_hbm.1), channel_id=1, source_target_pairs={{0,1},{1,0},{2,3},{3,2},{4,5},{5,4},{6,7},{7,6},{8,9},{9,8},{10,11... | collective-permute-start | bytes 1966088 | tf_op jit(solution)/shard_map/ppermute | solution.py:290
  1.2 2.6 %collective-permute-start.2 = (bf16[256,1280]{1,0:T(8,128)(2,1)}, bf16[256,1280]{1,0:T(8,128)(2,1)S(1)}, u32[]{:S(2)}, u32[]{:S(2)}) collective-permute-start(bf16[256,1280]{1,0:T(8,128)(2,1)} %og_hbm.1), channel_id=1, source_target_pairs={{0,2},{1,3},{2,0},{3,1},{4,6},{5,7},{6,4},{7,5},{8,10},{9,11},{10,... | collective-permute-start | bytes 1966088 | tf_op jit(solution)/shard_map/ppermute | solution.py:290
  3.7 6.6 %shard_map.121 = (f32[4608,256]{1,0:T(8,128)S(1)}, f32[4608,256]{1,0:T(8,128)S(1)}, f32[64,256]{1,0:T(8,128)S(1)}, f32[128,256]{1,0:T(8,128)S(1)}, bf16[2,768,25...) custom-call(bf16[256,1280]{1,0:T(8,128)(2,1)} %x_hbm.1, bf16[256,1280]{1,0:T(8,128)(2,1)} %og_hbm.1, ...), custom_call_target="tpu_custom_call" | custom-call | flops 754974720 | bytes 4718592 | tf_op jit(solution)/shard_map/pallas_call | solution.py:320
  10.3 0.0 collective-permute-done.1.mate_ref
  10.3 9.4 %shard_map.122 = (f32[4608,256]{1,0:T(8,128)S(1)}, bf16[2,1152,1280]{2,1,0:T(8,128)(2,1)S(1)}) custom-call(bf16[1280,256]{1,0:T(8,128)(2,1)S(1)} %get-tuple-element.16.own_ref, bf16[256,1280]{1,0:T(8,128)(2,1)S(1)} %collective-permute-done.1.mate_ref, bf16[2,768,2560]{2,1,0:T(8,128)(2,1)S(1)} %get-tuple-element.17.head_ref, bf16[4608,5120]{1,0:T(8,128)(2,1)} %w_hbm.7), custom_call_target="tpu_custom_call" | custom-call | flops 6039797760 | bytes 23592960 | tf_op jit(solution)/shard_map/pallas_call | solution.py:351
  19.7 0.0 collective-permute-done.2.array_ref
  19.7 0.2 collective-permute-start.4
  19.9 0.3 collective-permute-start
  20.3 5.0 %shard_map.124 = (f32[4608,256]{1,0:T(8,128)S(1)}, bf16[1,1152,1280]{2,1,0:T(8,128)(2,1)S(1)}) custom-call(f32[4608,256]{1,0:T(8,128)S(1)} %get-tuple-element.18.acc_in, bf16[256,1280]{1,0:T(8,128)(2,1)S(1)} %shard_map.123.og_ref, bf16[2,1152,1280]{2,1,0:T(8,128)(2,1)S(1)} %get-tuple-element.19.token_ref.head_ref, ...), custom_call_target="tpu_custom_call", output_to_operand_aliasing={{0}: (0, {})} | custom-call | flops 3019898880 | bytes 11796480 | tf_op jit(solution)/shard_map/pallas_call | solution.py:370
  25.3 0.0 collective-permute-done.theirs_ref
  25.4 1.3 %collective-permute-start.3 = (f32[128,256]{1,0:T(8,128)S(1)}, f32[128,256]{1,0:T(8,128)S(1)}, u32[]{:S(2)}, u32[]{:S(2)}) collective-permute-start(f32[128,256]{1,0:T(8,128)S(1)} %shard_map.125.chip_ref), channel_id=1, source_target_pairs={{0,2},{1,3},{2,0},{3,1},{4,6},{5,7},{6,4},{7,5},{8,10},{9,11},{10,... | collective-permute-start | bytes 393224 | tf_op jit(solution)/shard_map/ppermute | solution.py:290
  26.7 0.0 collective-permute-done.4.og_ref
  26.7 7.7 %shard_map.126 = (f32[64,256]{1,0:T(8,128)S(1)}, f32[64,256]{1,0:T(8,128)S(1)}) custom-call(f32[4608,256]{1,0:T(8,128)S(1)} %get-tuple-element.21.acc_ref, bf16[256,1280]{1,0:T(8,128)(2,1)S(1)} %collective-permute-done.4.og_ref, bf16[1,1152,1280]{2,1,0:T(8,128)(2,1)S(1)} %get-tuple-element.20.token_ref.head_ref, bf16[4608,5120]{1,0:T(8,128)(2,1)} %w_hbm.7, ...), custom_call_target="tpu_custom_call" | custom-call | flops 3019898880 | bytes 11796480 | tf_op jit(solution)/shard_map/pallas_call | solution.py:383
  34.4 0.0 collective-permute-done.3.other_ref
  34.4 0.5 %shard_map.127 = f32[192,128]{1,0:T(8,128)S(1)} custom-call(f32[128,256]{1,0:T(8,128)S(1)} %shard_map.125.chip_ref, f32[128,256]{1,0:T(8,128)S(1)} %collective-permute-done.3.other_ref, f32[64,256]{1,0:T(8,128)S(1)} %get-tuple-element.24.gate_ref, f32[64,256]{1,0:T(8,128)S(1)} %get-tuple-element.25.up_ref, f32[64,256]{1,0:T(8,128)S(1)} %get-tuple-element.26.ph_ref), custom_call_target="tpu_custom_call" | custom-call | tf_op jit(solution)/shard_map/pallas_call | solution.py:392
  34.9 0.1 collective-permute-start.5
  35.0 1.3 %collective-permute-done.5 = f32[192,128]{1,0:T(8,128)S(1)} collective-permute-done((f32[192,128]{1,0:T(8,128)S(1)}, f32[192,128]{1,0:T(8,128)S(1)}, u32[]{:S(2)}, u32[]{:S(2)}) %collective-permute-start.5) | collective-permute-done | bytes 98336 | tf_op jit(solution)/shard_map/ppermute | solution.py:290
  36.3 0.9 %collective-permute-start.6 = (f32[192,128]{1,0:T(8,128)S(1)}, f32[192,128]{1,0:T(8,128)S(1)}, u32[]{:S(2)}, u32[]{:S(2)}) collective-permute-start(f32[192,128]{1,0:T(8,128)S(1)} %add.3.mine_ref), channel_id=1, source_target_pairs={{0,2},{1,3},{2,0},{3,1},{4,6},{5,7},{6,4},{7,5},{8,10},{9,11},{10,... | collective-permute-start | bytes 294920 | tf_op jit(solution)/shard_map/ppermute | solution.py:290
  37.1 4.1 %collective-permute-done.6.theirs_ref = f32[192,128]{1,0:T(8,128)S(1)} collective-permute-done((f32[192,128]{1,0:T(8,128)S(1)}, f32[192,128]{1,0:T(8,128)S(1)}, u32[]{:S(2)}, u32[]{:S(2)}) %collective-permute-start.6) | collective-permute-done | bytes 98336 | tf_op jit(solution)/shard_map/ppermute | solution.py:290
  41.2 0.7 %shard_map.128 = (f32[2,64,64]{2,1,0:T(8,128)}, f32[2,64,64]{2,1,0:T(8,128)}, f32[2,64,64]{2,1,0:T(8,128)}) custom-call(f32[192,128]{1,0:T(8,128)S(1)} %add.3.mine_ref, f32[192,128]{1,0:T(8,128)S(1)} %collective-permute-done.6.theirs_ref), custom_call_target="tpu_custom_call" | custom-call | tf_op jit(solution)/shard_map/pallas_call | solution.py:397
  (3 shorter events, 0.0 us)
Async XLA Ops:
  0.6 9.7 %collective-permute-start.1 = (bf16[256,1280]{1,0:T(8,128)(2,1)}, bf16[256,1280]{1,0:T(8,128)(2,1)S(1)}, u32[]{:S(2)}, u32[]{:S(2)}) collective-permute-start(bf16[256,1280]{1,0:T(8,128)(2,1)} %og_hbm.1), channel_id=1, source_target_pairs={{0,1},{1,0},{2,3},{3,2},{4,5},{5,4},{6,7},{7,6},{8,9},{9,8},{10,11... | collective-permute-start | bytes 1966088 | tf_op jit(solution)/shard_map/ppermute | solution.py:290
  1.2 18.5 %collective-permute-start.2 = (bf16[256,1280]{1,0:T(8,128)(2,1)}, bf16[256,1280]{1,0:T(8,128)(2,1)S(1)}, u32[]{:S(2)}, u32[]{:S(2)}) collective-permute-start(bf16[256,1280]{1,0:T(8,128)(2,1)} %og_hbm.1), channel_id=1, source_target_pairs={{0,2},{1,3},{2,0},{3,1},{4,6},{5,7},{6,4},{7,5},{8,10},{9,11},{10,... | collective-permute-start | bytes 1966088 | tf_op jit(solution)/shard_map/ppermute | solution.py:290
  19.7 7.0 %collective-permute-start.4 = (bf16[256,1280]{1,0:T(8,128)(2,1)S(1)}, bf16[256,1280]{1,0:T(8,128)(2,1)S(1)}, u32[]{:S(2)}, u32[]{:S(2)}) collective-permute-start(bf16[256,1280]{1,0:T(8,128)(2,1)S(1)} %shard_map.123.og_ref), channel_id=1, source_target_pairs={{0,1},{1,0},{2,3},{3,2},{4,5},{5,4},{6,7},{7,6},{8,9},{9,8},{10,11... | collective-permute-start | bytes 1966088 | tf_op jit(solution)/shard_map/ppermute | solution.py:290
  19.9 5.4 %collective-permute-start = (f32[128,256]{1,0:T(8,128)S(1)}, f32[128,256]{1,0:T(8,128)S(1)}, u32[]{:S(2)}, u32[]{:S(2)}) collective-permute-start(f32[128,256]{1,0:T(8,128)S(1)} %get-tuple-element.15.mine_ref), channel_id=1, source_target_pairs={{0,1},{1,0},{2,3},{3,2},{4,5},{5,4},{6,7},{7,6},{8,9},{9,8},{10,11... | collective-permute-start | bytes 393224 | tf_op jit(solution)/shard_map/ppermute | solution.py:290
  25.4 9.0 %collective-permute-start.3 = (f32[128,256]{1,0:T(8,128)S(1)}, f32[128,256]{1,0:T(8,128)S(1)}, u32[]{:S(2)}, u32[]{:S(2)}) collective-permute-start(f32[128,256]{1,0:T(8,128)S(1)} %shard_map.125.chip_ref), channel_id=1, source_target_pairs={{0,2},{1,3},{2,0},{3,1},{4,6},{5,7},{6,4},{7,5},{8,10},{9,11},{10,... | collective-permute-start | bytes 393224 | tf_op jit(solution)/shard_map/ppermute | solution.py:290
  34.9 1.4 %collective-permute-start.5 = (f32[192,128]{1,0:T(8,128)S(1)}, f32[192,128]{1,0:T(8,128)S(1)}, u32[]{:S(2)}, u32[]{:S(2)}) collective-permute-start(f32[192,128]{1,0:T(8,128)S(1)} %shard_map.127), channel_id=1, source_target_pairs={{0,1},{1,0},{2,3},{3,2},{4,5},{5,4},{6,7},{7,6},{8,9},{9,8},{10,11... | collective-permute-start | bytes 294920 | tf_op jit(solution)/shard_map/ppermute | solution.py:290
  36.3 4.9 %collective-permute-start.6 = (f32[192,128]{1,0:T(8,128)S(1)}, f32[192,128]{1,0:T(8,128)S(1)}, u32[]{:S(2)}, u32[]{:S(2)}) collective-permute-start(f32[192,128]{1,0:T(8,128)S(1)} %add.3.mine_ref), channel_id=1, source_target_pairs={{0,2},{1,3},{2,0},{3,1},{4,6},{5,7},{6,4},{7,5},{8,10},{9,11},{10,... | collective-permute-start | bytes 294920 | tf_op jit(solution)/shard_map/ppermute | solution.py:290

commit v8 on v7

--- a/solution.py
+++ b/solution.py
@@ -10,8 +10,7 @@
 SEQS = 2
 LEN = 128
 BLOCK = 1152
-CHIP_BLOCK = 768
-AHEAD = 2
+CHIP_BLOCK = 512
 PARTS = 2
 MIB = 1 << 20
 ANY = pl.BlockSpec(memory_space=pl.ANY)
@@ -90,7 +89,7 @@
         copy.wait()
 
 
-def stream(step, following, blocks, head, w_v, next_head, sems, body):
+def stream(step, following, ahead, blocks, head, w_v, next_head, sems, body, body_of_head=None):
     heads = head.shape[0]
     slots = w_v.shape[0]
 
@@ -113,21 +112,21 @@
             def _():
                 start(next_copies(j - blocks))
 
-    for j in range(heads, AHEAD):
+    for j in range(heads, ahead):
         start(copies(j))
 
     @pl.loop(0, heads)
     def _(i):
-        begin(i + AHEAD)
-        body(i, head.at[i])
+        begin(i + ahead)
+        (body_of_head or body)(i, head.at[i])
 
     @pl.loop(heads, blocks)
     def _(i):
-        begin(i + AHEAD)
+        begin(i + ahead)
         wait(copies(i))
         body(i, w_v.at[(i - heads) % slots])
 
-    for j in range(blocks + AHEAD, last):
+    for j in range(blocks + ahead, last):
         start(next_copies(j - blocks))
     for j in range(last - blocks):
         wait(next_copies(j))
@@ -156,22 +155,17 @@
 
     start(gate_up(0))
     start(small[:1])
-    start(gate_up(1))
+    for i in range(1, turns):
+        start(gate_up(i))
     start(small[1:])
+    for i in range(heads):
+        start(following.copies(i, head_ref.at[i], w_sems.at[i]))
     ph_ref[...] = jnp.zeros_like(ph_ref)
     wait(gate_up(0))
     wait(small[:1])
 
     @pl.loop(0, turns)
     def _(i):
-        @pl.when(i + 2 < turns)
-        def _():
-            start(gate_up(i + 2))
-
-        @pl.when(i < heads)
-        def _():
-            start(following.copies(i, head_ref.at[i], w_sems.at[i]))
-
         @pl.when(i > 0)
         def _():
             wait(gate_up(i))
@@ -205,7 +199,7 @@
     def body(i, weights):
         acc_ref[step.units(i)] = product(weights[...], og_v[...])
 
-    stream(step, following, acc_ref.shape[0] // step.block, head_ref, w_v, next_ref, sems, body)
+    stream(step, following, 4, acc_ref.shape[0] // step.block, head_ref, w_v, next_ref, sems, body)
 
 
 def add_kernel(bits, following_bits, acc_in, og_ref, head_ref, w_hbm, acc_ref, next_ref, og_v, w_v, sems):
@@ -220,11 +214,11 @@
         at = step.units(i)
         acc_ref[at] = acc_in[at] + product(weights[...], og_v[...])
 
-    stream(step, following, acc_in.shape[0] // block, head_ref, w_v, next_ref, sems, body)
+    stream(step, following, 3, acc_in.shape[0] // block, head_ref, w_v, next_ref, sems, body)
 
 
 def far_kernel(bits, acc_ref, og_ref, head_ref, w_hbm, a_ref, b_ref, gf_hbm, uf_hbm, gate_ref, up_ref,
-               og_v, w_v, gf_ref, uf_ref, sems, factor_sems):
+               og_v, w_v, gf_ref, uf_ref, hidden_v, sems, factor_sems):
     _, block, width = w_v.shape
     step = Step(lax.axis_index("tensor") ^ bits, width, block, w_hbm)
     factors = [
@@ -235,18 +229,27 @@
     up_ref[...] = jnp.zeros_like(up_ref)
     og_v[...] = og_ref[...].T
 
-    def body(i, weights):
+    blocks = acc_ref.shape[0] // block
+
+    def multiply(i, weights):
+        hidden_v[i % 2] = acc_ref[step.units(i)] + product(weights[...], og_v[...])
+
+    def use(i):
         at = step.units(i)
-        hidden_grad = acc_ref[at] + product(weights[...], og_v[...])
-
-        @pl.when(i == 0)
-        def _():
-            wait(factors)
-
+        hidden_grad = hidden_v[i % 2]
         gate_ref[...] += product(gf_ref[:, at], (hidden_grad * a_ref[at]).astype(BF16))
         up_ref[...] += product(uf_ref[:, at], (hidden_grad * b_ref[at]).astype(BF16))
 
-    stream(step, None, acc_ref.shape[0] // block, head_ref, w_v, None, sems, body)
+    def body(i, weights):
+        use(i - 1)
+        multiply(i, weights)
+
+    def body_of_head(i, weights):
+        multiply(i, weights)
+        wait(factors)
+
+    stream(step, None, 3, blocks, head_ref, w_v, None, sems, body, body_of_head)
+    use(blocks - 1)
 
 
 def after_kernel(array_ref, token_ref, same_ref):
@@ -352,7 +355,7 @@
         chip_features_kernel,
         (held, blocks(2)),
         [VMEM] * 3 + [ANY],
-        [pltpu.VMEM((2 * width, tokens), BF16), chip_blocks(AHEAD + 1), dma((units // CHIP_BLOCK + 2, PARTS))],
+        [pltpu.VMEM((2 * width, tokens), BF16), chip_blocks(5), dma((units // CHIP_BLOCK + 2, PARTS))],
         16,
         2 * per_product,
         4 * units * width,
@@ -371,7 +374,7 @@
         functools.partial(add_kernel, 2, 3),
         (held, blocks(1)),
         [VMEM] * 3 + [ANY],
-        [turned, blocks(AHEAD), dma((turns + 1, PARTS))],
+        [turned, blocks(2), dma((turns + 1, PARTS))],
         10,
         per_product,
         2 * units * width,
@@ -384,7 +387,7 @@
         functools.partial(far_kernel, 3),
         (narrow, narrow),
         [VMEM] * 3 + [ANY] + [VMEM] * 2 + [ANY] * 2,
-        [turned, blocks(AHEAD + 1), factor, factor, dma((turns, PARTS)), dma((2,))],
+        [turned, blocks(3), factor, factor, pltpu.VMEM((2, BLOCK, tokens), F32), dma((turns, PARTS)), dma((2,))],
         16,
         per_product,
         2 * units * width,

time: 42.1 us -> 41.1 us (0.976)
  Pallas kernels: 29.9 us -> 26.9 us
  waiting for transfers between devices: 5.36 us -> 7.47 us
    ppermute x7, waiting for transfers between devices: 5.36 us -> 7.47 us  [swap(): return lax.ppermute(array, 'tensor', [(i, i ^ bits) for i in range(4)])]
    pallas_call x1, Pallas kernels: 6.56 us -> 5.35 us  [fast(): call(elementwise_kernel, (held, held, narrow, pltpu.VMEM((2 * rank, token...]
    pallas_call x1, Pallas kernels: 5.04 us -> 4.1 us  [fast(): call(functools.partial(add_kernel, 2, 3), (held, blocks(1)), [VMEM] * 3 +...]
    pallas_call x1, Pallas kernels: 9.38 us -> 8.53 us  [fast(): call(chip_features_kernel, (held, blocks(2)), [VMEM] * 3 + [ANY], [pltpu....]
  transfers between devices with their start and end apart: 7 -> 7, of which waited for: 2 -> 3; matrix products, arithmetic and copies ran while one was open for 0% -> 0% of each run, Pallas kernels for 68% -> 63%
where the time goes in v8:
time: 41.1 us; the launch traced here: 40.9 us
  Pallas kernels  26.9 us (65%)
  waiting for transfers between devices  7.47 us (18%)
  starting transfers between devices  5.86 us (14%)
  between operations  0.72 us (2%)
    pallas_call x1, Pallas kernels, fast(): call(chip_features_kernel, (held, blocks(2)), [VMEM] * 3 + [ANY], [pltpu....  8.53 us
    pallas_call x1, Pallas kernels, fast(): call(functools.partial(far_kernel, 3), (narrow, narrow), [VMEM] * 3 + [AN...  7.64 us
    ppermute x7, waiting for transfers between devices, swap(): return lax.ppermute(array, 'tensor', [(i, i ^ bits) for i in range(4)])  7.47 us
    ppermute x7, starting transfers between devices, swap(): return lax.ppermute(array, 'tensor', [(i, i ^ bits) for i in range(4)])  5.86 us
    pallas_call x1, Pallas kernels, fast(): call(elementwise_kernel, (held, held, narrow, pltpu.VMEM((2 * rank, token...  5.35 us
    pallas_call x1, Pallas kernels, fast(): call(functools.partial(add_kernel, 2, 3), (held, blocks(1)), [VMEM] * 3 +...  4.1 us
  transfers between devices with their start and end apart: 7, of which 3 were waited for; matrix products, arithmetic and copies ran while one was open for 0% of the time, Pallas kernels for 63%

profile of v8, /device:TPU:0, one launch (start us, length us, event | category | flops | bytes accessed | tf_op | source)
XLA Modules:
  0.0 40.9 jit_solution(14413030368037804782)
XLA Ops:
  0.6 0.5 %collective-permute-start.1 = (bf16[256,1280]{1,0:T(8,128)(2,1)}, bf16[256,1280]{1,0:T(8,128)(2,1)S(1)}, u32[]{:S(2)}, u32[]{:S(2)}) collective-permute-start(bf16[256,1280]{1,0:T(8,128)(2,1)} %og_hbm.1), channel_id=1, source_target_pairs={{0,1},{1,0},{2,3},{3,2},{4,5},{5,4},{6,7},{7,6},{8,9},{9,8},{10,11... | collective-permute-start | bytes 1966088 | tf_op jit(solution)/shard_map/ppermute | solution.py:293
  1.2 2.6 %collective-permute-start.2 = (bf16[256,1280]{1,0:T(8,128)(2,1)}, bf16[256,1280]{1,0:T(8,128)(2,1)S(1)}, u32[]{:S(2)}, u32[]{:S(2)}) collective-permute-start(bf16[256,1280]{1,0:T(8,128)(2,1)} %og_hbm.1), channel_id=1, source_target_pairs={{0,2},{1,3},{2,0},{3,1},{4,6},{5,7},{6,4},{7,5},{8,10},{9,11},{10,... | collective-permute-start | bytes 1966088 | tf_op jit(solution)/shard_map/ppermute | solution.py:293
  3.7 5.4 %shard_map.121 = (f32[4608,256]{1,0:T(8,128)S(1)}, f32[4608,256]{1,0:T(8,128)S(1)}, f32[64,256]{1,0:T(8,128)S(1)}, f32[128,256]{1,0:T(8,128)S(1)}, bf16[2,512,25...) custom-call(bf16[256,1280]{1,0:T(8,128)(2,1)} %x_hbm.1, bf16[256,1280]{1,0:T(8,128)(2,1)} %og_hbm.1, ...), custom_call_target="tpu_custom_call" | custom-call | flops 754974720 | bytes 4718592 | tf_op jit(solution)/shard_map/pallas_call | solution.py:323
  9.1 0.0 collective-permute-done.1.mate_ref
  9.1 8.5 %shard_map.122 = (f32[4608,256]{1,0:T(8,128)S(1)}, bf16[2,1152,1280]{2,1,0:T(8,128)(2,1)S(1)}) custom-call(bf16[1280,256]{1,0:T(8,128)(2,1)S(1)} %get-tuple-element.16.own_ref, bf16[256,1280]{1,0:T(8,128)(2,1)S(1)} %collective-permute-done.1.mate_ref, bf16[2,512,2560]{2,1,0:T(8,128)(2,1)S(1)} %get-tuple-element.17.head_ref, bf16[4608,5120]{1,0:T(8,128)(2,1)} %w_hbm.7), custom_call_target="tpu_custom_call" | custom-call | flops 6039797760 | bytes 23592960 | tf_op jit(solution)/shard_map/pallas_call | solution.py:354
  17.6 1.6 %collective-permute-done.2.array_ref = bf16[256,1280]{1,0:T(8,128)(2,1)S(1)} collective-permute-done((bf16[256,1280]{1,0:T(8,128)(2,1)}, bf16[256,1280]{1,0:T(8,128)(2,1)S(1)}, u32[]{:S(2)}, u32[]{:S(2)}) %collective-permute-start.2) | collective-permute-done | bytes 655392 | tf_op jit(solution)/shard_map/ppermute | solution.py:293
  19.3 0.0 collective-permute-start.4
  19.3 0.5 %collective-permute-start = (f32[128,256]{1,0:T(8,128)S(1)}, f32[128,256]{1,0:T(8,128)S(1)}, u32[]{:S(2)}, u32[]{:S(2)}) collective-permute-start(f32[128,256]{1,0:T(8,128)S(1)} %get-tuple-element.15.mine_ref), channel_id=1, source_target_pairs={{0,1},{1,0},{2,3},{3,2},{4,5},{5,4},{6,7},{7,6},{8,9},{9,8},{10,11... | collective-permute-start | bytes 393224 | tf_op jit(solution)/shard_map/ppermute | solution.py:293
  19.8 4.1 %shard_map.124 = (f32[4608,256]{1,0:T(8,128)S(1)}, bf16[1,1152,1280]{2,1,0:T(8,128)(2,1)S(1)}) custom-call(f32[4608,256]{1,0:T(8,128)S(1)} %get-tuple-element.18.acc_in, bf16[256,1280]{1,0:T(8,128)(2,1)S(1)} %shard_map.123.og_ref, bf16[2,1152,1280]{2,1,0:T(8,128)(2,1)S(1)} %get-tuple-element.19.token_ref.head_ref, ...), custom_call_target="tpu_custom_call", output_to_operand_aliasing={{0}: (0, {})} | custom-call | flops 3019898880 | bytes 11796480 | tf_op jit(solution)/shard_map/pallas_call | solution.py:373
  23.9 0.0 collective-permute-done.theirs_ref
  23.9 1.8 %collective-permute-start.3 = (f32[128,256]{1,0:T(8,128)S(1)}, f32[128,256]{1,0:T(8,128)S(1)}, u32[]{:S(2)}, u32[]{:S(2)}) collective-permute-start(f32[128,256]{1,0:T(8,128)S(1)} %shard_map.125.chip_ref), channel_id=1, source_target_pairs={{0,2},{1,3},{2,0},{3,1},{4,6},{5,7},{6,4},{7,5},{8,10},{9,11},{10,... | collective-permute-start | bytes 393224 | tf_op jit(solution)/shard_map/ppermute | solution.py:293
  25.7 0.0 collective-permute-done.4.og_ref
  25.7 7.6 %shard_map.126 = (f32[64,256]{1,0:T(8,128)S(1)}, f32[64,256]{1,0:T(8,128)S(1)}) custom-call(f32[4608,256]{1,0:T(8,128)S(1)} %get-tuple-element.21.acc_ref, bf16[256,1280]{1,0:T(8,128)(2,1)S(1)} %collective-permute-done.4.og_ref, bf16[1,1152,1280]{2,1,0:T(8,128)(2,1)S(1)} %get-tuple-element.20.token_ref.head_ref, bf16[4608,5120]{1,0:T(8,128)(2,1)} %w_hbm.7, ...), custom_call_target="tpu_custom_call" | custom-call | flops 3019898880 | bytes 11796480 | tf_op jit(solution)/shard_map/pallas_call | solution.py:386
  33.4 0.0 collective-permute-done.3.other_ref
  33.4 0.5 %shard_map.127 = f32[192,128]{1,0:T(8,128)S(1)} custom-call(f32[128,256]{1,0:T(8,128)S(1)} %shard_map.125.chip_ref, f32[128,256]{1,0:T(8,128)S(1)} %collective-permute-done.3.other_ref, f32[64,256]{1,0:T(8,128)S(1)} %get-tuple-element.24.gate_ref, f32[64,256]{1,0:T(8,128)S(1)} %get-tuple-element.25.up_ref, f32[64,256]{1,0:T(8,128)S(1)} %get-tuple-element.26.ph_ref), custom_call_target="tpu_custom_call" | custom-call | tf_op jit(solution)/shard_map/pallas_call | solution.py:395
  33.9 0.1 collective-permute-start.5
  34.0 1.3 %collective-permute-done.5 = f32[192,128]{1,0:T(8,128)S(1)} collective-permute-done((f32[192,128]{1,0:T(8,128)S(1)}, f32[192,128]{1,0:T(8,128)S(1)}, u32[]{:S(2)}, u32[]{:S(2)}) %collective-permute-start.5) | collective-permute-done | bytes 98336 | tf_op jit(solution)/shard_map/ppermute | solution.py:293
  35.3 0.4 collective-permute-start.6
  35.7 4.5 %collective-permute-done.6.theirs_ref = f32[192,128]{1,0:T(8,128)S(1)} collective-permute-done((f32[192,128]{1,0:T(8,128)S(1)}, f32[192,128]{1,0:T(8,128)S(1)}, u32[]{:S(2)}, u32[]{:S(2)}) %collective-permute-start.6) | collective-permute-done | bytes 98336 | tf_op jit(solution)/shard_map/ppermute | solution.py:293
  40.2 0.7 %shard_map.128 = (f32[2,64,64]{2,1,0:T(8,128)}, f32[2,64,64]{2,1,0:T(8,128)}, f32[2,64,64]{2,1,0:T(8,128)}) custom-call(f32[192,128]{1,0:T(8,128)S(1)} %add.3.mine_ref, f32[192,128]{1,0:T(8,128)S(1)} %collective-permute-done.6.theirs_ref), custom_call_target="tpu_custom_call" | custom-call | tf_op jit(solution)/shard_map/pallas_call | solution.py:400
  (3 shorter events, 0.0 us)
Async XLA Ops:
  0.6 8.4 %collective-permute-start.1 = (bf16[256,1280]{1,0:T(8,128)(2,1)}, bf16[256,1280]{1,0:T(8,128)(2,1)S(1)}, u32[]{:S(2)}, u32[]{:S(2)}) collective-permute-start(bf16[256,1280]{1,0:T(8,128)(2,1)} %og_hbm.1), channel_id=1, source_target_pairs={{0,1},{1,0},{2,3},{3,2},{4,5},{5,4},{6,7},{7,6},{8,9},{9,8},{10,11... | collective-permute-start | bytes 1966088 | tf_op jit(solution)/shard_map/ppermute | solution.py:293
  1.2 18.1 %collective-permute-start.2 = (bf16[256,1280]{1,0:T(8,128)(2,1)}, bf16[256,1280]{1,0:T(8,128)(2,1)S(1)}, u32[]{:S(2)}, u32[]{:S(2)}) collective-permute-start(bf16[256,1280]{1,0:T(8,128)(2,1)} %og_hbm.1), channel_id=1, source_target_pairs={{0,2},{1,3},{2,0},{3,1},{4,6},{5,7},{6,4},{7,5},{8,10},{9,11},{10,... | collective-permute-start | bytes 1966088 | tf_op jit(solution)/shard_map/ppermute | solution.py:293
  19.3 6.5 %collective-permute-start.4 = (bf16[256,1280]{1,0:T(8,128)(2,1)S(1)}, bf16[256,1280]{1,0:T(8,128)(2,1)S(1)}, u32[]{:S(2)}, u32[]{:S(2)}) collective-permute-start(bf16[256,1280]{1,0:T(8,128)(2,1)S(1)} %shard_map.123.og_ref), channel_id=1, source_target_pairs={{0,1},{1,0},{2,3},{3,2},{4,5},{5,4},{6,7},{7,6},{8,9},{9,8},{10,11... | collective-permute-start | bytes 1966088 | tf_op jit(solution)/shard_map/ppermute | solution.py:293
  19.3 4.6 %collective-permute-start = (f32[128,256]{1,0:T(8,128)S(1)}, f32[128,256]{1,0:T(8,128)S(1)}, u32[]{:S(2)}, u32[]{:S(2)}) collective-permute-start(f32[128,256]{1,0:T(8,128)S(1)} %get-tuple-element.15.mine_ref), channel_id=1, source_target_pairs={{0,1},{1,0},{2,3},{3,2},{4,5},{5,4},{6,7},{7,6},{8,9},{9,8},{10,11... | collective-permute-start | bytes 393224 | tf_op jit(solution)/shard_map/ppermute | solution.py:293
  23.9 9.5 %collective-permute-start.3 = (f32[128,256]{1,0:T(8,128)S(1)}, f32[128,256]{1,0:T(8,128)S(1)}, u32[]{:S(2)}, u32[]{:S(2)}) collective-permute-start(f32[128,256]{1,0:T(8,128)S(1)} %shard_map.125.chip_ref), channel_id=1, source_target_pairs={{0,2},{1,3},{2,0},{3,1},{4,6},{5,7},{6,4},{7,5},{8,10},{9,11},{10,... | collective-permute-start | bytes 393224 | tf_op jit(solution)/shard_map/ppermute | solution.py:293
  33.9 1.4 %collective-permute-start.5 = (f32[192,128]{1,0:T(8,128)S(1)}, f32[192,128]{1,0:T(8,128)S(1)}, u32[]{:S(2)}, u32[]{:S(2)}) collective-permute-start(f32[192,128]{1,0:T(8,128)S(1)} %shard_map.127), channel_id=1, source_target_pairs={{0,1},{1,0},{2,3},{3,2},{4,5},{5,4},{6,7},{7,6},{8,9},{9,8},{10,11... | collective-permute-start | bytes 294920 | tf_op jit(solution)/shard_map/ppermute | solution.py:293
  35.3 4.9 %collective-permute-start.6 = (f32[192,128]{1,0:T(8,128)S(1)}, f32[192,128]{1,0:T(8,128)S(1)}, u32[]{:S(2)}, u32[]{:S(2)}) collective-permute-start(f32[192,128]{1,0:T(8,128)S(1)} %add.3.mine_ref), channel_id=1, source_target_pairs={{0,2},{1,3},{2,0},{3,1},{4,6},{5,7},{6,4},{7,5},{8,10},{9,11},{10,... | collective-permute-start | bytes 294920 | tf_op jit(solution)/shard_map/ppermute | solution.py:293

commit v9 on v8

--- a/solution.py
+++ b/solution.py
@@ -11,6 +11,7 @@
 LEN = 128
 BLOCK = 1152
 CHIP_BLOCK = 512
+FIRST = 512
 PARTS = 2
 MIB = 1 << 20
 ANY = pl.BlockSpec(memory_space=pl.ANY)
@@ -60,14 +61,14 @@
 
 
 class Step:
-    def __init__(self, owner, width, block, w_hbm):
-        self.owner, self.width, self.block, self.w_hbm = owner, width, block, w_hbm
+    def __init__(self, column, width, block, w_hbm):
+        self.column, self.width, self.block, self.w_hbm = column, width, block, w_hbm
 
     def units(self, i):
         return pl.ds(pl.multiple_of(i * self.block, self.block), self.block)
 
     def copies(self, i, dst, sems):
-        columns = pl.ds(pl.multiple_of(self.owner * self.width, 128), self.width)
+        columns = pl.ds(pl.multiple_of(self.column, 128), self.width)
         part = self.block // PARTS
         return [
             pltpu.make_async_copy(
@@ -89,9 +90,9 @@
         copy.wait()
 
 
-def stream(step, following, ahead, blocks, head, w_v, next_head, sems, body, body_of_head=None):
+def stream(step, following, ahead, blocks, head, w_v, next_head, sems, body):
     heads = head.shape[0]
-    slots = w_v.shape[0]
+    slots = 1 if w_v is None else w_v.shape[0]
 
     def copies(j):
         return step.copies(j, w_v.at[(j - heads) % slots], sems.at[j])
@@ -118,7 +119,7 @@
     @pl.loop(0, heads)
     def _(i):
         begin(i + ahead)
-        (body_of_head or body)(i, head.at[i])
+        body(i, head.at[i])
 
     @pl.loop(heads, blocks)
     def _(i):
@@ -132,9 +133,18 @@
         wait(next_copies(j))
 
 
-def elementwise_kernel(x_hbm, og_hbm, gate_hbm, up_hbm, w_hbm, xf_hbm, yf_hbm, hf_hbm,
-                       a_ref, b_ref, ph_ref, pq_ref, head_ref, own_ref,
-                       x_v, og_v, gate_v, up_v, xf_v, yf_v, hf_v, sems, gate_sems, up_sems, w_sems):
+def entry_kernel(og_hbm, own_ref, first_ref, second_ref, og_v, sem):
+    copy = pltpu.make_async_copy(og_hbm, og_v, sem)
+    copy.start()
+    copy.wait()
+    own_ref[...] = og_v[...].T
+    first_ref[...] = own_ref[:FIRST]
+    second_ref[...] = own_ref[FIRST:]
+
+
+def elementwise_kernel(x_hbm, own_ref, gate_hbm, up_hbm, w_hbm, xf_hbm, yf_hbm, hf_hbm,
+                       a_ref, b_ref, ph_ref, pq_ref, head_ref,
+                       x_v, gate_v, up_v, xf_v, yf_v, hf_v, sems, gate_sems, up_sems, w_sems):
     units = a_ref.shape[0]
     rank = ph_ref.shape[0]
     turns = units // BLOCK
@@ -148,9 +158,9 @@
             pltpu.make_async_copy(up_hbm.at[:, at(i)], up_v.at[i], up_sems.at[i]),
         ]
 
-    pairs = ((hf_hbm, hf_v), (og_hbm, og_v), (x_hbm, x_v), (xf_hbm, xf_v), (yf_hbm, yf_v))
+    pairs = ((hf_hbm, hf_v), (x_hbm, x_v), (xf_hbm, xf_v), (yf_hbm, yf_v))
     small = [pltpu.make_async_copy(src, dst, sems.at[i]) for i, (src, dst) in enumerate(pairs)]
-    following = Step(lax.axis_index("tensor") // 2, head_ref.shape[2], head_ref.shape[1], w_hbm)
+    following = Step(lax.axis_index("tensor") // 2 * head_ref.shape[2], head_ref.shape[2], head_ref.shape[1], w_hbm)
     heads = head_ref.shape[0]
 
     start(gate_up(0))
@@ -180,7 +190,6 @@
 
     wait(small[1:])
     pq_ref[:rank] = rows_by_rows(xf_v[...], x_v[...])
-    own_ref[...] = og_v[...].T
     pq_ref[rank:] = product(yf_v[...], own_ref[...])
     for i in range(heads):
         wait(following.copies(i, head_ref.at[i], w_sems.at[i]))
@@ -189,12 +198,12 @@
 def chip_features_kernel(own_ref, mate_ref, head_ref, w_hbm, acc_ref, next_ref, og_v, w_v, sems):
     me = lax.axis_index("tensor")
     width = own_ref.shape[0]
-    step = Step(me // 2, 2 * width, w_v.shape[1], w_hbm)
-    following = Step(me ^ 2, width, next_ref.shape[1], w_hbm)
+    step = Step(me // 2 * 2 * width, 2 * width, w_v.shape[1], w_hbm)
+    following = Step((me ^ 2) * width, next_ref.shape[2], next_ref.shape[1], w_hbm)
     mine = pl.ds(pl.multiple_of(me % 2 * width, 128), width)
     theirs = pl.ds(pl.multiple_of((me + 1) % 2 * width, 128), width)
     og_v[mine] = own_ref[...]
-    og_v[theirs] = mate_ref[...].T
+    og_v[theirs] = mate_ref[...]
 
     def body(i, weights):
         acc_ref[step.units(i)] = product(weights[...], og_v[...])
@@ -202,54 +211,38 @@
     stream(step, following, 4, acc_ref.shape[0] // step.block, head_ref, w_v, next_ref, sems, body)
 
 
-def add_kernel(bits, following_bits, acc_in, og_ref, head_ref, w_hbm, acc_ref, next_ref, og_v, w_v, sems):
+def add_kernel(step_at, following_at, per_device, acc_in, og_ref, head_ref, w_hbm, acc_ref, next_ref, w_v, sems):
     me = lax.axis_index("tensor")
-    _, block, width = w_v.shape
-    step = Step(me ^ bits, width, block, w_hbm)
-    following = Step(me ^ following_bits, width, block, w_hbm)
-
-    og_v[...] = og_ref[...].T
+    block, width = head_ref.shape[1:]
+    step = Step((me ^ step_at[0]) * per_device + step_at[1], width, block, w_hbm)
+    following = Step((me ^ following_at[0]) * per_device + following_at[1], next_ref.shape[2], next_ref.shape[1], w_hbm)
 
     def body(i, weights):
         at = step.units(i)
-        acc_ref[at] = acc_in[at] + product(weights[...], og_v[...])
-
-    stream(step, following, 3, acc_in.shape[0] // block, head_ref, w_v, next_ref, sems, body)
-
-
-def far_kernel(bits, acc_ref, og_ref, head_ref, w_hbm, a_ref, b_ref, gf_hbm, uf_hbm, gate_ref, up_ref,
-               og_v, w_v, gf_ref, uf_ref, hidden_v, sems, factor_sems):
-    _, block, width = w_v.shape
-    step = Step(lax.axis_index("tensor") ^ bits, width, block, w_hbm)
+        acc_ref[at] = acc_in[at] + product(weights[...], og_ref[...])
+
+    stream(step, following, 4, acc_in.shape[0] // block, head_ref, w_v, next_ref, sems, body)
+
+
+def last_kernel(step_at, per_device, acc_ref, og_ref, head_ref, w_hbm, a_ref, b_ref, gf_hbm, uf_hbm, gate_ref, up_ref,
+                w_v, gf_ref, uf_ref, d_gate_v, d_up_v, sems, factor_sems):
+    block, width = head_ref.shape[1:]
+    step = Step((lax.axis_index("tensor") ^ step_at[0]) * per_device + step_at[1], width, block, w_hbm)
     factors = [
         pltpu.make_async_copy(src, dst, factor_sems.at[k]) for k, (src, dst) in enumerate(((gf_hbm, gf_ref), (uf_hbm, uf_ref)))
     ]
     start(factors)
-    gate_ref[...] = jnp.zeros_like(gate_ref)
-    up_ref[...] = jnp.zeros_like(up_ref)
-    og_v[...] = og_ref[...].T
-
-    blocks = acc_ref.shape[0] // block
-
-    def multiply(i, weights):
-        hidden_v[i % 2] = acc_ref[step.units(i)] + product(weights[...], og_v[...])
-
-    def use(i):
+
+    def body(i, weights):
         at = step.units(i)
-        hidden_grad = hidden_v[i % 2]
-        gate_ref[...] += product(gf_ref[:, at], (hidden_grad * a_ref[at]).astype(BF16))
-        up_ref[...] += product(uf_ref[:, at], (hidden_grad * b_ref[at]).astype(BF16))
-
-    def body(i, weights):
-        use(i - 1)
-        multiply(i, weights)
-
-    def body_of_head(i, weights):
-        multiply(i, weights)
-        wait(factors)
-
-    stream(step, None, 3, blocks, head_ref, w_v, None, sems, body, body_of_head)
-    use(blocks - 1)
+        hidden_grad = acc_ref[at] + product(weights[...], og_ref[...])
+        d_gate_v[at] = (hidden_grad * a_ref[at]).astype(BF16)
+        d_up_v[at] = (hidden_grad * b_ref[at]).astype(BF16)
+
+    stream(step, None, 4, acc_ref.shape[0] // block, head_ref, w_v, None, sems, body)
+    wait(factors)
+    gate_ref[...] = product(gf_ref[...], d_gate_v[...])
+    up_ref[...] = product(uf_ref[...], d_up_v[...])
 
 
 def after_kernel(array_ref, token_ref, same_ref):
@@ -312,27 +305,35 @@
     turned = pltpu.VMEM((width, tokens), BF16)
     weight = in_hbm(down_weight)
 
-    def blocks(count):
-        return pltpu.VMEM((count, BLOCK, width), BF16)
+    def blocks(count, features):
+        return pltpu.VMEM((count, BLOCK, features), BF16)
 
     def chip_blocks(count):
         return pltpu.VMEM((count, CHIP_BLOCK, 2 * width), BF16)
 
-    near = swap(out_grad, 2)
-    mate = swap(out_grad, 1)
-    a, b, ph, pq, head, own = call(
+    second = width - FIRST
+    own, piece, other_piece = call(
+        entry_kernel,
+        (turned, pltpu.VMEM((FIRST, tokens), BF16), pltpu.VMEM((second, tokens), BF16)),
+        [ANY],
+        [pltpu.VMEM((tokens, width), BF16), dma],
+        4,
+    )(in_hbm(out_grad))
+    near_first = swap(piece, 2)
+    near_second = swap(other_piece, 2)
+    mate = swap(own, 1)
+    a, b, ph, pq, head = call(
         elementwise_kernel,
-        (held, held, narrow, pltpu.VMEM((2 * rank, tokens), F32), chip_blocks(2), turned),
-        [ANY] * 8,
+        (held, held, narrow, pltpu.VMEM((2 * rank, tokens), F32), chip_blocks(2)),
+        [ANY, VMEM] + [ANY] * 6,
         [
-            pltpu.VMEM((tokens, width), BF16),
             pltpu.VMEM((tokens, width), BF16),
             pltpu.VMEM((turns, tokens, BLOCK), BF16),
             pltpu.VMEM((turns, tokens, BLOCK), BF16),
             pltpu.VMEM((rank, width), BF16),
             pltpu.VMEM((rank, width), BF16),
             pltpu.VMEM((rank, units), BF16),
-            dma((5,)),
+            dma((4,)),
             dma((turns,)),
             dma((turns,)),
             dma((2, PARTS)),
@@ -342,7 +343,7 @@
         4 * units * tokens,
     )(
         in_hbm(x_in),
-        in_hbm(out_grad),
+        own,
         in_hbm(gate_pre),
         in_hbm(up_pre),
         weight,
@@ -353,45 +354,57 @@
     pq_mate = swap(pq, 1)
     acc, head = call(
         chip_features_kernel,
-        (held, blocks(2)),
+        (held, blocks(4, FIRST)),
         [VMEM] * 3 + [ANY],
-        [pltpu.VMEM((2 * width, tokens), BF16), chip_blocks(5), dma((units // CHIP_BLOCK + 2, PARTS))],
+        [pltpu.VMEM((2 * width, tokens), BF16), chip_blocks(5), dma((units // CHIP_BLOCK + 4, PARTS))],
         16,
         2 * per_product,
         4 * units * width,
     )(own, mate, head, weight)
 
-    near = pl.pallas_call(
-        after_kernel,
-        out_shape=pltpu.VMEM(near.shape, near.dtype),
-        in_specs=[ANY, ANY],
-        out_specs=ANY,
-        input_output_aliases={0: 0},
-        compiler_params=pltpu.CompilerParams(vmem_limit_bytes=MIB),
-    )(near, head)
-    far = swap(near, 1)
-    acc, head = call(
-        functools.partial(add_kernel, 2, 3),
-        (held, blocks(1)),
-        [VMEM] * 3 + [ANY],
-        [turned, blocks(2), dma((turns + 1, PARTS))],
-        10,
-        per_product,
-        2 * units * width,
-        input_output_aliases={0: 0},
-    )(acc, near, head, weight)
+    def after(array, token):
+        return pl.pallas_call(
+            after_kernel,
+            out_shape=pltpu.VMEM(array.shape, array.dtype),
+            in_specs=[ANY, ANY],
+            out_specs=ANY,
+            input_output_aliases={0: 0},
+            compiler_params=pltpu.CompilerParams(vmem_limit_bytes=MIB),
+        )(array, token)
+
+    def add(step_at, following_at, features, acc, head, next_head):
+        count, size = head.shape[0], features.shape[0]
+        return call(
+            functools.partial(add_kernel, step_at, following_at, width),
+            (held, next_head),
+            [VMEM] * 3 + [ANY],
+            [blocks(max(turns - count, 1), size), dma((turns + next_head.shape[0], PARTS))],
+            8,
+            2 * tokens * size * units,
+            2 * units * size,
+            input_output_aliases={0: 0},
+        )(acc, features, head, weight)
+
+    near_first = after(near_first, head)
+    far_first = swap(near_first, 1)
+    acc, head = add((2, 0), (3, 0), near_first, acc, head, blocks(2, FIRST))
+    acc, head = add((3, 0), (2, FIRST), far_first, acc, head, blocks(3, second))
+    near_second = after(near_second, head)
+    far_second = swap(near_second, 1)
+    acc, head = add((2, FIRST), (3, FIRST), near_second, acc, head, blocks(2, second))
     chip = call(chip_kernel, pltpu.VMEM(pq.shape, F32), [VMEM, VMEM, ANY], [], 1)(pq, pq_mate, head)
     chip_across = swap(chip, 2)
     factor = pltpu.VMEM((rank, units), BF16)
+    kept = pltpu.VMEM((units, tokens), BF16)
     q_gate, q_up = call(
-        functools.partial(far_kernel, 3),
+        functools.partial(last_kernel, (3, FIRST), width),
         (narrow, narrow),
         [VMEM] * 3 + [ANY] + [VMEM] * 2 + [ANY] * 2,
-        [turned, blocks(3), factor, factor, pltpu.VMEM((2, BLOCK, tokens), F32), dma((turns, PARTS)), dma((2,))],
-        16,
-        per_product,
-        2 * units * width,
-    )(acc, far, head, weight, a, b, in_hbm(gate_factor.T), in_hbm(up_factor.T))
+        [blocks(turns - 2, second), factor, factor, kept, kept, dma((turns, PARTS)), dma((2,))],
+        14,
+        2 * tokens * second * units,
+        2 * units * second,
+    )(acc, far_second, head, weight, a, b, in_hbm(gate_factor.T), in_hbm(up_factor.T))
     share = call(gradients_kernel, pltpu.VMEM(((SEQS + 1) * rank, 2 * rank), F32), [VMEM] * 5, [], 4)(
         chip, chip_across, q_gate, q_up, ph
     )
@@ -407,9 +420,10 @@
             mesh.shape["tensor"] == 4
             and (tokens, rank) == (SEQS * LEN, LEN // 2)
             and width % 128 == 0
+            and width > FIRST
             and units % BLOCK == 0
             and units % CHIP_BLOCK == 0
-            and units // BLOCK > 3
+            and units // BLOCK == 4
         )
         return tuple((fast if fits else plain)(*arrays))
 

time: 41.1 us -> 42.7 us (1.039)
  waiting for transfers between devices: 7.47 us -> 4.33 us
  Pallas kernels: 26.9 us -> 29.3 us
  starting transfers between devices: 5.86 us -> 8.01 us
    ppermute x7 -> x9, waiting for transfers between devices: 7.47 us -> 4.33 us  [swap(): return lax.ppermute(array, 'tensor', [(i, i ^ bits) for i in range(4)])]
    pallas_call x4 -> x8, Pallas kernels: 20.3 us -> 22.9 us  [the longest x3 8.86 us: add(): call(functools.partial(add_kernel, step_at, following_at, width), (held,...]
    ppermute x7 -> x9, starting transfers between devices: 5.86 us -> 8.01 us  [swap(): return lax.ppermute(array, 'tensor', [(i, i ^ bits) for i in range(4)])]
  transfers between devices with their start and end apart: 7 -> 9, of which waited for: 3 -> 2; matrix products, arithmetic and copies ran while one was open for 0% -> 0% of each run, Pallas kernels for 63% -> 63%
where the time goes in v9:
time: 42.7 us; the launch traced here: 42.5 us
  Pallas kernels  29.3 us (69%)
  starting transfers between devices  8.01 us (19%)
  waiting for transfers between devices  4.33 us (10%)
  between operations  0.77 us (2%)
    pallas_call x3, Pallas kernels, add(): call(functools.partial(add_kernel, step_at, following_at, width), (held,...  8.86 us
    pallas_call x1, Pallas kernels, fast(): call(chip_features_kernel, (held, blocks(4, FIRST)), [VMEM] * 3 + [ANY],...  8.61 us
    ppermute x9, starting transfers between devices, swap(): return lax.ppermute(array, 'tensor', [(i, i ^ bits) for i in range(4)])  8.01 us
    pallas_call x1, Pallas kernels, fast(): call(elementwise_kernel, (held, held, narrow, pltpu.VMEM((2 * rank, token...  5.15 us
    ppermute x9, waiting for transfers between devices, swap(): return lax.ppermute(array, 'tensor', [(i, i ^ bits) for i in range(4)])  4.33 us
    pallas_call x1, Pallas kernels, fast(): call(functools.partial(last_kernel, (3, FIRST), width), (narrow, narrow),...  4.12 us
    pallas_call x1, Pallas kernels, fast(): call(entry_kernel, (turned, pltpu.VMEM((FIRST, tokens), BF16), pltpu.VMEM...  1.32 us
  transfers between devices with their start and end apart: 9, of which 2 were waited for; matrix products, arithmetic and copies ran while one was open for 0% of the time, Pallas kernels for 63%

profile of v9, /device:TPU:0, one launch (start us, length us, event | category | flops | bytes accessed | tf_op | source)
XLA Modules:
  0.0 42.5 jit_solution(7604095570482782433)
XLA Ops:
  0.6 1.3 %shard_map.121 = (bf16[1280,256]{1,0:T(8,128)(2,1)S(1)}, bf16[512,256]{1,0:T(8,128)(2,1)S(1)}, bf16[768,256]{1,0:T(8,128)(2,1)S(1)}) custom-call(bf16[256,1280]{1,0:T(8,128)(2,1)} %og_hbm.1), custom_call_target="tpu_custom_call" | custom-call | tf_op jit(solution)/shard_map/pallas_call | solution.py:315
  2.0 0.5 %collective-permute-start.1 = (bf16[1280,256]{1,0:T(8,128)(2,1)S(1)}, bf16[1280,256]{1,0:T(8,128)(2,1)S(1)}, u32[]{:S(2)}, u32[]{:S(2)}) collective-permute-start(bf16[1280,256]{1,0:T(8,128)(2,1)S(1)} %get-tuple-element.21.own_ref), channel_id=1, source_target_pairs={{0,1},{1,0},{2,3},{3,2},{4,5},{5,4},{6,7},{7,6},{8,9},{9,8},{10,11... | collective-permute-start | bytes 1966088 | tf_op jit(solution)/shard_map/ppermute | solution.py:286
  2.5 2.6 %collective-permute-start.2 = (bf16[512,256]{1,0:T(8,128)(2,1)S(1)}, bf16[512,256]{1,0:T(8,128)(2,1)S(1)}, u32[]{:S(2)}, u32[]{:S(2)}) collective-permute-start(bf16[512,256]{1,0:T(8,128)(2,1)S(1)} %get-tuple-element.25), channel_id=1, source_target_pairs={{0,2},{1,3},{2,0},{3,1},{4,6},{5,7},{6,4},{7,5},{8,10},{9,11},{10,... | collective-permute-start | bytes 786440 | tf_op jit(solution)/shard_map/ppermute | solution.py:286
  5.0 0.1 collective-permute-start.4
  5.1 5.2 %shard_map.122 = (f32[4608,256]{1,0:T(8,128)S(1)}, f32[4608,256]{1,0:T(8,128)S(1)}, f32[64,256]{1,0:T(8,128)S(1)}, f32[128,256]{1,0:T(8,128)S(1)}, bf16[2,512,2560]{2,1,0:T(8,128)(2,1)S(1)}) custom-call(bf16[256,1280]{1,0:T(8,128)(2,1)} %x_hbm.1, bf16[1280,256]{1,0:T(8,128)(2,1)S(1)} %get-tuple-element.21.own_ref, bf16[256,4608]{1,0:T(8,128)(2,1)} %gate_hbm.1, ...), custom_call_target="tpu_custom_call" | custom-call | flops 754974720 | bytes 4718592 | tf_op jit(solution)/shard_map/pallas_call | solution.py:325
  10.3 0.0 collective-permute-done.1.mate_ref
  10.3 8.6 %shard_map.123 = (f32[4608,256]{1,0:T(8,128)S(1)}, bf16[4,1152,512]{2,1,0:T(8,128)(2,1)S(1)}) custom-call(bf16[1280,256]{1,0:T(8,128)(2,1)S(1)} %get-tuple-element.21.own_ref, bf16[1280,256]{1,0:T(8,128)(2,1)S(1)} %collective-permute-done.1.mate_ref, bf16[2,512,2560]{2,1,0:T(8,128)(2,1)S(1)} %get-tuple-element.23.head_ref, bf16[4608,5120]{1,0:T(8,128)(2,1)} %w_hbm.11), custom_call_target="tpu_custom_call" | custom-call | flops 6039797760 | bytes 23592960 | tf_op jit(solution)/shard_map/pallas_call | solution.py:355
  18.9 0.0 collective-permute-done.2.array_ref
  18.9 0.2 collective-permute-start.3
  19.1 2.4 %shard_map.125 = (f32[4608,256]{1,0:T(8,128)S(1)}, bf16[2,1152,512]{2,1,0:T(8,128)(2,1)S(1)}) custom-call(f32[4608,256]{1,0:T(8,128)S(1)} %get-tuple-element.24.acc_in, bf16[512,256]{1,0:T(8,128)(2,1)S(1)} %shard_map.124.og_ref, bf16[4,1152,512]{2,1,0:T(8,128)(2,1)S(1)} %get-tuple-element.26.token_ref.head_ref, ...), custom_call_target="tpu_custom_call", output_to_operand_aliasing={{0}: (0, {})} | custom-call | flops 1207959552 | bytes 4718592 | tf_op jit(solution)/shard_map/pallas_call | solution.py:377
  21.5 0.0 collective-permute-done.3.og_ref
  21.6 3.6 %shard_map.126 = (f32[4608,256]{1,0:T(8,128)S(1)}, bf16[3,1152,768]{2,1,0:T(8,128)(2,1)S(1)}) custom-call(f32[4608,256]{1,0:T(8,128)S(1)} %get-tuple-element.27.acc_in, bf16[512,256]{1,0:T(8,128)(2,1)S(1)} %collective-permute-done.3.og_ref, bf16[2,1152,512]{2,1,0:T(8,128)(2,1)S(1)} %get-tuple-element.28.head_ref, ...), custom_call_target="tpu_custom_call", output_to_operand_aliasing={{0}: (0, {})} | custom-call | flops 1207959552 | bytes 4718592 | tf_op jit(solution)/shard_map/pallas_call | solution.py:377
  25.1 0.0 collective-permute-done.4.array_ref
  25.1 0.5 %collective-permute-start.6 = (bf16[768,256]{1,0:T(8,128)(2,1)S(1)}, bf16[768,256]{1,0:T(8,128)(2,1)S(1)}, u32[]{:S(2)}, u32[]{:S(2)}) collective-permute-start(bf16[768,256]{1,0:T(8,128)(2,1)S(1)} %shard_map.127.og_ref), channel_id=1, source_target_pairs={{0,1},{1,0},{2,3},{3,2},{4,5},{5,4},{6,7},{7,6},{8,9},{9,8},{10,11... | collective-permute-start | bytes 1179656 | tf_op jit(solution)/shard_map/ppermute | solution.py:286
  25.6 0.1 collective-permute-start
  25.7 2.9 %shard_map.128 = (f32[4608,256]{1,0:T(8,128)S(1)}, bf16[2,1152,768]{2,1,0:T(8,128)(2,1)S(1)}) custom-call(f32[4608,256]{1,0:T(8,128)S(1)} %get-tuple-element.29.acc_in, bf16[768,256]{1,0:T(8,128)(2,1)S(1)} %shard_map.127.og_ref, bf16[3,1152,768]{2,1,0:T(8,128)(2,1)S(1)} %get-tuple-element.31.token_ref.head_ref, ...), custom_call_target="tpu_custom_call", output_to_operand_aliasing={{0}: (0, {})} | custom-call | flops 1811939328 | bytes 7077888 | tf_op jit(solution)/shard_map/pallas_call | solution.py:377
  28.6 0.0 collective-permute-done.theirs_ref
  28.6 2.1 %collective-permute-start.5 = (f32[128,256]{1,0:T(8,128)S(1)}, f32[128,256]{1,0:T(8,128)S(1)}, u32[]{:S(2)}, u32[]{:S(2)}) collective-permute-start(f32[128,256]{1,0:T(8,128)S(1)} %shard_map.129.chip_ref), channel_id=1, source_target_pairs={{0,2},{1,3},{2,0},{3,1},{4,6},{5,7},{6,4},{7,5},{8,10},{9,11},{10,... | collective-permute-start | bytes 393224 | tf_op jit(solution)/shard_map/ppermute | solution.py:286
  30.8 0.0 collective-permute-done.6.og_ref
  30.8 4.1 %shard_map.130 = (f32[64,256]{1,0:T(8,128)S(1)}, f32[64,256]{1,0:T(8,128)S(1)}) custom-call(f32[4608,256]{1,0:T(8,128)S(1)} %get-tuple-element.33.acc_ref, bf16[768,256]{1,0:T(8,128)(2,1)S(1)} %collective-permute-done.6.og_ref, bf16[2,1152,768]{2,1,0:T(8,128)(2,1)S(1)} %get-tuple-element.32.token_ref.head_ref, bf16[4608,5120]{1,0:T(8,128)(2,1)} %w_hbm.11, ...), custom_call_target="tpu_custom_call" | custom-call | flops 1811939328 | bytes 7077888 | tf_op jit(solution)/shard_map/pallas_call | solution.py:399
  34.9 0.0 collective-permute-done.5.other_ref
  34.9 0.5 %shard_map.131 = f32[192,128]{1,0:T(8,128)S(1)} custom-call(f32[128,256]{1,0:T(8,128)S(1)} %shard_map.129.chip_ref, f32[128,256]{1,0:T(8,128)S(1)} %collective-permute-done.5.other_ref, f32[64,256]{1,0:T(8,128)S(1)} %get-tuple-element.36.gate_ref, f32[64,256]{1,0:T(8,128)S(1)} %get-tuple-element.37.up_ref, f32[64,256]{1,0:T(8,128)S(1)} %get-tuple-element.38.ph_ref), custom_call_target="tpu_custom_call" | custom-call | tf_op jit(solution)/shard_map/pallas_call | solution.py:408
  35.4 0.2 collective-permute-start.7
  35.6 1.2 %collective-permute-done.7 = f32[192,128]{1,0:T(8,128)S(1)} collective-permute-done((f32[192,128]{1,0:T(8,128)S(1)}, f32[192,128]{1,0:T(8,128)S(1)}, u32[]{:S(2)}, u32[]{:S(2)}) %collective-permute-start.7) | collective-permute-done | bytes 98336 | tf_op jit(solution)/shard_map/ppermute | solution.py:286
  36.8 1.8 %collective-permute-start.8 = (f32[192,128]{1,0:T(8,128)S(1)}, f32[192,128]{1,0:T(8,128)S(1)}, u32[]{:S(2)}, u32[]{:S(2)}) collective-permute-start(f32[192,128]{1,0:T(8,128)S(1)} %add.3.mine_ref), channel_id=1, source_target_pairs={{0,2},{1,3},{2,0},{3,1},{4,6},{5,7},{6,4},{7,5},{8,10},{9,11},{10,... | collective-permute-start | bytes 294920 | tf_op jit(solution)/shard_map/ppermute | solution.py:286
  38.6 3.1 %collective-permute-done.8.theirs_ref = f32[192,128]{1,0:T(8,128)S(1)} collective-permute-done((f32[192,128]{1,0:T(8,128)S(1)}, f32[192,128]{1,0:T(8,128)S(1)}, u32[]{:S(2)}, u32[]{:S(2)}) %collective-permute-start.8) | collective-permute-done | bytes 98336 | tf_op jit(solution)/shard_map/ppermute | solution.py:286
  41.7 0.7 %shard_map.132 = (f32[2,64,64]{2,1,0:T(8,128)}, f32[2,64,64]{2,1,0:T(8,128)}, f32[2,64,64]{2,1,0:T(8,128)}) custom-call(f32[192,128]{1,0:T(8,128)S(1)} %add.3.mine_ref, f32[192,128]{1,0:T(8,128)S(1)} %collective-permute-done.8.theirs_ref), custom_call_target="tpu_custom_call" | custom-call | tf_op jit(solution)/shard_map/pallas_call | solution.py:413
  (4 shorter events, 0.0 us)
Async XLA Ops:
  2.0 8.3 %collective-permute-start.1 = (bf16[1280,256]{1,0:T(8,128)(2,1)S(1)}, bf16[1280,256]{1,0:T(8,128)(2,1)S(1)}, u32[]{:S(2)}, u32[]{:S(2)}) collective-permute-start(bf16[1280,256]{1,0:T(8,128)(2,1)S(1)} %get-tuple-element.21.own_ref), channel_id=1, source_target_pairs={{0,1},{1,0},{2,3},{3,2},{4,5},{5,4},{6,7},{7,6},{8,9},{9,8},{10,11... | collective-permute-start | bytes 1966088 | tf_op jit(solution)/shard_map/ppermute | solution.py:286
  2.5 16.4 %collective-permute-start.2 = (bf16[512,256]{1,0:T(8,128)(2,1)S(1)}, bf16[512,256]{1,0:T(8,128)(2,1)S(1)}, u32[]{:S(2)}, u32[]{:S(2)}) collective-permute-start(bf16[512,256]{1,0:T(8,128)(2,1)S(1)} %get-tuple-element.25), channel_id=1, source_target_pairs={{0,2},{1,3},{2,0},{3,1},{4,6},{5,7},{6,4},{7,5},{8,10},{9,11},{10,... | collective-permute-start | bytes 786440 | tf_op jit(solution)/shard_map/ppermute | solution.py:286
  5.0 20.1 %collective-permute-start.4 = (bf16[768,256]{1,0:T(8,128)(2,1)S(1)}, bf16[768,256]{1,0:T(8,128)(2,1)S(1)}, u32[]{:S(2)}, u32[]{:S(2)}) collective-permute-start(bf16[768,256]{1,0:T(8,128)(2,1)S(1)} %get-tuple-element.30), channel_id=1, source_target_pairs={{0,2},{1,3},{2,0},{3,1},{4,6},{5,7},{6,4},{7,5},{8,10},{9,11},{10,... | collective-permute-start | bytes 1179656 | tf_op jit(solution)/shard_map/ppermute | solution.py:286
  18.9 2.6 %collective-permute-start.3 = (bf16[512,256]{1,0:T(8,128)(2,1)S(1)}, bf16[512,256]{1,0:T(8,128)(2,1)S(1)}, u32[]{:S(2)}, u32[]{:S(2)}) collective-permute-start(bf16[512,256]{1,0:T(8,128)(2,1)S(1)} %shard_map.124.og_ref), channel_id=1, source_target_pairs={{0,1},{1,0},{2,3},{3,2},{4,5},{5,4},{6,7},{7,6},{8,9},{9,8},{10,11... | collective-permute-start | bytes 786440 | tf_op jit(solution)/shard_map/ppermute | solution.py:286
  25.1 5.6 %collective-permute-start.6 = (bf16[768,256]{1,0:T(8,128)(2,1)S(1)}, bf16[768,256]{1,0:T(8,128)(2,1)S(1)}, u32[]{:S(2)}, u32[]{:S(2)}) collective-permute-start(bf16[768,256]{1,0:T(8,128)(2,1)S(1)} %shard_map.127.og_ref), channel_id=1, source_target_pairs={{0,1},{1,0},{2,3},{3,2},{4,5},{5,4},{6,7},{7,6},{8,9},{9,8},{10,11... | collective-permute-start | bytes 1179656 | tf_op jit(solution)/shard_map/ppermute | solution.py:286
  25.6 3.0 %collective-permute-start = (f32[128,256]{1,0:T(8,128)S(1)}, f32[128,256]{1,0:T(8,128)S(1)}, u32[]{:S(2)}, u32[]{:S(2)}) collective-permute-start(f32[128,256]{1,0:T(8,128)S(1)} %get-tuple-element.22.mine_ref), channel_id=1, source_target_pairs={{0,1},{1,0},{2,3},{3,2},{4,5},{5,4},{6,7},{7,6},{8,9},{9,8},{10,11... | collective-permute-start | bytes 393224 | tf_op jit(solution)/shard_map/ppermute | solution.py:286
  28.6 6.3 %collective-permute-start.5 = (f32[128,256]{1,0:T(8,128)S(1)}, f32[128,256]{1,0:T(8,128)S(1)}, u32[]{:S(2)}, u32[]{:S(2)}) collective-permute-start(f32[128,256]{1,0:T(8,128)S(1)} %shard_map.129.chip_ref), channel_id=1, source_target_pairs={{0,2},{1,3},{2,0},{3,1},{4,6},{5,7},{6,4},{7,5},{8,10},{9,11},{10,... | collective-permute-start | bytes 393224 | tf_op jit(solution)/shard_map/ppermute | solution.py:286
  35.4 1.4 %collective-permute-start.7 = (f32[192,128]{1,0:T(8,128)S(1)}, f32[192,128]{1,0:T(8,128)S(1)}, u32[]{:S(2)}, u32[]{:S(2)}) collective-permute-start(f32[192,128]{1,0:T(8,128)S(1)} %shard_map.131), channel_id=1, source_target_pairs={{0,1},{1,0},{2,3},{3,2},{4,5},{5,4},{6,7},{7,6},{8,9},{9,8},{10,11... | collective-permute-start | bytes 294920 | tf_op jit(solution)/shard_map/ppermute | solution.py:286
  36.8 4.9 %collective-permute-start.8 = (f32[192,128]{1,0:T(8,128)S(1)}, f32[192,128]{1,0:T(8,128)S(1)}, u32[]{:S(2)}, u32[]{:S(2)}) collective-permute-start(f32[192,128]{1,0:T(8,128)S(1)} %add.3.mine_ref), channel_id=1, source_target_pairs={{0,2},{1,3},{2,0},{3,1},{4,6},{5,7},{6,4},{7,5},{8,10},{9,11},{10,... | collective-permute-start | bytes 294920 | tf_op jit(solution)/shard_map/ppermute | solution.py:286

commit v10 on v8

--- a/solution.py
+++ b/solution.py
@@ -89,7 +89,7 @@
         copy.wait()
 
 
-def stream(step, following, ahead, blocks, head, w_v, next_head, sems, body, body_of_head=None):
+def stream(step, following, ahead, blocks, head, w_v, next_head, sems, body):
     heads = head.shape[0]
     slots = w_v.shape[0]
 
@@ -118,7 +118,7 @@
     @pl.loop(0, heads)
     def _(i):
         begin(i + ahead)
-        (body_of_head or body)(i, head.at[i])
+        body(i, head.at[i])
 
     @pl.loop(heads, blocks)
     def _(i):
@@ -199,7 +199,7 @@
     def body(i, weights):
         acc_ref[step.units(i)] = product(weights[...], og_v[...])
 
-    stream(step, following, 4, acc_ref.shape[0] // step.block, head_ref, w_v, next_ref, sems, body)
+    stream(step, following, 3, acc_ref.shape[0] // step.block, head_ref, w_v, next_ref, sems, body)
 
 
 def add_kernel(bits, following_bits, acc_in, og_ref, head_ref, w_hbm, acc_ref, next_ref, og_v, w_v, sems):
@@ -214,42 +214,29 @@
         at = step.units(i)
         acc_ref[at] = acc_in[at] + product(weights[...], og_v[...])
 
-    stream(step, following, 3, acc_in.shape[0] // block, head_ref, w_v, next_ref, sems, body)
+    stream(step, following, 4, acc_in.shape[0] // block, head_ref, w_v, next_ref, sems, body)
 
 
 def far_kernel(bits, acc_ref, og_ref, head_ref, w_hbm, a_ref, b_ref, gf_hbm, uf_hbm, gate_ref, up_ref,
-               og_v, w_v, gf_ref, uf_ref, hidden_v, sems, factor_sems):
+               og_v, w_v, gf_ref, uf_ref, d_gate_v, d_up_v, sems, factor_sems):
     _, block, width = w_v.shape
     step = Step(lax.axis_index("tensor") ^ bits, width, block, w_hbm)
     factors = [
         pltpu.make_async_copy(src, dst, factor_sems.at[k]) for k, (src, dst) in enumerate(((gf_hbm, gf_ref), (uf_hbm, uf_ref)))
     ]
     start(factors)
-    gate_ref[...] = jnp.zeros_like(gate_ref)
-    up_ref[...] = jnp.zeros_like(up_ref)
     og_v[...] = og_ref[...].T
 
-    blocks = acc_ref.shape[0] // block
-
-    def multiply(i, weights):
-        hidden_v[i % 2] = acc_ref[step.units(i)] + product(weights[...], og_v[...])
-
-    def use(i):
+    def body(i, weights):
         at = step.units(i)
-        hidden_grad = hidden_v[i % 2]
-        gate_ref[...] += product(gf_ref[:, at], (hidden_grad * a_ref[at]).astype(BF16))
-        up_ref[...] += product(uf_ref[:, at], (hidden_grad * b_ref[at]).astype(BF16))
-
-    def body(i, weights):
-        use(i - 1)
-        multiply(i, weights)
-
-    def body_of_head(i, weights):
-        multiply(i, weights)
-        wait(factors)
-
-    stream(step, None, 3, blocks, head_ref, w_v, None, sems, body, body_of_head)
-    use(blocks - 1)
+        hidden_grad = acc_ref[at] + product(weights[...], og_v[...])
+        d_gate_v[at] = (hidden_grad * a_ref[at]).astype(BF16)
+        d_up_v[at] = (hidden_grad * b_ref[at]).astype(BF16)
+
+    stream(step, None, 4, acc_ref.shape[0] // block, head_ref, w_v, None, sems, body)
+    wait(factors)
+    gate_ref[...] = product(gf_ref[...], d_gate_v[...])
+    up_ref[...] = product(uf_ref[...], d_up_v[...])
 
 
 def after_kernel(array_ref, token_ref, same_ref):
@@ -353,41 +340,46 @@
     pq_mate = swap(pq, 1)
     acc, head = call(
         chip_features_kernel,
-        (held, blocks(2)),
+        (held, blocks(turns)),
         [VMEM] * 3 + [ANY],
-        [pltpu.VMEM((2 * width, tokens), BF16), chip_blocks(5), dma((units // CHIP_BLOCK + 2, PARTS))],
+        [pltpu.VMEM((2 * width, tokens), BF16), chip_blocks(4), dma((units // CHIP_BLOCK + turns, PARTS))],
         16,
         2 * per_product,
         4 * units * width,
     )(own, mate, head, weight)
 
-    near = pl.pallas_call(
-        after_kernel,
-        out_shape=pltpu.VMEM(near.shape, near.dtype),
-        in_specs=[ANY, ANY],
-        out_specs=ANY,
-        input_output_aliases={0: 0},
-        compiler_params=pltpu.CompilerParams(vmem_limit_bytes=MIB),
-    )(near, head)
+    def after(array, token):
+        return pl.pallas_call(
+            after_kernel,
+            out_shape=pltpu.VMEM(array.shape, array.dtype),
+            in_specs=[ANY, ANY],
+            out_specs=ANY,
+            input_output_aliases={0: 0},
+            compiler_params=pltpu.CompilerParams(vmem_limit_bytes=MIB),
+        )(array, token)
+
+    chip = call(chip_kernel, pltpu.VMEM(pq.shape, F32), [VMEM, VMEM, ANY], [], 1)(pq, pq_mate, head)
+    near = after(near, chip)
+    chip = after(chip, near)
+    chip_across = swap(chip, 2)
     far = swap(near, 1)
     acc, head = call(
         functools.partial(add_kernel, 2, 3),
-        (held, blocks(1)),
+        (held, blocks(turns - 1)),
         [VMEM] * 3 + [ANY],
-        [turned, blocks(2), dma((turns + 1, PARTS))],
-        10,
+        [turned, blocks(1), dma((2 * turns - 1, PARTS))],
+        6,
         per_product,
         2 * units * width,
         input_output_aliases={0: 0},
     )(acc, near, head, weight)
-    chip = call(chip_kernel, pltpu.VMEM(pq.shape, F32), [VMEM, VMEM, ANY], [], 1)(pq, pq_mate, head)
-    chip_across = swap(chip, 2)
     factor = pltpu.VMEM((rank, units), BF16)
+    kept = pltpu.VMEM((units, tokens), BF16)
     q_gate, q_up = call(
         functools.partial(far_kernel, 3),
         (narrow, narrow),
         [VMEM] * 3 + [ANY] + [VMEM] * 2 + [ANY] * 2,
-        [turned, blocks(3), factor, factor, pltpu.VMEM((2, BLOCK, tokens), F32), dma((turns, PARTS)), dma((2,))],
+        [turned, blocks(1), factor, factor, kept, kept, dma((turns, PARTS)), dma((2,))],
         16,
         per_product,
         2 * units * width,

time: 41.1 us -> 40 us (0.973)
  waiting for transfers between devices: 7.47 us -> 4.87 us
  Pallas kernels: 26.9 us -> 28.1 us
    pallas_call x3 -> x4, Pallas kernels: 12.6 us -> 15.4 us  [the longest x1 10.4 us: fast(): call(chip_features_kernel, (held, blocks(turns)), [VMEM] * 3 + [ANY], [pl...]
    ppermute x7, waiting for transfers between devices: 7.47 us -> 4.87 us  [swap(): return lax.ppermute(array, 'tensor', [(i, i ^ bits) for i in range(4)])]
    pallas_call x1, Pallas kernels: 7.64 us -> 6.12 us  [fast(): call(functools.partial(far_kernel, 3), (narrow, narrow), [VMEM] * 3 + [AN...]
  transfers between devices with their start and end apart: 7 -> 7, of which waited for: 3 -> 2; matrix products, arithmetic and copies ran while one was open for 0% -> 0% of each run, Pallas kernels for 63% -> 68%
where the time goes in v10:
time: 40 us; the launch traced here: 39.8 us
  Pallas kernels  28.1 us (70%)
  starting transfers between devices  6.09 us (15%)
  waiting for transfers between devices  4.87 us (12%)
  between operations  0.73 us (2%)
    pallas_call x1, Pallas kernels, fast(): call(chip_features_kernel, (held, blocks(turns)), [VMEM] * 3 + [ANY], [pl...  10.4 us
    pallas_call x1, Pallas kernels, fast(): call(functools.partial(far_kernel, 3), (narrow, narrow), [VMEM] * 3 + [AN...  6.12 us
    ppermute x7, starting transfers between devices, swap(): return lax.ppermute(array, 'tensor', [(i, i ^ bits) for i in range(4)])  6.09 us
    pallas_call x1, Pallas kernels, fast(): call(elementwise_kernel, (held, held, narrow, pltpu.VMEM((2 * rank, token...  5.35 us
    pallas_call x1, Pallas kernels, fast(): call(functools.partial(add_kernel, 2, 3), (held, blocks(turns - 1)), [VME...  5.03 us
    ppermute x7, waiting for transfers between devices, swap(): return lax.ppermute(array, 'tensor', [(i, i ^ bits) for i in range(4)])  4.87 us
  transfers between devices with their start and end apart: 7, of which 2 were waited for; matrix products, arithmetic and copies ran while one was open for 0% of the time, Pallas kernels for 68%

profile of v10, /device:TPU:0, one launch (start us, length us, event | category | flops | bytes accessed | tf_op | source)
XLA Modules:
  0.0 39.8 jit_solution(851189386684346559)
XLA Ops:
  0.6 0.5 %collective-permute-start.1 = (bf16[256,1280]{1,0:T(8,128)(2,1)}, bf16[256,1280]{1,0:T(8,128)(2,1)S(1)}, u32[]{:S(2)}, u32[]{:S(2)}) collective-permute-start(bf16[256,1280]{1,0:T(8,128)(2,1)} %og_hbm.1), channel_id=1, source_target_pairs={{0,1},{1,0},{2,3},{3,2},{4,5},{5,4},{6,7},{7,6},{8,9},{9,8},{10,11... | collective-permute-start | bytes 1966088 | tf_op jit(solution)/shard_map/ppermute | solution.py:280
  1.2 2.6 %collective-permute-start.2 = (bf16[256,1280]{1,0:T(8,128)(2,1)}, bf16[256,1280]{1,0:T(8,128)(2,1)S(1)}, u32[]{:S(2)}, u32[]{:S(2)}) collective-permute-start(bf16[256,1280]{1,0:T(8,128)(2,1)} %og_hbm.1), channel_id=1, source_target_pairs={{0,2},{1,3},{2,0},{3,1},{4,6},{5,7},{6,4},{7,5},{8,10},{9,11},{10,... | collective-permute-start | bytes 1966088 | tf_op jit(solution)/shard_map/ppermute | solution.py:280
  3.7 5.4 %shard_map.121 = (f32[4608,256]{1,0:T(8,128)S(1)}, f32[4608,256]{1,0:T(8,128)S(1)}, f32[64,256]{1,0:T(8,128)S(1)}, f32[128,256]{1,0:T(8,128)S(1)}, bf16[2,512,25...) custom-call(bf16[256,1280]{1,0:T(8,128)(2,1)} %x_hbm.1, bf16[256,1280]{1,0:T(8,128)(2,1)} %og_hbm.1, ...), custom_call_target="tpu_custom_call" | custom-call | flops 754974720 | bytes 4718592 | tf_op jit(solution)/shard_map/pallas_call | solution.py:310
  9.1 0.2 collective-permute-start
  9.3 0.0 collective-permute-done.1.mate_ref
  9.3 10.4 %shard_map.122 = (f32[4608,256]{1,0:T(8,128)S(1)}, bf16[4,1152,1280]{2,1,0:T(8,128)(2,1)S(1)}) custom-call(bf16[1280,256]{1,0:T(8,128)(2,1)S(1)} %get-tuple-element.16.own_ref, bf16[256,1280]{1,0:T(8,128)(2,1)S(1)} %collective-permute-done.1.mate_ref, bf16[2,512,2560]{2,1,0:T(8,128)(2,1)S(1)} %get-tuple-element.17.head_ref, bf16[4608,5120]{1,0:T(8,128)(2,1)} %w_hbm.7), custom_call_target="tpu_custom_call" | custom-call | flops 6039797760 | bytes 23592960 | tf_op jit(solution)/shard_map/pallas_call | solution.py:341
  19.7 0.0 collective-permute-done.theirs_ref
  19.7 0.0 collective-permute-done.2.array_ref
  19.7 0.4 %collective-permute-start.4 = (bf16[256,1280]{1,0:T(8,128)(2,1)S(1)}, bf16[256,1280]{1,0:T(8,128)(2,1)S(1)}, u32[]{:S(2)}, u32[]{:S(2)}) collective-permute-start(bf16[256,1280]{1,0:T(8,128)(2,1)S(1)} %shard_map.124.token_ref.og_ref), channel_id=1, source_target_pairs={{0,1},{1,0},{2,3},{3,2},{4,5},{5,4},{6,7},{7,6},{8,9},{9,8},{10,11... | collective-permute-start | bytes 1966088 | tf_op jit(solution)/shard_map/ppermute | solution.py:280
  20.1 0.9 %collective-permute-start.3 = (f32[128,256]{1,0:T(8,128)S(1)}, f32[128,256]{1,0:T(8,128)S(1)}, u32[]{:S(2)}, u32[]{:S(2)}) collective-permute-start(f32[128,256]{1,0:T(8,128)S(1)} %shard_map.125.chip_ref), channel_id=1, source_target_pairs={{0,2},{1,3},{2,0},{3,1},{4,6},{5,7},{6,4},{7,5},{8,10},{9,11},{10,... | collective-permute-start | bytes 393224 | tf_op jit(solution)/shard_map/ppermute | solution.py:280
  21.0 5.0 %shard_map.126 = (f32[4608,256]{1,0:T(8,128)S(1)}, bf16[3,1152,1280]{2,1,0:T(8,128)(2,1)S(1)}) custom-call(f32[4608,256]{1,0:T(8,128)S(1)} %get-tuple-element.19.acc_in, bf16[256,1280]{1,0:T(8,128)(2,1)S(1)} %shard_map.124.token_ref.og_ref, bf16[4,1152,1280]{2,1,0:T(8,128)(2,1)S(1)} %get-tuple-element.18.token_ref.head_ref, ...), custom_call_target="tpu_custom_call", output_to_operand_aliasing={{0}: (0, {})} | custom-call | flops 3019898880 | bytes 11796480 | tf_op jit(solution)/shard_map/pallas_call | solution.py:366
  26.1 0.0 collective-permute-done.4.og_ref
  26.1 6.1 %shard_map.127 = (f32[64,256]{1,0:T(8,128)S(1)}, f32[64,256]{1,0:T(8,128)S(1)}) custom-call(f32[4608,256]{1,0:T(8,128)S(1)} %get-tuple-element.20.acc_ref, bf16[256,1280]{1,0:T(8,128)(2,1)S(1)} %collective-permute-done.4.og_ref, bf16[3,1152,1280]{2,1,0:T(8,128)(2,1)S(1)} %get-tuple-element.21.head_ref, bf16[4608,5120]{1,0:T(8,128)(2,1)} %w_hbm.7, ...), custom_call_target="tpu_custom_call" | custom-call | flops 3019898880 | bytes 11796480 | tf_op jit(solution)/shard_map/pallas_call | solution.py:378
  32.2 0.0 collective-permute-done.3.other_ref
  32.2 0.5 %shard_map.128 = f32[192,128]{1,0:T(8,128)S(1)} custom-call(f32[128,256]{1,0:T(8,128)S(1)} %shard_map.125.chip_ref, f32[128,256]{1,0:T(8,128)S(1)} %collective-permute-done.3.other_ref, f32[64,256]{1,0:T(8,128)S(1)} %get-tuple-element.24.gate_ref, f32[64,256]{1,0:T(8,128)S(1)} %get-tuple-element.25.up_ref, f32[64,256]{1,0:T(8,128)S(1)} %get-tuple-element.26.ph_ref), custom_call_target="tpu_custom_call" | custom-call | tf_op jit(solution)/shard_map/pallas_call | solution.py:387
  32.7 0.3 collective-permute-start.5
  33.0 1.1 %collective-permute-done.5 = f32[192,128]{1,0:T(8,128)S(1)} collective-permute-done((f32[192,128]{1,0:T(8,128)S(1)}, f32[192,128]{1,0:T(8,128)S(1)}, u32[]{:S(2)}, u32[]{:S(2)}) %collective-permute-start.5) | collective-permute-done | bytes 98336 | tf_op jit(solution)/shard_map/ppermute | solution.py:280
  34.1 1.2 %collective-permute-start.6 = (f32[192,128]{1,0:T(8,128)S(1)}, f32[192,128]{1,0:T(8,128)S(1)}, u32[]{:S(2)}, u32[]{:S(2)}) collective-permute-start(f32[192,128]{1,0:T(8,128)S(1)} %add.3.mine_ref), channel_id=1, source_target_pairs={{0,2},{1,3},{2,0},{3,1},{4,6},{5,7},{6,4},{7,5},{8,10},{9,11},{10,... | collective-permute-start | bytes 294920 | tf_op jit(solution)/shard_map/ppermute | solution.py:280
  35.3 3.8 %collective-permute-done.6.theirs_ref = f32[192,128]{1,0:T(8,128)S(1)} collective-permute-done((f32[192,128]{1,0:T(8,128)S(1)}, f32[192,128]{1,0:T(8,128)S(1)}, u32[]{:S(2)}, u32[]{:S(2)}) %collective-permute-start.6) | collective-permute-done | bytes 98336 | tf_op jit(solution)/shard_map/ppermute | solution.py:280
  39.1 0.7 %shard_map.129 = (f32[2,64,64]{2,1,0:T(8,128)}, f32[2,64,64]{2,1,0:T(8,128)}, f32[2,64,64]{2,1,0:T(8,128)}) custom-call(f32[192,128]{1,0:T(8,128)S(1)} %add.3.mine_ref, f32[192,128]{1,0:T(8,128)S(1)} %collective-permute-done.6.theirs_ref), custom_call_target="tpu_custom_call" | custom-call | tf_op jit(solution)/shard_map/pallas_call | solution.py:392
  (4 shorter events, 0.0 us)
Async XLA Ops:
  0.6 8.7 %collective-permute-start.1 = (bf16[256,1280]{1,0:T(8,128)(2,1)}, bf16[256,1280]{1,0:T(8,128)(2,1)S(1)}, u32[]{:S(2)}, u32[]{:S(2)}) collective-permute-start(bf16[256,1280]{1,0:T(8,128)(2,1)} %og_hbm.1), channel_id=1, source_target_pairs={{0,1},{1,0},{2,3},{3,2},{4,5},{5,4},{6,7},{7,6},{8,9},{9,8},{10,11... | collective-permute-start | bytes 1966088 | tf_op jit(solution)/shard_map/ppermute | solution.py:280
  1.2 18.6 %collective-permute-start.2 = (bf16[256,1280]{1,0:T(8,128)(2,1)}, bf16[256,1280]{1,0:T(8,128)(2,1)S(1)}, u32[]{:S(2)}, u32[]{:S(2)}) collective-permute-start(bf16[256,1280]{1,0:T(8,128)(2,1)} %og_hbm.1), channel_id=1, source_target_pairs={{0,2},{1,3},{2,0},{3,1},{4,6},{5,7},{6,4},{7,5},{8,10},{9,11},{10,... | collective-permute-start | bytes 1966088 | tf_op jit(solution)/shard_map/ppermute | solution.py:280
  9.1 10.6 %collective-permute-start = (f32[128,256]{1,0:T(8,128)S(1)}, f32[128,256]{1,0:T(8,128)S(1)}, u32[]{:S(2)}, u32[]{:S(2)}) collective-permute-start(f32[128,256]{1,0:T(8,128)S(1)} %get-tuple-element.15.mine_ref), channel_id=1, source_target_pairs={{0,1},{1,0},{2,3},{3,2},{4,5},{5,4},{6,7},{7,6},{8,9},{9,8},{10,11... | collective-permute-start | bytes 393224 | tf_op jit(solution)/shard_map/ppermute | solution.py:280
  19.7 6.3 %collective-permute-start.4 = (bf16[256,1280]{1,0:T(8,128)(2,1)S(1)}, bf16[256,1280]{1,0:T(8,128)(2,1)S(1)}, u32[]{:S(2)}, u32[]{:S(2)}) collective-permute-start(bf16[256,1280]{1,0:T(8,128)(2,1)S(1)} %shard_map.124.token_ref.og_ref), channel_id=1, source_target_pairs={{0,1},{1,0},{2,3},{3,2},{4,5},{5,4},{6,7},{7,6},{8,9},{9,8},{10,11... | collective-permute-start | bytes 1966088 | tf_op jit(solution)/shard_map/ppermute | solution.py:280
  20.1 12.1 %collective-permute-start.3 = (f32[128,256]{1,0:T(8,128)S(1)}, f32[128,256]{1,0:T(8,128)S(1)}, u32[]{:S(2)}, u32[]{:S(2)}) collective-permute-start(f32[128,256]{1,0:T(8,128)S(1)} %shard_map.125.chip_ref), channel_id=1, source_target_pairs={{0,2},{1,3},{2,0},{3,1},{4,6},{5,7},{6,4},{7,5},{8,10},{9,11},{10,... | collective-permute-start | bytes 393224 | tf_op jit(solution)/shard_map/ppermute | solution.py:280
  32.7 1.4 %collective-permute-start.5 = (f32[192,128]{1,0:T(8,128)S(1)}, f32[192,128]{1,0:T(8,128)S(1)}, u32[]{:S(2)}, u32[]{:S(2)}) collective-permute-start(f32[192,128]{1,0:T(8,128)S(1)} %shard_map.128), channel_id=1, source_target_pairs={{0,1},{1,0},{2,3},{3,2},{4,5},{5,4},{6,7},{7,6},{8,9},{9,8},{10,11... | collective-permute-start | bytes 294920 | tf_op jit(solution)/shard_map/ppermute | solution.py:280
  34.1 5.0 %collective-permute-start.6 = (f32[192,128]{1,0:T(8,128)S(1)}, f32[192,128]{1,0:T(8,128)S(1)}, u32[]{:S(2)}, u32[]{:S(2)}) collective-permute-start(f32[192,128]{1,0:T(8,128)S(1)} %add.3.mine_ref), channel_id=1, source_target_pairs={{0,2},{1,3},{2,0},{3,1},{4,6},{5,7},{6,4},{7,5},{8,10},{9,11},{10,... | collective-permute-start | bytes 294920 | tf_op jit(solution)/shard_map/ppermute | solution.py:280

commit v11 on v10

--- a/solution.py
+++ b/solution.py
@@ -1,5 +1,3 @@
-import functools
-
 import jax
 import jax.numpy as jnp
 from jax import lax
@@ -89,28 +87,23 @@
         copy.wait()
 
 
-def stream(step, following, ahead, blocks, head, w_v, next_head, sems, body):
+def stream(step, ahead, blocks, head, w_v, sems, body, later):
     heads = head.shape[0]
     slots = w_v.shape[0]
 
     def copies(j):
         return step.copies(j, w_v.at[(j - heads) % slots], sems.at[j])
-
-    def next_copies(j):
-        return following.copies(j, next_head.at[j], sems.at[blocks + j])
-
-    last = blocks + (0 if following is None else next_head.shape[0])
 
     def begin(j):
         @pl.when(j < blocks)
         def _():
             start(copies(j))
 
-        if following is not None:
-
-            @pl.when((j >= blocks) & (j < last))
+        for k, group in enumerate(later):
+
+            @pl.when(j == blocks + k)
             def _():
-                start(next_copies(j - blocks))
+                start(group)
 
     for j in range(heads, ahead):
         start(copies(j))
@@ -126,10 +119,11 @@
         wait(copies(i))
         body(i, w_v.at[(i - heads) % slots])
 
-    for j in range(blocks + ahead, last):
-        start(next_copies(j - blocks))
-    for j in range(last - blocks):
-        wait(next_copies(j))
+    for k, group in enumerate(later):
+        if k >= ahead:
+            start(group)
+    for group in later:
+        wait(group)
 
 
 def elementwise_kernel(x_hbm, og_hbm, gate_hbm, up_hbm, w_hbm, xf_hbm, yf_hbm, hf_hbm,
@@ -186,11 +180,12 @@
         wait(following.copies(i, head_ref.at[i], w_sems.at[i]))
 
 
-def chip_features_kernel(own_ref, mate_ref, head_ref, w_hbm, acc_ref, next_ref, og_v, w_v, sems):
+def chip_features_kernel(own_ref, mate_ref, head_ref, w_hbm, acc_ref, near_ref, far_ref, og_v, w_v, sems, near_sems, far_sems):
     me = lax.axis_index("tensor")
     width = own_ref.shape[0]
     step = Step(me // 2, 2 * width, w_v.shape[1], w_hbm)
-    following = Step(me ^ 2, width, next_ref.shape[1], w_hbm)
+    near = Step(me ^ 2, width, near_ref.shape[1], w_hbm)
+    far = Step(me ^ 3, width, far_ref.shape[1], w_hbm)
     mine = pl.ds(pl.multiple_of(me % 2 * width, 128), width)
     theirs = pl.ds(pl.multiple_of((me + 1) % 2 * width, 128), width)
     og_v[mine] = own_ref[...]
@@ -199,41 +194,64 @@
     def body(i, weights):
         acc_ref[step.units(i)] = product(weights[...], og_v[...])
 
-    stream(step, following, 3, acc_ref.shape[0] // step.block, head_ref, w_v, next_ref, sems, body)
-
-
-def add_kernel(bits, following_bits, acc_in, og_ref, head_ref, w_hbm, acc_ref, next_ref, og_v, w_v, sems):
+    later = [near.copies(k, near_ref.at[k], near_sems.at[k]) for k in range(near_ref.shape[0])]
+    later += [far.copies(k, far_ref.at[k], far_sems.at[k]) for k in range(far_ref.shape[0])]
+    stream(step, 3, acc_ref.shape[0] // step.block, head_ref, w_v, sems, body, later)
+
+
+def near_kernel(acc_in, og_ref, w_ref, w_hbm, acc_ref, far_ref, og_v, sems):
     me = lax.axis_index("tensor")
-    _, block, width = w_v.shape
-    step = Step(me ^ bits, width, block, w_hbm)
-    following = Step(me ^ following_bits, width, block, w_hbm)
-
+    blocks, block, width = w_ref.shape
+    far = Step(me ^ 3, width, block, w_hbm)
+    copies = [far.copies(k + 1, far_ref.at[k], sems.at[k]) for k in range(far_ref.shape[0])]
+    for group in copies:
+        start(group)
     og_v[...] = og_ref[...].T
 
-    def body(i, weights):
-        at = step.units(i)
-        acc_ref[at] = acc_in[at] + product(weights[...], og_v[...])
-
-    stream(step, following, 4, acc_in.shape[0] // block, head_ref, w_v, next_ref, sems, body)
-
-
-def far_kernel(bits, acc_ref, og_ref, head_ref, w_hbm, a_ref, b_ref, gf_hbm, uf_hbm, gate_ref, up_ref,
+    @pl.loop(0, blocks)
+    def _(i):
+        at = far.units(i)
+        acc_ref[at] = acc_in[at] + product(w_ref[i], og_v[...])
+
+    for group in copies:
+        wait(group)
+
+
+def far_kernel(acc_ref, og_ref, first_ref, second_ref, w_hbm, a_ref, b_ref, gf_hbm, uf_hbm, gate_ref, up_ref,
                og_v, w_v, gf_ref, uf_ref, d_gate_v, d_up_v, sems, factor_sems):
     _, block, width = w_v.shape
-    step = Step(lax.axis_index("tensor") ^ bits, width, block, w_hbm)
+    step = Step(lax.axis_index("tensor") ^ 3, width, block, w_hbm)
     factors = [
         pltpu.make_async_copy(src, dst, factor_sems.at[k]) for k, (src, dst) in enumerate(((gf_hbm, gf_ref), (uf_hbm, uf_ref)))
     ]
+    held = first_ref.shape[0] + second_ref.shape[0]
+    copies = [step.copies(held + k, w_v.at[k], sems.at[k]) for k in range(w_v.shape[0])]
+    for group in copies:
+        start(group)
     start(factors)
     og_v[...] = og_ref[...].T
 
     def body(i, weights):
         at = step.units(i)
-        hidden_grad = acc_ref[at] + product(weights[...], og_v[...])
+        hidden_grad = acc_ref[at] + product(weights, og_v[...])
         d_gate_v[at] = (hidden_grad * a_ref[at]).astype(BF16)
         d_up_v[at] = (hidden_grad * b_ref[at]).astype(BF16)
 
-    stream(step, None, 4, acc_ref.shape[0] // block, head_ref, w_v, None, sems, body)
+    @pl.loop(0, first_ref.shape[0])
+    def _(i):
+        body(i, first_ref[i])
+
+    @pl.loop(0, second_ref.shape[0])
+    def _(i):
+        body(first_ref.shape[0] + i, second_ref[i])
+
+    for group in copies:
+        wait(group)
+
+    @pl.loop(0, w_v.shape[0])
+    def _(i):
+        body(held + i, w_v[i])
+
     wait(factors)
     gate_ref[...] = product(gf_ref[...], d_gate_v[...])
     up_ref[...] = product(uf_ref[...], d_up_v[...])
@@ -338,12 +356,18 @@
         in_hbm(h_factor.T),
     )
     pq_mate = swap(pq, 1)
-    acc, head = call(
+    acc, w_near, far_first = call(
         chip_features_kernel,
-        (held, blocks(turns)),
+        (held, blocks(turns), blocks(1)),
         [VMEM] * 3 + [ANY],
-        [pltpu.VMEM((2 * width, tokens), BF16), chip_blocks(4), dma((units // CHIP_BLOCK + turns, PARTS))],
-        16,
+        [
+            pltpu.VMEM((2 * width, tokens), BF16),
+            chip_blocks(4),
+            dma((units // CHIP_BLOCK, PARTS)),
+            dma((turns, PARTS)),
+            dma((1, PARTS)),
+        ],
+        14,
         2 * per_product,
         4 * units * width,
     )(own, mate, head, weight)
@@ -358,32 +382,32 @@
             compiler_params=pltpu.CompilerParams(vmem_limit_bytes=MIB),
         )(array, token)
 
-    chip = call(chip_kernel, pltpu.VMEM(pq.shape, F32), [VMEM, VMEM, ANY], [], 1)(pq, pq_mate, head)
+    chip = call(chip_kernel, pltpu.VMEM(pq.shape, F32), [VMEM, VMEM, ANY], [], 1)(pq, pq_mate, far_first)
     near = after(near, chip)
-    chip = after(chip, near)
-    chip_across = swap(chip, 2)
     far = swap(near, 1)
-    acc, head = call(
-        functools.partial(add_kernel, 2, 3),
-        (held, blocks(turns - 1)),
+    acc, far_second = call(
+        near_kernel,
+        (held, blocks(2)),
         [VMEM] * 3 + [ANY],
-        [turned, blocks(1), dma((2 * turns - 1, PARTS))],
-        6,
+        [turned, dma((2, PARTS))],
+        4,
         per_product,
         2 * units * width,
         input_output_aliases={0: 0},
-    )(acc, near, head, weight)
+    )(acc, near, w_near, weight)
+    chip = after(chip, far_second)
+    chip_across = swap(chip, 2)
     factor = pltpu.VMEM((rank, units), BF16)
     kept = pltpu.VMEM((units, tokens), BF16)
     q_gate, q_up = call(
-        functools.partial(far_kernel, 3),
+        far_kernel,
         (narrow, narrow),
-        [VMEM] * 3 + [ANY] + [VMEM] * 2 + [ANY] * 2,
-        [turned, blocks(1), factor, factor, kept, kept, dma((turns, PARTS)), dma((2,))],
-        16,
+        [VMEM] * 4 + [ANY] + [VMEM] * 2 + [ANY] * 2,
+        [turned, blocks(turns - 3), factor, factor, kept, kept, dma((turns - 3, PARTS)), dma((2,))],
+        14,
         per_product,
         2 * units * width,
-    )(acc, far, head, weight, a, b, in_hbm(gate_factor.T), in_hbm(up_factor.T))
+    )(acc, far, far_first, far_second, weight, a, b, in_hbm(gate_factor.T), in_hbm(up_factor.T))
     share = call(gradients_kernel, pltpu.VMEM(((SEQS + 1) * rank, 2 * rank), F32), [VMEM] * 5, [], 4)(
         chip, chip_across, q_gate, q_up, ph
     )

time: 40 us -> 39.2 us (0.980)
  waiting for transfers between devices: 4.87 us -> 4.22 us
    ppermute x7, waiting for transfers between devices: 4.87 us -> 4.22 us  [swap(): return lax.ppermute(array, 'tensor', [(i, i ^ bits) for i in range(4)])]
where the time goes in v11:
time: 39.2 us; the launch traced here: 39.1 us
  Pallas kernels  28 us (71%)
  starting transfers between devices  6.11 us (16%)
  waiting for transfers between devices  4.22 us (11%)
  between operations  0.73 us (2%)
    pallas_call x1, Pallas kernels, fast(): call(chip_features_kernel, (held, blocks(turns), blocks(1)), [VMEM] * 3 +...  11.3 us
    pallas_call x1, Pallas kernels, fast(): call(far_kernel, (narrow, narrow), [VMEM] * 4 + [ANY] + [VMEM] * 2 + [ANY...  6.13 us
    ppermute x7, starting transfers between devices, swap(): return lax.ppermute(array, 'tensor', [(i, i ^ bits) for i in range(4)])  6.11 us
    pallas_call x1, Pallas kernels, fast(): call(elementwise_kernel, (held, held, narrow, pltpu.VMEM((2 * rank, token...  5.35 us
    ppermute x7, waiting for transfers between devices, swap(): return lax.ppermute(array, 'tensor', [(i, i ^ bits) for i in range(4)])  4.22 us
    pallas_call x1, Pallas kernels, fast(): call(near_kernel, (held, blocks(2)), [VMEM] * 3 + [ANY], [turned, dma((2,...  4 us
  transfers between devices with their start and end apart: 7, of which 2 were waited for; matrix products, arithmetic and copies ran while one was open for 0% of the time, Pallas kernels for 68%

profile of v11, /device:TPU:0, one launch (start us, length us, event | category | flops | bytes accessed | tf_op | source)
XLA Modules:
  0.0 39.1 jit_solution(1933709908884849536)
XLA Ops:
  0.6 0.5 %collective-permute-start.1 = (bf16[256,1280]{1,0:T(8,128)(2,1)}, bf16[256,1280]{1,0:T(8,128)(2,1)S(1)}, u32[]{:S(2)}, u32[]{:S(2)}) collective-permute-start(bf16[256,1280]{1,0:T(8,128)(2,1)} %og_hbm.1), channel_id=1, source_target_pairs={{0,1},{1,0},{2,3},{3,2},{4,5},{5,4},{6,7},{7,6},{8,9},{9,8},{10,11... | collective-permute-start | bytes 1966088 | tf_op jit(solution)/shard_map/ppermute | solution.py:298
  1.2 2.6 %collective-permute-start.2 = (bf16[256,1280]{1,0:T(8,128)(2,1)}, bf16[256,1280]{1,0:T(8,128)(2,1)S(1)}, u32[]{:S(2)}, u32[]{:S(2)}) collective-permute-start(bf16[256,1280]{1,0:T(8,128)(2,1)} %og_hbm.1), channel_id=1, source_target_pairs={{0,2},{1,3},{2,0},{3,1},{4,6},{5,7},{6,4},{7,5},{8,10},{9,11},{10,... | collective-permute-start | bytes 1966088 | tf_op jit(solution)/shard_map/ppermute | solution.py:298
  3.7 5.4 %shard_map.121 = (f32[4608,256]{1,0:T(8,128)S(1)}, f32[4608,256]{1,0:T(8,128)S(1)}, f32[64,256]{1,0:T(8,128)S(1)}, f32[128,256]{1,0:T(8,128)S(1)}, bf16[2,512,25...) custom-call(bf16[256,1280]{1,0:T(8,128)(2,1)} %x_hbm.1, bf16[256,1280]{1,0:T(8,128)(2,1)} %og_hbm.1, ...), custom_call_target="tpu_custom_call" | custom-call | flops 754974720 | bytes 4718592 | tf_op jit(solution)/shard_map/pallas_call | solution.py:328
  9.1 0.2 collective-permute-start
  9.3 0.0 collective-permute-done.1.mate_ref
  9.3 11.3 %shard_map.122 = (f32[4608,256]{1,0:T(8,128)S(1)}, bf16[4,1152,1280]{2,1,0:T(8,128)(2,1)S(1)}, bf16[1,1152,1280]{2,1,0:T(8,128)(2,1)S(1)}) custom-call(bf16[1280,256]{1,0:T(8,128)(2,1)S(1)} %get-tuple-element.17.own_ref, bf16[256,1280]{1,0:T(8,128)(2,1)S(1)} %collective-permute-done.1.mate_ref, bf16[2,512,2560]{2,1,0:T(8,128)(2,1)S(1)} %get-tuple-element.18.head_ref, ...), custom_call_target="tpu_custom_call" | custom-call | flops 6039797760 | bytes 23592960 | tf_op jit(solution)/shard_map/pallas_call | solution.py:359
  20.6 0.0 collective-permute-done.theirs_ref
  20.6 0.0 collective-permute-done.2.array_ref
  20.6 0.4 collective-permute-start.4
  21.0 4.0 %shard_map.125 = (f32[4608,256]{1,0:T(8,128)S(1)}, bf16[2,1152,1280]{2,1,0:T(8,128)(2,1)S(1)}) custom-call(f32[4608,256]{1,0:T(8,128)S(1)} %get-tuple-element.20.acc_in, bf16[256,1280]{1,0:T(8,128)(2,1)S(1)} %shard_map.124.og_ref, bf16[4,1152,1280]{2,1,0:T(8,128)(2,1)S(1)} %get-tuple-element.21.w_ref, ...), custom_call_target="tpu_custom_call", output_to_operand_aliasing={{0}: (0, {})} | custom-call | flops 3019898880 | bytes 11796480 | tf_op jit(solution)/shard_map/pallas_call | solution.py:388
  25.0 0.1 collective-permute-start.3
  25.1 0.0 collective-permute-done.4.og_ref
  25.1 6.1 %shard_map.127 = (f32[64,256]{1,0:T(8,128)S(1)}, f32[64,256]{1,0:T(8,128)S(1)}) custom-call(f32[4608,256]{1,0:T(8,128)S(1)} %get-tuple-element.23.acc_ref, bf16[256,1280]{1,0:T(8,128)(2,1)S(1)} %collective-permute-done.4.og_ref, bf16[1,1152,1280]{2,1,0:T(8,128)(2,1)S(1)} %get-tuple-element.19.token_ref.first_ref, ...), custom_call_target="tpu_custom_call" | custom-call | flops 3019898880 | bytes 11796480 | tf_op jit(solution)/shard_map/pallas_call | solution.py:402
  31.3 0.0 collective-permute-done.3.other_ref
  31.3 0.5 %shard_map.128 = f32[192,128]{1,0:T(8,128)S(1)} custom-call(f32[128,256]{1,0:T(8,128)S(1)} %shard_map.126.chip_ref, f32[128,256]{1,0:T(8,128)S(1)} %collective-permute-done.3.other_ref, f32[64,256]{1,0:T(8,128)S(1)} %get-tuple-element.26.gate_ref, f32[64,256]{1,0:T(8,128)S(1)} %get-tuple-element.27.up_ref, f32[64,256]{1,0:T(8,128)S(1)} %get-tuple-element.28.ph_ref), custom_call_target="tpu_custom_call" | custom-call | tf_op jit(solution)/shard_map/pallas_call | solution.py:411
  31.8 0.3 collective-permute-start.5
  32.1 1.1 %collective-permute-done.5 = f32[192,128]{1,0:T(8,128)S(1)} collective-permute-done((f32[192,128]{1,0:T(8,128)S(1)}, f32[192,128]{1,0:T(8,128)S(1)}, u32[]{:S(2)}, u32[]{:S(2)}) %collective-permute-start.5) | collective-permute-done | bytes 98336 | tf_op jit(solution)/shard_map/ppermute | solution.py:298
  33.2 2.1 %collective-permute-start.6 = (f32[192,128]{1,0:T(8,128)S(1)}, f32[192,128]{1,0:T(8,128)S(1)}, u32[]{:S(2)}, u32[]{:S(2)}) collective-permute-start(f32[192,128]{1,0:T(8,128)S(1)} %add.3.mine_ref), channel_id=1, source_target_pairs={{0,2},{1,3},{2,0},{3,1},{4,6},{5,7},{6,4},{7,5},{8,10},{9,11},{10,... | collective-permute-start | bytes 294920 | tf_op jit(solution)/shard_map/ppermute | solution.py:298
  35.2 3.1 %collective-permute-done.6.theirs_ref = f32[192,128]{1,0:T(8,128)S(1)} collective-permute-done((f32[192,128]{1,0:T(8,128)S(1)}, f32[192,128]{1,0:T(8,128)S(1)}, u32[]{:S(2)}, u32[]{:S(2)}) %collective-permute-start.6) | collective-permute-done | bytes 98336 | tf_op jit(solution)/shard_map/ppermute | solution.py:298
  38.3 0.7 %shard_map.129 = (f32[2,64,64]{2,1,0:T(8,128)}, f32[2,64,64]{2,1,0:T(8,128)}, f32[2,64,64]{2,1,0:T(8,128)}) custom-call(f32[192,128]{1,0:T(8,128)S(1)} %add.3.mine_ref, f32[192,128]{1,0:T(8,128)S(1)} %collective-permute-done.6.theirs_ref), custom_call_target="tpu_custom_call" | custom-call | tf_op jit(solution)/shard_map/pallas_call | solution.py:416
  (4 shorter events, 0.0 us)
Async XLA Ops:
  0.6 8.7 %collective-permute-start.1 = (bf16[256,1280]{1,0:T(8,128)(2,1)}, bf16[256,1280]{1,0:T(8,128)(2,1)S(1)}, u32[]{:S(2)}, u32[]{:S(2)}) collective-permute-start(bf16[256,1280]{1,0:T(8,128)(2,1)} %og_hbm.1), channel_id=1, source_target_pairs={{0,1},{1,0},{2,3},{3,2},{4,5},{5,4},{6,7},{7,6},{8,9},{9,8},{10,11... | collective-permute-start | bytes 1966088 | tf_op jit(solution)/shard_map/ppermute | solution.py:298
  1.2 19.5 %collective-permute-start.2 = (bf16[256,1280]{1,0:T(8,128)(2,1)}, bf16[256,1280]{1,0:T(8,128)(2,1)S(1)}, u32[]{:S(2)}, u32[]{:S(2)}) collective-permute-start(bf16[256,1280]{1,0:T(8,128)(2,1)} %og_hbm.1), channel_id=1, source_target_pairs={{0,2},{1,3},{2,0},{3,1},{4,6},{5,7},{6,4},{7,5},{8,10},{9,11},{10,... | collective-permute-start | bytes 1966088 | tf_op jit(solution)/shard_map/ppermute | solution.py:298
  9.1 11.5 %collective-permute-start = (f32[128,256]{1,0:T(8,128)S(1)}, f32[128,256]{1,0:T(8,128)S(1)}, u32[]{:S(2)}, u32[]{:S(2)}) collective-permute-start(f32[128,256]{1,0:T(8,128)S(1)} %get-tuple-element.16.mine_ref), channel_id=1, source_target_pairs={{0,1},{1,0},{2,3},{3,2},{4,5},{5,4},{6,7},{7,6},{8,9},{9,8},{10,11... | collective-permute-start | bytes 393224 | tf_op jit(solution)/shard_map/ppermute | solution.py:298
  20.6 4.5 %collective-permute-start.4 = (bf16[256,1280]{1,0:T(8,128)(2,1)S(1)}, bf16[256,1280]{1,0:T(8,128)(2,1)S(1)}, u32[]{:S(2)}, u32[]{:S(2)}) collective-permute-start(bf16[256,1280]{1,0:T(8,128)(2,1)S(1)} %shard_map.124.og_ref), channel_id=1, source_target_pairs={{0,1},{1,0},{2,3},{3,2},{4,5},{5,4},{6,7},{7,6},{8,9},{9,8},{10,11... | collective-permute-start | bytes 1966088 | tf_op jit(solution)/shard_map/ppermute | solution.py:298
  25.0 6.2 %collective-permute-start.3 = (f32[128,256]{1,0:T(8,128)S(1)}, f32[128,256]{1,0:T(8,128)S(1)}, u32[]{:S(2)}, u32[]{:S(2)}) collective-permute-start(f32[128,256]{1,0:T(8,128)S(1)} %shard_map.126.chip_ref), channel_id=1, source_target_pairs={{0,2},{1,3},{2,0},{3,1},{4,6},{5,7},{6,4},{7,5},{8,10},{9,11},{10,... | collective-permute-start | bytes 393224 | tf_op jit(solution)/shard_map/ppermute | solution.py:298
  31.8 1.4 %collective-permute-start.5 = (f32[192,128]{1,0:T(8,128)S(1)}, f32[192,128]{1,0:T(8,128)S(1)}, u32[]{:S(2)}, u32[]{:S(2)}) collective-permute-start(f32[192,128]{1,0:T(8,128)S(1)} %shard_map.128), channel_id=1, source_target_pairs={{0,1},{1,0},{2,3},{3,2},{4,5},{5,4},{6,7},{7,6},{8,9},{9,8},{10,11... | collective-permute-start | bytes 294920 | tf_op jit(solution)/shard_map/ppermute | solution.py:298
  33.2 5.2 %collective-permute-start.6 = (f32[192,128]{1,0:T(8,128)S(1)}, f32[192,128]{1,0:T(8,128)S(1)}, u32[]{:S(2)}, u32[]{:S(2)}) collective-permute-start(f32[192,128]{1,0:T(8,128)S(1)} %add.3.mine_ref), channel_id=1, source_target_pairs={{0,2},{1,3},{2,0},{3,1},{4,6},{5,7},{6,4},{7,5},{8,10},{9,11},{10,... | collective-permute-start | bytes 294920 | tf_op jit(solution)/shard_map/ppermute | solution.py:298

commit v12 on v11

--- a/solution.py
+++ b/solution.py
@@ -180,12 +180,11 @@
         wait(following.copies(i, head_ref.at[i], w_sems.at[i]))
 
 
-def chip_features_kernel(own_ref, mate_ref, head_ref, w_hbm, acc_ref, near_ref, far_ref, og_v, w_v, sems, near_sems, far_sems):
+def chip_features_kernel(own_ref, mate_ref, head_ref, w_hbm, acc_ref, near_ref, og_v, w_v, sems, near_sems):
     me = lax.axis_index("tensor")
     width = own_ref.shape[0]
     step = Step(me // 2, 2 * width, w_v.shape[1], w_hbm)
     near = Step(me ^ 2, width, near_ref.shape[1], w_hbm)
-    far = Step(me ^ 3, width, far_ref.shape[1], w_hbm)
     mine = pl.ds(pl.multiple_of(me % 2 * width, 128), width)
     theirs = pl.ds(pl.multiple_of((me + 1) % 2 * width, 128), width)
     og_v[mine] = own_ref[...]
@@ -195,39 +194,46 @@
         acc_ref[step.units(i)] = product(weights[...], og_v[...])
 
     later = [near.copies(k, near_ref.at[k], near_sems.at[k]) for k in range(near_ref.shape[0])]
-    later += [far.copies(k, far_ref.at[k], far_sems.at[k]) for k in range(far_ref.shape[0])]
     stream(step, 3, acc_ref.shape[0] // step.block, head_ref, w_v, sems, body, later)
 
 
-def near_kernel(acc_in, og_ref, w_ref, w_hbm, acc_ref, far_ref, og_v, sems):
+def near_kernel(acc_in, og_ref, head_ref, w_hbm, acc_ref, far_ref, og_v, w_v, sems, far_sems):
     me = lax.axis_index("tensor")
-    blocks, block, width = w_ref.shape
-    far = Step(me ^ 3, width, block, w_hbm)
-    copies = [far.copies(k + 1, far_ref.at[k], sems.at[k]) for k in range(far_ref.shape[0])]
-    for group in copies:
+    heads, block, width = head_ref.shape
+    near, far = Step(me ^ 2, width, block, w_hbm), Step(me ^ 3, width, block, w_hbm)
+    rest = [near.copies(heads + k, w_v.at[k], sems.at[k]) for k in range(w_v.shape[0])]
+    later = [far.copies(k, far_ref.at[k], far_sems.at[k]) for k in range(far_ref.shape[0])]
+    for group in rest + later:
         start(group)
     og_v[...] = og_ref[...].T
 
-    @pl.loop(0, blocks)
-    def _(i):
-        at = far.units(i)
-        acc_ref[at] = acc_in[at] + product(w_ref[i], og_v[...])
-
-    for group in copies:
+    def body(i, weights):
+        at = near.units(i)
+        acc_ref[at] = acc_in[at] + product(weights, og_v[...])
+
+    @pl.loop(0, heads)
+    def _(i):
+        body(i, head_ref[i])
+
+    for group in rest:
         wait(group)
 
-
-def far_kernel(acc_ref, og_ref, first_ref, second_ref, w_hbm, a_ref, b_ref, gf_hbm, uf_hbm, gate_ref, up_ref,
+    @pl.loop(0, w_v.shape[0])
+    def _(i):
+        body(heads + i, w_v[i])
+
+    for group in later:
+        wait(group)
+
+
+def far_kernel(acc_ref, og_ref, head_ref, w_hbm, a_ref, b_ref, gf_hbm, uf_hbm, gate_ref, up_ref,
                og_v, w_v, gf_ref, uf_ref, d_gate_v, d_up_v, sems, factor_sems):
-    _, block, width = w_v.shape
+    heads, block, width = head_ref.shape
     step = Step(lax.axis_index("tensor") ^ 3, width, block, w_hbm)
     factors = [
         pltpu.make_async_copy(src, dst, factor_sems.at[k]) for k, (src, dst) in enumerate(((gf_hbm, gf_ref), (uf_hbm, uf_ref)))
     ]
-    held = first_ref.shape[0] + second_ref.shape[0]
-    copies = [step.copies(held + k, w_v.at[k], sems.at[k]) for k in range(w_v.shape[0])]
-    for group in copies:
-        start(group)
+    start(step.copies(heads, w_v.at[0], sems.at[0]))
     start(factors)
     og_v[...] = og_ref[...].T
 
@@ -237,20 +243,18 @@
         d_gate_v[at] = (hidden_grad * a_ref[at]).astype(BF16)
         d_up_v[at] = (hidden_grad * b_ref[at]).astype(BF16)
 
-    @pl.loop(0, first_ref.shape[0])
-    def _(i):
-        body(i, first_ref[i])
-
-    @pl.loop(0, second_ref.shape[0])
-    def _(i):
-        body(first_ref.shape[0] + i, second_ref[i])
-
-    for group in copies:
-        wait(group)
+    @pl.loop(0, heads)
+    def _(i):
+        @pl.when((i > 0) & (i < w_v.shape[0]))
+        def _():
+            start(step.copies(heads + i, w_v.at[i], sems.at[i]))
+
+        body(i, head_ref[i])
 
     @pl.loop(0, w_v.shape[0])
     def _(i):
-        body(held + i, w_v[i])
+        wait(step.copies(heads + i, w_v.at[i], sems.at[i]))
+        body(heads + i, w_v[i])
 
     wait(factors)
     gate_ref[...] = product(gf_ref[...], d_gate_v[...])
@@ -279,7 +283,7 @@
 
 def sum_kernel(mine_ref, theirs_ref, gate_ref, up_ref, down_ref):
     rank = gate_ref.shape[1]
-    total = mine_ref[...] + theirs_ref[...]
+    total = mine_ref[...].astype(F32) + theirs_ref[...].astype(F32)
     for s in range(SEQS):
         gate_ref[s] = total[s * rank : (s + 1) * rank, :rank]
         up_ref[s] = total[s * rank : (s + 1) * rank, rank:]
@@ -356,16 +360,15 @@
         in_hbm(h_factor.T),
     )
     pq_mate = swap(pq, 1)
-    acc, w_near, far_first = call(
+    acc, head = call(
         chip_features_kernel,
-        (held, blocks(turns), blocks(1)),
+        (held, blocks(turns - 1)),
         [VMEM] * 3 + [ANY],
         [
             pltpu.VMEM((2 * width, tokens), BF16),
             chip_blocks(4),
             dma((units // CHIP_BLOCK, PARTS)),
-            dma((turns, PARTS)),
-            dma((1, PARTS)),
+            dma((turns - 1, PARTS)),
         ],
         14,
         2 * per_product,
@@ -382,36 +385,36 @@
             compiler_params=pltpu.CompilerParams(vmem_limit_bytes=MIB),
         )(array, token)
 
-    chip = call(chip_kernel, pltpu.VMEM(pq.shape, F32), [VMEM, VMEM, ANY], [], 1)(pq, pq_mate, far_first)
+    chip = call(chip_kernel, pltpu.VMEM(pq.shape, F32), [VMEM, VMEM, ANY], [], 1)(pq, pq_mate, head)
     near = after(near, chip)
     far = swap(near, 1)
-    acc, far_second = call(
+    acc, head = call(
         near_kernel,
         (held, blocks(2)),
         [VMEM] * 3 + [ANY],
-        [turned, dma((2, PARTS))],
-        4,
+        [turned, blocks(1), dma((1, PARTS)), dma((2, PARTS))],
+        6,
         per_product,
         2 * units * width,
         input_output_aliases={0: 0},
-    )(acc, near, w_near, weight)
-    chip = after(chip, far_second)
+    )(acc, near, head, weight)
+    chip = after(chip, head)
     chip_across = swap(chip, 2)
     factor = pltpu.VMEM((rank, units), BF16)
     kept = pltpu.VMEM((units, tokens), BF16)
     q_gate, q_up = call(
         far_kernel,
         (narrow, narrow),
-        [VMEM] * 4 + [ANY] + [VMEM] * 2 + [ANY] * 2,
-        [turned, blocks(turns - 3), factor, factor, kept, kept, dma((turns - 3, PARTS)), dma((2,))],
-        14,
+        [VMEM] * 3 + [ANY] + [VMEM] * 2 + [ANY] * 2,
+        [turned, blocks(turns - 2), factor, factor, kept, kept, dma((turns - 2, PARTS)), dma((2,))],
+        16,
         per_product,
         2 * units * width,
-    )(acc, far, far_first, far_second, weight, a, b, in_hbm(gate_factor.T), in_hbm(up_factor.T))
+    )(acc, far, head, weight, a, b, in_hbm(gate_factor.T), in_hbm(up_factor.T))
     share = call(gradients_kernel, pltpu.VMEM(((SEQS + 1) * rank, 2 * rank), F32), [VMEM] * 5, [], 4)(
         chip, chip_across, q_gate, q_up, ph
     )
-    chip_share = share + swap(share, 1)
+    chip_share = (share + swap(share, 1)).astype(BF16)
     out = jax.ShapeDtypeStruct((SEQS, rank, rank), F32)
     return call(sum_kernel, (out, out, out), [VMEM] * 2, [], 4)(chip_share, swap(chip_share, 2))
 
@@ -425,7 +428,7 @@
             and width % 128 == 0
             and units % BLOCK == 0
             and units % CHIP_BLOCK == 0
-            and units // BLOCK > 3
+            and units // BLOCK == 4
         )
         return tuple((fast if fits else plain)(*arrays))
 

time: 39.2 us -> 37.7 us (0.962)
  Pallas kernels: 28 us -> 25.8 us
  waiting for transfers between devices: 4.22 us -> 5.13 us
    pallas_call x3, Pallas kernels: 21.4 us -> 19.1 us  [the longest x1 9.49 us: fast(): call(chip_features_kernel, (held, blocks(turns - 1)), [VMEM] * 3 + [ANY],...]
    ppermute x7, waiting for transfers between devices: 4.22 us -> 5.13 us  [swap(): return lax.ppermute(array, 'tensor', [(i, i ^ bits) for i in range(4)])]
  transfers between devices with their start and end apart: 7 -> 7, of which waited for: 2 -> 3; matrix products, arithmetic and copies ran while one was open for 0% -> 0% of each run, Pallas kernels for 68% -> 65%
where the time goes in v12:
time: 37.7 us; the launch traced here: 37.6 us
  Pallas kernels  25.8 us (68%)
  starting transfers between devices  5.95 us (16%)
  waiting for transfers between devices  5.13 us (14%)
  between operations  0.71 us (2%)
    pallas_call x1, Pallas kernels, fast(): call(chip_features_kernel, (held, blocks(turns - 1)), [VMEM] * 3 + [ANY],...  9.49 us
    ppermute x7, starting transfers between devices, swap(): return lax.ppermute(array, 'tensor', [(i, i ^ bits) for i in range(4)])  5.95 us
    pallas_call x1, Pallas kernels, fast(): call(far_kernel, (narrow, narrow), [VMEM] * 3 + [ANY] + [VMEM] * 2 + [ANY...  5.45 us
    pallas_call x1, Pallas kernels, fast(): call(elementwise_kernel, (held, held, narrow, pltpu.VMEM((2 * rank, token...  5.35 us
    ppermute x7, waiting for transfers between devices, swap(): return lax.ppermute(array, 'tensor', [(i, i ^ bits) for i in range(4)])  5.13 us
    pallas_call x1, Pallas kernels, fast(): call(near_kernel, (held, blocks(2)), [VMEM] * 3 + [ANY], [turned, blocks(...  4.21 us
  transfers between devices with their start and end apart: 7, of which 3 were waited for; matrix products, arithmetic and copies ran while one was open for 0% of the time, Pallas kernels for 65%

profile of v12, /device:TPU:0, one launch (start us, length us, event | category | flops | bytes accessed | tf_op | source)
XLA Modules:
  0.0 37.6 jit_solution(9097066123524429187)
XLA Ops:
  0.6 0.5 %collective-permute-start.1 = (bf16[256,1280]{1,0:T(8,128)(2,1)}, bf16[256,1280]{1,0:T(8,128)(2,1)S(1)}, u32[]{:S(2)}, u32[]{:S(2)}) collective-permute-start(bf16[256,1280]{1,0:T(8,128)(2,1)} %og_hbm.1), channel_id=1, source_target_pairs={{0,1},{1,0},{2,3},{3,2},{4,5},{5,4},{6,7},{7,6},{8,9},{9,8},{10,11... | collective-permute-start | bytes 1966088 | tf_op jit(solution)/shard_map/ppermute | solution.py:302
  1.2 2.6 %collective-permute-start.2 = (bf16[256,1280]{1,0:T(8,128)(2,1)}, bf16[256,1280]{1,0:T(8,128)(2,1)S(1)}, u32[]{:S(2)}, u32[]{:S(2)}) collective-permute-start(bf16[256,1280]{1,0:T(8,128)(2,1)} %og_hbm.1), channel_id=1, source_target_pairs={{0,2},{1,3},{2,0},{3,1},{4,6},{5,7},{6,4},{7,5},{8,10},{9,11},{10,... | collective-permute-start | bytes 1966088 | tf_op jit(solution)/shard_map/ppermute | solution.py:302
  3.7 5.4 %shard_map.121 = (f32[4608,256]{1,0:T(8,128)S(1)}, f32[4608,256]{1,0:T(8,128)S(1)}, f32[64,256]{1,0:T(8,128)S(1)}, f32[128,256]{1,0:T(8,128)S(1)}, bf16[2,512,25...) custom-call(bf16[256,1280]{1,0:T(8,128)(2,1)} %x_hbm.1, bf16[256,1280]{1,0:T(8,128)(2,1)} %og_hbm.1, ...), custom_call_target="tpu_custom_call" | custom-call | flops 754974720 | bytes 4718592 | tf_op jit(solution)/shard_map/pallas_call | solution.py:332
  9.1 0.2 collective-permute-start
  9.3 0.0 collective-permute-done.1.mate_ref
  9.3 9.5 %shard_map.122 = (f32[4608,256]{1,0:T(8,128)S(1)}, bf16[3,1152,1280]{2,1,0:T(8,128)(2,1)S(1)}) custom-call(bf16[1280,256]{1,0:T(8,128)(2,1)S(1)} %get-tuple-element.16.own_ref, bf16[256,1280]{1,0:T(8,128)(2,1)S(1)} %collective-permute-done.1.mate_ref, bf16[2,512,2560]{2,1,0:T(8,128)(2,1)S(1)} %get-tuple-element.17.head_ref, bf16[4608,5120]{1,0:T(8,128)(2,1)} %w_hbm.7), custom_call_target="tpu_custom_call" | custom-call | flops 6039797760 | bytes 23592960 | tf_op jit(solution)/shard_map/pallas_call | solution.py:363
  18.8 0.0 collective-permute-done.theirs_ref
  18.8 0.4 %collective-permute-done.2.array_ref = bf16[256,1280]{1,0:T(8,128)(2,1)S(1)} collective-permute-done((bf16[256,1280]{1,0:T(8,128)(2,1)}, bf16[256,1280]{1,0:T(8,128)(2,1)S(1)}, u32[]{:S(2)}, u32[]{:S(2)}) %collective-permute-start.2) | collective-permute-done | bytes 655392 | tf_op jit(solution)/shard_map/ppermute | solution.py:302
  19.3 0.0 collective-permute-start.4
  19.3 4.2 %shard_map.125 = (f32[4608,256]{1,0:T(8,128)S(1)}, bf16[2,1152,1280]{2,1,0:T(8,128)(2,1)S(1)}) custom-call(f32[4608,256]{1,0:T(8,128)S(1)} %get-tuple-element.19.acc_in, bf16[256,1280]{1,0:T(8,128)(2,1)S(1)} %shard_map.124.og_ref, bf16[3,1152,1280]{2,1,0:T(8,128)(2,1)S(1)} %get-tuple-element.18.token_ref.head_ref, ...), custom_call_target="tpu_custom_call", output_to_operand_aliasing={{0}: (0, {})} | custom-call | flops 3019898880 | bytes 11796480 | tf_op jit(solution)/shard_map/pallas_call | solution.py:391
  23.5 1.8 %collective-permute-start.3 = (f32[128,256]{1,0:T(8,128)S(1)}, f32[128,256]{1,0:T(8,128)S(1)}, u32[]{:S(2)}, u32[]{:S(2)}) collective-permute-start(f32[128,256]{1,0:T(8,128)S(1)} %shard_map.126.chip_ref), channel_id=1, source_target_pairs={{0,2},{1,3},{2,0},{3,1},{4,6},{5,7},{6,4},{7,5},{8,10},{9,11},{10,... | collective-permute-start | bytes 393224 | tf_op jit(solution)/shard_map/ppermute | solution.py:302
  25.3 0.0 collective-permute-done.4.og_ref
  25.3 5.4 %shard_map.127 = (f32[64,256]{1,0:T(8,128)S(1)}, f32[64,256]{1,0:T(8,128)S(1)}) custom-call(f32[4608,256]{1,0:T(8,128)S(1)} %get-tuple-element.21.acc_ref, bf16[256,1280]{1,0:T(8,128)(2,1)S(1)} %collective-permute-done.4.og_ref, bf16[2,1152,1280]{2,1,0:T(8,128)(2,1)S(1)} %get-tuple-element.20.token_ref.head_ref, bf16[4608,5120]{1,0:T(8,128)(2,1)} %w_hbm.7, ...), custom_call_target="tpu_custom_call" | custom-call | flops 3019898880 | bytes 11796480 | tf_op jit(solution)/shard_map/pallas_call | solution.py:405
  30.8 0.0 collective-permute-done.3.other_ref
  30.8 0.5 %shard_map.128 = f32[192,128]{1,0:T(8,128)S(1)} custom-call(f32[128,256]{1,0:T(8,128)S(1)} %shard_map.126.chip_ref, f32[128,256]{1,0:T(8,128)S(1)} %collective-permute-done.3.other_ref, f32[64,256]{1,0:T(8,128)S(1)} %get-tuple-element.24.gate_ref, f32[64,256]{1,0:T(8,128)S(1)} %get-tuple-element.25.up_ref, f32[64,256]{1,0:T(8,128)S(1)} %get-tuple-element.26.ph_ref), custom_call_target="tpu_custom_call" | custom-call | tf_op jit(solution)/shard_map/pallas_call | solution.py:414
  31.3 0.3 collective-permute-start.5
  31.6 1.1 %collective-permute-done.5 = f32[192,128]{1,0:T(8,128)S(1)} collective-permute-done((f32[192,128]{1,0:T(8,128)S(1)}, f32[192,128]{1,0:T(8,128)S(1)}, u32[]{:S(2)}, u32[]{:S(2)}) %collective-permute-start.5) | collective-permute-done | bytes 98336 | tf_op jit(solution)/shard_map/ppermute | solution.py:302
  32.7 0.5 %collective-permute-start.6 = (bf16[192,128]{1,0:T(8,128)(2,1)S(1)}, bf16[192,128]{1,0:T(8,128)(2,1)S(1)}, u32[]{:S(2)}, u32[]{:S(2)}) collective-permute-start(bf16[192,128]{1,0:T(8,128)(2,1)S(1)} %add_convert_fusion.mine_ref), channel_id=1, source_target_pairs={{0,2},{1,3},{2,0},{3,1},{4,6},{5,7},{6,4},{7,5},{8,10},{9,11},{10,... | collective-permute-start | bytes 147464 | tf_op jit(solution)/shard_map/ppermute | solution.py:302
  33.2 3.6 %collective-permute-done.6.theirs_ref = bf16[192,128]{1,0:T(8,128)(2,1)S(1)} collective-permute-done((bf16[192,128]{1,0:T(8,128)(2,1)S(1)}, bf16[192,128]{1,0:T(8,128)(2,1)S(1)}, u32[]{:S(2)}, u32[]{:S(2)}) %collective-permute-start.6) | collective-permute-done | bytes 49184 | tf_op jit(solution)/shard_map/ppermute | solution.py:302
  36.8 0.7 %shard_map.129 = (f32[2,64,64]{2,1,0:T(8,128)}, f32[2,64,64]{2,1,0:T(8,128)}, f32[2,64,64]{2,1,0:T(8,128)}) custom-call(bf16[192,128]{1,0:T(8,128)(2,1)S(1)} %add_convert_fusion.mine_ref, bf16[192,128]{1,0:T(8,128)(2,1)S(1)} %collective-permute-done.6.theirs_ref), custom_call_target="tpu_custom_call" | custom-call | tf_op jit(solution)/shard_map/pallas_call | solution.py:419
  (4 shorter events, 0.0 us)
Async XLA Ops:
  0.6 8.7 %collective-permute-start.1 = (bf16[256,1280]{1,0:T(8,128)(2,1)}, bf16[256,1280]{1,0:T(8,128)(2,1)S(1)}, u32[]{:S(2)}, u32[]{:S(2)}) collective-permute-start(bf16[256,1280]{1,0:T(8,128)(2,1)} %og_hbm.1), channel_id=1, source_target_pairs={{0,1},{1,0},{2,3},{3,2},{4,5},{5,4},{6,7},{7,6},{8,9},{9,8},{10,11... | collective-permute-start | bytes 1966088 | tf_op jit(solution)/shard_map/ppermute | solution.py:302
  1.2 18.1 %collective-permute-start.2 = (bf16[256,1280]{1,0:T(8,128)(2,1)}, bf16[256,1280]{1,0:T(8,128)(2,1)S(1)}, u32[]{:S(2)}, u32[]{:S(2)}) collective-permute-start(bf16[256,1280]{1,0:T(8,128)(2,1)} %og_hbm.1), channel_id=1, source_target_pairs={{0,2},{1,3},{2,0},{3,1},{4,6},{5,7},{6,4},{7,5},{8,10},{9,11},{10,... | collective-permute-start | bytes 1966088 | tf_op jit(solution)/shard_map/ppermute | solution.py:302
  9.1 9.7 %collective-permute-start = (f32[128,256]{1,0:T(8,128)S(1)}, f32[128,256]{1,0:T(8,128)S(1)}, u32[]{:S(2)}, u32[]{:S(2)}) collective-permute-start(f32[128,256]{1,0:T(8,128)S(1)} %get-tuple-element.15.mine_ref), channel_id=1, source_target_pairs={{0,1},{1,0},{2,3},{3,2},{4,5},{5,4},{6,7},{7,6},{8,9},{9,8},{10,11... | collective-permute-start | bytes 393224 | tf_op jit(solution)/shard_map/ppermute | solution.py:302
  19.3 6.1 %collective-permute-start.4 = (bf16[256,1280]{1,0:T(8,128)(2,1)S(1)}, bf16[256,1280]{1,0:T(8,128)(2,1)S(1)}, u32[]{:S(2)}, u32[]{:S(2)}) collective-permute-start(bf16[256,1280]{1,0:T(8,128)(2,1)S(1)} %shard_map.124.og_ref), channel_id=1, source_target_pairs={{0,1},{1,0},{2,3},{3,2},{4,5},{5,4},{6,7},{7,6},{8,9},{9,8},{10,11... | collective-permute-start | bytes 1966088 | tf_op jit(solution)/shard_map/ppermute | solution.py:302
  23.5 7.3 %collective-permute-start.3 = (f32[128,256]{1,0:T(8,128)S(1)}, f32[128,256]{1,0:T(8,128)S(1)}, u32[]{:S(2)}, u32[]{:S(2)}) collective-permute-start(f32[128,256]{1,0:T(8,128)S(1)} %shard_map.126.chip_ref), channel_id=1, source_target_pairs={{0,2},{1,3},{2,0},{3,1},{4,6},{5,7},{6,4},{7,5},{8,10},{9,11},{10,... | collective-permute-start | bytes 393224 | tf_op jit(solution)/shard_map/ppermute | solution.py:302
  31.3 1.4 %collective-permute-start.5 = (f32[192,128]{1,0:T(8,128)S(1)}, f32[192,128]{1,0:T(8,128)S(1)}, u32[]{:S(2)}, u32[]{:S(2)}) collective-permute-start(f32[192,128]{1,0:T(8,128)S(1)} %shard_map.128), channel_id=1, source_target_pairs={{0,1},{1,0},{2,3},{3,2},{4,5},{5,4},{6,7},{7,6},{8,9},{9,8},{10,11... | collective-permute-start | bytes 294920 | tf_op jit(solution)/shard_map/ppermute | solution.py:302
  32.7 4.2 %collective-permute-start.6 = (bf16[192,128]{1,0:T(8,128)(2,1)S(1)}, bf16[192,128]{1,0:T(8,128)(2,1)S(1)}, u32[]{:S(2)}, u32[]{:S(2)}) collective-permute-start(bf16[192,128]{1,0:T(8,128)(2,1)S(1)} %add_convert_fusion.mine_ref), channel_id=1, source_target_pairs={{0,2},{1,3},{2,0},{3,1},{4,6},{5,7},{6,4},{7,5},{8,10},{9,11},{10,... | collective-permute-start | bytes 147464 | tf_op jit(solution)/shard_map/ppermute | solution.py:302

commit v13 on v12

--- a/solution.py
+++ b/solution.py
@@ -226,12 +226,14 @@
         wait(group)
 
 
-def far_kernel(acc_ref, og_ref, head_ref, w_hbm, a_ref, b_ref, gf_hbm, uf_hbm, gate_ref, up_ref,
-               og_v, w_v, gf_ref, uf_ref, d_gate_v, d_up_v, sems, factor_sems):
+def far_kernel(acc_ref, og_ref, head_ref, w_hbm, a_ref, b_ref, gf_hbm, uf_hbm, q_ref,
+               og_v, w_v, factors_v, d_v, sems, factor_sems):
     heads, block, width = head_ref.shape
     step = Step(lax.axis_index("tensor") ^ 3, width, block, w_hbm)
+    rank, tokens = q_ref.shape[0] // 2, q_ref.shape[1]
     factors = [
-        pltpu.make_async_copy(src, dst, factor_sems.at[k]) for k, (src, dst) in enumerate(((gf_hbm, gf_ref), (uf_hbm, uf_ref)))
+        pltpu.make_async_copy(src, factors_v.at[pl.ds(k * rank, rank)], factor_sems.at[k])
+        for k, src in enumerate((gf_hbm, uf_hbm))
     ]
     start(step.copies(heads, w_v.at[0], sems.at[0]))
     start(factors)
@@ -240,8 +242,8 @@
     def body(i, weights):
         at = step.units(i)
         hidden_grad = acc_ref[at] + product(weights, og_v[...])
-        d_gate_v[at] = (hidden_grad * a_ref[at]).astype(BF16)
-        d_up_v[at] = (hidden_grad * b_ref[at]).astype(BF16)
+        d_v[at, :tokens] = (hidden_grad * a_ref[at]).astype(BF16)
+        d_v[at, tokens:] = (hidden_grad * b_ref[at]).astype(BF16)
 
     @pl.loop(0, heads)
     def _(i):
@@ -257,8 +259,9 @@
         body(heads + i, w_v[i])
 
     wait(factors)
-    gate_ref[...] = product(gf_ref[...], d_gate_v[...])
-    up_ref[...] = product(uf_ref[...], d_up_v[...])
+    both = product(factors_v[...], d_v[...])
+    q_ref[:rank] = both[:rank, :tokens]
+    q_ref[rank:] = both[rank:, tokens:]
 
 
 def after_kernel(array_ref, token_ref, same_ref):
@@ -269,15 +272,14 @@
     chip_ref[...] = mine_ref[...] + theirs_ref[...]
 
 
-def gradients_kernel(chip_ref, other_ref, gate_ref, up_ref, ph_ref, share_ref):
+def gradients_kernel(chip_ref, other_ref, q_ref, ph_ref, share_ref):
     rank = ph_ref.shape[0]
     total = chip_ref[...] + other_ref[...]
     highest = lax.Precision.HIGHEST
     for s in range(SEQS):
         at = slice(s * LEN, (s + 1) * LEN)
         out = slice(s * rank, (s + 1) * rank)
-        share_ref[out, :rank] = rows_by_rows(total[:rank, at], gate_ref[:, at], highest)
-        share_ref[out, rank:] = rows_by_rows(total[:rank, at], up_ref[:, at], highest)
+        share_ref[out] = rows_by_rows(total[:rank, at], q_ref[:, at], highest)
         share_ref[SEQS * rank :, out] = rows_by_rows(ph_ref[:, at], total[rank:, at], highest)
 
 
@@ -400,20 +402,16 @@
     )(acc, near, head, weight)
     chip = after(chip, head)
     chip_across = swap(chip, 2)
-    factor = pltpu.VMEM((rank, units), BF16)
-    kept = pltpu.VMEM((units, tokens), BF16)
-    q_gate, q_up = call(
+    q = call(
         far_kernel,
-        (narrow, narrow),
+        pltpu.VMEM((2 * rank, tokens), F32),
         [VMEM] * 3 + [ANY] + [VMEM] * 2 + [ANY] * 2,
-        [turned, blocks(turns - 2), factor, factor, kept, kept, dma((turns - 2, PARTS)), dma((2,))],
+        [turned, blocks(turns - 2), pltpu.VMEM((2 * rank, units), BF16), pltpu.VMEM((units, 2 * tokens), BF16), dma((turns - 2, PARTS)), dma((2,))],
         16,
         per_product,
         2 * units * width,
     )(acc, far, head, weight, a, b, in_hbm(gate_factor.T), in_hbm(up_factor.T))
-    share = call(gradients_kernel, pltpu.VMEM(((SEQS + 1) * rank, 2 * rank), F32), [VMEM] * 5, [], 4)(
-        chip, chip_across, q_gate, q_up, ph
-    )
+    share = call(gradients_kernel, pltpu.VMEM(((SEQS + 1) * rank, 2 * rank), F32), [VMEM] * 4, [], 4)(chip, chip_across, q, ph)
     chip_share = (share + swap(share, 1)).astype(BF16)
     out = jax.ShapeDtypeStruct((SEQS, rank, rank), F32)
     return call(sum_kernel, (out, out, out), [VMEM] * 2, [], 4)(chip_share, swap(chip_share, 2))

time: 37.7 us -> 37.9 us (level)
  transfers between devices with their start and end apart: 7 -> 7, of which waited for: 3 -> 3; matrix products, arithmetic and copies ran while one was open for 0% -> 0% of each run, Pallas kernels for 65% -> 66%
where the time goes in v13:
time: 37.9 us; the launch traced here: 37.7 us
  Pallas kernels  26 us (69%)
  starting transfers between devices  5.74 us (15%)
  waiting for transfers between devices  5.29 us (14%)
  between operations  0.71 us (2%)
    pallas_call x1, Pallas kernels, fast(): call(chip_features_kernel, (held, blocks(turns - 1)), [VMEM] * 3 + [ANY],...  9.49 us
    ppermute x7, starting transfers between devices, swap(): return lax.ppermute(array, 'tensor', [(i, i ^ bits) for i in range(4)])  5.74 us
    pallas_call x1, Pallas kernels, fast(): call(far_kernel, pltpu.VMEM((2 * rank, tokens), F32), [VMEM] * 3 + [ANY]...  5.64 us
    pallas_call x1, Pallas kernels, fast(): call(elementwise_kernel, (held, held, narrow, pltpu.VMEM((2 * rank, token...  5.35 us
    ppermute x7, waiting for transfers between devices, swap(): return lax.ppermute(array, 'tensor', [(i, i ^ bits) for i in range(4)])  5.29 us
    pallas_call x1, Pallas kernels, fast(): call(near_kernel, (held, blocks(2)), [VMEM] * 3 + [ANY], [turned, blocks(...  4.21 us
  transfers between devices with their start and end apart: 7, of which 3 were waited for; matrix products, arithmetic and copies ran while one was open for 0% of the time, Pallas kernels for 66%

profile of v13, /device:TPU:0, one launch (start us, length us, event | category | flops | bytes accessed | tf_op | source)
XLA Modules:
  0.0 37.7 jit_solution(3806866201013472540)
XLA Ops:
  0.6 0.5 %collective-permute-start.1 = (bf16[256,1280]{1,0:T(8,128)(2,1)}, bf16[256,1280]{1,0:T(8,128)(2,1)S(1)}, u32[]{:S(2)}, u32[]{:S(2)}) collective-permute-start(bf16[256,1280]{1,0:T(8,128)(2,1)} %og_hbm.1), channel_id=1, source_target_pairs={{0,1},{1,0},{2,3},{3,2},{4,5},{5,4},{6,7},{7,6},{8,9},{9,8},{10,11... | collective-permute-start | bytes 1966088 | tf_op jit(solution)/shard_map/ppermute | solution.py:304
  1.2 2.6 %collective-permute-start.2 = (bf16[256,1280]{1,0:T(8,128)(2,1)}, bf16[256,1280]{1,0:T(8,128)(2,1)S(1)}, u32[]{:S(2)}, u32[]{:S(2)}) collective-permute-start(bf16[256,1280]{1,0:T(8,128)(2,1)} %og_hbm.1), channel_id=1, source_target_pairs={{0,2},{1,3},{2,0},{3,1},{4,6},{5,7},{6,4},{7,5},{8,10},{9,11},{10,... | collective-permute-start | bytes 1966088 | tf_op jit(solution)/shard_map/ppermute | solution.py:304
  3.7 5.4 %shard_map.121 = (f32[4608,256]{1,0:T(8,128)S(1)}, f32[4608,256]{1,0:T(8,128)S(1)}, f32[64,256]{1,0:T(8,128)S(1)}, f32[128,256]{1,0:T(8,128)S(1)}, bf16[2,512,25...) custom-call(bf16[256,1280]{1,0:T(8,128)(2,1)} %x_hbm.1, bf16[256,1280]{1,0:T(8,128)(2,1)} %og_hbm.1, ...), custom_call_target="tpu_custom_call" | custom-call | flops 754974720 | bytes 4718592 | tf_op jit(solution)/shard_map/pallas_call | solution.py:334
  9.1 0.2 collective-permute-start
  9.3 0.0 collective-permute-done.1.mate_ref
  9.3 9.5 %shard_map.122 = (f32[4608,256]{1,0:T(8,128)S(1)}, bf16[3,1152,1280]{2,1,0:T(8,128)(2,1)S(1)}) custom-call(bf16[1280,256]{1,0:T(8,128)(2,1)S(1)} %get-tuple-element.14.own_ref, bf16[256,1280]{1,0:T(8,128)(2,1)S(1)} %collective-permute-done.1.mate_ref, bf16[2,512,2560]{2,1,0:T(8,128)(2,1)S(1)} %get-tuple-element.15.head_ref, bf16[4608,5120]{1,0:T(8,128)(2,1)} %w_hbm.7), custom_call_target="tpu_custom_call" | custom-call | flops 6039797760 | bytes 23592960 | tf_op jit(solution)/shard_map/pallas_call | solution.py:365
  18.8 0.0 collective-permute-done.theirs_ref
  18.8 0.4 %collective-permute-done.2.array_ref = bf16[256,1280]{1,0:T(8,128)(2,1)S(1)} collective-permute-done((bf16[256,1280]{1,0:T(8,128)(2,1)}, bf16[256,1280]{1,0:T(8,128)(2,1)S(1)}, u32[]{:S(2)}, u32[]{:S(2)}) %collective-permute-start.2) | collective-permute-done | bytes 655392 | tf_op jit(solution)/shard_map/ppermute | solution.py:304
  19.3 0.0 collective-permute-start.4
  19.3 4.2 %shard_map.125 = (f32[4608,256]{1,0:T(8,128)S(1)}, bf16[2,1152,1280]{2,1,0:T(8,128)(2,1)S(1)}) custom-call(f32[4608,256]{1,0:T(8,128)S(1)} %get-tuple-element.17.acc_in, bf16[256,1280]{1,0:T(8,128)(2,1)S(1)} %shard_map.124.og_ref, bf16[3,1152,1280]{2,1,0:T(8,128)(2,1)S(1)} %get-tuple-element.16.token_ref.head_ref, ...), custom_call_target="tpu_custom_call", output_to_operand_aliasing={{0}: (0, {})} | custom-call | flops 3019898880 | bytes 11796480 | tf_op jit(solution)/shard_map/pallas_call | solution.py:393
  23.5 1.8 %collective-permute-start.3 = (f32[128,256]{1,0:T(8,128)S(1)}, f32[128,256]{1,0:T(8,128)S(1)}, u32[]{:S(2)}, u32[]{:S(2)}) collective-permute-start(f32[128,256]{1,0:T(8,128)S(1)} %shard_map.126.chip_ref), channel_id=1, source_target_pairs={{0,2},{1,3},{2,0},{3,1},{4,6},{5,7},{6,4},{7,5},{8,10},{9,11},{10,... | collective-permute-start | bytes 393224 | tf_op jit(solution)/shard_map/ppermute | solution.py:304
  25.3 0.0 collective-permute-done.4.og_ref
  25.3 5.6 %shard_map.127.q_ref = f32[128,256]{1,0:T(8,128)S(1)} custom-call(f32[4608,256]{1,0:T(8,128)S(1)} %get-tuple-element.19.acc_ref, bf16[256,1280]{1,0:T(8,128)(2,1)S(1)} %collective-permute-done.4.og_ref, bf16[2,1152,1280]{2,1,0:T(8,128)(2,1)S(1)} %get-tuple-element.18.token_ref.head_ref, bf16[4608,5120]{1,0:T(8,128)(2,1)} %w_hbm.7, ...), custom_call_target="tpu_custom_call" | custom-call | flops 3019898880 | bytes 11796480 | tf_op jit(solution)/shard_map/pallas_call | solution.py:405
  31.0 0.0 collective-permute-done.3.other_ref
  31.0 0.5 %shard_map.128 = f32[192,128]{1,0:T(8,128)S(1)} custom-call(f32[128,256]{1,0:T(8,128)S(1)} %shard_map.126.chip_ref, f32[128,256]{1,0:T(8,128)S(1)} %collective-permute-done.3.other_ref, f32[128,256]{1,0:T(8,128)S(1)} %shard_map.127.q_ref, f32[64,256]{1,0:T(8,128)S(1)} %get-tuple-element.22.ph_ref), custom_call_target="tpu_custom_call" | custom-call | tf_op jit(solution)/shard_map/pallas_call | solution.py:414
  31.5 0.2 collective-permute-start.5
  31.7 1.1 %collective-permute-done.5 = f32[192,128]{1,0:T(8,128)S(1)} collective-permute-done((f32[192,128]{1,0:T(8,128)S(1)}, f32[192,128]{1,0:T(8,128)S(1)}, u32[]{:S(2)}, u32[]{:S(2)}) %collective-permute-start.5) | collective-permute-done | bytes 98336 | tf_op jit(solution)/shard_map/ppermute | solution.py:304
  32.8 0.3 collective-permute-start.6
  33.2 3.8 %collective-permute-done.6.theirs_ref = bf16[192,128]{1,0:T(8,128)(2,1)S(1)} collective-permute-done((bf16[192,128]{1,0:T(8,128)(2,1)S(1)}, bf16[192,128]{1,0:T(8,128)(2,1)S(1)}, u32[]{:S(2)}, u32[]{:S(2)}) %collective-permute-start.6) | collective-permute-done | bytes 49184 | tf_op jit(solution)/shard_map/ppermute | solution.py:304
  37.0 0.7 %shard_map.129 = (f32[2,64,64]{2,1,0:T(8,128)}, f32[2,64,64]{2,1,0:T(8,128)}, f32[2,64,64]{2,1,0:T(8,128)}) custom-call(bf16[192,128]{1,0:T(8,128)(2,1)S(1)} %add_convert_fusion.mine_ref, bf16[192,128]{1,0:T(8,128)(2,1)S(1)} %collective-permute-done.6.theirs_ref), custom_call_target="tpu_custom_call" | custom-call | tf_op jit(solution)/shard_map/pallas_call | solution.py:417
  (4 shorter events, 0.0 us)
Async XLA Ops:
  0.6 8.7 %collective-permute-start.1 = (bf16[256,1280]{1,0:T(8,128)(2,1)}, bf16[256,1280]{1,0:T(8,128)(2,1)S(1)}, u32[]{:S(2)}, u32[]{:S(2)}) collective-permute-start(bf16[256,1280]{1,0:T(8,128)(2,1)} %og_hbm.1), channel_id=1, source_target_pairs={{0,1},{1,0},{2,3},{3,2},{4,5},{5,4},{6,7},{7,6},{8,9},{9,8},{10,11... | collective-permute-start | bytes 1966088 | tf_op jit(solution)/shard_map/ppermute | solution.py:304
  1.2 18.1 %collective-permute-start.2 = (bf16[256,1280]{1,0:T(8,128)(2,1)}, bf16[256,1280]{1,0:T(8,128)(2,1)S(1)}, u32[]{:S(2)}, u32[]{:S(2)}) collective-permute-start(bf16[256,1280]{1,0:T(8,128)(2,1)} %og_hbm.1), channel_id=1, source_target_pairs={{0,2},{1,3},{2,0},{3,1},{4,6},{5,7},{6,4},{7,5},{8,10},{9,11},{10,... | collective-permute-start | bytes 1966088 | tf_op jit(solution)/shard_map/ppermute | solution.py:304
  9.1 9.7 %collective-permute-start = (f32[128,256]{1,0:T(8,128)S(1)}, f32[128,256]{1,0:T(8,128)S(1)}, u32[]{:S(2)}, u32[]{:S(2)}) collective-permute-start(f32[128,256]{1,0:T(8,128)S(1)} %get-tuple-element.13.mine_ref), channel_id=1, source_target_pairs={{0,1},{1,0},{2,3},{3,2},{4,5},{5,4},{6,7},{7,6},{8,9},{9,8},{10,11... | collective-permute-start | bytes 393224 | tf_op jit(solution)/shard_map/ppermute | solution.py:304
  19.3 6.1 %collective-permute-start.4 = (bf16[256,1280]{1,0:T(8,128)(2,1)S(1)}, bf16[256,1280]{1,0:T(8,128)(2,1)S(1)}, u32[]{:S(2)}, u32[]{:S(2)}) collective-permute-start(bf16[256,1280]{1,0:T(8,128)(2,1)S(1)} %shard_map.124.og_ref), channel_id=1, source_target_pairs={{0,1},{1,0},{2,3},{3,2},{4,5},{5,4},{6,7},{7,6},{8,9},{9,8},{10,11... | collective-permute-start | bytes 1966088 | tf_op jit(solution)/shard_map/ppermute | solution.py:304
  23.5 7.5 %collective-permute-start.3 = (f32[128,256]{1,0:T(8,128)S(1)}, f32[128,256]{1,0:T(8,128)S(1)}, u32[]{:S(2)}, u32[]{:S(2)}) collective-permute-start(f32[128,256]{1,0:T(8,128)S(1)} %shard_map.126.chip_ref), channel_id=1, source_target_pairs={{0,2},{1,3},{2,0},{3,1},{4,6},{5,7},{6,4},{7,5},{8,10},{9,11},{10,... | collective-permute-start | bytes 393224 | tf_op jit(solution)/shard_map/ppermute | solution.py:304
  31.5 1.3 %collective-permute-start.5 = (f32[192,128]{1,0:T(8,128)S(1)}, f32[192,128]{1,0:T(8,128)S(1)}, u32[]{:S(2)}, u32[]{:S(2)}) collective-permute-start(f32[192,128]{1,0:T(8,128)S(1)} %shard_map.128), channel_id=1, source_target_pairs={{0,1},{1,0},{2,3},{3,2},{4,5},{5,4},{6,7},{7,6},{8,9},{9,8},{10,11... | collective-permute-start | bytes 294920 | tf_op jit(solution)/shard_map/ppermute | solution.py:304
  32.8 4.2 %collective-permute-start.6 = (bf16[192,128]{1,0:T(8,128)(2,1)S(1)}, bf16[192,128]{1,0:T(8,128)(2,1)S(1)}, u32[]{:S(2)}, u32[]{:S(2)}) collective-permute-start(bf16[192,128]{1,0:T(8,128)(2,1)S(1)} %add_convert_fusion.mine_ref), channel_id=1, source_target_pairs={{0,2},{1,3},{2,0},{3,1},{4,6},{5,7},{6,4},{7,5},{8,10},{9,11},{10,... | collective-permute-start | bytes 147464 | tf_op jit(solution)/shard_map/ppermute | solution.py:304

commit v14 on v12

--- a/solution.py
+++ b/solution.py
@@ -9,6 +9,8 @@
 LEN = 128
 BLOCK = 1152
 CHIP_BLOCK = 512
+FAR_BLOCK = 768
+NEAR = 1024
 PARTS = 2
 MIB = 1 << 20
 ANY = pl.BlockSpec(memory_space=pl.ANY)
@@ -58,14 +60,14 @@
 
 
 class Step:
-    def __init__(self, owner, width, block, w_hbm):
-        self.owner, self.width, self.block, self.w_hbm = owner, width, block, w_hbm
+    def __init__(self, column, width, block, w_hbm):
+        self.column, self.width, self.block, self.w_hbm = column, width, block, w_hbm
 
     def units(self, i):
         return pl.ds(pl.multiple_of(i * self.block, self.block), self.block)
 
     def copies(self, i, dst, sems):
-        columns = pl.ds(pl.multiple_of(self.owner * self.width, 128), self.width)
+        columns = pl.ds(pl.multiple_of(self.column, 128), self.width)
         part = self.block // PARTS
         return [
             pltpu.make_async_copy(
@@ -77,6 +79,16 @@
         ]
 
 
+def near_step(per_device, ref, w_hbm):
+    me = lax.axis_index("tensor")
+    return Step((1 - me // 2) * 2 * per_device + me % 2 * (2 * per_device - NEAR), NEAR, ref.shape[1], w_hbm)
+
+
+def far_step(per_device, ref, w_hbm):
+    me = lax.axis_index("tensor")
+    return Step((1 - me // 2) * 2 * per_device + (1 - me % 2) * NEAR, 2 * per_device - NEAR, ref.shape[1], w_hbm)
+
+
 def start(copies):
     for copy in copies:
         copy.start()
@@ -144,7 +156,7 @@
 
     pairs = ((hf_hbm, hf_v), (og_hbm, og_v), (x_hbm, x_v), (xf_hbm, xf_v), (yf_hbm, yf_v))
     small = [pltpu.make_async_copy(src, dst, sems.at[i]) for i, (src, dst) in enumerate(pairs)]
-    following = Step(lax.axis_index("tensor") // 2, head_ref.shape[2], head_ref.shape[1], w_hbm)
+    following = Step(lax.axis_index("tensor") // 2 * head_ref.shape[2], head_ref.shape[2], head_ref.shape[1], w_hbm)
     heads = head_ref.shape[0]
 
     start(gate_up(0))
@@ -183,8 +195,8 @@
 def chip_features_kernel(own_ref, mate_ref, head_ref, w_hbm, acc_ref, near_ref, og_v, w_v, sems, near_sems):
     me = lax.axis_index("tensor")
     width = own_ref.shape[0]
-    step = Step(me // 2, 2 * width, w_v.shape[1], w_hbm)
-    near = Step(me ^ 2, width, near_ref.shape[1], w_hbm)
+    step = Step(me // 2 * 2 * width, 2 * width, w_v.shape[1], w_hbm)
+    near = near_step(width, near_ref, w_hbm)
     mine = pl.ds(pl.multiple_of(me % 2 * width, 128), width)
     theirs = pl.ds(pl.multiple_of((me + 1) % 2 * width, 128), width)
     og_v[mine] = own_ref[...]
@@ -197,45 +209,43 @@
     stream(step, 3, acc_ref.shape[0] // step.block, head_ref, w_v, sems, body, later)
 
 
-def near_kernel(acc_in, og_ref, head_ref, w_hbm, acc_ref, far_ref, og_v, w_v, sems, far_sems):
-    me = lax.axis_index("tensor")
-    heads, block, width = head_ref.shape
-    near, far = Step(me ^ 2, width, block, w_hbm), Step(me ^ 3, width, block, w_hbm)
-    rest = [near.copies(heads + k, w_v.at[k], sems.at[k]) for k in range(w_v.shape[0])]
+def near_kernel(acc_in, og_ref, head_ref, w_hbm, acc_ref, left_ref, far_ref, og_v, far_sems):
+    core = lax.axis_index("tensor") % 2
+    width = og_ref.shape[1]
+    step = near_step(width, head_ref, w_hbm)
+    far = far_step(width, far_ref, w_hbm)
     later = [far.copies(k, far_ref.at[k], far_sems.at[k]) for k in range(far_ref.shape[0])]
-    for group in rest + later:
+    for group in later:
         start(group)
     og_v[...] = og_ref[...].T
-
-    def body(i, weights):
-        at = near.units(i)
-        acc_ref[at] = acc_in[at] + product(weights, og_v[...])
-
-    @pl.loop(0, heads)
-    def _(i):
-        body(i, head_ref[i])
-
-    for group in rest:
-        wait(group)
-
-    @pl.loop(0, w_v.shape[0])
-    def _(i):
-        body(heads + i, w_v[i])
+    left_ref[...] = og_v[pl.ds(pl.multiple_of((1 - core) * NEAR, 16), width - NEAR)]
+
+    @pl.loop(0, head_ref.shape[0])
+    def _(i):
+        at = step.units(i)
+        features = og_v[pl.ds(pl.multiple_of(core * (width - NEAR), 16), NEAR)]
+        acc_ref[at] = acc_in[at] + product(head_ref[i], features)
 
     for group in later:
         wait(group)
 
 
-def far_kernel(acc_ref, og_ref, head_ref, w_hbm, a_ref, b_ref, gf_hbm, uf_hbm, gate_ref, up_ref,
+def far_kernel(acc_ref, og_ref, left_ref, head_ref, w_hbm, a_ref, b_ref, gf_hbm, uf_hbm, gate_ref, up_ref,
                og_v, w_v, gf_ref, uf_ref, d_gate_v, d_up_v, sems, factor_sems):
-    heads, block, width = head_ref.shape
-    step = Step(lax.axis_index("tensor") ^ 3, width, block, w_hbm)
+    core = lax.axis_index("tensor") % 2
+    heads = head_ref.shape[0]
+    width, left = og_ref.shape[1], left_ref.shape[0]
+    step = far_step(width, head_ref, w_hbm)
     factors = [
         pltpu.make_async_copy(src, dst, factor_sems.at[k]) for k, (src, dst) in enumerate(((gf_hbm, gf_ref), (uf_hbm, uf_ref)))
     ]
-    start(step.copies(heads, w_v.at[0], sems.at[0]))
+    rest = w_v.shape[0]
+    ahead = rest - heads
+    for k in range(ahead):
+        start(step.copies(heads + k, w_v.at[k], sems.at[k]))
     start(factors)
-    og_v[...] = og_ref[...].T
+    og_v[pl.ds(pl.multiple_of(core * width, 16), left)] = left_ref[...]
+    og_v[pl.ds(pl.multiple_of((1 - core) * left, 16), width)] = og_ref[...].T
 
     def body(i, weights):
         at = step.units(i)
@@ -245,13 +255,10 @@
 
     @pl.loop(0, heads)
     def _(i):
-        @pl.when((i > 0) & (i < w_v.shape[0]))
-        def _():
-            start(step.copies(heads + i, w_v.at[i], sems.at[i]))
-
+        start(step.copies(heads + ahead + i, w_v.at[ahead + i], sems.at[ahead + i]))
         body(i, head_ref[i])
 
-    @pl.loop(0, w_v.shape[0])
+    @pl.loop(0, rest)
     def _(i):
         wait(step.copies(heads + i, w_v.at[i], sems.at[i]))
         body(heads + i, w_v[i])
@@ -320,9 +327,6 @@
     narrow = pltpu.VMEM((rank, tokens), F32)
     turned = pltpu.VMEM((width, tokens), BF16)
     weight = in_hbm(down_weight)
-
-    def blocks(count):
-        return pltpu.VMEM((count, BLOCK, width), BF16)
 
     def chip_blocks(count):
         return pltpu.VMEM((count, CHIP_BLOCK, 2 * width), BF16)
@@ -362,13 +366,13 @@
     pq_mate = swap(pq, 1)
     acc, head = call(
         chip_features_kernel,
-        (held, blocks(turns - 1)),
+        (held, pltpu.VMEM((turns, BLOCK, NEAR), BF16)),
         [VMEM] * 3 + [ANY],
         [
             pltpu.VMEM((2 * width, tokens), BF16),
             chip_blocks(4),
             dma((units // CHIP_BLOCK, PARTS)),
-            dma((turns - 1, PARTS)),
+            dma((turns, PARTS)),
         ],
         14,
         2 * per_product,
@@ -388,14 +392,16 @@
     chip = call(chip_kernel, pltpu.VMEM(pq.shape, F32), [VMEM, VMEM, ANY], [], 1)(pq, pq_mate, head)
     near = after(near, chip)
     far = swap(near, 1)
-    acc, head = call(
+    wide = 2 * width - NEAR
+    far_turns = units // FAR_BLOCK
+    acc, left, head = call(
         near_kernel,
-        (held, blocks(2)),
+        (held, pltpu.VMEM((width - NEAR, tokens), BF16), pltpu.VMEM((2, FAR_BLOCK, wide), BF16)),
         [VMEM] * 3 + [ANY],
-        [turned, blocks(1), dma((1, PARTS)), dma((2, PARTS))],
+        [turned, dma((2, PARTS))],
         6,
-        per_product,
-        2 * units * width,
+        2 * tokens * NEAR * units,
+        2 * units * NEAR,
         input_output_aliases={0: 0},
     )(acc, near, head, weight)
     chip = after(chip, head)
@@ -405,12 +411,21 @@
     q_gate, q_up = call(
         far_kernel,
         (narrow, narrow),
-        [VMEM] * 3 + [ANY] + [VMEM] * 2 + [ANY] * 2,
-        [turned, blocks(turns - 2), factor, factor, kept, kept, dma((turns - 2, PARTS)), dma((2,))],
-        16,
-        per_product,
-        2 * units * width,
-    )(acc, far, head, weight, a, b, in_hbm(gate_factor.T), in_hbm(up_factor.T))
+        [VMEM] * 4 + [ANY] + [VMEM] * 2 + [ANY] * 2,
+        [
+            pltpu.VMEM((wide, tokens), BF16),
+            pltpu.VMEM((far_turns - 2, FAR_BLOCK, wide), BF16),
+            factor,
+            factor,
+            kept,
+            kept,
+            dma((far_turns - 2, PARTS)),
+            dma((2,)),
+        ],
+        20,
+        2 * tokens * wide * units,
+        2 * units * wide,
+    )(acc, far, left, head, weight, a, b, in_hbm(gate_factor.T), in_hbm(up_factor.T))
     share = call(gradients_kernel, pltpu.VMEM(((SEQS + 1) * rank, 2 * rank), F32), [VMEM] * 5, [], 4)(
         chip, chip_across, q_gate, q_up, ph
     )
@@ -426,8 +441,10 @@
             mesh.shape["tensor"] == 4
             and (tokens, rank) == (SEQS * LEN, LEN // 2)
             and width % 128 == 0
+            and width > NEAR
             and units % BLOCK == 0
             and units % CHIP_BLOCK == 0
+            and units // FAR_BLOCK == 6
             and units // BLOCK == 4
         )
         return tuple((fast if fits else plain)(*arrays))

time: 37.7 us -> 37.7 us (level)
  waiting for transfers between devices: 5.13 us -> 4.46 us
  Pallas kernels: 25.8 us -> 26.2 us
    ppermute x7, waiting for transfers between devices: 5.13 us -> 4.46 us  [swap(): return lax.ppermute(array, 'tensor', [(i, i ^ bits) for i in range(4)])]
    pallas_call x3, Pallas kernels: 19.1 us -> 19.6 us  [the longest x1 9.94 us: fast(): call(chip_features_kernel, (held, pltpu.VMEM((turns, BLOCK, NEAR), BF16))...]
  transfers between devices with their start and end apart: 7 -> 7, of which waited for: 3 -> 2; matrix products, arithmetic and copies ran while one was open for 0% -> 0% of each run, Pallas kernels for 65% -> 66%
where the time goes in v14:
time: 37.7 us; the launch traced here: 37.6 us
  Pallas kernels  26.2 us (69%)
  starting transfers between devices  6.16 us (16%)
  waiting for transfers between devices  4.46 us (12%)
  between operations  0.73 us (2%)
    pallas_call x1, Pallas kernels, fast(): call(chip_features_kernel, (held, pltpu.VMEM((turns, BLOCK, NEAR), BF16))...  9.94 us
    pallas_call x1, Pallas kernels, fast(): call(far_kernel, (narrow, narrow), [VMEM] * 4 + [ANY] + [VMEM] * 2 + [ANY...  6.25 us
    ppermute x7, starting transfers between devices, swap(): return lax.ppermute(array, 'tensor', [(i, i ^ bits) for i in range(4)])  6.16 us
    pallas_call x1, Pallas kernels, fast(): call(elementwise_kernel, (held, held, narrow, pltpu.VMEM((2 * rank, token...  5.35 us
    ppermute x7, waiting for transfers between devices, swap(): return lax.ppermute(array, 'tensor', [(i, i ^ bits) for i in range(4)])  4.46 us
    pallas_call x1, Pallas kernels, fast(): call(near_kernel, (held, pltpu.VMEM((width - NEAR, tokens), BF16), pltpu....  3.41 us
  transfers between devices with their start and end apart: 7, of which 2 were waited for; matrix products, arithmetic and copies ran while one was open for 0% of the time, Pallas kernels for 66%

profile of v14, /device:TPU:0, one launch (start us, length us, event | category | flops | bytes accessed | tf_op | source)
XLA Modules:
  0.0 37.6 jit_solution(199062605248650501)
XLA Ops:
  0.6 0.5 %collective-permute-start.1 = (bf16[256,1280]{1,0:T(8,128)(2,1)}, bf16[256,1280]{1,0:T(8,128)(2,1)S(1)}, u32[]{:S(2)}, u32[]{:S(2)}) collective-permute-start(bf16[256,1280]{1,0:T(8,128)(2,1)} %og_hbm.1), channel_id=1, source_target_pairs={{0,1},{1,0},{2,3},{3,2},{4,5},{5,4},{6,7},{7,6},{8,9},{9,8},{10,11... | collective-permute-start | bytes 1966088 | tf_op jit(solution)/shard_map/ppermute | solution.py:309
  1.2 2.6 %collective-permute-start.2 = (bf16[256,1280]{1,0:T(8,128)(2,1)}, bf16[256,1280]{1,0:T(8,128)(2,1)S(1)}, u32[]{:S(2)}, u32[]{:S(2)}) collective-permute-start(bf16[256,1280]{1,0:T(8,128)(2,1)} %og_hbm.1), channel_id=1, source_target_pairs={{0,2},{1,3},{2,0},{3,1},{4,6},{5,7},{6,4},{7,5},{8,10},{9,11},{10,... | collective-permute-start | bytes 1966088 | tf_op jit(solution)/shard_map/ppermute | solution.py:309
  3.7 5.4 %shard_map.121 = (f32[4608,256]{1,0:T(8,128)S(1)}, f32[4608,256]{1,0:T(8,128)S(1)}, f32[64,256]{1,0:T(8,128)S(1)}, f32[128,256]{1,0:T(8,128)S(1)}, bf16[2,512,25...) custom-call(bf16[256,1280]{1,0:T(8,128)(2,1)} %x_hbm.1, bf16[256,1280]{1,0:T(8,128)(2,1)} %og_hbm.1, ...), custom_call_target="tpu_custom_call" | custom-call | flops 754974720 | bytes 4718592 | tf_op jit(solution)/shard_map/pallas_call | solution.py:336
  9.1 0.2 collective-permute-start
  9.3 0.0 collective-permute-done.1.mate_ref
  9.3 9.9 %shard_map.122 = (f32[4608,256]{1,0:T(8,128)S(1)}, bf16[4,1152,1024]{2,1,0:T(8,128)(2,1)S(1)}) custom-call(bf16[1280,256]{1,0:T(8,128)(2,1)S(1)} %get-tuple-element.17.own_ref, bf16[256,1280]{1,0:T(8,128)(2,1)S(1)} %collective-permute-done.1.mate_ref, bf16[2,512,2560]{2,1,0:T(8,128)(2,1)S(1)} %get-tuple-element.18.head_ref, bf16[4608,5120]{1,0:T(8,128)(2,1)} %w_hbm.7), custom_call_target="tpu_custom_call" | custom-call | flops 6039797760 | bytes 23592960 | tf_op jit(solution)/shard_map/pallas_call | solution.py:367
  19.3 0.0 collective-permute-done.theirs_ref
  19.3 0.0 collective-permute-done.2.array_ref
  19.3 0.4 %collective-permute-start.4 = (bf16[256,1280]{1,0:T(8,128)(2,1)S(1)}, bf16[256,1280]{1,0:T(8,128)(2,1)S(1)}, u32[]{:S(2)}, u32[]{:S(2)}) collective-permute-start(bf16[256,1280]{1,0:T(8,128)(2,1)S(1)} %shard_map.124.og_ref), channel_id=1, source_target_pairs={{0,1},{1,0},{2,3},{3,2},{4,5},{5,4},{6,7},{7,6},{8,9},{9,8},{10,11... | collective-permute-start | bytes 1966088 | tf_op jit(solution)/shard_map/ppermute | solution.py:309
  19.7 3.4 %shard_map.125 = (f32[4608,256]{1,0:T(8,128)S(1)}, bf16[256,256]{1,0:T(8,128)(2,1)S(1)}, bf16[2,768,1536]{2,1,0:T(8,128)(2,1)S(1)}) custom-call(f32[4608,256]{1,0:T(8,128)S(1)} %get-tuple-element.20.acc_in, bf16[256,1280]{1,0:T(8,128)(2,1)S(1)} %shard_map.124.og_ref, ...), custom_call_target="tpu_custom_call", output_to_operand_aliasing={{0}: (0, {})} | custom-call | flops 2415919104 | bytes 9437184 | tf_op jit(solution)/shard_map/pallas_call | solution.py:397
  23.1 1.4 %collective-permute-start.3 = (f32[128,256]{1,0:T(8,128)S(1)}, f32[128,256]{1,0:T(8,128)S(1)}, u32[]{:S(2)}, u32[]{:S(2)}) collective-permute-start(f32[128,256]{1,0:T(8,128)S(1)} %shard_map.126.chip_ref), channel_id=1, source_target_pairs={{0,2},{1,3},{2,0},{3,1},{4,6},{5,7},{6,4},{7,5},{8,10},{9,11},{10,... | collective-permute-start | bytes 393224 | tf_op jit(solution)/shard_map/ppermute | solution.py:309
  24.5 0.0 collective-permute-done.4.og_ref
  24.5 6.3 %shard_map.127 = (f32[64,256]{1,0:T(8,128)S(1)}, f32[64,256]{1,0:T(8,128)S(1)}) custom-call(f32[4608,256]{1,0:T(8,128)S(1)} %get-tuple-element.22.acc_ref, bf16[256,1280]{1,0:T(8,128)(2,1)S(1)} %collective-permute-done.4.og_ref, bf16[256,256]{1,0:T(8,128)(2,1)S(1)} %get-tuple-element.23.left_ref, ...), custom_call_target="tpu_custom_call" | custom-call | flops 3623878656 | bytes 14155776 | tf_op jit(solution)/shard_map/pallas_call | solution.py:411
  30.8 0.0 collective-permute-done.3.other_ref
  30.8 0.5 %shard_map.128 = f32[192,128]{1,0:T(8,128)S(1)} custom-call(f32[128,256]{1,0:T(8,128)S(1)} %shard_map.126.chip_ref, f32[128,256]{1,0:T(8,128)S(1)} %collective-permute-done.3.other_ref, f32[64,256]{1,0:T(8,128)S(1)} %get-tuple-element.26.gate_ref, f32[64,256]{1,0:T(8,128)S(1)} %get-tuple-element.27.up_ref, f32[64,256]{1,0:T(8,128)S(1)} %get-tuple-element.28.ph_ref), custom_call_target="tpu_custom_call" | custom-call | tf_op jit(solution)/shard_map/pallas_call | solution.py:429
  31.3 0.3 collective-permute-start.5
  31.6 1.1 %collective-permute-done.5 = f32[192,128]{1,0:T(8,128)S(1)} collective-permute-done((f32[192,128]{1,0:T(8,128)S(1)}, f32[192,128]{1,0:T(8,128)S(1)}, u32[]{:S(2)}, u32[]{:S(2)}) %collective-permute-start.5) | collective-permute-done | bytes 98336 | tf_op jit(solution)/shard_map/ppermute | solution.py:309
  32.7 0.8 %collective-permute-start.6 = (bf16[192,128]{1,0:T(8,128)(2,1)S(1)}, bf16[192,128]{1,0:T(8,128)(2,1)S(1)}, u32[]{:S(2)}, u32[]{:S(2)}) collective-permute-start(bf16[192,128]{1,0:T(8,128)(2,1)S(1)} %add_convert_fusion.mine_ref), channel_id=1, source_target_pairs={{0,2},{1,3},{2,0},{3,1},{4,6},{5,7},{6,4},{7,5},{8,10},{9,11},{10,... | collective-permute-start | bytes 147464 | tf_op jit(solution)/shard_map/ppermute | solution.py:309
  33.5 3.4 %collective-permute-done.6.theirs_ref = bf16[192,128]{1,0:T(8,128)(2,1)S(1)} collective-permute-done((bf16[192,128]{1,0:T(8,128)(2,1)S(1)}, bf16[192,128]{1,0:T(8,128)(2,1)S(1)}, u32[]{:S(2)}, u32[]{:S(2)}) %collective-permute-start.6) | collective-permute-done | bytes 49184 | tf_op jit(solution)/shard_map/ppermute | solution.py:309
  36.8 0.7 %shard_map.129 = (f32[2,64,64]{2,1,0:T(8,128)}, f32[2,64,64]{2,1,0:T(8,128)}, f32[2,64,64]{2,1,0:T(8,128)}) custom-call(bf16[192,128]{1,0:T(8,128)(2,1)S(1)} %add_convert_fusion.mine_ref, bf16[192,128]{1,0:T(8,128)(2,1)S(1)} %collective-permute-done.6.theirs_ref), custom_call_target="tpu_custom_call" | custom-call | tf_op jit(solution)/shard_map/pallas_call | solution.py:434
  (4 shorter events, 0.0 us)
Async XLA Ops:
  0.6 8.7 %collective-permute-start.1 = (bf16[256,1280]{1,0:T(8,128)(2,1)}, bf16[256,1280]{1,0:T(8,128)(2,1)S(1)}, u32[]{:S(2)}, u32[]{:S(2)}) collective-permute-start(bf16[256,1280]{1,0:T(8,128)(2,1)} %og_hbm.1), channel_id=1, source_target_pairs={{0,1},{1,0},{2,3},{3,2},{4,5},{5,4},{6,7},{7,6},{8,9},{9,8},{10,11... | collective-permute-start | bytes 1966088 | tf_op jit(solution)/shard_map/ppermute | solution.py:309
  1.2 18.1 %collective-permute-start.2 = (bf16[256,1280]{1,0:T(8,128)(2,1)}, bf16[256,1280]{1,0:T(8,128)(2,1)S(1)}, u32[]{:S(2)}, u32[]{:S(2)}) collective-permute-start(bf16[256,1280]{1,0:T(8,128)(2,1)} %og_hbm.1), channel_id=1, source_target_pairs={{0,2},{1,3},{2,0},{3,1},{4,6},{5,7},{6,4},{7,5},{8,10},{9,11},{10,... | collective-permute-start | bytes 1966088 | tf_op jit(solution)/shard_map/ppermute | solution.py:309
  9.1 10.2 %collective-permute-start = (f32[128,256]{1,0:T(8,128)S(1)}, f32[128,256]{1,0:T(8,128)S(1)}, u32[]{:S(2)}, u32[]{:S(2)}) collective-permute-start(f32[128,256]{1,0:T(8,128)S(1)} %get-tuple-element.16.mine_ref), channel_id=1, source_target_pairs={{0,1},{1,0},{2,3},{3,2},{4,5},{5,4},{6,7},{7,6},{8,9},{9,8},{10,11... | collective-permute-start | bytes 393224 | tf_op jit(solution)/shard_map/ppermute | solution.py:309
  19.3 5.2 %collective-permute-start.4 = (bf16[256,1280]{1,0:T(8,128)(2,1)S(1)}, bf16[256,1280]{1,0:T(8,128)(2,1)S(1)}, u32[]{:S(2)}, u32[]{:S(2)}) collective-permute-start(bf16[256,1280]{1,0:T(8,128)(2,1)S(1)} %shard_map.124.og_ref), channel_id=1, source_target_pairs={{0,1},{1,0},{2,3},{3,2},{4,5},{5,4},{6,7},{7,6},{8,9},{9,8},{10,11... | collective-permute-start | bytes 1966088 | tf_op jit(solution)/shard_map/ppermute | solution.py:309
  23.1 7.6 %collective-permute-start.3 = (f32[128,256]{1,0:T(8,128)S(1)}, f32[128,256]{1,0:T(8,128)S(1)}, u32[]{:S(2)}, u32[]{:S(2)}) collective-permute-start(f32[128,256]{1,0:T(8,128)S(1)} %shard_map.126.chip_ref), channel_id=1, source_target_pairs={{0,2},{1,3},{2,0},{3,1},{4,6},{5,7},{6,4},{7,5},{8,10},{9,11},{10,... | collective-permute-start | bytes 393224 | tf_op jit(solution)/shard_map/ppermute | solution.py:309
  31.3 1.4 %collective-permute-start.5 = (f32[192,128]{1,0:T(8,128)S(1)}, f32[192,128]{1,0:T(8,128)S(1)}, u32[]{:S(2)}, u32[]{:S(2)}) collective-permute-start(f32[192,128]{1,0:T(8,128)S(1)} %shard_map.128), channel_id=1, source_target_pairs={{0,1},{1,0},{2,3},{3,2},{4,5},{5,4},{6,7},{7,6},{8,9},{9,8},{10,11... | collective-permute-start | bytes 294920 | tf_op jit(solution)/shard_map/ppermute | solution.py:309
  32.7 4.2 %collective-permute-start.6 = (bf16[192,128]{1,0:T(8,128)(2,1)S(1)}, bf16[192,128]{1,0:T(8,128)(2,1)S(1)}, u32[]{:S(2)}, u32[]{:S(2)}) collective-permute-start(bf16[192,128]{1,0:T(8,128)(2,1)S(1)} %add_convert_fusion.mine_ref), channel_id=1, source_target_pairs={{0,2},{1,3},{2,0},{3,1},{4,6},{5,7},{6,4},{7,5},{8,10},{9,11},{10,... | collective-permute-start | bytes 147464 | tf_op jit(solution)/shard_map/ppermute | solution.py:309

commit v15 on v12

--- a/solution.py
+++ b/solution.py
@@ -207,20 +207,16 @@
         start(group)
     og_v[...] = og_ref[...].T
 
-    def body(i, weights):
-        at = near.units(i)
-        acc_ref[at] = acc_in[at] + product(weights, og_v[...])
-
-    @pl.loop(0, heads)
-    def _(i):
-        body(i, head_ref[i])
-
+    def body(first, weights):
+        rows = weights.shape[0] * block
+        at = slice(first * block, first * block + rows)
+        acc_ref[at] = acc_in[at] + product(weights.reshape(rows, width), og_v[...])
+
+    body(0, head_ref[:2])
+    body(2, head_ref[2:])
     for group in rest:
         wait(group)
-
-    @pl.loop(0, w_v.shape[0])
-    def _(i):
-        body(heads + i, w_v[i])
+    body(heads, w_v[...])
 
     for group in later:
         wait(group)
@@ -233,29 +229,22 @@
     factors = [
         pltpu.make_async_copy(src, dst, factor_sems.at[k]) for k, (src, dst) in enumerate(((gf_hbm, gf_ref), (uf_hbm, uf_ref)))
     ]
-    start(step.copies(heads, w_v.at[0], sems.at[0]))
+    def body(first, weights):
+        rows = weights.shape[0] * block
+        at = slice(first * block, first * block + rows)
+        hidden_grad = acc_ref[at] + product(weights.reshape(rows, width), og_v[...])
+        d_gate_v[at] = (hidden_grad * a_ref[at]).astype(BF16)
+        d_up_v[at] = (hidden_grad * b_ref[at]).astype(BF16)
+
+    rest = [step.copies(heads + k, w_v.at[k], sems.at[k]) for k in range(w_v.shape[0])]
+    for group in rest:
+        start(group)
     start(factors)
     og_v[...] = og_ref[...].T
-
-    def body(i, weights):
-        at = step.units(i)
-        hidden_grad = acc_ref[at] + product(weights, og_v[...])
-        d_gate_v[at] = (hidden_grad * a_ref[at]).astype(BF16)
-        d_up_v[at] = (hidden_grad * b_ref[at]).astype(BF16)
-
-    @pl.loop(0, heads)
-    def _(i):
-        @pl.when((i > 0) & (i < w_v.shape[0]))
-        def _():
-            start(step.copies(heads + i, w_v.at[i], sems.at[i]))
-
-        body(i, head_ref[i])
-
-    @pl.loop(0, w_v.shape[0])
-    def _(i):
-        wait(step.copies(heads + i, w_v.at[i], sems.at[i]))
-        body(heads + i, w_v[i])
-
+    body(0, head_ref[...])
+    for group in rest:
+        wait(group)
+    body(heads, w_v[...])
     wait(factors)
     gate_ref[...] = product(gf_ref[...], d_gate_v[...])
     up_ref[...] = product(uf_ref[...], d_up_v[...])
@@ -393,7 +382,7 @@
         (held, blocks(2)),
         [VMEM] * 3 + [ANY],
         [turned, blocks(1), dma((1, PARTS)), dma((2, PARTS))],
-        6,
+        10,
         per_product,
         2 * units * width,
         input_output_aliases={0: 0},
@@ -407,7 +396,7 @@
         (narrow, narrow),
         [VMEM] * 3 + [ANY] + [VMEM] * 2 + [ANY] * 2,
         [turned, blocks(turns - 2), factor, factor, kept, kept, dma((turns - 2, PARTS)), dma((2,))],
-        16,
+        20,
         per_product,
         2 * units * width,
     )(acc, far, head, weight, a, b, in_hbm(gate_factor.T), in_hbm(up_factor.T))

time: 37.7 us -> 46.7 us (1.24)
  Pallas kernels: 25.8 us -> 34.7 us
    pallas_call x1, Pallas kernels: 5.45 us -> 10.5 us  [fast(): call(far_kernel, (narrow, narrow), [VMEM] * 3 + [ANY] + [VMEM] * 2 + [ANY...]
    pallas_call x1, Pallas kernels: 4.21 us -> 8.1 us  [fast(): call(near_kernel, (held, blocks(2)), [VMEM] * 3 + [ANY], [turned, blocks(...]
  transfers between devices with their start and end apart: 7 -> 7, of which waited for: 3 -> 3; matrix products, arithmetic and copies ran while one was open for 0% -> 0% of each run, Pallas kernels for 65% -> 72%
where the time goes in v15:
time: 46.7 us; the launch traced here: 46.5 us
  Pallas kernels  34.7 us (74%)
  starting transfers between devices  5.75 us (12%)
  waiting for transfers between devices  5.33 us (11%)
  between operations  0.71 us (2%)
    pallas_call x1, Pallas kernels, fast(): call(far_kernel, (narrow, narrow), [VMEM] * 3 + [ANY] + [VMEM] * 2 + [ANY...  10.5 us
    pallas_call x1, Pallas kernels, fast(): call(chip_features_kernel, (held, blocks(turns - 1)), [VMEM] * 3 + [ANY],...  9.49 us
    pallas_call x1, Pallas kernels, fast(): call(near_kernel, (held, blocks(2)), [VMEM] * 3 + [ANY], [turned, blocks(...  8.1 us
    ppermute x7, starting transfers between devices, swap(): return lax.ppermute(array, 'tensor', [(i, i ^ bits) for i in range(4)])  5.75 us
    pallas_call x1, Pallas kernels, fast(): call(elementwise_kernel, (held, held, narrow, pltpu.VMEM((2 * rank, token...  5.35 us
    ppermute x7, waiting for transfers between devices, swap(): return lax.ppermute(array, 'tensor', [(i, i ^ bits) for i in range(4)])  5.33 us
  transfers between devices with their start and end apart: 7, of which 3 were waited for; matrix products, arithmetic and copies ran while one was open for 0% of the time, Pallas kernels for 72%

profile of v15, /device:TPU:0, one launch (start us, length us, event | category | flops | bytes accessed | tf_op | source)
XLA Modules:
  0.0 46.5 jit_solution(7674116646702286489)
XLA Ops:
  0.6 0.5 %collective-permute-start.1 = (bf16[256,1280]{1,0:T(8,128)(2,1)}, bf16[256,1280]{1,0:T(8,128)(2,1)S(1)}, u32[]{:S(2)}, u32[]{:S(2)}) collective-permute-start(bf16[256,1280]{1,0:T(8,128)(2,1)} %og_hbm.1), channel_id=1, source_target_pairs={{0,1},{1,0},{2,3},{3,2},{4,5},{5,4},{6,7},{7,6},{8,9},{9,8},{10,11... | collective-permute-start | bytes 1966088 | tf_op jit(solution)/shard_map/ppermute | solution.py:291
  1.2 2.6 %collective-permute-start.2 = (bf16[256,1280]{1,0:T(8,128)(2,1)}, bf16[256,1280]{1,0:T(8,128)(2,1)S(1)}, u32[]{:S(2)}, u32[]{:S(2)}) collective-permute-start(bf16[256,1280]{1,0:T(8,128)(2,1)} %og_hbm.1), channel_id=1, source_target_pairs={{0,2},{1,3},{2,0},{3,1},{4,6},{5,7},{6,4},{7,5},{8,10},{9,11},{10,... | collective-permute-start | bytes 1966088 | tf_op jit(solution)/shard_map/ppermute | solution.py:291
  3.7 5.3 %shard_map.121 = (f32[4608,256]{1,0:T(8,128)S(1)}, f32[4608,256]{1,0:T(8,128)S(1)}, f32[64,256]{1,0:T(8,128)S(1)}, f32[128,256]{1,0:T(8,128)S(1)}, bf16[2,512,25...) custom-call(bf16[256,1280]{1,0:T(8,128)(2,1)} %x_hbm.1, bf16[256,1280]{1,0:T(8,128)(2,1)} %og_hbm.1, ...), custom_call_target="tpu_custom_call" | custom-call | flops 754974720 | bytes 4718592 | tf_op jit(solution)/shard_map/pallas_call | solution.py:321
  9.1 0.2 collective-permute-start
  9.3 0.0 collective-permute-done.1.mate_ref
  9.3 9.5 %shard_map.122 = (f32[4608,256]{1,0:T(8,128)S(1)}, bf16[3,1152,1280]{2,1,0:T(8,128)(2,1)S(1)}) custom-call(bf16[1280,256]{1,0:T(8,128)(2,1)S(1)} %get-tuple-element.16.own_ref, bf16[256,1280]{1,0:T(8,128)(2,1)S(1)} %collective-permute-done.1.mate_ref, bf16[2,512,2560]{2,1,0:T(8,128)(2,1)S(1)} %get-tuple-element.17.head_ref, bf16[4608,5120]{1,0:T(8,128)(2,1)} %w_hbm.7), custom_call_target="tpu_custom_call" | custom-call | flops 6039797760 | bytes 23592960 | tf_op jit(solution)/shard_map/pallas_call | solution.py:352
  18.8 0.0 collective-permute-done.theirs_ref
  18.8 0.4 collective-permute-done.2.array_ref
  19.3 0.0 collective-permute-start.4
  19.3 8.1 %shard_map.125 = (f32[4608,256]{1,0:T(8,128)S(1)}, bf16[2,1152,1280]{2,1,0:T(8,128)(2,1)S(1)}) custom-call(f32[4608,256]{1,0:T(8,128)S(1)} %get-tuple-element.19.acc_in, bf16[256,1280]{1,0:T(8,128)(2,1)S(1)} %shard_map.124.og_ref, bf16[3,1152,1280]{2,1,0:T(8,128)(2,1)S(1)} %get-tuple-element.18.token_ref.head_ref, ...), custom_call_target="tpu_custom_call", output_to_operand_aliasing={{0}: (0, {})} | custom-call | flops 3019898880 | bytes 11796480 | tf_op jit(solution)/shard_map/pallas_call | solution.py:380
  27.4 1.8 %collective-permute-start.3 = (f32[128,256]{1,0:T(8,128)S(1)}, f32[128,256]{1,0:T(8,128)S(1)}, u32[]{:S(2)}, u32[]{:S(2)}) collective-permute-start(f32[128,256]{1,0:T(8,128)S(1)} %shard_map.126.chip_ref), channel_id=1, source_target_pairs={{0,2},{1,3},{2,0},{3,1},{4,6},{5,7},{6,4},{7,5},{8,10},{9,11},{10,... | collective-permute-start | bytes 393224 | tf_op jit(solution)/shard_map/ppermute | solution.py:291
  29.2 0.0 collective-permute-done.4.og_ref
  29.2 10.5 %shard_map.127 = (f32[64,256]{1,0:T(8,128)S(1)}, f32[64,256]{1,0:T(8,128)S(1)}) custom-call(f32[4608,256]{1,0:T(8,128)S(1)} %get-tuple-element.21.acc_ref, bf16[256,1280]{1,0:T(8,128)(2,1)S(1)} %collective-permute-done.4.og_ref, bf16[2,1152,1280]{2,1,0:T(8,128)(2,1)S(1)} %get-tuple-element.20.token_ref.head_ref, bf16[4608,5120]{1,0:T(8,128)(2,1)} %w_hbm.7, ...), custom_call_target="tpu_custom_call" | custom-call | flops 3019898880 | bytes 11796480 | tf_op jit(solution)/shard_map/pallas_call | solution.py:394
  39.7 0.0 collective-permute-done.3.other_ref
  39.7 0.5 %shard_map.128 = f32[192,128]{1,0:T(8,128)S(1)} custom-call(f32[128,256]{1,0:T(8,128)S(1)} %shard_map.126.chip_ref, f32[128,256]{1,0:T(8,128)S(1)} %collective-permute-done.3.other_ref, f32[64,256]{1,0:T(8,128)S(1)} %get-tuple-element.24.gate_ref, f32[64,256]{1,0:T(8,128)S(1)} %get-tuple-element.25.up_ref, f32[64,256]{1,0:T(8,128)S(1)} %get-tuple-element.26.ph_ref), custom_call_target="tpu_custom_call" | custom-call | tf_op jit(solution)/shard_map/pallas_call | solution.py:403
  40.2 0.3 collective-permute-start.5
  40.5 1.1 %collective-permute-done.5 = f32[192,128]{1,0:T(8,128)S(1)} collective-permute-done((f32[192,128]{1,0:T(8,128)S(1)}, f32[192,128]{1,0:T(8,128)S(1)}, u32[]{:S(2)}, u32[]{:S(2)}) %collective-permute-start.5) | collective-permute-done | bytes 98336 | tf_op jit(solution)/shard_map/ppermute | solution.py:291
  41.6 0.3 collective-permute-start.6
  41.9 3.8 %collective-permute-done.6.theirs_ref = bf16[192,128]{1,0:T(8,128)(2,1)S(1)} collective-permute-done((bf16[192,128]{1,0:T(8,128)(2,1)S(1)}, bf16[192,128]{1,0:T(8,128)(2,1)S(1)}, u32[]{:S(2)}, u32[]{:S(2)}) %collective-permute-start.6) | collective-permute-done | bytes 49184 | tf_op jit(solution)/shard_map/ppermute | solution.py:291
  45.8 0.7 %shard_map.129 = (f32[2,64,64]{2,1,0:T(8,128)}, f32[2,64,64]{2,1,0:T(8,128)}, f32[2,64,64]{2,1,0:T(8,128)}) custom-call(bf16[192,128]{1,0:T(8,128)(2,1)S(1)} %add_convert_fusion.mine_ref, bf16[192,128]{1,0:T(8,128)(2,1)S(1)} %collective-permute-done.6.theirs_ref), custom_call_target="tpu_custom_call" | custom-call | tf_op jit(solution)/shard_map/pallas_call | solution.py:408
  (4 shorter events, 0.0 us)
Async XLA Ops:
  0.6 8.7 %collective-permute-start.1 = (bf16[256,1280]{1,0:T(8,128)(2,1)}, bf16[256,1280]{1,0:T(8,128)(2,1)S(1)}, u32[]{:S(2)}, u32[]{:S(2)}) collective-permute-start(bf16[256,1280]{1,0:T(8,128)(2,1)} %og_hbm.1), channel_id=1, source_target_pairs={{0,1},{1,0},{2,3},{3,2},{4,5},{5,4},{6,7},{7,6},{8,9},{9,8},{10,11... | collective-permute-start | bytes 1966088 | tf_op jit(solution)/shard_map/ppermute | solution.py:291
  1.2 18.1 %collective-permute-start.2 = (bf16[256,1280]{1,0:T(8,128)(2,1)}, bf16[256,1280]{1,0:T(8,128)(2,1)S(1)}, u32[]{:S(2)}, u32[]{:S(2)}) collective-permute-start(bf16[256,1280]{1,0:T(8,128)(2,1)} %og_hbm.1), channel_id=1, source_target_pairs={{0,2},{1,3},{2,0},{3,1},{4,6},{5,7},{6,4},{7,5},{8,10},{9,11},{10,... | collective-permute-start | bytes 1966088 | tf_op jit(solution)/shard_map/ppermute | solution.py:291
  9.1 9.7 %collective-permute-start = (f32[128,256]{1,0:T(8,128)S(1)}, f32[128,256]{1,0:T(8,128)S(1)}, u32[]{:S(2)}, u32[]{:S(2)}) collective-permute-start(f32[128,256]{1,0:T(8,128)S(1)} %get-tuple-element.15.mine_ref), channel_id=1, source_target_pairs={{0,1},{1,0},{2,3},{3,2},{4,5},{5,4},{6,7},{7,6},{8,9},{9,8},{10,11... | collective-permute-start | bytes 393224 | tf_op jit(solution)/shard_map/ppermute | solution.py:291
  19.3 10.0 %collective-permute-start.4 = (bf16[256,1280]{1,0:T(8,128)(2,1)S(1)}, bf16[256,1280]{1,0:T(8,128)(2,1)S(1)}, u32[]{:S(2)}, u32[]{:S(2)}) collective-permute-start(bf16[256,1280]{1,0:T(8,128)(2,1)S(1)} %shard_map.124.og_ref), channel_id=1, source_target_pairs={{0,1},{1,0},{2,3},{3,2},{4,5},{5,4},{6,7},{7,6},{8,9},{9,8},{10,11... | collective-permute-start | bytes 1966088 | tf_op jit(solution)/shard_map/ppermute | solution.py:291
  27.4 12.3 %collective-permute-start.3 = (f32[128,256]{1,0:T(8,128)S(1)}, f32[128,256]{1,0:T(8,128)S(1)}, u32[]{:S(2)}, u32[]{:S(2)}) collective-permute-start(f32[128,256]{1,0:T(8,128)S(1)} %shard_map.126.chip_ref), channel_id=1, source_target_pairs={{0,2},{1,3},{2,0},{3,1},{4,6},{5,7},{6,4},{7,5},{8,10},{9,11},{10,... | collective-permute-start | bytes 393224 | tf_op jit(solution)/shard_map/ppermute | solution.py:291
  40.2 1.4 %collective-permute-start.5 = (f32[192,128]{1,0:T(8,128)S(1)}, f32[192,128]{1,0:T(8,128)S(1)}, u32[]{:S(2)}, u32[]{:S(2)}) collective-permute-start(f32[192,128]{1,0:T(8,128)S(1)} %shard_map.128), channel_id=1, source_target_pairs={{0,1},{1,0},{2,3},{3,2},{4,5},{5,4},{6,7},{7,6},{8,9},{9,8},{10,11... | collective-permute-start | bytes 294920 | tf_op jit(solution)/shard_map/ppermute | solution.py:291
  41.6 4.2 %collective-permute-start.6 = (bf16[192,128]{1,0:T(8,128)(2,1)S(1)}, bf16[192,128]{1,0:T(8,128)(2,1)S(1)}, u32[]{:S(2)}, u32[]{:S(2)}) collective-permute-start(bf16[192,128]{1,0:T(8,128)(2,1)S(1)} %add_convert_fusion.mine_ref), channel_id=1, source_target_pairs={{0,2},{1,3},{2,0},{3,1},{4,6},{5,7},{6,4},{7,5},{8,10},{9,11},{10,... | collective-permute-start | bytes 147464 | tf_op jit(solution)/shard_map/ppermute | solution.py:291

commit v16 on v12

--- a/solution.py
+++ b/solution.py
@@ -10,6 +10,7 @@
 BLOCK = 1152
 CHIP_BLOCK = 512
 PARTS = 2
+SPLIT = 2
 MIB = 1 << 20
 ANY = pl.BlockSpec(memory_space=pl.ANY)
 VMEM = pl.BlockSpec(memory_space=pltpu.VMEM)
@@ -207,20 +208,23 @@
         start(group)
     og_v[...] = og_ref[...].T
 
-    def body(i, weights):
-        at = near.units(i)
-        acc_ref[at] = acc_in[at] + product(weights, og_v[...])
-
-    @pl.loop(0, heads)
-    def _(i):
-        body(i, head_ref[i])
+    turn = block // SPLIT
+
+    def body(i, ref, j):
+        at = pl.ds(pl.multiple_of(i * turn, turn), turn)
+        part = pl.ds(pl.multiple_of(j % SPLIT * turn, turn), turn)
+        acc_ref[at] = acc_in[at] + product(ref[j // SPLIT, part], og_v[...])
+
+    @pl.loop(0, heads * SPLIT)
+    def _(i):
+        body(i, head_ref, i)
 
     for group in rest:
         wait(group)
 
-    @pl.loop(0, w_v.shape[0])
-    def _(i):
-        body(heads + i, w_v[i])
+    @pl.loop(0, w_v.shape[0] * SPLIT)
+    def _(i):
+        body(heads * SPLIT + i, w_v, i)
 
     for group in later:
         wait(group)
@@ -237,24 +241,31 @@
     start(factors)
     og_v[...] = og_ref[...].T
 
-    def body(i, weights):
-        at = step.units(i)
-        hidden_grad = acc_ref[at] + product(weights, og_v[...])
+    turn = block // SPLIT
+
+    def body(i, ref, j):
+        at = pl.ds(pl.multiple_of(i * turn, turn), turn)
+        part = pl.ds(pl.multiple_of(j % SPLIT * turn, turn), turn)
+        hidden_grad = acc_ref[at] + product(ref[j // SPLIT, part], og_v[...])
         d_gate_v[at] = (hidden_grad * a_ref[at]).astype(BF16)
         d_up_v[at] = (hidden_grad * b_ref[at]).astype(BF16)
 
-    @pl.loop(0, heads)
-    def _(i):
-        @pl.when((i > 0) & (i < w_v.shape[0]))
+    @pl.loop(0, heads * SPLIT)
+    def _(i):
+        @pl.when(i == SPLIT)
         def _():
-            start(step.copies(heads + i, w_v.at[i], sems.at[i]))
-
-        body(i, head_ref[i])
-
-    @pl.loop(0, w_v.shape[0])
-    def _(i):
-        wait(step.copies(heads + i, w_v.at[i], sems.at[i]))
-        body(heads + i, w_v[i])
+            start(step.copies(heads + 1, w_v.at[1], sems.at[1]))
+
+        body(i, head_ref, i)
+
+    @pl.loop(0, w_v.shape[0] * SPLIT)
+    def _(i):
+        @pl.when(i % SPLIT == 0)
+        def _():
+            k = i // SPLIT
+            wait(step.copies(heads + k, w_v.at[k], sems.at[k]))
+
+        body(heads * SPLIT + i, w_v, i)
 
     wait(factors)
     gate_ref[...] = product(gf_ref[...], d_gate_v[...])

time: 37.7 us -> 38.4 us (1.019)
  Pallas kernels: 25.8 us -> 26.5 us
    pallas_call x1, Pallas kernels: 4.21 us -> 4.7 us  [fast(): call(near_kernel, (held, blocks(2)), [VMEM] * 3 + [ANY], [turned, blocks(...]
  transfers between devices with their start and end apart: 7 -> 7, of which waited for: 3 -> 3; matrix products, arithmetic and copies ran while one was open for 0% -> 0% of each run, Pallas kernels for 65% -> 66%
where the time goes in v16:
time: 38.4 us; the launch traced here: 38.3 us
  Pallas kernels  26.5 us (69%)
  starting transfers between devices  5.78 us (15%)
  waiting for transfers between devices  5.3 us (14%)
  between operations  0.71 us (2%)
    pallas_call x1, Pallas kernels, fast(): call(chip_features_kernel, (held, blocks(turns - 1)), [VMEM] * 3 + [ANY],...  9.49 us
    ppermute x7, starting transfers between devices, swap(): return lax.ppermute(array, 'tensor', [(i, i ^ bits) for i in range(4)])  5.78 us
    pallas_call x1, Pallas kernels, fast(): call(far_kernel, (narrow, narrow), [VMEM] * 3 + [ANY] + [VMEM] * 2 + [ANY...  5.66 us
    pallas_call x1, Pallas kernels, fast(): call(elementwise_kernel, (held, held, narrow, pltpu.VMEM((2 * rank, token...  5.35 us
    ppermute x7, waiting for transfers between devices, swap(): return lax.ppermute(array, 'tensor', [(i, i ^ bits) for i in range(4)])  5.3 us
    pallas_call x1, Pallas kernels, fast(): call(near_kernel, (held, blocks(2)), [VMEM] * 3 + [ANY], [turned, blocks(...  4.7 us
  transfers between devices with their start and end apart: 7, of which 3 were waited for; matrix products, arithmetic and copies ran while one was open for 0% of the time, Pallas kernels for 66%

profile of v16, /device:TPU:0, one launch (start us, length us, event | category | flops | bytes accessed | tf_op | source)
XLA Modules:
  0.0 38.3 jit_solution(15000099797514276054)
XLA Ops:
  0.6 0.5 %collective-permute-start.1 = (bf16[256,1280]{1,0:T(8,128)(2,1)}, bf16[256,1280]{1,0:T(8,128)(2,1)S(1)}, u32[]{:S(2)}, u32[]{:S(2)}) collective-permute-start(bf16[256,1280]{1,0:T(8,128)(2,1)} %og_hbm.1), channel_id=1, source_target_pairs={{0,1},{1,0},{2,3},{3,2},{4,5},{5,4},{6,7},{7,6},{8,9},{9,8},{10,11... | collective-permute-start | bytes 1966088 | tf_op jit(solution)/shard_map/ppermute | solution.py:313
  1.2 2.6 %collective-permute-start.2 = (bf16[256,1280]{1,0:T(8,128)(2,1)}, bf16[256,1280]{1,0:T(8,128)(2,1)S(1)}, u32[]{:S(2)}, u32[]{:S(2)}) collective-permute-start(bf16[256,1280]{1,0:T(8,128)(2,1)} %og_hbm.1), channel_id=1, source_target_pairs={{0,2},{1,3},{2,0},{3,1},{4,6},{5,7},{6,4},{7,5},{8,10},{9,11},{10,... | collective-permute-start | bytes 1966088 | tf_op jit(solution)/shard_map/ppermute | solution.py:313
  3.7 5.4 %shard_map.121 = (f32[4608,256]{1,0:T(8,128)S(1)}, f32[4608,256]{1,0:T(8,128)S(1)}, f32[64,256]{1,0:T(8,128)S(1)}, f32[128,256]{1,0:T(8,128)S(1)}, bf16[2,512,25...) custom-call(bf16[256,1280]{1,0:T(8,128)(2,1)} %x_hbm.1, bf16[256,1280]{1,0:T(8,128)(2,1)} %og_hbm.1, ...), custom_call_target="tpu_custom_call" | custom-call | flops 754974720 | bytes 4718592 | tf_op jit(solution)/shard_map/pallas_call | solution.py:343
  9.1 0.2 collective-permute-start
  9.3 0.0 collective-permute-done.1.mate_ref
  9.3 9.5 %shard_map.122 = (f32[4608,256]{1,0:T(8,128)S(1)}, bf16[3,1152,1280]{2,1,0:T(8,128)(2,1)S(1)}) custom-call(bf16[1280,256]{1,0:T(8,128)(2,1)S(1)} %get-tuple-element.16.own_ref, bf16[256,1280]{1,0:T(8,128)(2,1)S(1)} %collective-permute-done.1.mate_ref, bf16[2,512,2560]{2,1,0:T(8,128)(2,1)S(1)} %get-tuple-element.17.head_ref, bf16[4608,5120]{1,0:T(8,128)(2,1)} %w_hbm.7), custom_call_target="tpu_custom_call" | custom-call | flops 6039797760 | bytes 23592960 | tf_op jit(solution)/shard_map/pallas_call | solution.py:374
  18.8 0.0 collective-permute-done.theirs_ref
  18.8 0.4 %collective-permute-done.2.array_ref = bf16[256,1280]{1,0:T(8,128)(2,1)S(1)} collective-permute-done((bf16[256,1280]{1,0:T(8,128)(2,1)}, bf16[256,1280]{1,0:T(8,128)(2,1)S(1)}, u32[]{:S(2)}, u32[]{:S(2)}) %collective-permute-start.2) | collective-permute-done | bytes 655392 | tf_op jit(solution)/shard_map/ppermute | solution.py:313
  19.3 0.0 collective-permute-start.4
  19.3 4.7 %shard_map.125 = (f32[4608,256]{1,0:T(8,128)S(1)}, bf16[2,1152,1280]{2,1,0:T(8,128)(2,1)S(1)}) custom-call(f32[4608,256]{1,0:T(8,128)S(1)} %get-tuple-element.19.acc_in, bf16[256,1280]{1,0:T(8,128)(2,1)S(1)} %shard_map.124.og_ref, bf16[3,1152,1280]{2,1,0:T(8,128)(2,1)S(1)} %get-tuple-element.18.token_ref.head_ref, ...), custom_call_target="tpu_custom_call", output_to_operand_aliasing={{0}: (0, {})} | custom-call | flops 3019898880 | bytes 11796480 | tf_op jit(solution)/shard_map/pallas_call | solution.py:402
  24.0 1.8 %collective-permute-start.3 = (f32[128,256]{1,0:T(8,128)S(1)}, f32[128,256]{1,0:T(8,128)S(1)}, u32[]{:S(2)}, u32[]{:S(2)}) collective-permute-start(f32[128,256]{1,0:T(8,128)S(1)} %shard_map.126.chip_ref), channel_id=1, source_target_pairs={{0,2},{1,3},{2,0},{3,1},{4,6},{5,7},{6,4},{7,5},{8,10},{9,11},{10,... | collective-permute-start | bytes 393224 | tf_op jit(solution)/shard_map/ppermute | solution.py:313
  25.8 0.0 collective-permute-done.4.og_ref
  25.8 5.7 %shard_map.127 = (f32[64,256]{1,0:T(8,128)S(1)}, f32[64,256]{1,0:T(8,128)S(1)}) custom-call(f32[4608,256]{1,0:T(8,128)S(1)} %get-tuple-element.21.acc_ref, bf16[256,1280]{1,0:T(8,128)(2,1)S(1)} %collective-permute-done.4.og_ref, bf16[2,1152,1280]{2,1,0:T(8,128)(2,1)S(1)} %get-tuple-element.20.token_ref.head_ref, bf16[4608,5120]{1,0:T(8,128)(2,1)} %w_hbm.7, ...), custom_call_target="tpu_custom_call" | custom-call | flops 3019898880 | bytes 11796480 | tf_op jit(solution)/shard_map/pallas_call | solution.py:416
  31.5 0.0 collective-permute-done.3.other_ref
  31.5 0.5 %shard_map.128 = f32[192,128]{1,0:T(8,128)S(1)} custom-call(f32[128,256]{1,0:T(8,128)S(1)} %shard_map.126.chip_ref, f32[128,256]{1,0:T(8,128)S(1)} %collective-permute-done.3.other_ref, f32[64,256]{1,0:T(8,128)S(1)} %get-tuple-element.24.gate_ref, f32[64,256]{1,0:T(8,128)S(1)} %get-tuple-element.25.up_ref, f32[64,256]{1,0:T(8,128)S(1)} %get-tuple-element.26.ph_ref), custom_call_target="tpu_custom_call" | custom-call | tf_op jit(solution)/shard_map/pallas_call | solution.py:425
  32.0 0.3 collective-permute-start.5
  32.3 1.1 %collective-permute-done.5 = f32[192,128]{1,0:T(8,128)S(1)} collective-permute-done((f32[192,128]{1,0:T(8,128)S(1)}, f32[192,128]{1,0:T(8,128)S(1)}, u32[]{:S(2)}, u32[]{:S(2)}) %collective-permute-start.5) | collective-permute-done | bytes 98336 | tf_op jit(solution)/shard_map/ppermute | solution.py:313
  33.4 0.3 collective-permute-start.6
  33.7 3.8 %collective-permute-done.6.theirs_ref = bf16[192,128]{1,0:T(8,128)(2,1)S(1)} collective-permute-done((bf16[192,128]{1,0:T(8,128)(2,1)S(1)}, bf16[192,128]{1,0:T(8,128)(2,1)S(1)}, u32[]{:S(2)}, u32[]{:S(2)}) %collective-permute-start.6) | collective-permute-done | bytes 49184 | tf_op jit(solution)/shard_map/ppermute | solution.py:313
  37.5 0.7 %shard_map.129 = (f32[2,64,64]{2,1,0:T(8,128)}, f32[2,64,64]{2,1,0:T(8,128)}, f32[2,64,64]{2,1,0:T(8,128)}) custom-call(bf16[192,128]{1,0:T(8,128)(2,1)S(1)} %add_convert_fusion.mine_ref, bf16[192,128]{1,0:T(8,128)(2,1)S(1)} %collective-permute-done.6.theirs_ref), custom_call_target="tpu_custom_call" | custom-call | tf_op jit(solution)/shard_map/pallas_call | solution.py:430
  (4 shorter events, 0.0 us)
Async XLA Ops:
  0.6 8.7 %collective-permute-start.1 = (bf16[256,1280]{1,0:T(8,128)(2,1)}, bf16[256,1280]{1,0:T(8,128)(2,1)S(1)}, u32[]{:S(2)}, u32[]{:S(2)}) collective-permute-start(bf16[256,1280]{1,0:T(8,128)(2,1)} %og_hbm.1), channel_id=1, source_target_pairs={{0,1},{1,0},{2,3},{3,2},{4,5},{5,4},{6,7},{7,6},{8,9},{9,8},{10,11... | collective-permute-start | bytes 1966088 | tf_op jit(solution)/shard_map/ppermute | solution.py:313
  1.2 18.1 %collective-permute-start.2 = (bf16[256,1280]{1,0:T(8,128)(2,1)}, bf16[256,1280]{1,0:T(8,128)(2,1)S(1)}, u32[]{:S(2)}, u32[]{:S(2)}) collective-permute-start(bf16[256,1280]{1,0:T(8,128)(2,1)} %og_hbm.1), channel_id=1, source_target_pairs={{0,2},{1,3},{2,0},{3,1},{4,6},{5,7},{6,4},{7,5},{8,10},{9,11},{10,... | collective-permute-start | bytes 1966088 | tf_op jit(solution)/shard_map/ppermute | solution.py:313
  9.1 9.7 %collective-permute-start = (f32[128,256]{1,0:T(8,128)S(1)}, f32[128,256]{1,0:T(8,128)S(1)}, u32[]{:S(2)}, u32[]{:S(2)}) collective-permute-start(f32[128,256]{1,0:T(8,128)S(1)} %get-tuple-element.15.mine_ref), channel_id=1, source_target_pairs={{0,1},{1,0},{2,3},{3,2},{4,5},{5,4},{6,7},{7,6},{8,9},{9,8},{10,11... | collective-permute-start | bytes 393224 | tf_op jit(solution)/shard_map/ppermute | solution.py:313
  19.3 6.5 %collective-permute-start.4 = (bf16[256,1280]{1,0:T(8,128)(2,1)S(1)}, bf16[256,1280]{1,0:T(8,128)(2,1)S(1)}, u32[]{:S(2)}, u32[]{:S(2)}) collective-permute-start(bf16[256,1280]{1,0:T(8,128)(2,1)S(1)} %shard_map.124.og_ref), channel_id=1, source_target_pairs={{0,1},{1,0},{2,3},{3,2},{4,5},{5,4},{6,7},{7,6},{8,9},{9,8},{10,11... | collective-permute-start | bytes 1966088 | tf_op jit(solution)/shard_map/ppermute | solution.py:313
  24.0 7.5 %collective-permute-start.3 = (f32[128,256]{1,0:T(8,128)S(1)}, f32[128,256]{1,0:T(8,128)S(1)}, u32[]{:S(2)}, u32[]{:S(2)}) collective-permute-start(f32[128,256]{1,0:T(8,128)S(1)} %shard_map.126.chip_ref), channel_id=1, source_target_pairs={{0,2},{1,3},{2,0},{3,1},{4,6},{5,7},{6,4},{7,5},{8,10},{9,11},{10,... | collective-permute-start | bytes 393224 | tf_op jit(solution)/shard_map/ppermute | solution.py:313
  32.0 1.4 %collective-permute-start.5 = (f32[192,128]{1,0:T(8,128)S(1)}, f32[192,128]{1,0:T(8,128)S(1)}, u32[]{:S(2)}, u32[]{:S(2)}) collective-permute-start(f32[192,128]{1,0:T(8,128)S(1)} %shard_map.128), channel_id=1, source_target_pairs={{0,1},{1,0},{2,3},{3,2},{4,5},{5,4},{6,7},{7,6},{8,9},{9,8},{10,11... | collective-permute-start | bytes 294920 | tf_op jit(solution)/shard_map/ppermute | solution.py:313
  33.4 4.2 %collective-permute-start.6 = (bf16[192,128]{1,0:T(8,128)(2,1)S(1)}, bf16[192,128]{1,0:T(8,128)(2,1)S(1)}, u32[]{:S(2)}, u32[]{:S(2)}) collective-permute-start(bf16[192,128]{1,0:T(8,128)(2,1)S(1)} %add_convert_fusion.mine_ref), channel_id=1, source_target_pairs={{0,2},{1,3},{2,0},{3,1},{4,6},{5,7},{6,4},{7,5},{8,10},{9,11},{10,... | collective-permute-start | bytes 147464 | tf_op jit(solution)/shard_map/ppermute | solution.py:313

commit v17 on v12

--- a/solution.py
+++ b/solution.py
@@ -9,7 +9,7 @@
 LEN = 128
 BLOCK = 1152
 CHIP_BLOCK = 512
-PARTS = 2
+PARTS = 4
 MIB = 1 << 20
 ANY = pl.BlockSpec(memory_space=pl.ANY)
 VMEM = pl.BlockSpec(memory_space=pltpu.VMEM)

time: 37.7 us -> 38.2 us (1.013)
  Pallas kernels: 25.8 us -> 26.8 us
  waiting for transfers between devices: 5.13 us -> 4.3 us
    ppermute x7, waiting for transfers between devices: 5.13 us -> 4.3 us  [swap(): return lax.ppermute(array, 'tensor', [(i, i ^ bits) for i in range(4)])]
  transfers between devices with their start and end apart: 7 -> 7, of which waited for: 3 -> 2; matrix products, arithmetic and copies ran while one was open for 0% -> 0% of each run, Pallas kernels for 65% -> 67%
where the time goes in v17:
time: 38.2 us; the launch traced here: 38 us
  Pallas kernels  26.8 us (70%)
  starting transfers between devices  6.19 us (16%)
  waiting for transfers between devices  4.3 us (11%)
  between operations  0.73 us (2%)
    pallas_call x1, Pallas kernels, fast(): call(chip_features_kernel, (held, blocks(turns - 1)), [VMEM] * 3 + [ANY],...  9.7 us
    ppermute x7, starting transfers between devices, swap(): return lax.ppermute(array, 'tensor', [(i, i ^ bits) for i in range(4)])  6.19 us
    pallas_call x1, Pallas kernels, fast(): call(elementwise_kernel, (held, held, narrow, pltpu.VMEM((2 * rank, token...  5.72 us
    pallas_call x1, Pallas kernels, fast(): call(far_kernel, (narrow, narrow), [VMEM] * 3 + [ANY] + [VMEM] * 2 + [ANY...  5.61 us
    pallas_call x1, Pallas kernels, fast(): call(near_kernel, (held, blocks(2)), [VMEM] * 3 + [ANY], [turned, blocks(...  4.48 us
    ppermute x7, waiting for transfers between devices, swap(): return lax.ppermute(array, 'tensor', [(i, i ^ bits) for i in range(4)])  4.3 us
  transfers between devices with their start and end apart: 7, of which 2 were waited for; matrix products, arithmetic and copies ran while one was open for 0% of the time, Pallas kernels for 67%

profile of v17, /device:TPU:0, one launch (start us, length us, event | category | flops | bytes accessed | tf_op | source)
XLA Modules:
  0.0 38.0 jit_solution(8548247137090093766)
XLA Ops:
  0.6 0.5 %collective-permute-start.1 = (bf16[256,1280]{1,0:T(8,128)(2,1)}, bf16[256,1280]{1,0:T(8,128)(2,1)S(1)}, u32[]{:S(2)}, u32[]{:S(2)}) collective-permute-start(bf16[256,1280]{1,0:T(8,128)(2,1)} %og_hbm.1), channel_id=1, source_target_pairs={{0,1},{1,0},{2,3},{3,2},{4,5},{5,4},{6,7},{7,6},{8,9},{9,8},{10,11... | collective-permute-start | bytes 1966088 | tf_op jit(solution)/shard_map/ppermute | solution.py:302
  1.2 2.6 %collective-permute-start.2 = (bf16[256,1280]{1,0:T(8,128)(2,1)}, bf16[256,1280]{1,0:T(8,128)(2,1)S(1)}, u32[]{:S(2)}, u32[]{:S(2)}) collective-permute-start(bf16[256,1280]{1,0:T(8,128)(2,1)} %og_hbm.1), channel_id=1, source_target_pairs={{0,2},{1,3},{2,0},{3,1},{4,6},{5,7},{6,4},{7,5},{8,10},{9,11},{10,... | collective-permute-start | bytes 1966088 | tf_op jit(solution)/shard_map/ppermute | solution.py:302
  3.7 5.7 %shard_map.121 = (f32[4608,256]{1,0:T(8,128)S(1)}, f32[4608,256]{1,0:T(8,128)S(1)}, f32[64,256]{1,0:T(8,128)S(1)}, f32[128,256]{1,0:T(8,128)S(1)}, bf16[2,512,25...) custom-call(bf16[256,1280]{1,0:T(8,128)(2,1)} %x_hbm.1, bf16[256,1280]{1,0:T(8,128)(2,1)} %og_hbm.1, ...), custom_call_target="tpu_custom_call" | custom-call | flops 754974720 | bytes 4718592 | tf_op jit(solution)/shard_map/pallas_call | solution.py:332
  9.4 0.2 collective-permute-start
  9.7 0.0 collective-permute-done.1.mate_ref
  9.7 9.7 %shard_map.122 = (f32[4608,256]{1,0:T(8,128)S(1)}, bf16[3,1152,1280]{2,1,0:T(8,128)(2,1)S(1)}) custom-call(bf16[1280,256]{1,0:T(8,128)(2,1)S(1)} %get-tuple-element.16.own_ref, bf16[256,1280]{1,0:T(8,128)(2,1)S(1)} %collective-permute-done.1.mate_ref, bf16[2,512,2560]{2,1,0:T(8,128)(2,1)S(1)} %get-tuple-element.17.head_ref, bf16[4608,5120]{1,0:T(8,128)(2,1)} %w_hbm.7), custom_call_target="tpu_custom_call" | custom-call | flops 6039797760 | bytes 23592960 | tf_op jit(solution)/shard_map/pallas_call | solution.py:363
  19.4 0.0 collective-permute-done.theirs_ref
  19.4 0.0 collective-permute-done.2.array_ref
  19.4 0.4 %collective-permute-start.4 = (bf16[256,1280]{1,0:T(8,128)(2,1)S(1)}, bf16[256,1280]{1,0:T(8,128)(2,1)S(1)}, u32[]{:S(2)}, u32[]{:S(2)}) collective-permute-start(bf16[256,1280]{1,0:T(8,128)(2,1)S(1)} %shard_map.124.og_ref), channel_id=1, source_target_pairs={{0,1},{1,0},{2,3},{3,2},{4,5},{5,4},{6,7},{7,6},{8,9},{9,8},{10,11... | collective-permute-start | bytes 1966088 | tf_op jit(solution)/shard_map/ppermute | solution.py:302
  19.9 4.5 %shard_map.125 = (f32[4608,256]{1,0:T(8,128)S(1)}, bf16[2,1152,1280]{2,1,0:T(8,128)(2,1)S(1)}) custom-call(f32[4608,256]{1,0:T(8,128)S(1)} %get-tuple-element.19.acc_in, bf16[256,1280]{1,0:T(8,128)(2,1)S(1)} %shard_map.124.og_ref, bf16[3,1152,1280]{2,1,0:T(8,128)(2,1)S(1)} %get-tuple-element.18.token_ref.head_ref, ...), custom_call_target="tpu_custom_call", output_to_operand_aliasing={{0}: (0, {})} | custom-call | flops 3019898880 | bytes 11796480 | tf_op jit(solution)/shard_map/pallas_call | solution.py:391
  24.4 1.2 %collective-permute-start.3 = (f32[128,256]{1,0:T(8,128)S(1)}, f32[128,256]{1,0:T(8,128)S(1)}, u32[]{:S(2)}, u32[]{:S(2)}) collective-permute-start(f32[128,256]{1,0:T(8,128)S(1)} %shard_map.126.chip_ref), channel_id=1, source_target_pairs={{0,2},{1,3},{2,0},{3,1},{4,6},{5,7},{6,4},{7,5},{8,10},{9,11},{10,... | collective-permute-start | bytes 393224 | tf_op jit(solution)/shard_map/ppermute | solution.py:302
  25.6 0.0 collective-permute-done.4.og_ref
  25.6 5.6 %shard_map.127 = (f32[64,256]{1,0:T(8,128)S(1)}, f32[64,256]{1,0:T(8,128)S(1)}) custom-call(f32[4608,256]{1,0:T(8,128)S(1)} %get-tuple-element.21.acc_ref, bf16[256,1280]{1,0:T(8,128)(2,1)S(1)} %collective-permute-done.4.og_ref, bf16[2,1152,1280]{2,1,0:T(8,128)(2,1)S(1)} %get-tuple-element.20.token_ref.head_ref, bf16[4608,5120]{1,0:T(8,128)(2,1)} %w_hbm.7, ...), custom_call_target="tpu_custom_call" | custom-call | flops 3019898880 | bytes 11796480 | tf_op jit(solution)/shard_map/pallas_call | solution.py:405
  31.2 0.0 collective-permute-done.3.other_ref
  31.2 0.5 %shard_map.128 = f32[192,128]{1,0:T(8,128)S(1)} custom-call(f32[128,256]{1,0:T(8,128)S(1)} %shard_map.126.chip_ref, f32[128,256]{1,0:T(8,128)S(1)} %collective-permute-done.3.other_ref, f32[64,256]{1,0:T(8,128)S(1)} %get-tuple-element.24.gate_ref, f32[64,256]{1,0:T(8,128)S(1)} %get-tuple-element.25.up_ref, f32[64,256]{1,0:T(8,128)S(1)} %get-tuple-element.26.ph_ref), custom_call_target="tpu_custom_call" | custom-call | tf_op jit(solution)/shard_map/pallas_call | solution.py:414
  31.7 0.3 collective-permute-start.5
  32.0 1.1 %collective-permute-done.5 = f32[192,128]{1,0:T(8,128)S(1)} collective-permute-done((f32[192,128]{1,0:T(8,128)S(1)}, f32[192,128]{1,0:T(8,128)S(1)}, u32[]{:S(2)}, u32[]{:S(2)}) %collective-permute-start.5) | collective-permute-done | bytes 98336 | tf_op jit(solution)/shard_map/ppermute | solution.py:302
  33.1 0.9 %collective-permute-start.6 = (bf16[192,128]{1,0:T(8,128)(2,1)S(1)}, bf16[192,128]{1,0:T(8,128)(2,1)S(1)}, u32[]{:S(2)}, u32[]{:S(2)}) collective-permute-start(bf16[192,128]{1,0:T(8,128)(2,1)S(1)} %add_convert_fusion.mine_ref), channel_id=1, source_target_pairs={{0,2},{1,3},{2,0},{3,1},{4,6},{5,7},{6,4},{7,5},{8,10},{9,11},{10,... | collective-permute-start | bytes 147464 | tf_op jit(solution)/shard_map/ppermute | solution.py:302
  34.0 3.2 %collective-permute-done.6.theirs_ref = bf16[192,128]{1,0:T(8,128)(2,1)S(1)} collective-permute-done((bf16[192,128]{1,0:T(8,128)(2,1)S(1)}, bf16[192,128]{1,0:T(8,128)(2,1)S(1)}, u32[]{:S(2)}, u32[]{:S(2)}) %collective-permute-start.6) | collective-permute-done | bytes 49184 | tf_op jit(solution)/shard_map/ppermute | solution.py:302
  37.3 0.7 %shard_map.129 = (f32[2,64,64]{2,1,0:T(8,128)}, f32[2,64,64]{2,1,0:T(8,128)}, f32[2,64,64]{2,1,0:T(8,128)}) custom-call(bf16[192,128]{1,0:T(8,128)(2,1)S(1)} %add_convert_fusion.mine_ref, bf16[192,128]{1,0:T(8,128)(2,1)S(1)} %collective-permute-done.6.theirs_ref), custom_call_target="tpu_custom_call" | custom-call | tf_op jit(solution)/shard_map/pallas_call | solution.py:419
  (4 shorter events, 0.0 us)
Async XLA Ops:
  0.6 9.0 %collective-permute-start.1 = (bf16[256,1280]{1,0:T(8,128)(2,1)}, bf16[256,1280]{1,0:T(8,128)(2,1)S(1)}, u32[]{:S(2)}, u32[]{:S(2)}) collective-permute-start(bf16[256,1280]{1,0:T(8,128)(2,1)} %og_hbm.1), channel_id=1, source_target_pairs={{0,1},{1,0},{2,3},{3,2},{4,5},{5,4},{6,7},{7,6},{8,9},{9,8},{10,11... | collective-permute-start | bytes 1966088 | tf_op jit(solution)/shard_map/ppermute | solution.py:302
  1.2 18.3 %collective-permute-start.2 = (bf16[256,1280]{1,0:T(8,128)(2,1)}, bf16[256,1280]{1,0:T(8,128)(2,1)S(1)}, u32[]{:S(2)}, u32[]{:S(2)}) collective-permute-start(bf16[256,1280]{1,0:T(8,128)(2,1)} %og_hbm.1), channel_id=1, source_target_pairs={{0,2},{1,3},{2,0},{3,1},{4,6},{5,7},{6,4},{7,5},{8,10},{9,11},{10,... | collective-permute-start | bytes 1966088 | tf_op jit(solution)/shard_map/ppermute | solution.py:302
  9.4 9.9 %collective-permute-start = (f32[128,256]{1,0:T(8,128)S(1)}, f32[128,256]{1,0:T(8,128)S(1)}, u32[]{:S(2)}, u32[]{:S(2)}) collective-permute-start(f32[128,256]{1,0:T(8,128)S(1)} %get-tuple-element.15.mine_ref), channel_id=1, source_target_pairs={{0,1},{1,0},{2,3},{3,2},{4,5},{5,4},{6,7},{7,6},{8,9},{9,8},{10,11... | collective-permute-start | bytes 393224 | tf_op jit(solution)/shard_map/ppermute | solution.py:302
  19.4 6.1 %collective-permute-start.4 = (bf16[256,1280]{1,0:T(8,128)(2,1)S(1)}, bf16[256,1280]{1,0:T(8,128)(2,1)S(1)}, u32[]{:S(2)}, u32[]{:S(2)}) collective-permute-start(bf16[256,1280]{1,0:T(8,128)(2,1)S(1)} %shard_map.124.og_ref), channel_id=1, source_target_pairs={{0,1},{1,0},{2,3},{3,2},{4,5},{5,4},{6,7},{7,6},{8,9},{9,8},{10,11... | collective-permute-start | bytes 1966088 | tf_op jit(solution)/shard_map/ppermute | solution.py:302
  24.4 6.8 %collective-permute-start.3 = (f32[128,256]{1,0:T(8,128)S(1)}, f32[128,256]{1,0:T(8,128)S(1)}, u32[]{:S(2)}, u32[]{:S(2)}) collective-permute-start(f32[128,256]{1,0:T(8,128)S(1)} %shard_map.126.chip_ref), channel_id=1, source_target_pairs={{0,2},{1,3},{2,0},{3,1},{4,6},{5,7},{6,4},{7,5},{8,10},{9,11},{10,... | collective-permute-start | bytes 393224 | tf_op jit(solution)/shard_map/ppermute | solution.py:302
  31.7 1.4 %collective-permute-start.5 = (f32[192,128]{1,0:T(8,128)S(1)}, f32[192,128]{1,0:T(8,128)S(1)}, u32[]{:S(2)}, u32[]{:S(2)}) collective-permute-start(f32[192,128]{1,0:T(8,128)S(1)} %shard_map.128), channel_id=1, source_target_pairs={{0,1},{1,0},{2,3},{3,2},{4,5},{5,4},{6,7},{7,6},{8,9},{9,8},{10,11... | collective-permute-start | bytes 294920 | tf_op jit(solution)/shard_map/ppermute | solution.py:302
  33.1 4.2 %collective-permute-start.6 = (bf16[192,128]{1,0:T(8,128)(2,1)S(1)}, bf16[192,128]{1,0:T(8,128)(2,1)S(1)}, u32[]{:S(2)}, u32[]{:S(2)}) collective-permute-start(bf16[192,128]{1,0:T(8,128)(2,1)S(1)} %add_convert_fusion.mine_ref), channel_id=1, source_target_pairs={{0,2},{1,3},{2,0},{3,1},{4,6},{5,7},{6,4},{7,5},{8,10},{9,11},{10,... | collective-permute-start | bytes 147464 | tf_op jit(solution)/shard_map/ppermute | solution.py:302
